TPU v7x, 32 devices: a whole 2x2x4 slice. The times are simulated.
32 devices in a mesh: shard: 8 (over z, x), tensor: 4 (over y, core).
Axes of the slice: x: 2, y: 2, z: 4, core: 2. Of those that a mesh axis runs over, the one named last changes fastest.
Arguments:
- acts: bfloat16 [16384, 2048], P('shard', 'tensor'), may hold values from -6 to 6
- out_grad: bfloat16 [16384, 1920], P('shard'), may hold values from -6 to 6
- sample_rows: int32 [512], P('shard'), may hold values from 0 to 2047
- own_a: int32 [4, 4], replicated, may hold values from 0 to 3, each once within a row
- own_g: int32 [4, 5], replicated, may hold values from 0 to 4, each once within a row
- a_state: float32 [4, 4, 128, 128], P('tensor'), as said below
- g_state: float32 [4, 5, 96, 96], P('tensor'), as said below
- momentum: float32 [1920, 2048], P('shard', 'tensor'), may hold values from -6 to 6
- weight: float32 [1920, 2048], P('shard', 'tensor'), may hold values from -6 to 6
Outputs:
- a_state_new: float32 [4, 4, 128, 128], P('tensor')
- g_state_new: float32 [4, 5, 96, 96], P('tensor')
- momentum_new: float32 [1920, 2048], P('shard', 'tensor')
- weight_new: float32 [1920, 2048], P('shard', 'tensor')
- weight_bf16: bfloat16 [1920, 2048], P(None, 'tensor')
Inputs may be any that keep to these rules, and one draw needn't show every extreme that they name: `own_a`: slot s of a group is owned by the shard index s times the whole part of the shard axis's size over the group's number of slots. `own_g`: slot s of a group is owned by the shard index s times the whole part of the shard axis's size over the group's number of slots. `a_state`: every slot is symmetric positive definite. `g_state`: every slot is symmetric positive definite.
All inputs are finite; a program needn't handle non-finite values. Where the computation divides by a largest or mean magnitude, that divisor is 1e-20 or more.
Results may differ from a plain program's by a relative error of at most 0.0004.
Values may be sent and summed in bfloat16 or wider, within the bound.
No kernel may reach another device: no remote copies, remote signals or barrier semaphores. Data moves between devices by JAX's collectives and lax.ppermute only.
A program may use at most 64 MiB of HBM per device.

v0:
```python
import jax
import jax.numpy as jnp
from jax import lax
from jax.sharding import PartitionSpec as P

NS_IT = 5


factor_decay = 0.8
damping_rate = 0.03
momentum_rate = 0.9
decay_rate = 0.01
learn_rate = 0.05
epsilon_sq = 1e-06
highest = lax.Precision.HIGHEST


def newton_inverse(factor):
    width = factor.shape[-1]
    identity = jnp.eye(width, dtype=jnp.float32)
    trace_mean = jnp.trace(factor, axis1=-2, axis2=-1) / width
    damped = factor + damping_rate * trace_mean[:, None, None] * identity
    bound = jnp.max(jnp.sum(jnp.abs(damped), axis=-1), axis=-1)
    guess = identity[None] / bound[:, None, None]
    for iteration in range(NS_IT):
        product = jnp.einsum("bij,bjk->bik", damped, guess, precision=highest)
        guess = jnp.einsum("bij,bjk->bik", guess, 2.0 * identity - product, precision=highest)
    return guess


def local_stats(rows, width):
    blocks = rows.reshape(rows.shape[0], -1, width)
    return jnp.einsum("sbi,sbj->bij", blocks, blocks, preferred_element_type=jnp.float32)


def owner_part(slots, shard_pos, shard_count):
    count = slots.shape[0]
    stride = shard_count // count
    slot_pos = jnp.minimum(shard_pos // stride, count - 1)
    mine = lax.dynamic_index_in_dim(slots, slot_pos, 0, keepdims=True)
    inverse = newton_inverse(mine)
    marker = (jnp.arange(count, dtype=jnp.int32) * stride == shard_pos).astype(jnp.float32)
    return marker[:, None, None] * inverse


def local(acts, out_grad, sample_rows, own_a, own_g, a_state, g_state, momentum, weight):
    shard_count = lax.axis_size("shard")
    tensor_count = lax.axis_size("tensor")
    shard_pos = lax.axis_index("shard")
    tensor_pos = lax.axis_index("tensor")
    block_a = a_state.shape[-1]
    block_g = g_state.shape[-1]
    samples = sample_rows.shape[0] * shard_count
    fresh_share = (1.0 - factor_decay) / samples
    picked_a = jnp.take(acts, sample_rows, axis=0)
    picked_g = jnp.take(out_grad, sample_rows, axis=0)
    group_cols = out_grad.shape[1] // tensor_count
    picked_g = lax.dynamic_slice_in_dim(picked_g, tensor_pos * group_cols, group_cols, 1)
    stats_a = local_stats(picked_a, block_a)
    stats_g = local_stats(picked_g, block_g)
    row_a = lax.dynamic_index_in_dim(own_a, tensor_pos, 0, keepdims=False)
    row_g = lax.dynamic_index_in_dim(own_g, tensor_pos, 0, keepdims=False)
    select_a = (row_a[None, :] == jnp.arange(row_a.shape[0], dtype=jnp.int32)[:, None]).astype(
        jnp.float32
    )
    select_g = (row_g[None, :] == jnp.arange(row_g.shape[0], dtype=jnp.int32)[:, None]).astype(
        jnp.float32
    )
    summed_a, summed_g = lax.psum((fresh_share * stats_a, fresh_share * stats_g), "shard")
    stored_a = jnp.einsum("sb,sij->bij", select_a, a_state[0], precision=highest)
    stored_g = jnp.einsum("sb,sij->bij", select_g, g_state[0], precision=highest)
    fac_a = factor_decay * stored_a + summed_a
    fac_g = factor_decay * stored_g + summed_g
    slots_a = jnp.einsum("sb,bij->sij", select_a, fac_a, precision=highest)
    slots_g = jnp.einsum("sb,bij->sij", select_g, fac_g, precision=highest)
    new_a_state = slots_a[None]
    new_g_state = slots_g[None]
    slot_inv_a, slot_inv_g = lax.psum(
        (owner_part(slots_a, shard_pos, shard_count), owner_part(slots_g, shard_pos, shard_count)),
        "shard",
    )
    inv_a = jnp.einsum("sb,sij->bij", select_a, slot_inv_a, precision=highest)
    local_inv_g = jnp.einsum("sb,sij->bij", select_g, slot_inv_g, precision=highest)
    inv_g = lax.all_gather(local_inv_g, "tensor", axis=0, tiled=True)
    raw_product = lax.dot_general(
        out_grad, acts, (((0,), (0,)), ((), ())), preferred_element_type=jnp.float32
    )
    left_done = jnp.einsum(
        "bij,bjd->bid", inv_g, raw_product.reshape(inv_g.shape[0], block_g, -1), precision=highest
    ).reshape(raw_product.shape)
    owned_rows = lax.psum_scatter(left_done, "shard", scatter_dimension=0, tiled=True)
    precon = jnp.einsum(
        "qbi,bij->qbj",
        owned_rows.reshape(owned_rows.shape[0], -1, block_a),
        inv_a,
        precision=highest,
    ).reshape(owned_rows.shape)
    square_total = lax.psum(jnp.sum(precon * precon), ("shard", "tensor"))
    mean_sq = square_total / (momentum.shape[0] * shard_count * momentum.shape[1] * tensor_count)
    update = precon / jnp.sqrt(mean_sq + epsilon_sq)
    momentum_new = momentum_rate * momentum + update + decay_rate * weight
    weight_new = weight - learn_rate * momentum_new
    gathered = lax.all_gather(weight_new.astype(jnp.bfloat16), "shard", axis=0, tiled=True)
    return (new_a_state, new_g_state, momentum_new, weight_new, gathered)


def solution(mesh):
    return jax.shard_map(
        local,
        mesh=mesh,
        in_specs=(
            P("shard", "tensor"),
            P("shard", None),
            P("shard"),
            P(),
            P(),
            P("tensor", None, None, None),
            P("tensor", None, None, None),
            P("shard", "tensor"),
            P("shard", "tensor"),
        ),
        out_specs=(
            P("tensor", None, None, None),
            P("tensor", None, None, None),
            P("shard", "tensor"),
            P("shard", "tensor"),
            P(None, "tensor"),
        ),
        check_vma=False,
    )
```

profile of v0, /device:TPU:0, one launch (start us, length us, event | category | flops | bytes accessed | tf_op | source)
XLA Modules:
  0.0 385.5 jit_solution(14376181277049762788)
XLA Ops:
  7.3 0.8 compare_and_fusion
  8.1 0.7 compare_select_fusion
  8.8 0.7 gather_fusion
  9.5 5.2 %gather_fusion.1 = bf16[64,1920]{1,0:T(8,128)(2,1)S(1)} fusion(bf16[2048,1920]{1,0:T(8,128)(2,1)} %param.10, s32[1024]{0:T(1024)S(1)} %pad_clamp_fusion), kind=kCustom, calls=%fused_computation.1 | custom fusion | bytes 491776 | tf_op jit(solution)/shard_map/jit(_take)/gather | solution.py:56
  14.7 1.0 convolution_multiply_fusion
  15.9 0.9 convolution_multiply_fusion.1
  17.0 0.7 fusion.42
  17.7 0.7 fusion.43
  19.4 72.7 %all-reduce.7.cloned.1.call-done = (f32[4,128,128]{2,1,0:T(8,128)}, f32[5,96,96]{2,1,0:T(8,128)}) async-done(((f32[4,128,128]{2,1,0:T(8,128)}, f32[5,96,96]{2,1,0:T(8,128)}), (f32[4,128,128]{2,1,0:T(8,128)}, f32[5,96,96]{2,1,0:T(8,128)})) %all-reduce.7.cloned.1.call-update) | async-done | bytes 446480 | tf_op jit(solution)/shard_map/psum | solution.py:69
  92.1 1.0 fusion.11
  93.1 0.6 fusion.9
  93.7 0.7 select_reduce_fusion
  95.1 1.0 abs_reduce_fusion
  99.5 1.0 fusion.14
  101.1 0.7 select_reduce_fusion.1
  102.4 0.8 abs_reduce_fusion.1
  106.4 0.8 broadcast_multiply_fusion.1
  107.3 0.8 broadcast_multiply_fusion
  108.4 9.4 %fusion.63 = f32[1920,512]{1,0:T(8,128)} fusion(bf16[2048,1920]{1,0:T(8,128)(2,1)} %param.10, bf16[2048,512]{1,0:T(8,128)(2,1)S(1)} %copy-done), kind=kOutput, calls=%fused_computation.99 | convolution fusion | flops 4026531840 | bytes 13893632 | tf_op jit(solution)/shard_map/dot_general | solution.py:85
  117.8 63.3 %all-reduce.5.cloned.1.call-done = (f32[5,96,96]{2,0,1:T(8,128)}, f32[4,128,128]{2,0,1:T(4,128)}) async-done(((f32[5,96,96]{2,0,1:T(8,128)}, f32[4,128,128]{2,0,1:T(4,128)}), (f32[5,96,96]{2,0,1:T(8,128)}, f32[4,128,128]{2,0,1:T(4,128)})) %all-reduce.5.cloned.1.call-update) | async-done | bytes 446480 | tf_op jit(solution)/shard_map/psum | solution.py:78
  181.1 1.4 fusion.34
  182.5 9.6 %all_gather.6 = f32[20,96,96]{2,1,0:T(8,128)S(1)} all-gather(f32[5,96,96]{2,1,0:T(8,128)S(1)} %copy.46), channel_id=1, replica_groups=mesh['shard'=8,'tensor'=4] {'tensor'}, dimensions={0}, use_global_device_ids=true | all-gather | bytes 921600 | tf_op jit(solution)/shard_map/all_gather | solution.py:84
  192.1 7.4 %fusion.64 = f32[20,96,512]{2,1,0:T(8,128)} fusion(f32[20,96,96]{2,1,0:T(8,128)S(1)} %all_gather.6, f32[20,96,512]{2,1,0:T(8,128)} %bitcast.92), kind=kOutput, calls=%fused_computation.100 | convolution fusion | flops 1132462080 | bytes 8601600 | tf_op jit(solution)/shard_map/bij,bjd->bid/dot_general | solution.py:88
  199.7 0.9 copy-done.3
  201.0 82.0 %reduce-scatter.2.cloned.1.call-done = f32[240,512]{1,0:T(8,128)} async-done(((f32[1920,512]{1,0:T(8,128)}), f32[240,512]{1,0:T(8,128)}) %reduce-scatter.2.cloned.1.call-update) | async-done | bytes 491536 | tf_op jit(solution)/shard_map/reduce_scatter | solution.py:91
  282.9 2.3 multiply_reduce_fusion
  285.2 40.5 %psum.39 = f32[]{:T(128)} all-reduce(f32[]{:T(128)} %get-tuple-element.36), channel_id=1, replica_groups=mesh['shard'=8,'tensor'=4] {'shard','tensor'}, use_global_device_ids=true, to_apply=%region_12.13 | all-reduce | flops 1 | bytes 8 | tf_op jit(solution)/shard_map/psum | solution.py:98
  326.4 2.4 fusion.53
  328.8 0.7 copy.50
  329.5 0.7 copy.51
  330.2 45.8 %all-gather.2.cloned.1.call-done = bf16[1920,512]{1,0:T(8,128)(2,1)} async-done(((bf16[240,512]{1,0:T(8,128)(2,1)}), bf16[1920,512]{1,0:T(8,128)(2,1)}) %all-gather.2.cloned.1.call-update) | async-done | bytes 1966096 | tf_op jit(solution)/shard_map/all_gather | solution.py:103
  376.0 2.9 copy.96
  (47 shorter events, 7.8 us)
Async XLA Ops:
  7.2 1.6 copy-start
  7.2 11.2 %copy-start.2 = (f32[1,4,128,128]{3,2,1,0:T(8,128)S(1)}, f32[1,4,128,128]{3,2,1,0:T(8,128)}, u32[]{:S(2)}) copy-start(f32[1,4,128,128]{3,2,1,0:T(8,128)} %param.14) | copy-start | bytes 786436
  7.2 11.7 %copy-start.1 = (f32[1,5,96,96]{3,2,1,0:T(8,128)S(1)}, f32[1,5,96,96]{3,2,1,0:T(8,128)}, u32[]{:S(2)}) copy-start(f32[1,5,96,96]{3,2,1,0:T(8,128)} %param.15) | copy-start | bytes 552964
  7.2 84.9 %all-reduce.7.cloned.1.call-start = ((), (), s32[]{:S(2)}) async-start(), calls=%async_computation.4 | async-start | bytes 1015808 | tf_op jit(solution)/shard_map/psum | solution.py:69
  16.9 164.2 %all-reduce.5.cloned.1.call-start = ((), (), s32[]{:S(2)}) async-start(), calls=%async_computation.3 | async-start | bytes 1310720 | tf_op jit(solution)/shard_map/psum | solution.py:78
  108.1 174.8 %reduce-scatter.2.cloned.1.call-start = ((), (), s32[]{:S(2)}) async-start(), calls=%async_computation.1 | async-start | bytes 4423680 | tf_op jit(solution)/shard_map/reduce_scatter | solution.py:91
  199.6 0.9 copy-start.3
  199.6 176.4 %all-gather.2.cloned.1.call-start = ((), (), s32[]{:S(2)}) async-start(), calls=%async_computation.2 | async-start | bytes 2211840 | tf_op jit(solution)/shard_map/all_gather | solution.py:103
Sparse Core Ops, SparseCore 0:
  17.0 75.0 all-reduce.6
  108.2 72.7 all-reduce.4
  199.7 83.1 reduce-scatter.1
  328.9 47.1 all-gather.1
where the time goes:
time: 386 us
  waiting for transfers between devices  264 us (68%)
  blocking collectives  50.1 us (13%)
  matrix products  28.9 us (7%)
  between operations  17.4 us (5%)
  local copies, waits for them, and re-layouts  12.8 us (3%)
  other arithmetic  12.1 us (3%)
    reduce_scatter x1, waiting for transfers between devices, local(): lax.psum_scatter(left_done, 'shard', scatter_dimension=0, tiled=True)  82 us
    psum x1, waiting for transfers between devices, local(): lax.psum((fresh_share * stats_a, fresh_share * stats_g), 'shard')  72.7 us
    psum x1, waiting for transfers between devices, local(): lax.psum((owner_part(slots_a, shard_pos, shard_count), owner_part(slots_g...  63.3 us
    all_gather x1, waiting for transfers between devices, local(): lax.all_gather(weight_new.astype(jnp.bfloat16), 'shard', axis=0, tiled=True)  45.8 us
    psum x1, blocking collectives, local(): square_total = lax.psum(jnp.sum(precon * precon), ('shard', 'tensor'))  40.5 us
    all_gather x1, blocking collectives, local(): inv_g = lax.all_gather(local_inv_g, 'tensor', axis=0, tiled=True)  9.62 us
    dot_general x1, matrix products, local(): lax.dot_general(out_grad, acts, (((0,), (0,)), ((), ())), preferred_eleme...  9.42 us
  transfers between devices with their start and end apart: 4, of which 4 were waited for; matrix products, arithmetic and copies ran while one was open for 4% of the time, Pallas kernels for 0%

commit v1 on v0

--- a/solution.py
+++ b/solution.py
@@ -1,6 +1,8 @@
 import jax
 import jax.numpy as jnp
 from jax import lax
+from jax.experimental import pallas as pl
+from jax.experimental.pallas import tpu as pltpu
 from jax.sharding import PartitionSpec as P
 
 NS_IT = 5
@@ -13,6 +15,8 @@
 learn_rate = 0.05
 epsilon_sq = 1e-06
 highest = lax.Precision.HIGHEST
+f32 = jnp.float32
+bf16 = jnp.bfloat16
 
 
 def newton_inverse(factor):
@@ -43,7 +47,7 @@
     return marker[:, None, None] * inverse
 
 
-def local(acts, out_grad, sample_rows, own_a, own_g, a_state, g_state, momentum, weight):
+def general(acts, out_grad, sample_rows, own_a, own_g, a_state, g_state, momentum, weight):
     shard_count = lax.axis_size("shard")
     tensor_count = lax.axis_size("tensor")
     shard_pos = lax.axis_index("shard")
@@ -104,6 +108,258 @@
     return (new_a_state, new_g_state, momentum_new, weight_new, gathered)
 
 
+def swap(value, bit):
+    return lax.ppermute(value, "shard", [(i, i ^ bit) for i in range(8)])
+
+
+def swap_t(value, bit):
+    return lax.ppermute(value, "tensor", [(i, i ^ bit) for i in range(4)])
+
+
+def encode(value):
+    top = jnp.max(jnp.abs(value))
+    power = jnp.floor(jnp.log2(jnp.maximum(top, 1e-30)))
+    scaled = (value * jnp.exp2(14.0 - power)).astype(jnp.float16)
+    tail = jnp.full((16, value.shape[1]), power, jnp.float16)
+    return jnp.concatenate([scaled, tail], axis=0)
+
+
+def decode(packed):
+    power = packed[-1, 0].astype(f32)
+    return packed[:-16].astype(f32) * jnp.exp2(power - 14.0)
+
+
+def pick(flag, if_zero, if_one):
+    return jnp.where(flag == 0, if_zero, if_one)
+
+
+def factor_kernel(
+    share, info, picks, a_state, g_state, a_new, g_new, inv_a, inv_g
+):
+    count_a, width_a = a_state.shape[0], a_state.shape[1]
+    count_g, width_g = g_state.shape[0], g_state.shape[1]
+    errors, inverses, scales = [], [], []
+    for index in range(count_a + count_g):
+        is_a = index < count_a
+        width = width_a if is_a else width_g
+        place = index if is_a else index - count_a
+        start = place * width_a if is_a else count_a * width_a + place * width_g
+        rows = picks[:, start : start + width]
+        stats = lax.dot_general(
+            rows, rows, (((0,), (0,)), ((), ())), preferred_element_type=f32
+        )
+        slot = info[index]
+        stored = (a_state if is_a else g_state)[slot]
+        factor = factor_decay * stored + share * stats
+        (a_new if is_a else g_new)[slot] = factor
+        row = lax.broadcasted_iota(jnp.int32, (width, width), 0)
+        col = lax.broadcasted_iota(jnp.int32, (width, width), 1)
+        identity = (row == col).astype(f32)
+        trace = jnp.sum(factor * identity) / width
+        damped = factor + (damping_rate * trace) * identity
+        bound = jnp.max(jnp.sum(jnp.abs(damped), axis=0))
+        error = identity - damped / bound
+        errors.append(error)
+        inverses.append(identity + error)
+        scales.append(bound)
+    blocks = range(count_a + count_g)
+    dot = lambda p, q: jnp.dot(p, q, preferred_element_type=f32, precision=highest)
+    errors = [dot(errors[i], errors[i]) for i in blocks]
+    for step in range(1, NS_IT - 1):
+        grown = [dot(inverses[i], errors[i]) for i in blocks]
+        squares = [dot(errors[i], errors[i]) for i in blocks]
+        inverses = [inverses[i] + grown[i] for i in blocks]
+        errors = squares
+    inverses = [(inverses[i] + dot(inverses[i], errors[i])) / scales[i] for i in blocks]
+    for index in blocks:
+        if index < count_a:
+            inv_a[index] = inverses[index]
+        else:
+            inv_g[index - count_a] = inverses[index]
+
+
+def precon_kernel(info, part_a, part_b, inv_g, inv_a, top, mid, total):
+    side = info[0]
+    width_g, width_a = inv_g.shape[-1], inv_a.shape[-1]
+    half = width_g // 2
+    dot = lambda p, q: jnp.dot(p, q, preferred_element_type=f32, precision=highest)
+    squares = jnp.zeros((width_g, width_a), f32)
+    for piece, part in enumerate((part_a, part_b)):
+        for place in range(2):
+            for block in range(2):
+                values = dot(
+                    inv_g[place],
+                    part[
+                        place * width_g : (place + 1) * width_g,
+                        block * width_a : (block + 1) * width_a,
+                    ],
+                )
+                values = dot(values, inv_a[2 * piece + block])
+                squares += values * values
+                column = (2 * piece + block) * width_a
+                top[place * width_g : (place + 1) * width_g, column : column + width_a] = values
+        packed = part[2 * width_g : 2 * width_g + half, :]
+        values = jnp.concatenate([packed[:, :width_a], packed[:, width_a:]], axis=0)
+        values = dot(dot(inv_g[2], values), inv_a[2 * piece + side])
+        squares += values * values
+        mid[:, piece * width_a : (piece + 1) * width_a] = values
+    total[...] = jnp.full(total.shape, jnp.sum(squares), f32)
+
+
+def fast(acts, out_grad, sample_rows, own_a, own_g, a_state, g_state, momentum, weight):
+    shard_pos = lax.axis_index("shard")
+    tensor_pos = lax.axis_index("tensor")
+    side, low, high = shard_pos & 1, (shard_pos >> 1) & 1, shard_pos >> 2
+    count_a, width_a = a_state.shape[1], a_state.shape[2]
+    count_g, width_g = g_state.shape[1], g_state.shape[2]
+    group_cols = count_g * width_g
+    cols = acts.shape[1]
+    rows = momentum.shape[0]
+    samples = sample_rows.shape[0] * 8
+    share = (1.0 - factor_decay) / samples
+    vmem = pl.BlockSpec(memory_space=pltpu.VMEM)
+    smem = pl.BlockSpec(memory_space=pltpu.SMEM)
+
+    picked_a = jnp.take(acts, sample_rows, axis=0)
+    picked_g = jnp.take(out_grad, sample_rows, axis=0)
+    picked_g = lax.dynamic_slice_in_dim(picked_g, tensor_pos * group_cols, group_cols, 1)
+    picks = jnp.concatenate([picked_a, picked_g], axis=1)[None]
+    for bit, flag in ((4, high), (2, low), (1, side)):
+        other = swap(picks, bit)
+        picks = jnp.stack([pick(flag, picks, other), pick(flag, other, picks)], axis=1)
+        picks = picks.reshape((-1,) + picks.shape[2:])
+    picks = picks.reshape(2, 2, 2, -1, picks.shape[-1]).transpose(0, 1, 2, 3, 4)
+    picks = picks.reshape(samples, -1)
+
+    row_a = lax.dynamic_index_in_dim(own_a, tensor_pos, 0, keepdims=False)
+    row_g = lax.dynamic_index_in_dim(own_g, tensor_pos, 0, keepdims=False)
+    new_a, new_g, inv_a, inv_g = pl.pallas_call(
+        lambda *refs: factor_kernel(share, *refs),
+        in_specs=[smem, vmem, vmem, vmem],
+        out_specs=[vmem] * 4,
+        out_shape=[
+            jax.ShapeDtypeStruct(a_state.shape[1:], f32),
+            jax.ShapeDtypeStruct(g_state.shape[1:], f32),
+            jax.ShapeDtypeStruct(a_state.shape[1:], f32),
+            jax.ShapeDtypeStruct(g_state.shape[1:], f32),
+        ],
+        compiler_params=pltpu.CompilerParams(vmem_limit_bytes=32 * 2**20),
+        name="factors",
+    )(jnp.concatenate([row_a, row_g]), picks, a_state[0], g_state[0])
+    needed = pick(side, inv_g[jnp.array([0, 1, 2])], inv_g[jnp.array([3, 4, 2])])
+    route = [
+        ((2 * a + b) * 4 + c, (2 * c + b) * 4 + a)
+        for a in range(4)
+        for b in range(2)
+        for c in range(4)
+    ]
+    inv_rows = lax.ppermute(needed, ("shard", "tensor"), route)
+
+    half = cols // 2
+    head = 2 * width_g
+    mid = width_g // 2
+
+    def units(first):
+        raw = lax.dot_general(
+            out_grad,
+            acts[:, first : first + half],
+            (((0,), (0,)), ((), ())),
+            preferred_element_type=f32,
+        )
+        groups = raw.reshape(4, group_cols, half)
+        middle = groups[:, head : head + width_g]
+        left, right = middle[:, :, : half // 2], middle[:, :, half // 2 :]
+        packed = [jnp.concatenate([m[:, :mid], m[:, mid:]], axis=2) for m in (left, right)]
+        zero = jnp.concatenate([groups[:, :head], packed[0]], axis=1)
+        one = jnp.concatenate([groups[:, head + width_g :], packed[1]], axis=1)
+        return zero.reshape(2, 2, -1, half), one.reshape(2, 2, -1, half)
+
+    def exchange(keep, send, bit):
+        got = decode(swap(encode(send.reshape(-1, half)), bit))
+        return keep + got.reshape(keep.shape)
+
+    zero, one = units(0)
+    part = exchange(pick(side, zero, one), pick(side, one, zero), 1)
+    part = exchange(pick(low, part[:, 0], part[:, 1]), pick(low, part[:, 1], part[:, 0]), 2)
+    part_a = exchange(pick(high, part[0], part[1]), pick(high, part[1], part[0]), 4)
+
+    zero, one = units(half)
+    both = jnp.stack([zero, one], axis=0)
+    part = exchange(
+        pick(low, both[:, :, 0], both[:, :, 1]), pick(low, both[:, :, 1], both[:, :, 0]), 2
+    )
+    part = exchange(pick(high, part[:, 0], part[:, 1]), pick(high, part[:, 1], part[:, 0]), 4)
+    part_b = exchange(pick(side, part[0], part[1]), pick(side, part[1], part[0]), 1)
+
+    top, middle, total = pl.pallas_call(
+        precon_kernel,
+        in_specs=[smem, vmem, vmem, vmem, vmem],
+        out_specs=[vmem] * 3,
+        out_shape=[
+            jax.ShapeDtypeStruct((head, cols), f32),
+            jax.ShapeDtypeStruct((width_g, half), f32),
+            jax.ShapeDtypeStruct((8, half), f32),
+        ],
+        compiler_params=pltpu.CompilerParams(vmem_limit_bytes=32 * 2**20),
+        name="precon",
+    )(side.reshape(1), part_a, part_b, inv_rows, inv_a)
+
+    total = total + swap_t(total, 1)
+    total = total + swap_t(total, 2)
+    own_mid = pick(side, middle[:mid], middle[mid:])
+    give = pick(side, middle[mid:], middle[:mid])
+    got = swap(jnp.concatenate([give, total], axis=0), 1)
+    total = total + got[mid:]
+    total = total + swap(total, 2)
+    total = total + swap(total, 4)
+    mean_sq = total[0, 0] / (rows * 8 * cols * 4)
+    other_mid = got[:mid]
+    quarter = half // 2
+    pairs = []
+    for piece in range(2):
+        span = slice(piece * quarter, (piece + 1) * quarter)
+        pairs += [
+            pick(side, own_mid[:, span], other_mid[:, span]),
+            pick(side, other_mid[:, span], own_mid[:, span]),
+        ]
+    middle_rows = jnp.concatenate(pairs, axis=1)
+    precon = pick(
+        side,
+        jnp.concatenate([top, middle_rows], axis=0),
+        jnp.concatenate([middle_rows, top], axis=0),
+    )
+    update = precon / jnp.sqrt(mean_sq + epsilon_sq)
+    momentum_new = momentum_rate * momentum + update + decay_rate * weight
+    weight_new = weight - learn_rate * momentum_new
+    rounded = weight_new.astype(bf16)
+
+    def spread(values, bit, flag, axis):
+        other = swap(values, bit)
+        return jnp.stack([pick(flag, values, other), pick(flag, other, values)], axis=axis)
+
+    piece = rounded[:, :half]
+    piece = spread(piece, 4, high, 0)
+    piece = spread(piece, 2, low, 1)
+    whole_a = spread(piece, 1, side, 2).reshape(-1, half)
+    piece = rounded[:, half:]
+    piece = spread(piece, 1, side, 0)
+    piece = spread(piece, 4, high, 0)
+    whole_b = spread(piece, 2, low, 1).reshape(-1, half)
+    gathered = jnp.concatenate([whole_a, whole_b], axis=1)
+    return (new_a[None], new_g[None], momentum_new, weight_new, gathered)
+
+
+def local(acts, out_grad, sample_rows, own_a, own_g, a_state, g_state, momentum, weight):
+    shapes_fit = (
+        lax.axis_size("shard") == 8
+        and lax.axis_size("tensor") == 4
+        and a_state.shape[1:] == (4, 128, 128)
+        and g_state.shape[1:] == (5, 96, 96)
+    )
+    plan = fast if shapes_fit else general
+    return plan(acts, out_grad, sample_rows, own_a, own_g, a_state, g_state, momentum, weight)
+
+
 def solution(mesh):
     return jax.shard_map(
         local,

time: 386 us -> 159 us (0.41)
  waiting for transfers between devices: 264 us -> 58.7 us
  blocking collectives: 50.1 us -> 0 us
  starting transfers between devices: 0.34 us -> 27.6 us
  matrix products: 28.9 us -> 11.4 us
  other arithmetic: 12.1 us -> 20.7 us
  local copies, waits for them, and re-layouts: 12.8 us -> 21.3 us
  Pallas kernels: 0 us -> 7.11 us
  between operations: 17.4 us -> 11.2 us
    psum x2 -> x0, waiting for transfers between devices: 136 us -> none  [the longest x1 72.7 us: local(): lax.psum((fresh_share * stats_a, fresh_share * stats_g), 'shard')]
    reduce_scatter x1 -> x0, waiting for transfers between devices: 82 us -> none  [local(): lax.psum_scatter(left_done, 'shard', scatter_dimension=0, tiled=True)]
    ppermute x0 -> x21, waiting for transfers between devices: none -> 58.7 us  [the longest x18 56.2 us: swap(): return lax.ppermute(value, 'shard', [(i, i ^ bit) for i in range(8)])]
    all_gather x1 -> x0, waiting for transfers between devices: 45.8 us -> none  [local(): lax.all_gather(weight_new.astype(jnp.bfloat16), 'shard', axis=0, tiled=True)]
    psum x1 -> x0, blocking collectives: 40.5 us -> none  [local(): square_total = lax.psum(jnp.sum(precon * precon), ('shard', 'tensor'))]
    ppermute x0 -> x21, starting transfers between devices: none -> 27.6 us  [the longest x18 15.5 us: swap(): return lax.ppermute(value, 'shard', [(i, i ^ bit) for i in range(8)])]
    dot_general x31 -> x2, matrix products: 28.9 us -> 11.4 us  [units(): lax.dot_general(out_grad, acts[:, first:first + half], (((0,), (0,)), (()...]
    all_gather x1 -> x0, blocking collectives: 9.62 us -> none  [local(): inv_g = lax.all_gather(local_inv_g, 'tensor', axis=0, tiled=True)]
  transfers between devices with their start and end apart: 4 -> 21, of which waited for: 4 -> 14; matrix products, arithmetic and copies ran while one was open for 4% -> 23% of each run, Pallas kernels for 0% -> 0%
where the time goes in v1:
time: 159 us; the launch traced here: 158 us
  waiting for transfers between devices  58.7 us (37%)
  starting transfers between devices  27.6 us (17%)
  local copies, waits for them, and re-layouts  21.3 us (13%)
  other arithmetic  20.7 us (13%)
  matrix products  11.4 us (7%)
  between operations  11.2 us (7%)
  Pallas kernels  7.11 us (4%)
    ppermute x18, waiting for transfers between devices, swap(): return lax.ppermute(value, 'shard', [(i, i ^ bit) for i in range(8)])  56.2 us
    ppermute x18, starting transfers between devices, swap(): return lax.ppermute(value, 'shard', [(i, i ^ bit) for i in range(8)])  15.5 us
    ppermute x2, starting transfers between devices, swap_t(): return lax.ppermute(value, 'tensor', [(i, i ^ bit) for i in range(4)])  11.5 us
    dot_general x2, matrix products, units(): lax.dot_general(out_grad, acts[:, first:first + half], (((0,), (0,)), (()...  11.4 us
    slice x6, local copies, waits for them, and re-layouts, decode(): power = packed[-1, 0].astype(f32)  5.79 us
    pallas_call x1, Pallas kernels, fast(): pl.pallas_call(lambda *refs: factor_kernel(share, *refs), in_specs=[smem,...  5.46 us
    gather x1, local copies, waits for them, and re-layouts, fast(): picked_g = jnp.take(out_grad, sample_rows, axis=0)  5.23 us
    reduce_max x6, other arithmetic, encode(): top = jnp.max(jnp.abs(value))  5.08 us
  transfers between devices with their start and end apart: 21, of which 14 were waited for; matrix products, arithmetic and copies ran while one was open for 23% of the time, Pallas kernels for 0%

profile of v1, /device:TPU:0, one launch (start us, length us, event | category | flops | bytes accessed | tf_op | source)
XLA Modules:
  0.0 158.1 jit_solution(197435657199657093)
XLA Ops:
  2.1 2.6 %gather_fusion = bf16[64,512]{1,0:T(8,128)(2,1)S(1)} fusion(bf16[2048,512]{1,0:T(8,128)(2,1)} %param.11, s32[1024]{0:T(1024)S(1)} %pad_clamp_fusion.2), kind=kCustom, calls=%fused_computation | custom fusion | bytes 131328 | tf_op jit(solution)/shard_map/jit(_take)/gather | solution.py:223
  4.7 5.2 %gather_fusion.1 = bf16[64,1920]{1,0:T(8,128)(2,1)S(1)} fusion(bf16[2048,1920]{1,0:T(8,128)(2,1)} %param.12, s32[1024]{0:T(1024)S(1)} %pad_clamp_fusion.2), kind=kCustom, calls=%fused_computation.1 | custom fusion | bytes 491776 | tf_op jit(solution)/shard_map/jit(_take)/gather | solution.py:224
  10.8 4.0 %collective-permute-start = (bf16[1,64,992]{2,1,0:T(8,128)(2,1)}, bf16[1,64,992]{2,1,0:T(8,128)(2,1)}, u32[]{:S(2)}, u32[]{:S(2)}) collective-permute-start(bf16[1,64,992]{2,1,0:T(8,128)(2,1)} %maximum_bitcast_fusion.1), channel_id=1, source_target_pairs={{0,16},{4,20},{8,24},{12,28},{16,0},{20,4},{24,8},{28,12},{1,17},{... | collective-permute-start | bytes 380936 | tf_op jit(solution)/shard_map/ppermute | solution.py:112
  14.9 5.6 %fusion = f32[1920,256]{1,0:T(8,128)S(1)} fusion(bf16[2048,1920]{1,0:T(8,128)(2,1)} %param.12, bf16[2048,512]{1,0:T(8,128)(2,1)S(1)} %copy-done.8), kind=kOutput, calls=%fused_computation.8 | convolution fusion | flops 2013265920 | bytes 10878976 | tf_op jit(solution)/shard_map/dot_general | solution.py:263
  23.7 1.6 collective-permute-start.6
  25.3 5.8 %fusion.2 = f32[1920,256]{1,0:T(8,128)S(1)} fusion(bf16[2048,1920]{1,0:T(8,128)(2,1)} %param.12, bf16[2048,512]{1,0:T(8,128)(2,1)} %param.11), kind=kOutput, calls=%fused_computation.10 | convolution fusion | flops 2013265920 | bytes 10878976 | tf_op jit(solution)/shard_map/dot_general | solution.py:263
  31.9 1.8 %abs_reduce_fusion.1 = f32[]{:T(128)} fusion(f32[4,48,128]{2,1,0:T(8,128)} %get-tuple-element.36, f32[4,48,128]{2,1,0:T(8,128)} %get-tuple-element.37, f32[4,192,256]{2,1,0:T(8,128)S(1)} %get-tuple-element.33, f32[4,48,128]{2,1,0:T(8,128)} %get-tuple-element.35, f32[4,48,128]{2,1,0:T(8,128)} %get-tuple-element.34, f32[4,192,256]{2,1,0:T(8,128)S(1)} %get-tuple-element.32, ...), kind=kLoop, calls=%fused_computation.27 | loop fusion | flops 1720319 | bytes 1966085 | tf_op jit(solution)/shard_map/reduce_max | solution.py:120
  34.5 2.2 %fusion.6 = (f32[4,240,256]{2,1,0:T(8,128)}, f16[4,240,256]{2,1,0:T(8,128)(2,1)S(1)}) fusion(f32[4,48,128]{2,1,0:T(8,128)} %get-tuple-element.35, f32[4,48,128]{2,1,0:T(8,128)} %get-tuple-element.34, f32[4,192,256]{2,1,0:T(8,128)S(1)} %get-tuple-element.32, f32[4,48,128]{2,1,0:T(8,128)} %get-tuple-element.36, f32[4,48,128]{2,1,0:T(8,128)} %get-tuple-element.37, ...), kind=kLoop, calls=%fused_computation.30 | loop fusion | flops 1966080 | bytes 3440645 | tf_op jit(solution)/shard_map/jit(_where)/select_n | solution.py:133
  37.6 1.5 collective-permute-start.3
  41.3 6.0 %collective-permute-done.1 = bf16[2,64,992]{2,1,0:T(8,128)(2,1)S(1)} collective-permute-done((bf16[2,64,992]{2,1,0:T(8,128)(2,1)S(1)}, bf16[2,64,992]{2,1,0:T(8,128)(2,1)S(1)}, u32[]{:S(2)}, u32[]{:S(2)}) %collective-permute-start.1) | collective-permute-done | bytes 253984 | tf_op jit(solution)/shard_map/ppermute | solution.py:112
  48.1 1.2 slice.254
  53.9 1.2 slice.236
  59.0 7.1 %collective-permute-done.7 = f16[496,256]{1,0:T(8,128)(2,1)} collective-permute-done((f16[496,256]{1,0:T(8,128)(2,1)}, f16[496,256]{1,0:T(8,128)(2,1)}, u32[]{:S(2)}, u32[]{:S(2)}) %collective-permute-start.7) | collective-permute-done | bytes 253984 | tf_op jit(solution)/shard_map/ppermute | solution.py:112
  66.1 1.2 slice.258
  70.4 1.2 slice.240
  74.9 1.6 collective-permute-start.8
  76.7 3.2 %collective-permute-done.8 = f16[256,256]{1,0:T(8,128)(2,1)S(1)} collective-permute-done((f16[256,256]{1,0:T(8,128)(2,1)S(1)}, f16[256,256]{1,0:T(8,128)(2,1)S(1)}, u32[]{:S(2)}, u32[]{:S(2)}) %collective-permute-start.8) | collective-permute-done | bytes 131104 | tf_op jit(solution)/shard_map/ppermute | solution.py:112
  81.2 2.0 %collective-permute-done.5 = f16[256,256]{1,0:T(8,128)(2,1)S(1)} collective-permute-done((f16[256,256]{1,0:T(8,128)(2,1)S(1)}, f16[256,256]{1,0:T(8,128)(2,1)S(1)}, u32[]{:S(2)}, u32[]{:S(2)}) %collective-permute-start.5) | collective-permute-done | bytes 131104 | tf_op jit(solution)/shard_map/ppermute | solution.py:112
  86.6 5.5 %factors.1 = (f32[4,128,128]{2,1,0:T(8,128)}, f32[5,96,96]{2,1,0:T(8,128)}, f32[4,128,128]{2,1,0:T(8,128)S(1)}, f32[5,96,96]{2,1,0:T(8,128)S(1)}) custom-call(s32[9]{0:T(128)S(1)} %pad_add_fusion.refs_0_, bf16[512,992]{1,0:T(8,128)(2,1)S(1)} %bitcast.99, f32[4,128,128]{2,1,0:T(8,128)S(1)} %bitcast.100, f32[5,96,96]{2,1,0:T(8,128)S(1)} %bitcast.101), custom_call_target="tpu_custom_call" | custom-call | tf_op jit(solution)/shard_map/factors/pallas_call | solution.py:236
  94.0 1.6 %precon.1 = (f32[192,512]{1,0:T(8,128)S(1)}, f32[96,256]{1,0:T(8,128)S(1)}, f32[8,256]{1,0:T(8,128)S(1)}) custom-call(s32[1]{0:T(128)} %bitcast.16.info, f32[240,256]{1,0:T(8,128)S(1)} %bitcast_add_fusion.4.part_a, f32[240,256]{1,0:T(8,128)S(1)} %bitcast_add_fusion.3.part_b, f32[3,96,96]{2,1,0:T(8,128)S(1)} %collective-permute-done.9.inv_g, ...), custom_call_target="tpu_custom_call" | custom-call | tf_op jit(solution)/shard_map/precon/pallas_call | solution.py:294
  95.7 5.1 %collective-permute-start.10 = (f32[8,256]{1,0:T(8,128)S(1)}, f32[8,256]{1,0:T(8,128)S(1)}, u32[]{:S(2)}, u32[]{:S(2)}) collective-permute-start(f32[8,256]{1,0:T(8,128)S(1)} %get-tuple-element.18), channel_id=1, source_target_pairs={{0,1},{1,0},{2,3},{3,2},{4,5},{5,4},{6,7},{7,6},{8,9},{9,8},{10,11... | collective-permute-start | bytes 24584 | tf_op jit(solution)/shard_map/ppermute | solution.py:116
  101.7 6.3 %collective-permute-start.11 = (f32[8,256]{1,0:T(8,128)S(1)}, f32[8,256]{1,0:T(8,128)S(1)}, u32[]{:S(2)}, u32[]{:S(2)}) collective-permute-start(f32[8,256]{1,0:T(8,128)S(1)} %add.106), channel_id=1, source_target_pairs={{0,2},{1,3},{2,0},{3,1},{4,6},{5,7},{6,4},{7,5},{8,10},{9,11},{10,... | collective-permute-start | bytes 24584 | tf_op jit(solution)/shard_map/ppermute | solution.py:116
  108.0 1.6 %collective-permute-done.11 = f32[8,256]{1,0:T(8,128)S(1)} collective-permute-done((f32[8,256]{1,0:T(8,128)S(1)}, f32[8,256]{1,0:T(8,128)S(1)}, u32[]{:S(2)}, u32[]{:S(2)}) %collective-permute-start.11) | collective-permute-done | bytes 8224 | tf_op jit(solution)/shard_map/ppermute | solution.py:116
  110.2 3.6 %collective-permute-done.12 = f32[56,256]{1,0:T(8,128)S(1)} collective-permute-done((f32[56,256]{1,0:T(8,128)S(1)}, f32[56,256]{1,0:T(8,128)S(1)}, u32[]{:S(2)}, u32[]{:S(2)}) %collective-permute-start.12) | collective-permute-done | bytes 57376 | tf_op jit(solution)/shard_map/ppermute | solution.py:112
  113.9 3.6 %collective-permute-done.13 = f32[8,256]{1,0:T(8,128)S(1)} collective-permute-done((f32[8,256]{1,0:T(8,128)S(1)}, f32[8,256]{1,0:T(8,128)S(1)}, u32[]{:S(2)}, u32[]{:S(2)}) %collective-permute-start.13) | collective-permute-done | bytes 8224 | tf_op jit(solution)/shard_map/ppermute | solution.py:112
  118.2 3.9 %collective-permute-done.14 = f32[8,256]{1,0:T(8,128)S(1)} collective-permute-done((f32[8,256]{1,0:T(8,128)S(1)}, f32[8,256]{1,0:T(8,128)S(1)}, u32[]{:S(2)}, u32[]{:S(2)}) %collective-permute-start.14) | collective-permute-done | bytes 8224 | tf_op jit(solution)/shard_map/ppermute | solution.py:112
  126.0 9.6 %collective-permute-done.15 = bf16[240,256]{1,0:T(8,128)(2,1)S(1)} collective-permute-done((bf16[240,256]{1,0:T(8,128)(2,1)S(1)}, bf16[240,256]{1,0:T(8,128)(2,1)S(1)}, u32[]{:S(2)}, u32[]{:S(2)}) %collective-permute-start.15) | collective-permute-done | bytes 122912 | tf_op jit(solution)/shard_map/ppermute | solution.py:112
  135.8 2.2 %collective-permute-start.16 = (bf16[2,240,256]{2,1,0:T(8,128)(2,1)S(1)}, bf16[2,240,256]{2,1,0:T(8,128)(2,1)S(1)}, u32[]{:S(2)}, u32[]{:S(2)}) collective-permute-start(bf16[2,240,256]{2,1,0:T(8,128)(2,1)S(1)} %pad_maximum_fusion.8), channel_id=1, source_target_pairs={{0,8},{4,12},{8,0},{12,4},{16,24},{20,28},{24,16},{28,20},{1,9},{5... | collective-permute-start | bytes 737288 | tf_op jit(solution)/shard_map/ppermute | solution.py:112
  138.0 6.7 %collective-permute-done.19 = bf16[2,240,256]{2,1,0:T(8,128)(2,1)S(1)} collective-permute-done((bf16[2,240,256]{2,1,0:T(8,128)(2,1)S(1)}, bf16[2,240,256]{2,1,0:T(8,128)(2,1)S(1)}, u32[]{:S(2)}, u32[]{:S(2)}) %collective-permute-start.19) | collective-permute-done | bytes 245792 | tf_op jit(solution)/shard_map/ppermute | solution.py:112
  144.9 2.5 %collective-permute-done.16 = bf16[2,240,256]{2,1,0:T(8,128)(2,1)S(1)} collective-permute-done((bf16[2,240,256]{2,1,0:T(8,128)(2,1)S(1)}, bf16[2,240,256]{2,1,0:T(8,128)(2,1)S(1)}, u32[]{:S(2)}, u32[]{:S(2)}) %collective-permute-start.16) | collective-permute-done | bytes 245792 | tf_op jit(solution)/shard_map/ppermute | solution.py:112
  148.3 7.0 %collective-permute-done.20 = bf16[2,2,240,256]{3,2,1,0:T(8,128)(2,1)S(1)} collective-permute-done((bf16[2,2,240,256]{3,2,1,0:T(8,128)(2,1)S(1)}, bf16[2,2,240,256]{3,2,1,0:T(8,128)(2,1)S(1)}, u32[]{:S(2)}, u32[]{:S(2)}) %collective-permute-start.20) | collective-permute-done | bytes 491552 | tf_op jit(solution)/shard_map/ppermute | solution.py:112
  156.7 1.4 pad_maximum_fusion
  (125 shorter events, 31.1 us)
Async XLA Ops:
  0.6 40.6 %copy-start = (s32[4,5]{1,0:T(4,128)S(1)}, s32[4,5]{1,0:T(4,128)}, u32[]{:S(2)}) copy-start(s32[4,5]{1,0:T(4,128)} %param.15) | copy-start | bytes 244
  0.6 14.2 %copy-start.8 = (bf16[2048,512]{1,0:T(8,128)(2,1)S(1)}, bf16[2048,512]{1,0:T(8,128)(2,1)}, u32[]{:S(2)}) copy-start(bf16[2048,512]{1,0:T(8,128)(2,1)} %param.11) | copy-start | bytes 6291460
  10.0 0.8 copy-start.4
  10.1 0.7 copy-start.5
  10.8 28.2 %collective-permute-start = (bf16[1,64,992]{2,1,0:T(8,128)(2,1)}, bf16[1,64,992]{2,1,0:T(8,128)(2,1)}, u32[]{:S(2)}, u32[]{:S(2)}) collective-permute-start(bf16[1,64,992]{2,1,0:T(8,128)(2,1)} %maximum_bitcast_fusion.1), channel_id=1, source_target_pairs={{0,16},{4,20},{8,24},{12,28},{16,0},{20,4},{24,8},{28,12},{1,17},{... | collective-permute-start | bytes 380936 | tf_op jit(solution)/shard_map/ppermute | solution.py:112
  23.7 24.4 %collective-permute-start.6 = (f16[976,256]{1,0:T(8,128)(2,1)}, f16[976,256]{1,0:T(8,128)(2,1)}, u32[]{:S(2)}, u32[]{:S(2)}) collective-permute-start(f16[976,256]{1,0:T(8,128)(2,1)} %concatenate.76), channel_id=1, source_target_pairs={{0,8},{4,12},{8,0},{12,4},{16,24},{20,28},{24,16},{28,20},{1,9},{5... | collective-permute-start | bytes 1499144 | tf_op jit(solution)/shard_map/ppermute | solution.py:112
  37.6 16.3 %collective-permute-start.3 = (f16[976,256]{1,0:T(8,128)(2,1)}, f16[976,256]{1,0:T(8,128)(2,1)}, u32[]{:S(2)}, u32[]{:S(2)}) collective-permute-start(f16[976,256]{1,0:T(8,128)(2,1)} %concatenate.69), channel_id=1, source_target_pairs={{0,4},{4,0},{8,12},{12,8},{16,20},{20,16},{24,28},{28,24},{1,5},{5... | collective-permute-start | bytes 1499144 | tf_op jit(solution)/shard_map/ppermute | solution.py:112
  40.1 7.3 %collective-permute-start.1 = (bf16[2,64,992]{2,1,0:T(8,128)(2,1)S(1)}, bf16[2,64,992]{2,1,0:T(8,128)(2,1)S(1)}, u32[]{:S(2)}, u32[]{:S(2)}) collective-permute-start(bf16[2,64,992]{2,1,0:T(8,128)(2,1)S(1)} %maximum_bitcast_fusion), channel_id=1, source_target_pairs={{0,8},{4,12},{8,0},{12,4},{16,24},{20,28},{24,16},{28,20},{1,9},{5... | collective-permute-start | bytes 761864 | tf_op jit(solution)/shard_map/ppermute | solution.py:112
  47.5 37.0 %collective-permute-start.2 = (bf16[4,64,992]{2,1,0:T(8,128)(2,1)S(1)}, bf16[4,64,992]{2,1,0:T(8,128)(2,1)}, u32[]{:S(2)}, u32[]{:S(2)}) collective-permute-start(bf16[4,64,992]{2,1,0:T(8,128)(2,1)S(1)} %bitcast.109), channel_id=1, source_target_pairs={{0,4},{4,0},{8,12},{12,8},{16,20},{20,16},{24,28},{28,24},{1,5},{5... | collective-permute-start | bytes 1523720 | tf_op jit(solution)/shard_map/ppermute | solution.py:112
  51.3 5.6 %copy-start.3 = (f32[4,240,256]{2,1,0:T(8,128)S(1)}, f32[4,240,256]{2,1,0:T(8,128)}, u32[]{:S(2)}) copy-start(f32[4,240,256]{2,1,0:T(8,128)} %get-tuple-element.30) | copy-start | bytes 2949124
  53.5 12.6 %collective-permute-start.7 = (f16[496,256]{1,0:T(8,128)(2,1)}, f16[496,256]{1,0:T(8,128)(2,1)}, u32[]{:S(2)}, u32[]{:S(2)}) collective-permute-start(f16[496,256]{1,0:T(8,128)(2,1)} %concatenate.77), channel_id=1, source_target_pairs={{0,16},{4,20},{8,24},{12,28},{16,0},{20,4},{24,8},{28,12},{1,17},{... | collective-permute-start | bytes 761864 | tf_op jit(solution)/shard_map/ppermute | solution.py:112
  58.6 11.9 %collective-permute-start.4 = (f16[496,256]{1,0:T(8,128)(2,1)S(1)}, f16[496,256]{1,0:T(8,128)(2,1)}, u32[]{:S(2)}, u32[]{:S(2)}) collective-permute-start(f16[496,256]{1,0:T(8,128)(2,1)S(1)} %concatenate.70), channel_id=1, source_target_pairs={{0,8},{4,12},{8,0},{12,4},{16,24},{20,28},{24,16},{28,20},{1,9},{5... | collective-permute-start | bytes 761864 | tf_op jit(solution)/shard_map/ppermute | solution.py:112
  73.3 3.4 %copy-start.9 = (s32[3]{0:T(128)S(1)}, s32[3]{0:T(128)}, u32[]{:S(2)}) copy-start(s32[3]{0:T(128)} %constant.125) | copy-start | bytes 40
  74.9 5.1 %collective-permute-start.8 = (f16[256,256]{1,0:T(8,128)(2,1)S(1)}, f16[256,256]{1,0:T(8,128)(2,1)S(1)}, u32[]{:S(2)}, u32[]{:S(2)}) collective-permute-start(f16[256,256]{1,0:T(8,128)(2,1)S(1)} %concatenate.78), channel_id=1, source_target_pairs={{0,4},{4,0},{8,12},{12,8},{16,20},{20,16},{24,28},{28,24},{1,5},{5... | collective-permute-start | bytes 393224 | tf_op jit(solution)/shard_map/ppermute | solution.py:112
  76.6 6.6 %collective-permute-start.5 = (f16[256,256]{1,0:T(8,128)(2,1)S(1)}, f16[256,256]{1,0:T(8,128)(2,1)S(1)}, u32[]{:S(2)}, u32[]{:S(2)}) collective-permute-start(f16[256,256]{1,0:T(8,128)(2,1)S(1)} %concatenate.71), channel_id=1, source_target_pairs={{0,16},{4,20},{8,24},{12,28},{16,0},{20,4},{24,8},{28,12},{1,17},{... | collective-permute-start | bytes 393224 | tf_op jit(solution)/shard_map/ppermute | solution.py:112
  85.6 1.0 copy-start.1
  85.6 1.0 copy-start.2
  92.1 31.8 %copy-start.6 = (f32[240,512]{1,0:T(8,128)S(1)}, f32[240,512]{1,0:T(8,128)}, u32[]{:S(2)}) copy-start(f32[240,512]{1,0:T(8,128)} %param.19) | copy-start | bytes 1474564
  92.1 31.8 %copy-start.7 = (f32[240,512]{1,0:T(8,128)S(1)}, f32[240,512]{1,0:T(8,128)}, u32[]{:S(2)}) copy-start(f32[240,512]{1,0:T(8,128)} %param.18) | copy-start | bytes 1474564
  93.3 0.7 collective-permute-start.9
  95.7 6.0 %collective-permute-start.10 = (f32[8,256]{1,0:T(8,128)S(1)}, f32[8,256]{1,0:T(8,128)S(1)}, u32[]{:S(2)}, u32[]{:S(2)}) collective-permute-start(f32[8,256]{1,0:T(8,128)S(1)} %get-tuple-element.18), channel_id=1, source_target_pairs={{0,1},{1,0},{2,3},{3,2},{4,5},{5,4},{6,7},{7,6},{8,9},{9,8},{10,11... | collective-permute-start | bytes 24584 | tf_op jit(solution)/shard_map/ppermute | solution.py:116
  101.7 7.9 %collective-permute-start.11 = (f32[8,256]{1,0:T(8,128)S(1)}, f32[8,256]{1,0:T(8,128)S(1)}, u32[]{:S(2)}, u32[]{:S(2)}) collective-permute-start(f32[8,256]{1,0:T(8,128)S(1)} %add.106), channel_id=1, source_target_pairs={{0,2},{1,3},{2,0},{3,1},{4,6},{5,7},{6,4},{7,5},{8,10},{9,11},{10,... | collective-permute-start | bytes 24584 | tf_op jit(solution)/shard_map/ppermute | solution.py:116
  109.6 4.2 %collective-permute-start.12 = (f32[56,256]{1,0:T(8,128)S(1)}, f32[56,256]{1,0:T(8,128)S(1)}, u32[]{:S(2)}, u32[]{:S(2)}) collective-permute-start(f32[56,256]{1,0:T(8,128)S(1)} %pad_maximum_fusion.10), channel_id=1, source_target_pairs={{0,4},{4,0},{8,12},{12,8},{16,20},{20,16},{24,28},{28,24},{1,5},{5... | collective-permute-start | bytes 172040 | tf_op jit(solution)/shard_map/ppermute | solution.py:112
  113.9 3.7 %collective-permute-start.13 = (f32[8,256]{1,0:T(8,128)S(1)}, f32[8,256]{1,0:T(8,128)S(1)}, u32[]{:S(2)}, u32[]{:S(2)}) collective-permute-start(f32[8,256]{1,0:T(8,128)S(1)} %slice_add_fusion), channel_id=1, source_target_pairs={{0,8},{4,12},{8,0},{12,4},{16,24},{20,28},{24,16},{28,20},{1,9},{5... | collective-permute-start | bytes 24584 | tf_op jit(solution)/shard_map/ppermute | solution.py:112
  117.5 4.5 %collective-permute-start.14 = (f32[8,256]{1,0:T(8,128)S(1)}, f32[8,256]{1,0:T(8,128)S(1)}, u32[]{:S(2)}, u32[]{:S(2)}) collective-permute-start(f32[8,256]{1,0:T(8,128)S(1)} %add.109), channel_id=1, source_target_pairs={{0,16},{4,20},{8,24},{12,28},{16,0},{20,4},{24,8},{28,12},{1,17},{... | collective-permute-start | bytes 24584 | tf_op jit(solution)/shard_map/ppermute | solution.py:112
  125.1 10.5 %collective-permute-start.15 = (bf16[240,256]{1,0:T(8,128)(2,1)S(1)}, bf16[240,256]{1,0:T(8,128)(2,1)S(1)}, u32[]{:S(2)}, u32[]{:S(2)}) collective-permute-start(bf16[240,256]{1,0:T(8,128)(2,1)S(1)} %get-tuple-element.58), channel_id=1, source_target_pairs={{0,16},{4,20},{8,24},{12,28},{16,0},{20,4},{24,8},{28,12},{1,17},{... | collective-permute-start | bytes 368648 | tf_op jit(solution)/shard_map/ppermute | solution.py:112
  125.3 10.3 %collective-permute-start.18 = (bf16[240,256]{1,0:T(8,128)(2,1)S(1)}, bf16[240,256]{1,0:T(8,128)(2,1)S(1)}, u32[]{:S(2)}, u32[]{:S(2)}) collective-permute-start(bf16[240,256]{1,0:T(8,128)(2,1)S(1)} %get-tuple-element.59), channel_id=1, source_target_pairs={{0,4},{4,0},{8,12},{12,8},{16,20},{20,16},{24,28},{28,24},{1,5},{5... | collective-permute-start | bytes 368648 | tf_op jit(solution)/shard_map/ppermute | solution.py:112
  135.7 9.0 %collective-permute-start.19 = (bf16[2,240,256]{2,1,0:T(8,128)(2,1)S(1)}, bf16[2,240,256]{2,1,0:T(8,128)(2,1)S(1)}, u32[]{:S(2)}, u32[]{:S(2)}) collective-permute-start(bf16[2,240,256]{2,1,0:T(8,128)(2,1)S(1)} %pad_maximum_fusion.9), channel_id=1, source_target_pairs={{0,16},{4,20},{8,24},{12,28},{16,0},{20,4},{24,8},{28,12},{1,17},{... | collective-permute-start | bytes 737288 | tf_op jit(solution)/shard_map/ppermute | solution.py:112
  135.8 11.6 %collective-permute-start.16 = (bf16[2,240,256]{2,1,0:T(8,128)(2,1)S(1)}, bf16[2,240,256]{2,1,0:T(8,128)(2,1)S(1)}, u32[]{:S(2)}, u32[]{:S(2)}) collective-permute-start(bf16[2,240,256]{2,1,0:T(8,128)(2,1)S(1)} %pad_maximum_fusion.8), channel_id=1, source_target_pairs={{0,8},{4,12},{8,0},{12,4},{16,24},{20,28},{24,16},{28,20},{1,9},{5... | collective-permute-start | bytes 737288 | tf_op jit(solution)/shard_map/ppermute | solution.py:112
  144.8 10.5 %collective-permute-start.20 = (bf16[2,2,240,256]{3,2,1,0:T(8,128)(2,1)S(1)}, bf16[2,2,240,256]{3,2,1,0:T(8,128)(2,1)S(1)}, u32[]{:S(2)}, u32[]{:S(2)}) collective-permute-start(bf16[2,2,240,256]{3,2,1,0:T(8,128)(2,1)S(1)} %pad_maximum_fusion.7), channel_id=1, source_target_pairs={{0,8},{4,12},{8,0},{12,4},{16,24},{20,28},{24,16},{28,20},{1,9},{5... | collective-permute-start | bytes 1474568 | tf_op jit(solution)/shard_map/ppermute | solution.py:112
  147.5 8.9 %collective-permute-start.17 = (bf16[2,2,240,256]{3,2,0,1:T(8,128)(2,1)S(1)}, bf16[2,2,240,256]{3,2,0,1:T(8,128)(2,1)S(1)}, u32[]{:S(2)}, u32[]{:S(2)}) collective-permute-start(bf16[2,2,240,256]{3,2,0,1:T(8,128)(2,1)S(1)} %pad_maximum_fusion.6), channel_id=1, source_target_pairs={{0,4},{4,0},{8,12},{12,8},{16,20},{20,16},{24,28},{28,24},{1,5},{5... | collective-permute-start | bytes 1474568 | tf_op jit(solution)/shard_map/ppermute | solution.py:112

commit v2 on v1

--- a/solution.py
+++ b/solution.py
@@ -108,6 +108,20 @@
     return (new_a_state, new_g_state, momentum_new, weight_new, gathered)
 
 
+GROUP = 16
+vmem = pl.BlockSpec(memory_space=pltpu.VMEM)
+smem = pl.BlockSpec(memory_space=pltpu.SMEM)
+anywhere = pl.BlockSpec(memory_space=pl.ANY)
+
+
+def params(mib):
+    return pltpu.CompilerParams(vmem_limit_bytes=mib * 2**20)
+
+
+def shaped(shape, kind):
+    return jax.ShapeDtypeStruct(shape, kind)
+
+
 def swap(value, bit):
     return lax.ppermute(value, "shard", [(i, i ^ bit) for i in range(8)])
 
@@ -116,39 +130,182 @@
     return lax.ppermute(value, "tensor", [(i, i ^ bit) for i in range(4)])
 
 
-def encode(value):
-    top = jnp.max(jnp.abs(value))
-    power = jnp.floor(jnp.log2(jnp.maximum(top, 1e-30)))
-    scaled = (value * jnp.exp2(14.0 - power)).astype(jnp.float16)
-    tail = jnp.full((16, value.shape[1]), power, jnp.float16)
-    return jnp.concatenate([scaled, tail], axis=0)
-
-
-def decode(packed):
-    power = packed[-1, 0].astype(f32)
-    return packed[:-16].astype(f32) * jnp.exp2(power - 14.0)
-
-
 def pick(flag, if_zero, if_one):
     return jnp.where(flag == 0, if_zero, if_one)
 
 
+def encode(value, store):
+    rows, width = value.shape
+    powers = []
+    for first in range(0, rows, GROUP):
+        part = value[first : first + GROUP]
+        top = jnp.max(jnp.abs(part), axis=0, keepdims=True)
+        power = jnp.floor(jnp.log2(jnp.maximum(top, 1e-30)))
+        scaled = jnp.clip(jnp.round(part * jnp.exp2(14.0 - power)), -32767.0, 32767.0)
+        store(first, scaled.astype(jnp.int32).astype(jnp.int16))
+        powers.append(power)
+    powers += [jnp.zeros((1, width), f32)] * (GROUP - len(powers))
+    store(rows, jnp.concatenate(powers, axis=0).astype(jnp.int32).astype(jnp.int16))
+
+
+def decode(packed, rows):
+    whole = packed.astype(jnp.int32).astype(f32)
+    scales = jnp.exp2(whole[rows : rows + GROUP] - 14.0)
+    parts = [
+        whole[first : first + GROUP] * scales[first // GROUP : first // GROUP + 1]
+        for first in range(0, rows, GROUP)
+    ]
+    return jnp.concatenate(parts, axis=0)
+
+
+def encode_to(ref, index, value):
+    def store(first, data):
+        ref[index, first : first + GROUP, :] = data
+
+    encode(value, store)
+
+
+def picks_kernel(group_cols, info, sampled, acts, out_grad, picks, acts_buf, grad_buf, sems):
+    group = info[0]
+    block = 128
+    span = grad_buf.shape[1]
+    tokens, cols = acts.shape
+    last = out_grad.shape[1] // block - span // block
+    start = jnp.minimum((group * group_cols) // block, last)
+    first = pltpu.make_async_copy(acts, acts_buf, sems.at[0])
+    second = pltpu.make_async_copy(
+        out_grad.at[:, pl.ds(pl.multiple_of(start * block, block), span)], grad_buf, sems.at[1]
+    )
+    first.start()
+    second.start()
+    place = lax.broadcasted_iota(jnp.int32, (sampled.shape[0], tokens), 1)
+    chosen = (place == sampled[...]).astype(bf16)
+    first.wait()
+    picks[:, :cols] = jnp.dot(chosen, acts_buf[...], preferred_element_type=f32).astype(bf16)
+    second.wait()
+    grads = jnp.dot(chosen, grad_buf[...], preferred_element_type=f32)
+    pad = jnp.zeros((grads.shape[0], picks.shape[1] - cols - group_cols), f32)
+    for which in range(4):
+        begin = min((which * group_cols) // block, last) * block
+        offset = which * group_cols - begin
+
+        @pl.when(group == which)
+        def _():
+            part = jnp.concatenate([grads[:, offset : offset + group_cols], pad], axis=1)
+            picks[:, cols:] = part.astype(bf16)
+
+
+def split_units(group, head, width_g):
+    half = group.shape[1] // 2
+    mid = width_g // 2
+    middle = group[head : head + width_g]
+    packed = [
+        jnp.concatenate([middle[:mid, cols], middle[mid:, cols]], axis=1)
+        for cols in (slice(0, half), slice(half, 2 * half))
+    ]
+    return (
+        jnp.concatenate([group[:head], packed[0]], axis=0),
+        jnp.concatenate([group[head + width_g :], packed[1]], axis=0),
+    )
+
+
+def partial_kernel_x(group_cols, width_g, info, out_grad, acts, send, keep, turned, raw):
+    step = pl.program_id(0)
+    side = info[1]
+    head = 2 * width_g
+    block = out_grad.shape[1]
+    flipped = out_grad[...].T
+    turned[...] = flipped
+    first = pl.multiple_of(step * block, block)
+    raw[pl.ds(first, block), :] = jnp.dot(flipped, acts[...], preferred_element_type=f32)
+
+    @pl.when(step > 0)
+    def _():
+        place = step - 1
+        start = pl.multiple_of(place * group_cols, 8)
+        units = split_units(raw[pl.ds(start, group_cols), :], head, width_g)
+        for x in range(2):
+
+            @pl.when(side == x)
+            def _():
+                keep[place] = units[x]
+                encode_to(send, place, units[1 - x])
+
+
+def partial_kernel_l(width_g, info, turned, acts, send, keep):
+    place = pl.program_id(0)
+    low = info[2]
+    raw = jnp.dot(turned[...], acts[...], preferred_element_type=f32)
+    units = split_units(raw, 2 * width_g, width_g)
+    high = place // 2
+
+    @pl.when(place % 2 == low)
+    def _():
+        for x in range(2):
+            keep[2 * high + x] = units[x]
+
+    @pl.when(place % 2 != low)
+    def _():
+        for x in range(2):
+            encode_to(send, 2 * high + x, units[x])
+
+
+def add_kernel(bit_at, inner, info, got, held, send, keep):
+    bit = info[bit_at]
+    rows = held.shape[1]
+    count = send.shape[0]
+
+    def place(j, value):
+        return 2 * j + value if inner else value * count + j
+
+    for j in range(count):
+        away = place(j, 1 - bit)
+        encode_to(send, j, held[away] + decode(got[away], rows))
+    for j in range(count):
+        home = place(j, bit)
+        keep[j] = held[home] + decode(got[home], rows)
+
+
+def add_step(info, bit_at, inner, got, held):
+    count = held.shape[0] // 2
+    return pl.pallas_call(
+        lambda *refs: add_kernel(bit_at, inner, *refs),
+        in_specs=[smem, vmem, vmem],
+        out_specs=[vmem, vmem],
+        out_shape=[
+            shaped((count,) + got.shape[1:], jnp.int16),
+            shaped((count,) + held.shape[1:], f32),
+        ],
+        compiler_params=params(24),
+        name="add",
+    )(info, got, held)
+
+
 def factor_kernel(
-    share, info, picks, a_state, g_state, a_new, g_new, inv_a, inv_g
+    share, info, own, one, two, four, a_state, g_state, a_new, g_new, inv_a, needed, picks, inv_g
 ):
+    shard = info[3]
+    picks[shard] = own[...]
+    picks[shard ^ 4] = one[...]
+    for j in range(2):
+        picks[shard ^ 2 ^ (4 * j)] = two[j]
+    for j in range(4):
+        picks[shard ^ 1 ^ (4 * (j % 2)) ^ (2 * (j // 2))] = four[j]
     count_a, width_a = a_state.shape[0], a_state.shape[1]
     count_g, width_g = g_state.shape[0], g_state.shape[1]
+    samples = picks.shape[0] * picks.shape[1]
+    everything = picks[...].reshape(samples, picks.shape[2])
     errors, inverses, scales = [], [], []
     for index in range(count_a + count_g):
         is_a = index < count_a
         width = width_a if is_a else width_g
         place = index if is_a else index - count_a
         start = place * width_a if is_a else count_a * width_a + place * width_g
-        rows = picks[:, start : start + width]
+        rows = everything[:, start : start + width]
         stats = lax.dot_general(
             rows, rows, (((0,), (0,)), ((), ())), preferred_element_type=f32
         )
-        slot = info[index]
+        slot = info[4 + index]
         stored = (a_state if is_a else g_state)[slot]
         factor = factor_decay * stored + share * stats
         (a_new if is_a else g_new)[slot] = factor
@@ -176,15 +333,20 @@
             inv_a[index] = inverses[index]
         else:
             inv_g[index - count_a] = inverses[index]
-
-
-def precon_kernel(info, part_a, part_b, inv_g, inv_a, top, mid, total):
-    side = info[0]
+    side = info[1]
+    needed[0] = inv_g[3 * side]
+    needed[1] = inv_g[1 + 3 * side]
+    needed[2] = inv_g[2]
+
+
+def precon_kernel(info, got_a, held_a, got_b, held_b, inv_g, inv_a, top, mid, total):
+    side = info[1]
     width_g, width_a = inv_g.shape[-1], inv_a.shape[-1]
     half = width_g // 2
     dot = lambda p, q: jnp.dot(p, q, preferred_element_type=f32, precision=highest)
     squares = jnp.zeros((width_g, width_a), f32)
-    for piece, part in enumerate((part_a, part_b)):
+    for piece, (got, held) in enumerate(((got_a, held_a), (got_b, held_b))):
+        part = held[0] + decode(got[0], held.shape[1])
         for place in range(2):
             for block in range(2):
                 values = dot(
@@ -213,40 +375,110 @@
     count_a, width_a = a_state.shape[1], a_state.shape[2]
     count_g, width_g = g_state.shape[1], g_state.shape[2]
     group_cols = count_g * width_g
-    cols = acts.shape[1]
+    tokens, cols = acts.shape
+    outs = out_grad.shape[1]
     rows = momentum.shape[0]
-    samples = sample_rows.shape[0] * 8
+    drawn = sample_rows.shape[0]
+    samples = drawn * 8
     share = (1.0 - factor_decay) / samples
-    vmem = pl.BlockSpec(memory_space=pltpu.VMEM)
-    smem = pl.BlockSpec(memory_space=pltpu.SMEM)
-
-    picked_a = jnp.take(acts, sample_rows, axis=0)
-    picked_g = jnp.take(out_grad, sample_rows, axis=0)
-    picked_g = lax.dynamic_slice_in_dim(picked_g, tensor_pos * group_cols, group_cols, 1)
-    picks = jnp.concatenate([picked_a, picked_g], axis=1)[None]
-    for bit, flag in ((4, high), (2, low), (1, side)):
-        other = swap(picks, bit)
-        picks = jnp.stack([pick(flag, picks, other), pick(flag, other, picks)], axis=1)
-        picks = picks.reshape((-1,) + picks.shape[2:])
-    picks = picks.reshape(2, 2, 2, -1, picks.shape[-1]).transpose(0, 1, 2, 3, 4)
-    picks = picks.reshape(samples, -1)
-
+    half = cols // 2
+    head = 2 * width_g
+    mid = width_g // 2
     row_a = lax.dynamic_index_in_dim(own_a, tensor_pos, 0, keepdims=False)
     row_g = lax.dynamic_index_in_dim(own_g, tensor_pos, 0, keepdims=False)
-    new_a, new_g, inv_a, inv_g = pl.pallas_call(
+    info = jnp.concatenate(
+        [jnp.stack([tensor_pos, side, low, shard_pos]), row_a, row_g, high.reshape(1)]
+    )
+    high_at = 4 + count_a + count_g
+
+    wide = cols + -(-group_cols // 128) * 128
+    picks = pl.pallas_call(
+        lambda *refs: picks_kernel(group_cols, *refs),
+        in_specs=[smem, vmem, anywhere, anywhere],
+        out_specs=vmem,
+        out_shape=shaped((drawn, wide), bf16),
+        scratch_shapes=[
+            pltpu.VMEM((tokens, cols), bf16),
+            pltpu.VMEM((tokens, 640), bf16),
+            pltpu.SemaphoreType.DMA((2,)),
+        ],
+        compiler_params=params(24),
+        name="picks",
+    )(info, sample_rows.reshape(-1, 1), acts, out_grad)
+    one = swap(picks, 4)
+    two = swap(jnp.stack([picks, one]), 2)
+    four = swap(jnp.concatenate([picks[None], one[None], two]), 1)
+
+    block = outs // 5
+    send_a, keep_a, turned = pl.pallas_call(
+        lambda *refs: partial_kernel_x(group_cols, width_g, *refs),
+        grid=(5,),
+        in_specs=[
+            smem,
+            pl.BlockSpec((tokens, block), lambda i: (0, i)),
+            pl.BlockSpec((tokens, half), lambda i: (0, 0)),
+        ],
+        out_specs=[
+            pl.BlockSpec((4, rows + GROUP, half), lambda i: (0, 0, 0)),
+            pl.BlockSpec((4, rows, half), lambda i: (0, 0, 0)),
+            pl.BlockSpec((block, tokens), lambda i: (i, 0)),
+        ],
+        out_shape=[
+            shaped((4, rows + GROUP, half), jnp.int16),
+            shaped((4, rows, half), f32),
+            shaped((outs, tokens), bf16),
+        ],
+        scratch_shapes=[pltpu.VMEM((outs, half), f32)],
+        compiler_params=params(40),
+        name="partial_x",
+    )(info, out_grad, acts)
+    got_a = swap(send_a, 1)
+    send_b, keep_b = pl.pallas_call(
+        lambda *refs: partial_kernel_l(width_g, *refs),
+        grid=(4,),
+        in_specs=[
+            smem,
+            pl.BlockSpec((group_cols, tokens), lambda i: (i, 0)),
+            pl.BlockSpec((tokens, half), lambda i: (0, 1)),
+        ],
+        out_specs=[
+            pl.BlockSpec((4, rows + GROUP, half), lambda i: (0, 0, 0)),
+            pl.BlockSpec((4, rows, half), lambda i: (0, 0, 0)),
+        ],
+        out_shape=[
+            shaped((4, rows + GROUP, half), jnp.int16),
+            shaped((4, rows, half), f32),
+        ],
+        compiler_params=params(40),
+        name="partial_l",
+    )(info, turned, acts)
+    got_b = swap(send_b, 2)
+    send_a, keep_a = add_step(info, 2, True, got_a, keep_a)
+    got_a = swap(send_a, 2)
+    send_b, keep_b = add_step(info, 1, True, got_b, keep_b)
+    got_b = swap(send_b, 1)
+    send_a, keep_a = add_step(info, high_at, True, got_a, keep_a)
+    got_a = swap(send_a, 4)
+    send_b, keep_b = add_step(info, high_at, True, got_b, keep_b)
+    got_b = swap(send_b, 4)
+
+    new_a, new_g, inv_a, needed = pl.pallas_call(
         lambda *refs: factor_kernel(share, *refs),
-        in_specs=[smem, vmem, vmem, vmem],
+        in_specs=[smem] + [vmem] * 6,
         out_specs=[vmem] * 4,
         out_shape=[
-            jax.ShapeDtypeStruct(a_state.shape[1:], f32),
-            jax.ShapeDtypeStruct(g_state.shape[1:], f32),
-            jax.ShapeDtypeStruct(a_state.shape[1:], f32),
-            jax.ShapeDtypeStruct(g_state.shape[1:], f32),
-        ],
-        compiler_params=pltpu.CompilerParams(vmem_limit_bytes=32 * 2**20),
+            shaped(a_state.shape[1:], f32),
+            shaped(g_state.shape[1:], f32),
+            shaped(a_state.shape[1:], f32),
+            shaped((3, width_g, width_g), f32),
+        ],
+        scratch_shapes=[
+            pltpu.VMEM((8, drawn, wide), bf16),
+            pltpu.VMEM(g_state.shape[1:], f32),
+        ],
+        compiler_params=params(24),
         name="factors",
-    )(jnp.concatenate([row_a, row_g]), picks, a_state[0], g_state[0])
-    needed = pick(side, inv_g[jnp.array([0, 1, 2])], inv_g[jnp.array([3, 4, 2])])
+    )(info, picks, one, two, four, a_state[0], g_state[0])
     route = [
         ((2 * a + b) * 4 + c, (2 * c + b) * 4 + a)
         for a in range(4)
@@ -255,54 +487,18 @@
     ]
     inv_rows = lax.ppermute(needed, ("shard", "tensor"), route)
 
-    half = cols // 2
-    head = 2 * width_g
-    mid = width_g // 2
-
-    def units(first):
-        raw = lax.dot_general(
-            out_grad,
-            acts[:, first : first + half],
-            (((0,), (0,)), ((), ())),
-            preferred_element_type=f32,
-        )
-        groups = raw.reshape(4, group_cols, half)
-        middle = groups[:, head : head + width_g]
-        left, right = middle[:, :, : half // 2], middle[:, :, half // 2 :]
-        packed = [jnp.concatenate([m[:, :mid], m[:, mid:]], axis=2) for m in (left, right)]
-        zero = jnp.concatenate([groups[:, :head], packed[0]], axis=1)
-        one = jnp.concatenate([groups[:, head + width_g :], packed[1]], axis=1)
-        return zero.reshape(2, 2, -1, half), one.reshape(2, 2, -1, half)
-
-    def exchange(keep, send, bit):
-        got = decode(swap(encode(send.reshape(-1, half)), bit))
-        return keep + got.reshape(keep.shape)
-
-    zero, one = units(0)
-    part = exchange(pick(side, zero, one), pick(side, one, zero), 1)
-    part = exchange(pick(low, part[:, 0], part[:, 1]), pick(low, part[:, 1], part[:, 0]), 2)
-    part_a = exchange(pick(high, part[0], part[1]), pick(high, part[1], part[0]), 4)
-
-    zero, one = units(half)
-    both = jnp.stack([zero, one], axis=0)
-    part = exchange(
-        pick(low, both[:, :, 0], both[:, :, 1]), pick(low, both[:, :, 1], both[:, :, 0]), 2
-    )
-    part = exchange(pick(high, part[:, 0], part[:, 1]), pick(high, part[:, 1], part[:, 0]), 4)
-    part_b = exchange(pick(side, part[0], part[1]), pick(side, part[1], part[0]), 1)
-
     top, middle, total = pl.pallas_call(
         precon_kernel,
-        in_specs=[smem, vmem, vmem, vmem, vmem],
+        in_specs=[smem] + [vmem] * 6,
         out_specs=[vmem] * 3,
         out_shape=[
-            jax.ShapeDtypeStruct((head, cols), f32),
-            jax.ShapeDtypeStruct((width_g, half), f32),
-            jax.ShapeDtypeStruct((8, half), f32),
-        ],
-        compiler_params=pltpu.CompilerParams(vmem_limit_bytes=32 * 2**20),
+            shaped((head, cols), f32),
+            shaped((width_g, half), f32),
+            shaped((8, half), f32),
+        ],
+        compiler_params=params(24),
         name="precon",
-    )(side.reshape(1), part_a, part_b, inv_rows, inv_a)
+    )(info, got_a, keep_a, got_b, keep_b, inv_rows, inv_a)
 
     total = total + swap_t(total, 1)
     total = total + swap_t(total, 2)

time: 159 us -> 138 us (0.87)
  other arithmetic: 20.7 us -> 3.26 us
  Pallas kernels: 7.11 us -> 23.4 us
  local copies, waits for them, and re-layouts: 21.3 us -> 8.21 us
  starting transfers between devices: 27.6 us -> 39.1 us
  matrix products: 11.4 us -> 0 us
  between operations: 11.2 us -> 2.2 us
  waiting for transfers between devices: 58.7 us -> 61.8 us
    pallas_call x2 -> x9, Pallas kernels: 7.11 us -> 23.4 us  [the longest x1 6.56 us: fast(): pl.pallas_call(lambda *refs: partial_kernel_x(group_cols, width_g, *refs)...]
    ppermute x18, starting transfers between devices: 15.5 us -> 29.1 us  [swap(): return lax.ppermute(value, 'shard', [(i, i ^ bit) for i in range(8)])]
    dot_general x2 -> x0, matrix products: 11.4 us -> none  [units(): lax.dot_general(out_grad, acts[:, first:first + half], (((0,), (0,)), (()...]
    gather x4 -> x0, local copies, waits for them, and re-layouts: 8.92 us -> none  [the longest x1 5.23 us: fast(): picked_g = jnp.take(out_grad, sample_rows, axis=0)]
    slice x10 -> x0, local copies, waits for them, and re-layouts: 6.77 us -> none  [the longest x6 5.79 us: decode(): power = packed[-1, 0].astype(f32)]
    reduce_max x6 -> x0, other arithmetic: 5.08 us -> none  [encode(): top = jnp.max(jnp.abs(value))]
    unnamed x20 -> x16, local copies, waits for them, and re-layouts: 0.87 us -> 5.53 us
    mul x4 -> x0, other arithmetic: 4.16 us -> none  [decode(): return packed[:-16].astype(f32) * jnp.exp2(power - 14.0)]
  transfers between devices with their start and end apart: 21 -> 21, of which waited for: 14 -> 16; matrix products, arithmetic and copies ran while one was open for 23% -> 1% of each run, Pallas kernels for 0% -> 14%
where the time goes in v2:
time: 138 us
  waiting for transfers between devices  61.8 us (45%)
  starting transfers between devices  39.1 us (28%)
  Pallas kernels  23.4 us (17%)
  local copies, waits for them, and re-layouts  8.21 us (6%)
  other arithmetic  3.26 us (2%)
  between operations  2.2 us (2%)
    ppermute x18, waiting for transfers between devices, swap(): return lax.ppermute(value, 'shard', [(i, i ^ bit) for i in range(8)])  59.4 us
    ppermute x18, starting transfers between devices, swap(): return lax.ppermute(value, 'shard', [(i, i ^ bit) for i in range(8)])  29.1 us
    ppermute x2, starting transfers between devices, swap_t(): return lax.ppermute(value, 'tensor', [(i, i ^ bit) for i in range(4)])  9.21 us
    pallas_call x1, Pallas kernels, fast(): pl.pallas_call(lambda *refs: partial_kernel_x(group_cols, width_g, *refs)...  6.56 us
    unnamed x16, local copies, waits for them, and re-layouts  5.53 us
    pallas_call x1, Pallas kernels, fast(): pl.pallas_call(lambda *refs: factor_kernel(share, *refs), in_specs=[smem]...  5.39 us
    pallas_call x1, Pallas kernels, fast(): pl.pallas_call(lambda *refs: partial_kernel_l(width_g, *refs), grid=(4,),...  3.76 us
    pallas_call x4, Pallas kernels, add_step(): pl.pallas_call(lambda *refs: add_kernel(bit_at, inner, *refs), in_specs=[...  3.35 us
  transfers between devices with their start and end apart: 21, of which 16 were waited for; matrix products, arithmetic and copies ran while one was open for 1% of the time, Pallas kernels for 14%

profile of v2, /device:TPU:0, one launch (start us, length us, event | category | flops | bytes accessed | tf_op | source)
XLA Modules:
  0.0 138.0 jit_solution(17510606793562205578)
XLA Ops:
  2.8 3.2 %copy-done.1 = bf16[2048,1920]{1,0:T(8,128)(2,1)S(1)} copy-done((bf16[2048,1920]{1,0:T(8,128)(2,1)S(1)}, bf16[2048,1920]{1,0:T(8,128)(2,1)}, u32[]{:S(2)}) %copy-start.1) | copy-done | bytes 7864344
  6.1 1.6 %copy-done.2 = bf16[2048,512]{1,0:T(8,128)(2,1)S(1)} copy-done((bf16[2048,512]{1,0:T(8,128)(2,1)S(1)}, bf16[2048,512]{1,0:T(8,128)(2,1)}, u32[]{:S(2)}) %copy-start.2) | copy-done | bytes 2097176
  7.7 2.1 %picks.1.refs_1_ = bf16[64,1024]{1,0:T(8,128)(2,1)S(1)} custom-call(s32[14]{0:T(128)S(1)} %concatenate.21.refs_0_.info, s32[64,1]{1,0:T(8,128)S(1)} %copy.15.refs_1_, bf16[2048,512]{1,0:T(8,128)(2,1)S(1)} %copy-done.2, bf16[2048,1920]{1,0:T(8,128)(2,1)S(1)} %copy-done.1), custom_call_target="tpu_custom_call" | custom-call | tf_op jit(solution)/shard_map/picks/pallas_call | solution.py:395
  9.8 4.1 %collective-permute-start = (bf16[64,1024]{1,0:T(8,128)(2,1)S(1)}, bf16[64,1024]{1,0:T(8,128)(2,1)S(1)}, u32[]{:S(2)}, u32[]{:S(2)}) collective-permute-start(bf16[64,1024]{1,0:T(8,128)(2,1)S(1)} %picks.1.refs_1_), channel_id=1, source_target_pairs={{0,16},{4,20},{8,24},{12,28},{16,0},{20,4},{24,8},{28,12},{1,17},{... | collective-permute-start | bytes 393224 | tf_op jit(solution)/shard_map/ppermute | solution.py:126
  13.9 6.4 %collective-permute-done.refs_2_ = bf16[64,1024]{1,0:T(8,128)(2,1)S(1)} collective-permute-done((bf16[64,1024]{1,0:T(8,128)(2,1)S(1)}, bf16[64,1024]{1,0:T(8,128)(2,1)S(1)}, u32[]{:S(2)}, u32[]{:S(2)}) %collective-permute-start) | collective-permute-done | bytes 131104 | tf_op jit(solution)/shard_map/ppermute | solution.py:126
  21.1 6.6 %partial_x.1 = (s16[4,256,256]{2,1,0:T(8,128)(2,1)S(1)}, f32[4,240,256]{2,1,0:T(8,128)S(1)}, bf16[1920,2048]{1,0:T(8,128)(2,1)S(1)}) custom-call(s32[14]{0:T(128)S(1)} %concatenate.21.refs_0_.info, bf16[2048,1920]{1,0:T(8,128)(2,1)} %refs_1_.1, bf16[2048,512]{1,0:T(8,128)(2,1)S(1)} %copy-done.3), custom_call_target="tpu_custom_call" | custom-call | tf_op jit(solution)/shard_map/partial_x/pallas_call | solution.py:413
  27.7 3.8 %partial_l.1 = (s16[4,256,256]{2,1,0:T(8,128)(2,1)S(1)}, f32[4,240,256]{2,1,0:T(8,128)S(1)}) custom-call(s32[14]{0:T(128)S(1)} %concatenate.21.refs_0_.info, bf16[1920,2048]{1,0:T(8,128)(2,1)S(1)} %get-tuple-element.33.refs_1_, bf16[2048,512]{1,0:T(8,128)(2,1)S(1)} %copy-done.3), custom_call_target="tpu_custom_call" | custom-call | tf_op jit(solution)/shard_map/partial_l/pallas_call | solution.py:436
  32.8 1.5 %collective-permute-start.3 = (s16[4,256,256]{2,1,0:T(8,128)(2,1)S(1)}, s16[4,256,256]{2,1,0:T(8,128)(2,1)S(1)}, u32[]{:S(2)}, u32[]{:S(2)}) collective-permute-start(s16[4,256,256]{2,1,0:T(8,128)(2,1)S(1)} %get-tuple-element.27), channel_id=1, source_target_pairs={{0,4},{4,0},{8,12},{12,8},{16,20},{20,16},{24,28},{28,24},{1,5},{5... | collective-permute-start | bytes 1572872 | tf_op jit(solution)/shard_map/ppermute | solution.py:126
  35.0 10.1 %collective-permute-done.6.refs_1_ = s16[4,256,256]{2,1,0:T(8,128)(2,1)S(1)} collective-permute-done((s16[4,256,256]{2,1,0:T(8,128)(2,1)S(1)}, s16[4,256,256]{2,1,0:T(8,128)(2,1)S(1)}, u32[]{:S(2)}, u32[]{:S(2)}) %collective-permute-start.6) | collective-permute-done | bytes 524320 | tf_op jit(solution)/shard_map/ppermute | solution.py:126
  46.0 1.5 %collective-permute-start.7 = (s16[2,256,256]{2,1,0:T(8,128)(2,1)S(1)}, s16[2,256,256]{2,1,0:T(8,128)(2,1)S(1)}, u32[]{:S(2)}, u32[]{:S(2)}) collective-permute-start(s16[2,256,256]{2,1,0:T(8,128)(2,1)S(1)} %get-tuple-element.36), channel_id=1, source_target_pairs={{0,4},{4,0},{8,12},{12,8},{16,20},{20,16},{24,28},{28,24},{1,5},{5... | collective-permute-start | bytes 786440 | tf_op jit(solution)/shard_map/ppermute | solution.py:126
  49.4 12.9 %collective-permute-done.7.refs_1_ = s16[2,256,256]{2,1,0:T(8,128)(2,1)S(1)} collective-permute-done((s16[2,256,256]{2,1,0:T(8,128)(2,1)S(1)}, s16[2,256,256]{2,1,0:T(8,128)(2,1)S(1)}, u32[]{:S(2)}, u32[]{:S(2)}) %collective-permute-start.7) | collective-permute-done | bytes 262176 | tf_op jit(solution)/shard_map/ppermute | solution.py:126
  63.1 3.1 %collective-permute-start.8 = (s16[1,256,256]{2,1,0:T(8,128)(2,1)S(1)}, s16[1,256,256]{2,1,0:T(8,128)(2,1)S(1)}, u32[]{:S(2)}, u32[]{:S(2)}) collective-permute-start(s16[1,256,256]{2,1,0:T(8,128)(2,1)S(1)} %get-tuple-element.38), channel_id=1, source_target_pairs={{0,16},{4,20},{8,24},{12,28},{16,0},{20,4},{24,8},{28,12},{1,17},{... | collective-permute-start | bytes 393224 | tf_op jit(solution)/shard_map/ppermute | solution.py:126
  67.1 5.4 %factors.1 = (f32[4,128,128]{2,1,0:T(8,128)}, f32[5,96,96]{2,1,0:T(8,128)}, f32[4,128,128]{2,1,0:T(8,128)S(1)}, f32[3,96,96]{2,1,0:T(8,128)S(1)}) custom-call(s32[14]{0:T(128)S(1)} %concatenate.21.refs_0_.info, bf16[64,1024]{1,0:T(8,128)(2,1)S(1)} %picks.1.refs_1_, bf16[64,1024]{1,0:T(8,128)(2,1)S(1)} %collective-permute-done.refs_2_, ...), custom_call_target="tpu_custom_call" | custom-call | tf_op jit(solution)/shard_map/factors/pallas_call | solution.py:465
  73.3 2.0 %collective-permute-done.8.got_b = s16[1,256,256]{2,1,0:T(8,128)(2,1)S(1)} collective-permute-done((s16[1,256,256]{2,1,0:T(8,128)(2,1)S(1)}, s16[1,256,256]{2,1,0:T(8,128)(2,1)S(1)}, u32[]{:S(2)}, u32[]{:S(2)}) %collective-permute-start.8) | collective-permute-done | bytes 131104 | tf_op jit(solution)/shard_map/ppermute | solution.py:126
  75.3 1.9 %collective-permute-done.5.got_a = s16[1,256,256]{2,1,0:T(8,128)(2,1)S(1)} collective-permute-done((s16[1,256,256]{2,1,0:T(8,128)(2,1)S(1)}, s16[1,256,256]{2,1,0:T(8,128)(2,1)S(1)}, u32[]{:S(2)}, u32[]{:S(2)}) %collective-permute-start.5) | collective-permute-done | bytes 131104 | tf_op jit(solution)/shard_map/ppermute | solution.py:126
  77.2 2.2 %precon.1 = (f32[192,512]{1,0:T(8,128)S(1)}, f32[96,256]{1,0:T(8,128)S(1)}, f32[8,256]{1,0:T(8,128)S(1)}) custom-call(s32[14]{0:T(128)S(1)} %concatenate.21.refs_0_.info, s16[1,256,256]{2,1,0:T(8,128)(2,1)S(1)} %collective-permute-done.5.got_a, f32[1,240,256]{2,1,0:T(8,128)S(1)} %get-tuple-element.32.held_a, ...), custom_call_target="tpu_custom_call" | custom-call | tf_op jit(solution)/shard_map/precon/pallas_call | solution.py:490
  79.4 1.9 %collective-permute-start.10 = (f32[8,256]{1,0:T(8,128)S(1)}, f32[8,256]{1,0:T(8,128)S(1)}, u32[]{:S(2)}, u32[]{:S(2)}) collective-permute-start(f32[8,256]{1,0:T(8,128)S(1)} %get-tuple-element.44), channel_id=1, source_target_pairs={{0,1},{1,0},{2,3},{3,2},{4,5},{5,4},{6,7},{7,6},{8,9},{9,8},{10,11... | collective-permute-start | bytes 24584 | tf_op jit(solution)/shard_map/ppermute | solution.py:130
  82.1 7.3 %collective-permute-start.11 = (f32[8,256]{1,0:T(8,128)S(1)}, f32[8,256]{1,0:T(8,128)S(1)}, u32[]{:S(2)}, u32[]{:S(2)}) collective-permute-start(f32[8,256]{1,0:T(8,128)S(1)} %add.36), channel_id=1, source_target_pairs={{0,2},{1,3},{2,0},{3,1},{4,6},{5,7},{6,4},{7,5},{8,10},{9,11},{10,... | collective-permute-start | bytes 24584 | tf_op jit(solution)/shard_map/ppermute | solution.py:130
  89.4 1.6 %collective-permute-done.11 = f32[8,256]{1,0:T(8,128)S(1)} collective-permute-done((f32[8,256]{1,0:T(8,128)S(1)}, f32[8,256]{1,0:T(8,128)S(1)}, u32[]{:S(2)}, u32[]{:S(2)}) %collective-permute-start.11) | collective-permute-done | bytes 8224 | tf_op jit(solution)/shard_map/ppermute | solution.py:130
  91.0 1.5 %collective-permute-start.12 = (f32[56,256]{1,0:T(8,128)S(1)}, f32[56,256]{1,0:T(8,128)S(1)}, u32[]{:S(2)}, u32[]{:S(2)}) collective-permute-start(f32[56,256]{1,0:T(8,128)S(1)} %pad_maximum_fusion.9), channel_id=1, source_target_pairs={{0,4},{4,0},{8,12},{12,8},{16,20},{20,16},{24,28},{28,24},{1,5},{5... | collective-permute-start | bytes 172040 | tf_op jit(solution)/shard_map/ppermute | solution.py:126
  92.6 2.7 %collective-permute-done.12 = f32[56,256]{1,0:T(8,128)S(1)} collective-permute-done((f32[56,256]{1,0:T(8,128)S(1)}, f32[56,256]{1,0:T(8,128)S(1)}, u32[]{:S(2)}, u32[]{:S(2)}) %collective-permute-start.12) | collective-permute-done | bytes 57376 | tf_op jit(solution)/shard_map/ppermute | solution.py:126
  95.8 3.1 %collective-permute-done.13 = f32[8,256]{1,0:T(8,128)S(1)} collective-permute-done((f32[8,256]{1,0:T(8,128)S(1)}, f32[8,256]{1,0:T(8,128)S(1)}, u32[]{:S(2)}, u32[]{:S(2)}) %collective-permute-start.13) | collective-permute-done | bytes 8224 | tf_op jit(solution)/shard_map/ppermute | solution.py:126
  98.9 2.5 %collective-permute-start.14 = (f32[8,256]{1,0:T(8,128)S(1)}, f32[8,256]{1,0:T(8,128)S(1)}, u32[]{:S(2)}, u32[]{:S(2)}) collective-permute-start(f32[8,256]{1,0:T(8,128)S(1)} %add.39), channel_id=1, source_target_pairs={{0,16},{4,20},{8,24},{12,28},{16,0},{20,4},{24,8},{28,12},{1,17},{... | collective-permute-start | bytes 24584 | tf_op jit(solution)/shard_map/ppermute | solution.py:126
  102.0 1.5 %collective-permute-done.14 = f32[8,256]{1,0:T(8,128)S(1)} collective-permute-done((f32[8,256]{1,0:T(8,128)S(1)}, f32[8,256]{1,0:T(8,128)S(1)}, u32[]{:S(2)}, u32[]{:S(2)}) %collective-permute-start.14) | collective-permute-done | bytes 8224 | tf_op jit(solution)/shard_map/ppermute | solution.py:126
  106.5 2.6 %collective-permute-start.15 = (bf16[240,256]{1,0:T(8,128)(2,1)S(1)}, bf16[240,256]{1,0:T(8,128)(2,1)S(1)}, u32[]{:S(2)}, u32[]{:S(2)}) collective-permute-start(bf16[240,256]{1,0:T(8,128)(2,1)S(1)} %get-tuple-element.62), channel_id=1, source_target_pairs={{0,16},{4,20},{8,24},{12,28},{16,0},{20,4},{24,8},{28,12},{1,17},{... | collective-permute-start | bytes 368648 | tf_op jit(solution)/shard_map/ppermute | solution.py:126
  109.1 1.5 %collective-permute-start.18 = (bf16[240,256]{1,0:T(8,128)(2,1)S(1)}, bf16[240,256]{1,0:T(8,128)(2,1)S(1)}, u32[]{:S(2)}, u32[]{:S(2)}) collective-permute-start(bf16[240,256]{1,0:T(8,128)(2,1)S(1)} %get-tuple-element.63), channel_id=1, source_target_pairs={{0,4},{4,0},{8,12},{12,8},{16,20},{20,16},{24,28},{28,24},{1,5},{5... | collective-permute-start | bytes 368648 | tf_op jit(solution)/shard_map/ppermute | solution.py:126
  110.6 3.8 %collective-permute-done.15 = bf16[240,256]{1,0:T(8,128)(2,1)S(1)} collective-permute-done((bf16[240,256]{1,0:T(8,128)(2,1)S(1)}, bf16[240,256]{1,0:T(8,128)(2,1)S(1)}, u32[]{:S(2)}, u32[]{:S(2)}) %collective-permute-start.15) | collective-permute-done | bytes 122912 | tf_op jit(solution)/shard_map/ppermute | solution.py:126
  115.4 3.1 %collective-permute-start.19 = (bf16[2,240,256]{2,1,0:T(8,128)(2,1)S(1)}, bf16[2,240,256]{2,1,0:T(8,128)(2,1)S(1)}, u32[]{:S(2)}, u32[]{:S(2)}) collective-permute-start(bf16[2,240,256]{2,1,0:T(8,128)(2,1)S(1)} %pad_maximum_fusion.8), channel_id=1, source_target_pairs={{0,16},{4,20},{8,24},{12,28},{16,0},{20,4},{24,8},{28,12},{1,17},{... | collective-permute-start | bytes 737288 | tf_op jit(solution)/shard_map/ppermute | solution.py:126
  118.5 5.7 %collective-permute-done.16 = bf16[2,240,256]{2,1,0:T(8,128)(2,1)S(1)} collective-permute-done((bf16[2,240,256]{2,1,0:T(8,128)(2,1)S(1)}, bf16[2,240,256]{2,1,0:T(8,128)(2,1)S(1)}, u32[]{:S(2)}, u32[]{:S(2)}) %collective-permute-start.16) | collective-permute-done | bytes 245792 | tf_op jit(solution)/shard_map/ppermute | solution.py:126
  125.6 1.8 %collective-permute-start.17 = (bf16[2,2,240,256]{3,2,0,1:T(8,128)(2,1)S(1)}, bf16[2,2,240,256]{3,2,0,1:T(8,128)(2,1)S(1)}, u32[]{:S(2)}, u32[]{:S(2)}) collective-permute-start(bf16[2,2,240,256]{3,2,0,1:T(8,128)(2,1)S(1)} %pad_maximum_fusion.4), channel_id=1, source_target_pairs={{0,4},{4,0},{8,12},{12,8},{16,20},{20,16},{24,28},{28,24},{1,5},{5... | collective-permute-start | bytes 1474568 | tf_op jit(solution)/shard_map/ppermute | solution.py:126
  128.2 6.3 %collective-permute-done.17 = bf16[2,2,240,256]{3,2,0,1:T(8,128)(2,1)S(1)} collective-permute-done((bf16[2,2,240,256]{3,2,0,1:T(8,128)(2,1)S(1)}, bf16[2,2,240,256]{3,2,0,1:T(8,128)(2,1)S(1)}, u32[]{:S(2)}, u32[]{:S(2)}) %collective-permute-start.17) | collective-permute-done | bytes 491552 | tf_op jit(solution)/shard_map/ppermute | solution.py:126
  134.7 1.6 %collective-permute-done.20 = bf16[2,2,240,256]{3,2,1,0:T(8,128)(2,1)S(1)} collective-permute-done((bf16[2,2,240,256]{3,2,1,0:T(8,128)(2,1)S(1)}, bf16[2,2,240,256]{3,2,1,0:T(8,128)(2,1)S(1)}, u32[]{:S(2)}, u32[]{:S(2)}) %collective-permute-start.20) | collective-permute-done | bytes 491552 | tf_op jit(solution)/shard_map/ppermute | solution.py:126
  (65 shorter events, 18.8 us)
Async XLA Ops:
  0.6 0.7 copy-start
  2.8 3.2 %copy-start.1 = (bf16[2048,1920]{1,0:T(8,128)(2,1)S(1)}, bf16[2048,1920]{1,0:T(8,128)(2,1)}, u32[]{:S(2)}) copy-start(bf16[2048,1920]{1,0:T(8,128)(2,1)} %refs_1_.1) | copy-start | bytes 23592964
  6.1 1.6 %copy-start.2 = (bf16[2048,512]{1,0:T(8,128)(2,1)S(1)}, bf16[2048,512]{1,0:T(8,128)(2,1)}, u32[]{:S(2)}) copy-start(bf16[2048,512]{1,0:T(8,128)(2,1)} %refs_2_.5) | copy-start | bytes 6291460
  7.7 13.4 %copy-start.3 = (bf16[2048,512]{1,0:T(8,128)(2,1)S(1)}, bf16[2048,512]{1,0:T(8,128)(2,1)}, u32[]{:S(2)}) copy-start(bf16[2048,512]{1,0:T(8,128)(2,1)} %refs_2_.5) | copy-start | bytes 6291460
  9.8 10.5 %collective-permute-start = (bf16[64,1024]{1,0:T(8,128)(2,1)S(1)}, bf16[64,1024]{1,0:T(8,128)(2,1)S(1)}, u32[]{:S(2)}, u32[]{:S(2)}) collective-permute-start(bf16[64,1024]{1,0:T(8,128)(2,1)S(1)} %picks.1.refs_1_), channel_id=1, source_target_pairs={{0,16},{4,20},{8,24},{12,28},{16,0},{20,4},{24,8},{28,12},{1,17},{... | collective-permute-start | bytes 393224 | tf_op jit(solution)/shard_map/ppermute | solution.py:126
  20.3 14.1 %collective-permute-start.1 = (bf16[2,64,1024]{2,1,0:T(8,128)(2,1)S(1)}, bf16[2,64,1024]{2,1,0:T(8,128)(2,1)S(1)}, u32[]{:S(2)}, u32[]{:S(2)}) collective-permute-start(bf16[2,64,1024]{2,1,0:T(8,128)(2,1)S(1)} %pad_maximum_fusion.6), channel_id=1, source_target_pairs={{0,8},{4,12},{8,0},{12,4},{16,24},{20,28},{24,16},{28,20},{1,9},{5... | collective-permute-start | bytes 786440 | tf_op jit(solution)/shard_map/ppermute | solution.py:126
  31.4 35.6 %copy-start.4 = (f32[1,4,128,128]{3,2,1,0:T(8,128)S(1)}, f32[1,4,128,128]{3,2,1,0:T(8,128)}, u32[]{:S(2)}) copy-start(f32[1,4,128,128]{3,2,1,0:T(8,128)} %param.14) | copy-start | bytes 786436
  31.5 35.6 %copy-start.5 = (f32[1,5,96,96]{3,2,1,0:T(8,128)S(1)}, f32[1,5,96,96]{3,2,1,0:T(8,128)}, u32[]{:S(2)}) copy-start(f32[1,5,96,96]{3,2,1,0:T(8,128)} %param.15) | copy-start | bytes 552964
  31.5 13.6 %collective-permute-start.6 = (s16[4,256,256]{2,1,0:T(8,128)(2,1)S(1)}, s16[4,256,256]{2,1,0:T(8,128)(2,1)S(1)}, u32[]{:S(2)}, u32[]{:S(2)}) collective-permute-start(s16[4,256,256]{2,1,0:T(8,128)(2,1)S(1)} %get-tuple-element.34), channel_id=1, source_target_pairs={{0,8},{4,12},{8,0},{12,4},{16,24},{20,28},{24,16},{28,20},{1,9},{5... | collective-permute-start | bytes 1572872 | tf_op jit(solution)/shard_map/ppermute | solution.py:126
  32.8 14.9 %collective-permute-start.3 = (s16[4,256,256]{2,1,0:T(8,128)(2,1)S(1)}, s16[4,256,256]{2,1,0:T(8,128)(2,1)S(1)}, u32[]{:S(2)}, u32[]{:S(2)}) collective-permute-start(s16[4,256,256]{2,1,0:T(8,128)(2,1)S(1)} %get-tuple-element.27), channel_id=1, source_target_pairs={{0,4},{4,0},{8,12},{12,8},{16,20},{20,16},{24,28},{28,24},{1,5},{5... | collective-permute-start | bytes 1572872 | tf_op jit(solution)/shard_map/ppermute | solution.py:126
  34.4 32.6 %collective-permute-start.2 = (bf16[4,64,1024]{2,1,0:T(8,128)(2,1)S(1)}, bf16[4,64,1024]{2,1,0:T(8,128)(2,1)S(1)}, u32[]{:S(2)}, u32[]{:S(2)}) collective-permute-start(bf16[4,64,1024]{2,1,0:T(8,128)(2,1)S(1)} %pad_maximum_fusion.3), channel_id=1, source_target_pairs={{0,4},{4,0},{8,12},{12,8},{16,20},{20,16},{24,28},{28,24},{1,5},{5... | collective-permute-start | bytes 1572872 | tf_op jit(solution)/shard_map/ppermute | solution.py:126
  45.1 60.3 %copy-start.6 = (f32[240,512]{1,0:T(8,128)S(1)}, f32[240,512]{1,0:T(8,128)}, u32[]{:S(2)}) copy-start(f32[240,512]{1,0:T(8,128)} %param.17) | copy-start | bytes 1474564
  45.1 60.3 %copy-start.7 = (f32[240,512]{1,0:T(8,128)S(1)}, f32[240,512]{1,0:T(8,128)}, u32[]{:S(2)}) copy-start(f32[240,512]{1,0:T(8,128)} %param.16) | copy-start | bytes 1474564
  46.0 16.3 %collective-permute-start.7 = (s16[2,256,256]{2,1,0:T(8,128)(2,1)S(1)}, s16[2,256,256]{2,1,0:T(8,128)(2,1)S(1)}, u32[]{:S(2)}, u32[]{:S(2)}) collective-permute-start(s16[2,256,256]{2,1,0:T(8,128)(2,1)S(1)} %get-tuple-element.36), channel_id=1, source_target_pairs={{0,4},{4,0},{8,12},{12,8},{16,20},{20,16},{24,28},{28,24},{1,5},{5... | collective-permute-start | bytes 786440 | tf_op jit(solution)/shard_map/ppermute | solution.py:126
  48.6 17.6 %collective-permute-start.4 = (s16[2,256,256]{2,1,0:T(8,128)(2,1)S(1)}, s16[2,256,256]{2,1,0:T(8,128)(2,1)S(1)}, u32[]{:S(2)}, u32[]{:S(2)}) collective-permute-start(s16[2,256,256]{2,1,0:T(8,128)(2,1)S(1)} %get-tuple-element.29), channel_id=1, source_target_pairs={{0,8},{4,12},{8,0},{12,4},{16,24},{20,28},{24,16},{28,20},{1,9},{5... | collective-permute-start | bytes 786440 | tf_op jit(solution)/shard_map/ppermute | solution.py:126
  63.1 12.2 %collective-permute-start.8 = (s16[1,256,256]{2,1,0:T(8,128)(2,1)S(1)}, s16[1,256,256]{2,1,0:T(8,128)(2,1)S(1)}, u32[]{:S(2)}, u32[]{:S(2)}) collective-permute-start(s16[1,256,256]{2,1,0:T(8,128)(2,1)S(1)} %get-tuple-element.38), channel_id=1, source_target_pairs={{0,16},{4,20},{8,24},{12,28},{16,0},{20,4},{24,8},{28,12},{1,17},{... | collective-permute-start | bytes 393224 | tf_op jit(solution)/shard_map/ppermute | solution.py:126
  67.0 10.2 %collective-permute-start.5 = (s16[1,256,256]{2,1,0:T(8,128)(2,1)S(1)}, s16[1,256,256]{2,1,0:T(8,128)(2,1)S(1)}, u32[]{:S(2)}, u32[]{:S(2)}) collective-permute-start(s16[1,256,256]{2,1,0:T(8,128)(2,1)S(1)} %get-tuple-element.31), channel_id=1, source_target_pairs={{0,16},{4,20},{8,24},{12,28},{16,0},{20,4},{24,8},{28,12},{1,17},{... | collective-permute-start | bytes 393224 | tf_op jit(solution)/shard_map/ppermute | solution.py:126
  72.5 4.7 %collective-permute-start.9 = (f32[3,96,96]{2,1,0:T(8,128)S(1)}, f32[3,96,96]{2,1,0:T(8,128)S(1)}, u32[]{:S(2)}, u32[]{:S(2)}) collective-permute-start(f32[3,96,96]{2,1,0:T(8,128)S(1)} %get-tuple-element.40), channel_id=1, source_target_pairs={{0,0},{1,8},{2,16},{3,24},{4,4},{5,12},{6,20},{7,28},{8,1},{9,9},{... | collective-permute-start | bytes 331784 | tf_op jit(solution)/shard_map/ppermute | solution.py:488
  79.4 2.7 %collective-permute-start.10 = (f32[8,256]{1,0:T(8,128)S(1)}, f32[8,256]{1,0:T(8,128)S(1)}, u32[]{:S(2)}, u32[]{:S(2)}) collective-permute-start(f32[8,256]{1,0:T(8,128)S(1)} %get-tuple-element.44), channel_id=1, source_target_pairs={{0,1},{1,0},{2,3},{3,2},{4,5},{5,4},{6,7},{7,6},{8,9},{9,8},{10,11... | collective-permute-start | bytes 24584 | tf_op jit(solution)/shard_map/ppermute | solution.py:130
  82.1 8.9 %collective-permute-start.11 = (f32[8,256]{1,0:T(8,128)S(1)}, f32[8,256]{1,0:T(8,128)S(1)}, u32[]{:S(2)}, u32[]{:S(2)}) collective-permute-start(f32[8,256]{1,0:T(8,128)S(1)} %add.36), channel_id=1, source_target_pairs={{0,2},{1,3},{2,0},{3,1},{4,6},{5,7},{6,4},{7,5},{8,10},{9,11},{10,... | collective-permute-start | bytes 24584 | tf_op jit(solution)/shard_map/ppermute | solution.py:130
  91.0 4.2 %collective-permute-start.12 = (f32[56,256]{1,0:T(8,128)S(1)}, f32[56,256]{1,0:T(8,128)S(1)}, u32[]{:S(2)}, u32[]{:S(2)}) collective-permute-start(f32[56,256]{1,0:T(8,128)S(1)} %pad_maximum_fusion.9), channel_id=1, source_target_pairs={{0,4},{4,0},{8,12},{12,8},{16,20},{20,16},{24,28},{28,24},{1,5},{5... | collective-permute-start | bytes 172040 | tf_op jit(solution)/shard_map/ppermute | solution.py:126
  95.3 3.7 %collective-permute-start.13 = (f32[8,256]{1,0:T(8,128)S(1)}, f32[8,256]{1,0:T(8,128)S(1)}, u32[]{:S(2)}, u32[]{:S(2)}) collective-permute-start(f32[8,256]{1,0:T(8,128)S(1)} %slice_add_fusion), channel_id=1, source_target_pairs={{0,8},{4,12},{8,0},{12,4},{16,24},{20,28},{24,16},{28,20},{1,9},{5... | collective-permute-start | bytes 24584 | tf_op jit(solution)/shard_map/ppermute | solution.py:126
  98.9 4.5 %collective-permute-start.14 = (f32[8,256]{1,0:T(8,128)S(1)}, f32[8,256]{1,0:T(8,128)S(1)}, u32[]{:S(2)}, u32[]{:S(2)}) collective-permute-start(f32[8,256]{1,0:T(8,128)S(1)} %add.39), channel_id=1, source_target_pairs={{0,16},{4,20},{8,24},{12,28},{16,0},{20,4},{24,8},{28,12},{1,17},{... | collective-permute-start | bytes 24584 | tf_op jit(solution)/shard_map/ppermute | solution.py:126
  106.5 7.9 %collective-permute-start.15 = (bf16[240,256]{1,0:T(8,128)(2,1)S(1)}, bf16[240,256]{1,0:T(8,128)(2,1)S(1)}, u32[]{:S(2)}, u32[]{:S(2)}) collective-permute-start(bf16[240,256]{1,0:T(8,128)(2,1)S(1)} %get-tuple-element.62), channel_id=1, source_target_pairs={{0,16},{4,20},{8,24},{12,28},{16,0},{20,4},{24,8},{28,12},{1,17},{... | collective-permute-start | bytes 368648 | tf_op jit(solution)/shard_map/ppermute | solution.py:126
  109.1 5.3 %collective-permute-start.18 = (bf16[240,256]{1,0:T(8,128)(2,1)S(1)}, bf16[240,256]{1,0:T(8,128)(2,1)S(1)}, u32[]{:S(2)}, u32[]{:S(2)}) collective-permute-start(bf16[240,256]{1,0:T(8,128)(2,1)S(1)} %get-tuple-element.63), channel_id=1, source_target_pairs={{0,4},{4,0},{8,12},{12,8},{16,20},{20,16},{24,28},{28,24},{1,5},{5... | collective-permute-start | bytes 368648 | tf_op jit(solution)/shard_map/ppermute | solution.py:126
  114.5 9.7 %collective-permute-start.16 = (bf16[2,240,256]{2,1,0:T(8,128)(2,1)S(1)}, bf16[2,240,256]{2,1,0:T(8,128)(2,1)S(1)}, u32[]{:S(2)}, u32[]{:S(2)}) collective-permute-start(bf16[2,240,256]{2,1,0:T(8,128)(2,1)S(1)} %pad_maximum_fusion.7), channel_id=1, source_target_pairs={{0,8},{4,12},{8,0},{12,4},{16,24},{20,28},{24,16},{28,20},{1,9},{5... | collective-permute-start | bytes 737288 | tf_op jit(solution)/shard_map/ppermute | solution.py:126
  115.4 10.1 %collective-permute-start.19 = (bf16[2,240,256]{2,1,0:T(8,128)(2,1)S(1)}, bf16[2,240,256]{2,1,0:T(8,128)(2,1)S(1)}, u32[]{:S(2)}, u32[]{:S(2)}) collective-permute-start(bf16[2,240,256]{2,1,0:T(8,128)(2,1)S(1)} %pad_maximum_fusion.8), channel_id=1, source_target_pairs={{0,16},{4,20},{8,24},{12,28},{16,0},{20,4},{24,8},{28,12},{1,17},{... | collective-permute-start | bytes 737288 | tf_op jit(solution)/shard_map/ppermute | solution.py:126
  125.6 8.9 %collective-permute-start.17 = (bf16[2,2,240,256]{3,2,0,1:T(8,128)(2,1)S(1)}, bf16[2,2,240,256]{3,2,0,1:T(8,128)(2,1)S(1)}, u32[]{:S(2)}, u32[]{:S(2)}) collective-permute-start(bf16[2,2,240,256]{3,2,0,1:T(8,128)(2,1)S(1)} %pad_maximum_fusion.4), channel_id=1, source_target_pairs={{0,4},{4,0},{8,12},{12,8},{16,20},{20,16},{24,28},{28,24},{1,5},{5... | collective-permute-start | bytes 1474568 | tf_op jit(solution)/shard_map/ppermute | solution.py:126
  127.4 8.9 %collective-permute-start.20 = (bf16[2,2,240,256]{3,2,1,0:T(8,128)(2,1)S(1)}, bf16[2,2,240,256]{3,2,1,0:T(8,128)(2,1)S(1)}, u32[]{:S(2)}, u32[]{:S(2)}) collective-permute-start(bf16[2,2,240,256]{3,2,1,0:T(8,128)(2,1)S(1)} %pad_maximum_fusion.5), channel_id=1, source_target_pairs={{0,8},{4,12},{8,0},{12,4},{16,24},{20,28},{24,16},{28,20},{1,9},{5... | collective-permute-start | bytes 1474568 | tf_op jit(solution)/shard_map/ppermute | solution.py:126

commit v3 on v2

--- a/solution.py
+++ b/solution.py
@@ -111,7 +111,7 @@
 GROUP = 16
 vmem = pl.BlockSpec(memory_space=pltpu.VMEM)
 smem = pl.BlockSpec(memory_space=pltpu.SMEM)
-anywhere = pl.BlockSpec(memory_space=pl.ANY)
+main = pl.BlockSpec(memory_space=pl.ANY)
 
 
 def params(mib):
@@ -120,6 +120,10 @@
 
 def shaped(shape, kind):
     return jax.ShapeDtypeStruct(shape, kind)
+
+
+def cost(flops, moved):
+    return pl.CostEstimate(flops=flops, bytes_accessed=moved, transcendentals=0)
 
 
 def swap(value, bit):
@@ -170,21 +174,38 @@
     block = 128
     span = grad_buf.shape[1]
     tokens, cols = acts.shape
+    chunk = tokens // 4
     last = out_grad.shape[1] // block - span // block
-    start = jnp.minimum((group * group_cols) // block, last)
-    first = pltpu.make_async_copy(acts, acts_buf, sems.at[0])
-    second = pltpu.make_async_copy(
-        out_grad.at[:, pl.ds(pl.multiple_of(start * block, block), span)], grad_buf, sems.at[1]
-    )
-    first.start()
-    second.start()
-    place = lax.broadcasted_iota(jnp.int32, (sampled.shape[0], tokens), 1)
-    chosen = (place == sampled[...]).astype(bf16)
-    first.wait()
-    picks[:, :cols] = jnp.dot(chosen, acts_buf[...], preferred_element_type=f32).astype(bf16)
-    second.wait()
-    grads = jnp.dot(chosen, grad_buf[...], preferred_element_type=f32)
-    pad = jnp.zeros((grads.shape[0], picks.shape[1] - cols - group_cols), f32)
+    start = pl.multiple_of(jnp.minimum((group * group_cols) // block, last) * block, block)
+    copies = []
+    for part in range(4):
+        some = pl.ds(part * chunk, chunk)
+        copies.append(
+            (
+                pltpu.make_async_copy(acts.at[some, :], acts_buf.at[some, :], sems.at[part]),
+                pltpu.make_async_copy(
+                    out_grad.at[some, pl.ds(start, span)], grad_buf.at[some, :], sems.at[4 + part]
+                ),
+            )
+        )
+        for copy in copies[-1]:
+            copy.start()
+    drawn = sampled.shape[1]
+    row = lax.broadcasted_iota(jnp.int32, (drawn, drawn), 0)
+    col = lax.broadcasted_iota(jnp.int32, (drawn, drawn), 1)
+    upright = jnp.sum(jnp.where(row == col, sampled[...], 0), axis=1, keepdims=True)
+    found = jnp.zeros((drawn, cols), f32)
+    grads = jnp.zeros((drawn, span), f32)
+    for part in range(4):
+        place = lax.broadcasted_iota(jnp.int32, (drawn, chunk), 1) + part * chunk
+        chosen = (place == upright).astype(bf16)
+        some = slice(part * chunk, (part + 1) * chunk)
+        copies[part][0].wait()
+        found += jnp.dot(chosen, acts_buf[some, :], preferred_element_type=f32)
+        copies[part][1].wait()
+        grads += jnp.dot(chosen, grad_buf[some, :], preferred_element_type=f32)
+    picks[:, :cols] = found.astype(bf16)
+    pad = jnp.zeros((drawn, picks.shape[1] - cols - group_cols), f32)
     for which in range(4):
         begin = min((which * group_cols) // block, last) * block
         offset = which * group_cols - begin
@@ -209,45 +230,54 @@
     )
 
 
-def partial_kernel_x(group_cols, width_g, info, out_grad, acts, send, keep, turned, raw):
-    step = pl.program_id(0)
-    side = info[1]
+def partial_kernel(
+    group_cols, width_g, info, out_grad, acts, send_a, keep_a, send_b, keep_b, grad_buf, acts_buf,
+    raw, sems
+):
+    side, low = info[1], info[2]
     head = 2 * width_g
-    block = out_grad.shape[1]
-    flipped = out_grad[...].T
-    turned[...] = flipped
-    first = pl.multiple_of(step * block, block)
-    raw[pl.ds(first, block), :] = jnp.dot(flipped, acts[...], preferred_element_type=f32)
-
-    @pl.when(step > 0)
-    def _():
-        place = step - 1
-        start = pl.multiple_of(place * group_cols, 8)
-        units = split_units(raw[pl.ds(start, group_cols), :], head, width_g)
-        for x in range(2):
-
-            @pl.when(side == x)
+    outs = out_grad.shape[1]
+    half = acts.shape[1] // 2
+    block = outs // 5
+    first = pltpu.make_async_copy(acts, acts_buf, sems.at[5])
+    first.start()
+    copies = []
+    for step in range(5):
+        columns = pl.ds(step * block, block)
+        copies.append(
+            pltpu.make_async_copy(out_grad.at[:, columns], grad_buf.at[:, columns], sems.at[step])
+        )
+        copies[-1].start()
+    first.wait()
+    for step in range(5):
+        copies[step].wait()
+        columns = slice(step * block, (step + 1) * block)
+        raw[columns, :] = jnp.dot(
+            grad_buf[:, columns].T, acts_buf[...], preferred_element_type=f32
+        )
+        if step > 0:
+            place = step - 1
+            span = slice(place * group_cols, (place + 1) * group_cols)
+            units = split_units(raw[span, :half], head, width_g)
+            for x in range(2):
+
+                @pl.when(side == x)
+                def _():
+                    keep_a[place] = units[x]
+                    encode_to(send_a, place, units[1 - x])
+
+            units = split_units(raw[span, half:], head, width_g)
+            high = place // 2
+
+            @pl.when(place % 2 == low)
             def _():
-                keep[place] = units[x]
-                encode_to(send, place, units[1 - x])
-
-
-def partial_kernel_l(width_g, info, turned, acts, send, keep):
-    place = pl.program_id(0)
-    low = info[2]
-    raw = jnp.dot(turned[...], acts[...], preferred_element_type=f32)
-    units = split_units(raw, 2 * width_g, width_g)
-    high = place // 2
-
-    @pl.when(place % 2 == low)
-    def _():
-        for x in range(2):
-            keep[2 * high + x] = units[x]
-
-    @pl.when(place % 2 != low)
-    def _():
-        for x in range(2):
-            encode_to(send, 2 * high + x, units[x])
+                for x in range(2):
+                    keep_b[2 * high + x] = units[x]
+
+            @pl.when(place % 2 != low)
+            def _():
+                for x in range(2):
+                    encode_to(send_b, 2 * high + x, units[x])
 
 
 def add_kernel(bit_at, inner, info, got, held, send, keep):
@@ -282,9 +312,9 @@
 
 
 def factor_kernel(
-    share, info, own, one, two, four, a_state, g_state, a_new, g_new, inv_a, needed, picks, inv_g
+    share, info, own_a, own_g, own, one, two, four, a_state, g_state, a_new, g_new, inv_a, needed, picks, inv_g
 ):
-    shard = info[3]
+    group, shard = info[0], info[3]
     picks[shard] = own[...]
     picks[shard ^ 4] = one[...]
     for j in range(2):
@@ -305,7 +335,7 @@
         stats = lax.dot_general(
             rows, rows, (((0,), (0,)), ((), ())), preferred_element_type=f32
         )
-        slot = info[4 + index]
+        slot = own_a[group, place] if is_a else own_g[group, place]
         stored = (a_state if is_a else g_state)[slot]
         factor = factor_decay * stored + share * stats
         (a_new if is_a else g_new)[slot] = factor
@@ -368,6 +398,42 @@
     total[...] = jnp.full(total.shape, jnp.sum(squares), f32)
 
 
+def update_kernel(
+    entries, info, total, got_total, top, middle, got, momentum, weight, momentum_new, weight_new,
+    rounded_a, rounded_b
+):
+    rows, cols = momentum.shape
+    half = cols // 2
+    quarter = half // 2
+    head = top.shape[0]
+    mid = rows - head
+    mean_sq = (total[0:1, :] + got_total[0:1, :]) / entries
+    factor = 1.0 / jnp.sqrt(mean_sq + epsilon_sq)
+    factor = jnp.concatenate([factor, factor], axis=1)
+
+    def step(place, precon):
+        span = slice(place, place + precon.shape[0])
+        moved = momentum_rate * momentum[span, :] + precon * factor + decay_rate * weight[span, :]
+        fresh = weight[span, :] - learn_rate * moved
+        momentum_new[span, :] = moved
+        weight_new[span, :] = fresh
+        rounded_a[span, :] = fresh[:, :half].astype(bf16)
+        rounded_b[span, :] = fresh[:, half:].astype(bf16)
+
+    for x in range(2):
+
+        @pl.when(info[1] == x)
+        def _():
+            own = middle[mid * x : mid * (x + 1), :]
+            pairs = []
+            for piece in range(2):
+                columns = slice(piece * quarter, (piece + 1) * quarter)
+                both = [own[:, columns], got[:mid, columns]]
+                pairs += both if x == 0 else both[::-1]
+            step(head * (1 - x), jnp.concatenate(pairs, axis=1))
+            step(mid * x, top[...])
+
+
 def fast(acts, out_grad, sample_rows, own_a, own_g, a_state, g_state, momentum, weight):
     shard_pos = lax.axis_index("shard")
     tensor_pos = lax.axis_index("tensor")
@@ -384,75 +450,50 @@
     half = cols // 2
     head = 2 * width_g
     mid = width_g // 2
-    row_a = lax.dynamic_index_in_dim(own_a, tensor_pos, 0, keepdims=False)
-    row_g = lax.dynamic_index_in_dim(own_g, tensor_pos, 0, keepdims=False)
-    info = jnp.concatenate(
-        [jnp.stack([tensor_pos, side, low, shard_pos]), row_a, row_g, high.reshape(1)]
-    )
-    high_at = 4 + count_a + count_g
+    info = jnp.stack([tensor_pos, side, low, shard_pos, high])
+    high_at = 4
 
     wide = cols + -(-group_cols // 128) * 128
     picks = pl.pallas_call(
         lambda *refs: picks_kernel(group_cols, *refs),
-        in_specs=[smem, vmem, anywhere, anywhere],
+        in_specs=[smem, vmem, main, main],
         out_specs=vmem,
         out_shape=shaped((drawn, wide), bf16),
         scratch_shapes=[
             pltpu.VMEM((tokens, cols), bf16),
             pltpu.VMEM((tokens, 640), bf16),
-            pltpu.SemaphoreType.DMA((2,)),
+            pltpu.SemaphoreType.DMA((8,)),
         ],
-        compiler_params=params(24),
+        compiler_params=params(60),
+        cost_estimate=cost(2 * drawn * tokens * (cols + 640), 5 * 2**20),
         name="picks",
-    )(info, sample_rows.reshape(-1, 1), acts, out_grad)
+    )(info, sample_rows.reshape(1, -1), acts, out_grad)
     one = swap(picks, 4)
-    two = swap(jnp.stack([picks, one]), 2)
-    four = swap(jnp.concatenate([picks[None], one[None], two]), 1)
-
-    block = outs // 5
-    send_a, keep_a, turned = pl.pallas_call(
-        lambda *refs: partial_kernel_x(group_cols, width_g, *refs),
-        grid=(5,),
-        in_specs=[
-            smem,
-            pl.BlockSpec((tokens, block), lambda i: (0, i)),
-            pl.BlockSpec((tokens, half), lambda i: (0, 0)),
-        ],
-        out_specs=[
-            pl.BlockSpec((4, rows + GROUP, half), lambda i: (0, 0, 0)),
-            pl.BlockSpec((4, rows, half), lambda i: (0, 0, 0)),
-            pl.BlockSpec((block, tokens), lambda i: (i, 0)),
-        ],
+
+    send_a, keep_a, send_b, keep_b = pl.pallas_call(
+        lambda *refs: partial_kernel(group_cols, width_g, *refs),
+        in_specs=[smem, main, main],
+        out_specs=[vmem] * 4,
         out_shape=[
             shaped((4, rows + GROUP, half), jnp.int16),
             shaped((4, rows, half), f32),
-            shaped((outs, tokens), bf16),
+        ]
+        * 2,
+        scratch_shapes=[
+            pltpu.VMEM((tokens, outs), bf16),
+            pltpu.VMEM((tokens, cols), bf16),
+            pltpu.VMEM((outs, cols), f32),
+            pltpu.SemaphoreType.DMA((6,)),
         ],
-        scratch_shapes=[pltpu.VMEM((outs, half), f32)],
-        compiler_params=params(40),
-        name="partial_x",
+        compiler_params=params(60),
+        cost_estimate=cost(2 * outs * tokens * cols, 10 * 2**20),
+        name="partial",
     )(info, out_grad, acts)
+    one, send_a, send_b = lax.optimization_barrier((one, send_a, send_b))
     got_a = swap(send_a, 1)
-    send_b, keep_b = pl.pallas_call(
-        lambda *refs: partial_kernel_l(width_g, *refs),
-        grid=(4,),
-        in_specs=[
-            smem,
-            pl.BlockSpec((group_cols, tokens), lambda i: (i, 0)),
-            pl.BlockSpec((tokens, half), lambda i: (0, 1)),
-        ],
-        out_specs=[
-            pl.BlockSpec((4, rows + GROUP, half), lambda i: (0, 0, 0)),
-            pl.BlockSpec((4, rows, half), lambda i: (0, 0, 0)),
-        ],
-        out_shape=[
-            shaped((4, rows + GROUP, half), jnp.int16),
-            shaped((4, rows, half), f32),
-        ],
-        compiler_params=params(40),
-        name="partial_l",
-    )(info, turned, acts)
     got_b = swap(send_b, 2)
+    two = swap(jnp.stack([picks, one]), 2)
+    four = swap(jnp.concatenate([picks[None], one[None], two]), 1)
     send_a, keep_a = add_step(info, 2, True, got_a, keep_a)
     got_a = swap(send_a, 2)
     send_b, keep_b = add_step(info, 1, True, got_b, keep_b)
@@ -464,7 +505,7 @@
 
     new_a, new_g, inv_a, needed = pl.pallas_call(
         lambda *refs: factor_kernel(share, *refs),
-        in_specs=[smem] + [vmem] * 6,
+        in_specs=[smem] * 3 + [vmem] * 6,
         out_specs=[vmem] * 4,
         out_shape=[
             shaped(a_state.shape[1:], f32),
@@ -478,7 +519,7 @@
         ],
         compiler_params=params(24),
         name="factors",
-    )(info, picks, one, two, four, a_state[0], g_state[0])
+    )(info, own_a, own_g, picks, one, two, four, a_state[0], g_state[0])
     route = [
         ((2 * a + b) * 4 + c, (2 * c + b) * 4 + a)
         for a in range(4)
@@ -502,42 +543,33 @@
 
     total = total + swap_t(total, 1)
     total = total + swap_t(total, 2)
-    own_mid = pick(side, middle[:mid], middle[mid:])
     give = pick(side, middle[mid:], middle[:mid])
     got = swap(jnp.concatenate([give, total], axis=0), 1)
     total = total + got[mid:]
     total = total + swap(total, 2)
-    total = total + swap(total, 4)
-    mean_sq = total[0, 0] / (rows * 8 * cols * 4)
-    other_mid = got[:mid]
-    quarter = half // 2
-    pairs = []
-    for piece in range(2):
-        span = slice(piece * quarter, (piece + 1) * quarter)
-        pairs += [
-            pick(side, own_mid[:, span], other_mid[:, span]),
-            pick(side, other_mid[:, span], own_mid[:, span]),
-        ]
-    middle_rows = jnp.concatenate(pairs, axis=1)
-    precon = pick(
-        side,
-        jnp.concatenate([top, middle_rows], axis=0),
-        jnp.concatenate([middle_rows, top], axis=0),
-    )
-    update = precon / jnp.sqrt(mean_sq + epsilon_sq)
-    momentum_new = momentum_rate * momentum + update + decay_rate * weight
-    weight_new = weight - learn_rate * momentum_new
-    rounded = weight_new.astype(bf16)
+    momentum_new, weight_new, rounded_a, rounded_b = pl.pallas_call(
+        lambda *refs: update_kernel(rows * 8 * cols * 4, *refs),
+        in_specs=[smem] + [vmem] * 7,
+        out_specs=[vmem] * 4,
+        out_shape=[
+            shaped((rows, cols), f32),
+            shaped((rows, cols), f32),
+            shaped((rows, half), bf16),
+            shaped((rows, half), bf16),
+        ],
+        compiler_params=params(24),
+        name="update",
+    )(info, total, swap(total, 4), top, middle, got, momentum, weight)
 
     def spread(values, bit, flag, axis):
         other = swap(values, bit)
         return jnp.stack([pick(flag, values, other), pick(flag, other, values)], axis=axis)
 
-    piece = rounded[:, :half]
+    piece = rounded_a
     piece = spread(piece, 4, high, 0)
     piece = spread(piece, 2, low, 1)
     whole_a = spread(piece, 1, side, 2).reshape(-1, half)
-    piece = rounded[:, half:]
+    piece = rounded_b
     piece = spread(piece, 1, side, 0)
     piece = spread(piece, 4, high, 0)
     whole_b = spread(piece, 2, low, 1).reshape(-1, half)

time: 138 us -> 123 us (0.89)
  waiting for transfers between devices: 61.8 us -> 53 us
  local copies, waits for them, and re-layouts: 8.21 us -> 1.98 us
  Pallas kernels: 23.4 us -> 27.3 us
  starting transfers between devices: 39.1 us -> 36.4 us
    ppermute x18, waiting for transfers between devices: 59.4 us -> 50.6 us  [swap(): return lax.ppermute(value, 'shard', [(i, i ^ bit) for i in range(8)])]
    unnamed x16 -> x20, local copies, waits for them, and re-layouts: 5.53 us -> 1.25 us
    ppermute x18, starting transfers between devices: 29.1 us -> 24.8 us  [swap(): return lax.ppermute(value, 'shard', [(i, i ^ bit) for i in range(8)])]
    pallas_call x1, Pallas kernels: 2.12 us -> 4.16 us  [fast(): pl.pallas_call(lambda *refs: picks_kernel(group_cols, *refs), in_specs=[s...]
    pallas_call x2, Pallas kernels: 10.3 us -> 12.2 us  [the longest x1 10.5 us: fast(): pl.pallas_call(lambda *refs: partial_kernel(group_cols, width_g, *refs),...]
    ppermute x2, starting transfers between devices: 9.21 us -> 10.9 us  [swap_t(): return lax.ppermute(value, 'tensor', [(i, i ^ bit) for i in range(4)])]
  transfers between devices with their start and end apart: 21 -> 21, of which waited for: 16 -> 15; matrix products, arithmetic and copies ran while one was open for 1% -> 0% of each run, Pallas kernels for 14% -> 16%
where the time goes in v3:
time: 123 us; the launch traced here: 122 us
  waiting for transfers between devices  53 us (43%)
  starting transfers between devices  36.4 us (30%)
  Pallas kernels  27.3 us (22%)
  other arithmetic  2.16 us (2%)
  local copies, waits for them, and re-layouts  1.98 us (2%)
    ppermute x18, waiting for transfers between devices, swap(): return lax.ppermute(value, 'shard', [(i, i ^ bit) for i in range(8)])  50.6 us
    ppermute x18, starting transfers between devices, swap(): return lax.ppermute(value, 'shard', [(i, i ^ bit) for i in range(8)])  24.8 us
    ppermute x2, starting transfers between devices, swap_t(): return lax.ppermute(value, 'tensor', [(i, i ^ bit) for i in range(4)])  10.9 us
    pallas_call x1, Pallas kernels, fast(): pl.pallas_call(lambda *refs: partial_kernel(group_cols, width_g, *refs),...  10.5 us
    pallas_call x1, Pallas kernels, fast(): pl.pallas_call(lambda *refs: factor_kernel(share, *refs), in_specs=[smem]...  5.46 us
    pallas_call x1, Pallas kernels, fast(): pl.pallas_call(lambda *refs: picks_kernel(group_cols, *refs), in_specs=[s...  4.16 us
    pallas_call x4, Pallas kernels, add_step(): pl.pallas_call(lambda *refs: add_kernel(bit_at, inner, *refs), in_specs=[...  3.34 us
  transfers between devices with their start and end apart: 21, of which 15 were waited for; matrix products, arithmetic and copies ran while one was open for 0% of the time, Pallas kernels for 16%

profile of v3, /device:TPU:0, one launch (start us, length us, event | category | flops | bytes accessed | tf_op | source)
XLA Modules:
  0.0 121.8 jit_solution(2779556111017311526)
XLA Ops:
  1.2 4.2 %picks.1.refs_3_ = bf16[64,1024]{1,0:T(8,128)(2,1)} custom-call(s32[5]{0:T(128)} %stack.86.refs_0_.info, s32[1,64]{1,0:T(1,128)} %bitcast.46, bf16[2048,512]{1,0:T(8,128)(2,1)} %refs_2_.4, bf16[2048,1920]{1,0:T(8,128)(2,1)} %refs_1_.2), custom_call_target="tpu_custom_call" | custom-call | flops 301989888 | bytes 5242880 | tf_op jit(solution)/shard_map/picks/pallas_call | solution.py:457
  5.4 4.1 %collective-permute-start = (bf16[64,1024]{1,0:T(8,128)(2,1)}, bf16[64,1024]{1,0:T(8,128)(2,1)S(1)}, u32[]{:S(2)}, u32[]{:S(2)}) collective-permute-start(bf16[64,1024]{1,0:T(8,128)(2,1)} %picks.1.refs_3_), channel_id=1, source_target_pairs={{0,16},{4,20},{8,24},{12,28},{16,0},{20,4},{24,8},{28,12},{1,17},{... | collective-permute-start | bytes 393224 | tf_op jit(solution)/shard_map/ppermute | solution.py:130
  9.5 10.5 %partial.1 = (s16[4,256,256]{2,1,0:T(8,128)(2,1)}, f32[4,240,256]{2,1,0:T(8,128)}, s16[4,256,256]{2,1,0:T(8,128)(2,1)}, f32[4,240,256]{2,1,0:T(8,128)}) custom-call(s32[5]{0:T(128)} %stack.86.refs_0_.info, bf16[2048,1920]{1,0:T(8,128)(2,1)} %refs_1_.2, bf16[2048,512]{1,0:T(8,128)(2,1)} %refs_2_.4), custom_call_target="tpu_custom_call" | custom-call | flops 4026531840 | bytes 10485760 | tf_op jit(solution)/shard_map/partial/pallas_call | solution.py:473
  20.1 1.6 %collective-permute-start.1 = (bf16[2,64,1024]{2,1,0:T(8,128)(2,1)S(1)}, bf16[2,64,1024]{2,1,0:T(8,128)(2,1)S(1)}, u32[]{:S(2)}, u32[]{:S(2)}) collective-permute-start(bf16[2,64,1024]{2,1,0:T(8,128)(2,1)S(1)} %pad_maximum_fusion.6), channel_id=1, source_target_pairs={{0,8},{4,12},{8,0},{12,4},{16,24},{20,28},{24,16},{28,20},{1,9},{5... | collective-permute-start | bytes 786440 | tf_op jit(solution)/shard_map/ppermute | solution.py:130
  21.7 1.6 %collective-permute-start.3 = (s16[4,256,256]{2,1,0:T(8,128)(2,1)}, s16[4,256,256]{2,1,0:T(8,128)(2,1)S(1)}, u32[]{:S(2)}, u32[]{:S(2)}) collective-permute-start(s16[4,256,256]{2,1,0:T(8,128)(2,1)} %get-tuple-element.36), channel_id=1, source_target_pairs={{0,4},{4,0},{8,12},{12,8},{16,20},{20,16},{24,28},{28,24},{1,5},{5... | collective-permute-start | bytes 1572872 | tf_op jit(solution)/shard_map/ppermute | solution.py:130
  23.7 5.6 %collective-permute-done.1.refs_5_ = bf16[2,64,1024]{2,1,0:T(8,128)(2,1)S(1)} collective-permute-done((bf16[2,64,1024]{2,1,0:T(8,128)(2,1)S(1)}, bf16[2,64,1024]{2,1,0:T(8,128)(2,1)S(1)}, u32[]{:S(2)}, u32[]{:S(2)}) %collective-permute-start.1) | collective-permute-done | bytes 262176 | tf_op jit(solution)/shard_map/ppermute | solution.py:130
  29.4 1.6 %collective-permute-start.2 = (bf16[4,64,1024]{2,1,0:T(8,128)(2,1)S(1)}, bf16[4,64,1024]{2,1,0:T(8,128)(2,1)S(1)}, u32[]{:S(2)}, u32[]{:S(2)}) collective-permute-start(bf16[4,64,1024]{2,1,0:T(8,128)(2,1)S(1)} %pad_maximum_fusion.3), channel_id=1, source_target_pairs={{0,4},{4,0},{8,12},{12,8},{16,20},{20,16},{24,28},{28,24},{1,5},{5... | collective-permute-start | bytes 1572872 | tf_op jit(solution)/shard_map/ppermute | solution.py:130
  31.1 5.8 %collective-permute-done.3.refs_1_ = s16[4,256,256]{2,1,0:T(8,128)(2,1)S(1)} collective-permute-done((s16[4,256,256]{2,1,0:T(8,128)(2,1)}, s16[4,256,256]{2,1,0:T(8,128)(2,1)S(1)}, u32[]{:S(2)}, u32[]{:S(2)}) %collective-permute-start.3) | collective-permute-done | bytes 524320 | tf_op jit(solution)/shard_map/ppermute | solution.py:130
  36.8 1.2 copy-done.2
  41.0 1.6 %collective-permute-start.7 = (s16[2,256,256]{2,1,0:T(8,128)(2,1)S(1)}, s16[2,256,256]{2,1,0:T(8,128)(2,1)S(1)}, u32[]{:S(2)}, u32[]{:S(2)}) collective-permute-start(s16[2,256,256]{2,1,0:T(8,128)(2,1)S(1)} %get-tuple-element.44), channel_id=1, source_target_pairs={{0,4},{4,0},{8,12},{12,8},{16,20},{20,16},{24,28},{28,24},{1,5},{5... | collective-permute-start | bytes 786440 | tf_op jit(solution)/shard_map/ppermute | solution.py:130
  42.6 2.8 %collective-permute-done.4.refs_1_ = s16[2,256,256]{2,1,0:T(8,128)(2,1)S(1)} collective-permute-done((s16[2,256,256]{2,1,0:T(8,128)(2,1)S(1)}, s16[2,256,256]{2,1,0:T(8,128)(2,1)S(1)}, u32[]{:S(2)}, u32[]{:S(2)}) %collective-permute-start.4) | collective-permute-done | bytes 262176 | tf_op jit(solution)/shard_map/ppermute | solution.py:130
  46.6 5.4 %collective-permute-done.7.refs_1_ = s16[2,256,256]{2,1,0:T(8,128)(2,1)S(1)} collective-permute-done((s16[2,256,256]{2,1,0:T(8,128)(2,1)S(1)}, s16[2,256,256]{2,1,0:T(8,128)(2,1)S(1)}, u32[]{:S(2)}, u32[]{:S(2)}) %collective-permute-start.7) | collective-permute-done | bytes 262176 | tf_op jit(solution)/shard_map/ppermute | solution.py:130
  53.2 5.5 %factors.1 = (f32[4,128,128]{2,1,0:T(8,128)}, f32[5,96,96]{2,1,0:T(8,128)}, f32[4,128,128]{2,1,0:T(8,128)S(1)}, f32[3,96,96]{2,1,0:T(8,128)S(1)}) custom-call(s32[5]{0:T(128)S(1)} %copy-done.7, s32[4,4]{1,0:T(4,128)S(1)} %copy-done.8, s32[4,5]{1,0:T(4,128)S(1)} %copy-done.9, bf16[64,1024]{1,0:T(8,128)(2,1)S(1)} %copy-done, ...), custom_call_target="tpu_custom_call" | custom-call | tf_op jit(solution)/shard_map/factors/pallas_call | solution.py:506
  60.2 2.2 %precon.1 = (f32[192,512]{1,0:T(8,128)S(1)}, f32[96,256]{1,0:T(8,128)S(1)}, f32[8,256]{1,0:T(8,128)S(1)}) custom-call(s32[5]{0:T(128)S(1)} %copy-done.7, s16[1,256,256]{2,1,0:T(8,128)(2,1)S(1)} %collective-permute-done.5.got_a, f32[1,240,256]{2,1,0:T(8,128)S(1)} %get-tuple-element.41.held_a, s16[1,256,256]{2,1,0:T(8,128)(2,1)S(1)} %collective-permute-done.8.got_b, ...), custom_call_target="tpu_custom_call" | custom-call | tf_op jit(solution)/shard_map/precon/pallas_call | solution.py:531
  62.4 3.7 %collective-permute-start.10 = (f32[8,256]{1,0:T(8,128)S(1)}, f32[8,256]{1,0:T(8,128)S(1)}, u32[]{:S(2)}, u32[]{:S(2)}) collective-permute-start(f32[8,256]{1,0:T(8,128)S(1)} %get-tuple-element.50), channel_id=1, source_target_pairs={{0,1},{1,0},{2,3},{3,2},{4,5},{5,4},{6,7},{7,6},{8,9},{9,8},{10,11... | collective-permute-start | bytes 24584 | tf_op jit(solution)/shard_map/ppermute | solution.py:134
  67.0 7.2 %collective-permute-start.11 = (f32[8,256]{1,0:T(8,128)S(1)}, f32[8,256]{1,0:T(8,128)S(1)}, u32[]{:S(2)}, u32[]{:S(2)}) collective-permute-start(f32[8,256]{1,0:T(8,128)S(1)} %add.16), channel_id=1, source_target_pairs={{0,2},{1,3},{2,0},{3,1},{4,6},{5,7},{6,4},{7,5},{8,10},{9,11},{10,... | collective-permute-start | bytes 24584 | tf_op jit(solution)/shard_map/ppermute | solution.py:134
  74.2 1.6 %collective-permute-done.11 = f32[8,256]{1,0:T(8,128)S(1)} collective-permute-done((f32[8,256]{1,0:T(8,128)S(1)}, f32[8,256]{1,0:T(8,128)S(1)}, u32[]{:S(2)}, u32[]{:S(2)}) %collective-permute-start.11) | collective-permute-done | bytes 8224 | tf_op jit(solution)/shard_map/ppermute | solution.py:134
  75.8 1.6 %collective-permute-start.12 = (f32[56,256]{1,0:T(8,128)S(1)}, f32[56,256]{1,0:T(8,128)S(1)}, u32[]{:S(2)}, u32[]{:S(2)}) collective-permute-start(f32[56,256]{1,0:T(8,128)S(1)} %pad_maximum_fusion.9), channel_id=1, source_target_pairs={{0,4},{4,0},{8,12},{12,8},{16,20},{20,16},{24,28},{28,24},{1,5},{5... | collective-permute-start | bytes 172040 | tf_op jit(solution)/shard_map/ppermute | solution.py:130
  77.4 2.6 %collective-permute-done.12.refs_5_ = f32[56,256]{1,0:T(8,128)S(1)} collective-permute-done((f32[56,256]{1,0:T(8,128)S(1)}, f32[56,256]{1,0:T(8,128)S(1)}, u32[]{:S(2)}, u32[]{:S(2)}) %collective-permute-start.12) | collective-permute-done | bytes 57376 | tf_op jit(solution)/shard_map/ppermute | solution.py:130
  80.5 3.2 %collective-permute-done.13 = f32[8,256]{1,0:T(8,128)S(1)} collective-permute-done((f32[8,256]{1,0:T(8,128)S(1)}, f32[8,256]{1,0:T(8,128)S(1)}, u32[]{:S(2)}, u32[]{:S(2)}) %collective-permute-start.13) | collective-permute-done | bytes 8224 | tf_op jit(solution)/shard_map/ppermute | solution.py:130
  83.7 2.3 %collective-permute-start.14 = (f32[8,256]{1,0:T(8,128)S(1)}, f32[8,256]{1,0:T(8,128)S(1)}, u32[]{:S(2)}, u32[]{:S(2)}) collective-permute-start(f32[8,256]{1,0:T(8,128)S(1)} %add.19.refs_1_), channel_id=1, source_target_pairs={{0,16},{4,20},{8,24},{12,28},{16,0},{20,4},{24,8},{28,12},{1,17},{... | collective-permute-start | bytes 24584 | tf_op jit(solution)/shard_map/ppermute | solution.py:130
  86.0 2.3 %collective-permute-done.14.refs_2_ = f32[8,256]{1,0:T(8,128)S(1)} collective-permute-done((f32[8,256]{1,0:T(8,128)S(1)}, f32[8,256]{1,0:T(8,128)S(1)}, u32[]{:S(2)}, u32[]{:S(2)}) %collective-permute-start.14) | collective-permute-done | bytes 8224 | tf_op jit(solution)/shard_map/ppermute | solution.py:130
  88.3 1.7 %update.1 = (f32[240,512]{1,0:T(8,128)}, f32[240,512]{1,0:T(8,128)}, bf16[240,256]{1,0:T(8,128)(2,1)S(1)}, bf16[240,256]{1,0:T(8,128)(2,1)S(1)}) custom-call(s32[5]{0:T(128)S(1)} %copy-done.7, f32[8,256]{1,0:T(8,128)S(1)} %add.19.refs_1_, f32[8,256]{1,0:T(8,128)S(1)} %collective-permute-done.14.refs_2_, f32[192,512]{1,0:T(8,128)S(1)} %get-tuple-element.52.refs_3_, ...), custom_call_target="tpu_custom_call" | custom-call | tf_op jit(solution)/shard_map/update/pallas_call | solution.py:550
  89.9 2.3 %collective-permute-start.15 = (bf16[240,256]{1,0:T(8,128)(2,1)S(1)}, bf16[240,256]{1,0:T(8,128)(2,1)S(1)}, u32[]{:S(2)}, u32[]{:S(2)}) collective-permute-start(bf16[240,256]{1,0:T(8,128)(2,1)S(1)} %get-tuple-element.55), channel_id=1, source_target_pairs={{0,16},{4,20},{8,24},{12,28},{16,0},{20,4},{24,8},{28,12},{1,17},{... | collective-permute-start | bytes 368648 | tf_op jit(solution)/shard_map/ppermute | solution.py:130
  92.2 1.5 %collective-permute-start.18 = (bf16[240,256]{1,0:T(8,128)(2,1)S(1)}, bf16[240,256]{1,0:T(8,128)(2,1)S(1)}, u32[]{:S(2)}, u32[]{:S(2)}) collective-permute-start(bf16[240,256]{1,0:T(8,128)(2,1)S(1)} %get-tuple-element.56), channel_id=1, source_target_pairs={{0,4},{4,0},{8,12},{12,8},{16,20},{20,16},{24,28},{28,24},{1,5},{5... | collective-permute-start | bytes 368648 | tf_op jit(solution)/shard_map/ppermute | solution.py:130
  93.7 4.3 %collective-permute-done.15 = bf16[240,256]{1,0:T(8,128)(2,1)S(1)} collective-permute-done((bf16[240,256]{1,0:T(8,128)(2,1)S(1)}, bf16[240,256]{1,0:T(8,128)(2,1)S(1)}, u32[]{:S(2)}, u32[]{:S(2)}) %collective-permute-start.15) | collective-permute-done | bytes 122912 | tf_op jit(solution)/shard_map/ppermute | solution.py:130
  98.3 2.6 %collective-permute-start.19 = (bf16[2,240,256]{2,1,0:T(8,128)(2,1)S(1)}, bf16[2,240,256]{2,1,0:T(8,128)(2,1)S(1)}, u32[]{:S(2)}, u32[]{:S(2)}) collective-permute-start(bf16[2,240,256]{2,1,0:T(8,128)(2,1)S(1)} %pad_maximum_fusion.8), channel_id=1, source_target_pairs={{0,16},{4,20},{8,24},{12,28},{16,0},{20,4},{24,8},{28,12},{1,17},{... | collective-permute-start | bytes 737288 | tf_op jit(solution)/shard_map/ppermute | solution.py:130
  100.9 8.5 %collective-permute-done.16 = bf16[2,240,256]{2,1,0:T(8,128)(2,1)S(1)} collective-permute-done((bf16[2,240,256]{2,1,0:T(8,128)(2,1)S(1)}, bf16[2,240,256]{2,1,0:T(8,128)(2,1)S(1)}, u32[]{:S(2)}, u32[]{:S(2)}) %collective-permute-start.16) | collective-permute-done | bytes 245792 | tf_op jit(solution)/shard_map/ppermute | solution.py:130
  109.5 1.6 %collective-permute-start.17 = (bf16[2,2,240,256]{3,2,0,1:T(8,128)(2,1)S(1)}, bf16[2,2,240,256]{3,2,0,1:T(8,128)(2,1)S(1)}, u32[]{:S(2)}, u32[]{:S(2)}) collective-permute-start(bf16[2,2,240,256]{3,2,0,1:T(8,128)(2,1)S(1)} %pad_maximum_fusion.4), channel_id=1, source_target_pairs={{0,4},{4,0},{8,12},{12,8},{16,20},{20,16},{24,28},{28,24},{1,5},{5... | collective-permute-start | bytes 1474568 | tf_op jit(solution)/shard_map/ppermute | solution.py:130
  111.3 7.1 %collective-permute-done.17 = bf16[2,2,240,256]{3,2,0,1:T(8,128)(2,1)S(1)} collective-permute-done((bf16[2,2,240,256]{3,2,0,1:T(8,128)(2,1)S(1)}, bf16[2,2,240,256]{3,2,0,1:T(8,128)(2,1)S(1)}, u32[]{:S(2)}, u32[]{:S(2)}) %collective-permute-start.17) | collective-permute-done | bytes 491552 | tf_op jit(solution)/shard_map/ppermute | solution.py:130
  118.6 1.5 %collective-permute-done.20 = bf16[2,2,240,256]{3,2,1,0:T(8,128)(2,1)S(1)} collective-permute-done((bf16[2,2,240,256]{3,2,1,0:T(8,128)(2,1)S(1)}, bf16[2,2,240,256]{3,2,1,0:T(8,128)(2,1)S(1)}, u32[]{:S(2)}, u32[]{:S(2)}) %collective-permute-start.20) | collective-permute-done | bytes 491552 | tf_op jit(solution)/shard_map/ppermute | solution.py:130
  120.3 1.4 %pad_maximum_fusion = bf16[1920,512]{1,0:T(8,128)(2,1)} fusion(bf16[1920,256]{1,0:T(8,128)(2,1)S(1)} %bitcast.45, bf16[1920,256]{1,0:T(8,128)(2,1)S(1)} %bitcast.44), kind=kLoop, calls=%fused_computation | loop fusion | flops 3932160 | bytes 3932160 | tf_op jit(solution)/shard_map/concatenate | solution.py:576
  (63 shorter events, 10.2 us)
Async XLA Ops:
  5.4 14.7 %copy-start = (bf16[64,1024]{1,0:T(8,128)(2,1)S(1)}, bf16[64,1024]{1,0:T(8,128)(2,1)}, u32[]{:S(2)}) copy-start(bf16[64,1024]{1,0:T(8,128)(2,1)} %picks.1.refs_3_) | copy-start | bytes 393220
  5.4 31.4 %copy-start.7 = (s32[5]{0:T(128)S(1)}, s32[5]{0:T(128)}, u32[]{:S(2)}) copy-start(s32[5]{0:T(128)} %stack.86.refs_0_.info) | copy-start | bytes 64
  5.4 14.6 %collective-permute-start = (bf16[64,1024]{1,0:T(8,128)(2,1)}, bf16[64,1024]{1,0:T(8,128)(2,1)S(1)}, u32[]{:S(2)}, u32[]{:S(2)}) collective-permute-start(bf16[64,1024]{1,0:T(8,128)(2,1)} %picks.1.refs_3_), channel_id=1, source_target_pairs={{0,16},{4,20},{8,24},{12,28},{16,0},{20,4},{24,8},{28,12},{1,17},{... | collective-permute-start | bytes 393224 | tf_op jit(solution)/shard_map/ppermute | solution.py:130
  20.0 20.0 %copy-start.1 = (f32[4,240,256]{2,1,0:T(8,128)S(1)}, f32[4,240,256]{2,1,0:T(8,128)}, u32[]{:S(2)}) copy-start(f32[4,240,256]{2,1,0:T(8,128)} %get-tuple-element.43.refs_2_) | copy-start | bytes 2949124
  20.1 9.3 %collective-permute-start.1 = (bf16[2,64,1024]{2,1,0:T(8,128)(2,1)S(1)}, bf16[2,64,1024]{2,1,0:T(8,128)(2,1)S(1)}, u32[]{:S(2)}, u32[]{:S(2)}) collective-permute-start(bf16[2,64,1024]{2,1,0:T(8,128)(2,1)S(1)} %pad_maximum_fusion.6), channel_id=1, source_target_pairs={{0,8},{4,12},{8,0},{12,4},{16,24},{20,28},{24,16},{28,20},{1,9},{5... | collective-permute-start | bytes 786440 | tf_op jit(solution)/shard_map/ppermute | solution.py:130
  21.7 15.1 %collective-permute-start.3 = (s16[4,256,256]{2,1,0:T(8,128)(2,1)}, s16[4,256,256]{2,1,0:T(8,128)(2,1)S(1)}, u32[]{:S(2)}, u32[]{:S(2)}) collective-permute-start(s16[4,256,256]{2,1,0:T(8,128)(2,1)} %get-tuple-element.36), channel_id=1, source_target_pairs={{0,4},{4,0},{8,12},{12,8},{16,20},{20,16},{24,28},{28,24},{1,5},{5... | collective-permute-start | bytes 1572872 | tf_op jit(solution)/shard_map/ppermute | solution.py:130
  23.3 16.8 %collective-permute-start.6 = (s16[4,256,256]{2,1,0:T(8,128)(2,1)}, s16[4,256,256]{2,1,0:T(8,128)(2,1)S(1)}, u32[]{:S(2)}, u32[]{:S(2)}) collective-permute-start(s16[4,256,256]{2,1,0:T(8,128)(2,1)} %get-tuple-element.42), channel_id=1, source_target_pairs={{0,8},{4,12},{8,0},{12,4},{16,24},{20,28},{24,16},{28,20},{1,9},{5... | collective-permute-start | bytes 1572872 | tf_op jit(solution)/shard_map/ppermute | solution.py:130
  29.4 23.7 %collective-permute-start.2 = (bf16[4,64,1024]{2,1,0:T(8,128)(2,1)S(1)}, bf16[4,64,1024]{2,1,0:T(8,128)(2,1)S(1)}, u32[]{:S(2)}, u32[]{:S(2)}) collective-permute-start(bf16[4,64,1024]{2,1,0:T(8,128)(2,1)S(1)} %pad_maximum_fusion.3), channel_id=1, source_target_pairs={{0,4},{4,0},{8,12},{12,8},{16,20},{20,16},{24,28},{28,24},{1,5},{5... | collective-permute-start | bytes 1572872 | tf_op jit(solution)/shard_map/ppermute | solution.py:130
  36.8 1.2 copy-start.2
  38.0 15.1 %copy-start.5 = (f32[1,4,128,128]{3,2,1,0:T(8,128)S(1)}, f32[1,4,128,128]{3,2,1,0:T(8,128)}, u32[]{:S(2)}) copy-start(f32[1,4,128,128]{3,2,1,0:T(8,128)} %param.14) | copy-start | bytes 786436
  38.0 15.1 %copy-start.6 = (f32[1,5,96,96]{3,2,1,0:T(8,128)S(1)}, f32[1,5,96,96]{3,2,1,0:T(8,128)}, u32[]{:S(2)}) copy-start(f32[1,5,96,96]{3,2,1,0:T(8,128)} %param.15) | copy-start | bytes 552964
  38.0 15.1 %copy-start.8 = (s32[4,4]{1,0:T(4,128)S(1)}, s32[4,4]{1,0:T(4,128)}, u32[]{:S(2)}) copy-start(s32[4,4]{1,0:T(4,128)} %refs_1_.3) | copy-start | bytes 196
  38.0 15.1 %copy-start.9 = (s32[4,5]{1,0:T(4,128)S(1)}, s32[4,5]{1,0:T(4,128)}, u32[]{:S(2)}) copy-start(s32[4,5]{1,0:T(4,128)} %refs_2_.5) | copy-start | bytes 244
  39.0 6.4 %collective-permute-start.4 = (s16[2,256,256]{2,1,0:T(8,128)(2,1)S(1)}, s16[2,256,256]{2,1,0:T(8,128)(2,1)S(1)}, u32[]{:S(2)}, u32[]{:S(2)}) collective-permute-start(s16[2,256,256]{2,1,0:T(8,128)(2,1)S(1)} %get-tuple-element.38), channel_id=1, source_target_pairs={{0,8},{4,12},{8,0},{12,4},{16,24},{20,28},{24,16},{28,20},{1,9},{5... | collective-permute-start | bytes 786440 | tf_op jit(solution)/shard_map/ppermute | solution.py:130
  41.0 11.0 %collective-permute-start.7 = (s16[2,256,256]{2,1,0:T(8,128)(2,1)S(1)}, s16[2,256,256]{2,1,0:T(8,128)(2,1)S(1)}, u32[]{:S(2)}, u32[]{:S(2)}) collective-permute-start(s16[2,256,256]{2,1,0:T(8,128)(2,1)S(1)} %get-tuple-element.44), channel_id=1, source_target_pairs={{0,4},{4,0},{8,12},{12,8},{16,20},{20,16},{24,28},{28,24},{1,5},{5... | collective-permute-start | bytes 786440 | tf_op jit(solution)/shard_map/ppermute | solution.py:130
  46.1 42.1 %copy-start.3 = (f32[240,512]{1,0:T(8,128)S(1)}, f32[240,512]{1,0:T(8,128)}, u32[]{:S(2)}) copy-start(f32[240,512]{1,0:T(8,128)} %refs_6_.1) | copy-start | bytes 1474564
  46.2 42.1 %copy-start.4 = (f32[240,512]{1,0:T(8,128)S(1)}, f32[240,512]{1,0:T(8,128)}, u32[]{:S(2)}) copy-start(f32[240,512]{1,0:T(8,128)} %refs_7_.1) | copy-start | bytes 1474564
  46.2 13.2 %collective-permute-start.5 = (s16[1,256,256]{2,1,0:T(8,128)(2,1)S(1)}, s16[1,256,256]{2,1,0:T(8,128)(2,1)S(1)}, u32[]{:S(2)}, u32[]{:S(2)}) collective-permute-start(s16[1,256,256]{2,1,0:T(8,128)(2,1)S(1)} %get-tuple-element.40), channel_id=1, source_target_pairs={{0,16},{4,20},{8,24},{12,28},{16,0},{20,4},{24,8},{28,12},{1,17},{... | collective-permute-start | bytes 393224 | tf_op jit(solution)/shard_map/ppermute | solution.py:130
  52.7 7.5 %collective-permute-start.8 = (s16[1,256,256]{2,1,0:T(8,128)(2,1)S(1)}, s16[1,256,256]{2,1,0:T(8,128)(2,1)S(1)}, u32[]{:S(2)}, u32[]{:S(2)}) collective-permute-start(s16[1,256,256]{2,1,0:T(8,128)(2,1)S(1)} %get-tuple-element.46), channel_id=1, source_target_pairs={{0,16},{4,20},{8,24},{12,28},{16,0},{20,4},{24,8},{28,12},{1,17},{... | collective-permute-start | bytes 393224 | tf_op jit(solution)/shard_map/ppermute | solution.py:130
  58.6 0.7 collective-permute-start.9
  62.4 4.6 %collective-permute-start.10 = (f32[8,256]{1,0:T(8,128)S(1)}, f32[8,256]{1,0:T(8,128)S(1)}, u32[]{:S(2)}, u32[]{:S(2)}) collective-permute-start(f32[8,256]{1,0:T(8,128)S(1)} %get-tuple-element.50), channel_id=1, source_target_pairs={{0,1},{1,0},{2,3},{3,2},{4,5},{5,4},{6,7},{7,6},{8,9},{9,8},{10,11... | collective-permute-start | bytes 24584 | tf_op jit(solution)/shard_map/ppermute | solution.py:134
  67.0 8.8 %collective-permute-start.11 = (f32[8,256]{1,0:T(8,128)S(1)}, f32[8,256]{1,0:T(8,128)S(1)}, u32[]{:S(2)}, u32[]{:S(2)}) collective-permute-start(f32[8,256]{1,0:T(8,128)S(1)} %add.16), channel_id=1, source_target_pairs={{0,2},{1,3},{2,0},{3,1},{4,6},{5,7},{6,4},{7,5},{8,10},{9,11},{10,... | collective-permute-start | bytes 24584 | tf_op jit(solution)/shard_map/ppermute | solution.py:134
  75.8 4.2 %collective-permute-start.12 = (f32[56,256]{1,0:T(8,128)S(1)}, f32[56,256]{1,0:T(8,128)S(1)}, u32[]{:S(2)}, u32[]{:S(2)}) collective-permute-start(f32[56,256]{1,0:T(8,128)S(1)} %pad_maximum_fusion.9), channel_id=1, source_target_pairs={{0,4},{4,0},{8,12},{12,8},{16,20},{20,16},{24,28},{28,24},{1,5},{5... | collective-permute-start | bytes 172040 | tf_op jit(solution)/shard_map/ppermute | solution.py:130
  80.0 3.7 %collective-permute-start.13 = (f32[8,256]{1,0:T(8,128)S(1)}, f32[8,256]{1,0:T(8,128)S(1)}, u32[]{:S(2)}, u32[]{:S(2)}) collective-permute-start(f32[8,256]{1,0:T(8,128)S(1)} %slice_add_fusion), channel_id=1, source_target_pairs={{0,8},{4,12},{8,0},{12,4},{16,24},{20,28},{24,16},{28,20},{1,9},{5... | collective-permute-start | bytes 24584 | tf_op jit(solution)/shard_map/ppermute | solution.py:130
  83.7 4.5 %collective-permute-start.14 = (f32[8,256]{1,0:T(8,128)S(1)}, f32[8,256]{1,0:T(8,128)S(1)}, u32[]{:S(2)}, u32[]{:S(2)}) collective-permute-start(f32[8,256]{1,0:T(8,128)S(1)} %add.19.refs_1_), channel_id=1, source_target_pairs={{0,16},{4,20},{8,24},{12,28},{16,0},{20,4},{24,8},{28,12},{1,17},{... | collective-permute-start | bytes 24584 | tf_op jit(solution)/shard_map/ppermute | solution.py:130
  89.9 8.2 %collective-permute-start.15 = (bf16[240,256]{1,0:T(8,128)(2,1)S(1)}, bf16[240,256]{1,0:T(8,128)(2,1)S(1)}, u32[]{:S(2)}, u32[]{:S(2)}) collective-permute-start(bf16[240,256]{1,0:T(8,128)(2,1)S(1)} %get-tuple-element.55), channel_id=1, source_target_pairs={{0,16},{4,20},{8,24},{12,28},{16,0},{20,4},{24,8},{28,12},{1,17},{... | collective-permute-start | bytes 368648 | tf_op jit(solution)/shard_map/ppermute | solution.py:130
  92.2 6.0 %collective-permute-start.18 = (bf16[240,256]{1,0:T(8,128)(2,1)S(1)}, bf16[240,256]{1,0:T(8,128)(2,1)S(1)}, u32[]{:S(2)}, u32[]{:S(2)}) collective-permute-start(bf16[240,256]{1,0:T(8,128)(2,1)S(1)} %get-tuple-element.56), channel_id=1, source_target_pairs={{0,4},{4,0},{8,12},{12,8},{16,20},{20,16},{24,28},{28,24},{1,5},{5... | collective-permute-start | bytes 368648 | tf_op jit(solution)/shard_map/ppermute | solution.py:130
  98.1 11.2 %collective-permute-start.16 = (bf16[2,240,256]{2,1,0:T(8,128)(2,1)S(1)}, bf16[2,240,256]{2,1,0:T(8,128)(2,1)S(1)}, u32[]{:S(2)}, u32[]{:S(2)}) collective-permute-start(bf16[2,240,256]{2,1,0:T(8,128)(2,1)S(1)} %pad_maximum_fusion.7), channel_id=1, source_target_pairs={{0,8},{4,12},{8,0},{12,4},{16,24},{20,28},{24,16},{28,20},{1,9},{5... | collective-permute-start | bytes 737288 | tf_op jit(solution)/shard_map/ppermute | solution.py:130
  98.3 12.8 %collective-permute-start.19 = (bf16[2,240,256]{2,1,0:T(8,128)(2,1)S(1)}, bf16[2,240,256]{2,1,0:T(8,128)(2,1)S(1)}, u32[]{:S(2)}, u32[]{:S(2)}) collective-permute-start(bf16[2,240,256]{2,1,0:T(8,128)(2,1)S(1)} %pad_maximum_fusion.8), channel_id=1, source_target_pairs={{0,16},{4,20},{8,24},{12,28},{16,0},{20,4},{24,8},{28,12},{1,17},{... | collective-permute-start | bytes 737288 | tf_op jit(solution)/shard_map/ppermute | solution.py:130
  109.5 8.9 %collective-permute-start.17 = (bf16[2,2,240,256]{3,2,0,1:T(8,128)(2,1)S(1)}, bf16[2,2,240,256]{3,2,0,1:T(8,128)(2,1)S(1)}, u32[]{:S(2)}, u32[]{:S(2)}) collective-permute-start(bf16[2,2,240,256]{3,2,0,1:T(8,128)(2,1)S(1)} %pad_maximum_fusion.4), channel_id=1, source_target_pairs={{0,4},{4,0},{8,12},{12,8},{16,20},{20,16},{24,28},{28,24},{1,5},{5... | collective-permute-start | bytes 1474568 | tf_op jit(solution)/shard_map/ppermute | solution.py:130
  111.2 8.9 %collective-permute-start.20 = (bf16[2,2,240,256]{3,2,1,0:T(8,128)(2,1)S(1)}, bf16[2,2,240,256]{3,2,1,0:T(8,128)(2,1)S(1)}, u32[]{:S(2)}, u32[]{:S(2)}) collective-permute-start(bf16[2,2,240,256]{3,2,1,0:T(8,128)(2,1)S(1)} %pad_maximum_fusion.5), channel_id=1, source_target_pairs={{0,8},{4,12},{8,0},{12,4},{16,24},{20,28},{24,16},{28,20},{1,9},{5... | collective-permute-start | bytes 1474568 | tf_op jit(solution)/shard_map/ppermute | solution.py:130

commit v4 on v3

--- a/solution.py
+++ b/solution.py
@@ -255,29 +255,21 @@
         raw[columns, :] = jnp.dot(
             grad_buf[:, columns].T, acts_buf[...], preferred_element_type=f32
         )
-        if step > 0:
-            place = step - 1
-            span = slice(place * group_cols, (place + 1) * group_cols)
-            units = split_units(raw[span, :half], head, width_g)
-            for x in range(2):
-
-                @pl.when(side == x)
-                def _():
-                    keep_a[place] = units[x]
-                    encode_to(send_a, place, units[1 - x])
-
-            units = split_units(raw[span, half:], head, width_g)
-            high = place // 2
-
-            @pl.when(place % 2 == low)
-            def _():
-                for x in range(2):
-                    keep_b[2 * high + x] = units[x]
-
-            @pl.when(place % 2 != low)
-            def _():
-                for x in range(2):
-                    encode_to(send_b, 2 * high + x, units[x])
+        if step == 0:
+            continue
+        place = step - 1
+        span = slice(place * group_cols, (place + 1) * group_cols)
+        zero, one = split_units(raw[span, :half], head, width_g)
+        keep_a[place] = jnp.where(side == 0, zero, one)
+        encode_to(send_a, place, jnp.where(side == 0, one, zero))
+        if place % 2 == 0:
+            continue
+        before = slice((place - 1) * group_cols, place * group_cols)
+        zero = split_units(raw[before, half:], head, width_g)
+        one = split_units(raw[span, half:], head, width_g)
+        for x in range(2):
+            keep_b[place - 1 + x] = jnp.where(low == 0, zero[x], one[x])
+            encode_to(send_b, place - 1 + x, jnp.where(low == 0, one[x], zero[x]))
 
 
 def add_kernel(bit_at, inner, info, got, held, send, keep):
@@ -294,6 +286,14 @@
     for j in range(count):
         home = place(j, bit)
         keep[j] = held[home] + decode(got[home], rows)
+
+
+def last_add_kernel(info, got_a, held_a, got_b, held_b, send, keep):
+    high = info[4]
+    rows = keep.shape[1]
+    for piece, (got, held) in enumerate(((got_a, held_a), (got_b, held_b))):
+        encode_to(send, piece, held[1 - high] + decode(got[1 - high], rows))
+        keep[piece] = held[high] + decode(got[high], rows)
 
 
 def add_step(info, bit_at, inner, got, held):
@@ -311,30 +311,49 @@
     )(info, got, held)
 
 
-def factor_kernel(
-    share, info, own_a, own_g, own, one, two, four, a_state, g_state, a_new, g_new, inv_a, needed, picks, inv_g
-):
-    group, shard = info[0], info[3]
-    picks[shard] = own[...]
-    picks[shard ^ 4] = one[...]
-    for j in range(2):
-        picks[shard ^ 2 ^ (4 * j)] = two[j]
-    for j in range(4):
-        picks[shard ^ 1 ^ (4 * (j % 2)) ^ (2 * (j // 2))] = four[j]
-    count_a, width_a = a_state.shape[0], a_state.shape[1]
-    count_g, width_g = g_state.shape[0], g_state.shape[1]
-    samples = picks.shape[0] * picks.shape[1]
-    everything = picks[...].reshape(samples, picks.shape[2])
-    errors, inverses, scales = [], [], []
-    for index in range(count_a + count_g):
-        is_a = index < count_a
-        width = width_a if is_a else width_g
-        place = index if is_a else index - count_a
-        start = place * width_a if is_a else count_a * width_a + place * width_g
-        rows = everything[:, start : start + width]
+def block_places(count_a, width_a, count_g, width_g):
+    blocks, column, row = [], 0, 0
+    for is_a, count, width in ((True, count_a, width_a), (False, count_g, width_g)):
+        for place in range(count):
+            blocks.append((is_a, place, width, column, row))
+            column += width
+            row += width + GROUP
+    return blocks, row
+
+
+def stats_kernel(blocks, info, own, one, two, packed, picks):
+    place = info[3] >> 1
+    picks[place] = own[...]
+    picks[place ^ 2] = one[...]
+    picks[place ^ 1] = two[0]
+    picks[place ^ 3] = two[1]
+    everything = picks[...].reshape(picks.shape[0] * picks.shape[1], picks.shape[2])
+    for _, _, width, column, row in blocks:
+        rows = everything[:, column : column + width]
         stats = lax.dot_general(
             rows, rows, (((0,), (0,)), ((), ())), preferred_element_type=f32
         )
+        missing = packed.shape[1] - width
+        if missing:
+            stats = jnp.concatenate([stats, jnp.zeros((width, missing), f32)], axis=1)
+
+        def store(first, data):
+            packed[row + first : row + first + GROUP, :] = data
+
+        encode(stats, store)
+
+
+def factor_kernel(
+    share, blocks, info, own_a, own_g, packed, got, a_state, g_state, a_new, g_new, inv_a, needed,
+    inv_g
+):
+    group = info[0]
+    count_a, count_g = a_state.shape[0], g_state.shape[0]
+    errors, inverses, scales = [], [], []
+    for is_a, place, width, _, first in blocks:
+        span = slice(first, first + width + GROUP)
+        stats = decode(packed[span, :], width) + decode(got[span, :], width)
+        stats = stats[:, :width]
         slot = own_a[group, place] if is_a else own_g[group, place]
         stored = (a_state if is_a else g_state)[slot]
         factor = factor_decay * stored + share * stats
@@ -349,16 +368,16 @@
         errors.append(error)
         inverses.append(identity + error)
         scales.append(bound)
-    blocks = range(count_a + count_g)
+    every = range(count_a + count_g)
     dot = lambda p, q: jnp.dot(p, q, preferred_element_type=f32, precision=highest)
-    errors = [dot(errors[i], errors[i]) for i in blocks]
+    errors = [dot(errors[i], errors[i]) for i in every]
     for step in range(1, NS_IT - 1):
-        grown = [dot(inverses[i], errors[i]) for i in blocks]
-        squares = [dot(errors[i], errors[i]) for i in blocks]
-        inverses = [inverses[i] + grown[i] for i in blocks]
+        grown = [dot(inverses[i], errors[i]) for i in every]
+        squares = [dot(errors[i], errors[i]) for i in every]
+        inverses = [inverses[i] + grown[i] for i in every]
         errors = squares
-    inverses = [(inverses[i] + dot(inverses[i], errors[i])) / scales[i] for i in blocks]
-    for index in blocks:
+    inverses = [(inverses[i] + dot(inverses[i], errors[i])) / scales[i] for i in every]
+    for index in every:
         if index < count_a:
             inv_a[index] = inverses[index]
         else:
@@ -369,14 +388,14 @@
     needed[2] = inv_g[2]
 
 
-def precon_kernel(info, got_a, held_a, got_b, held_b, inv_g, inv_a, top, mid, total):
+def precon_kernel(info, got, held, inv_g, inv_a, top, mid, total):
     side = info[1]
     width_g, width_a = inv_g.shape[-1], inv_a.shape[-1]
     half = width_g // 2
     dot = lambda p, q: jnp.dot(p, q, preferred_element_type=f32, precision=highest)
     squares = jnp.zeros((width_g, width_a), f32)
-    for piece, (got, held) in enumerate(((got_a, held_a), (got_b, held_b))):
-        part = held[0] + decode(got[0], held.shape[1])
+    for piece in range(2):
+        part = held[piece] + decode(got[piece], held.shape[1])
         for place in range(2):
             for block in range(2):
                 values = dot(
@@ -451,7 +470,6 @@
     head = 2 * width_g
     mid = width_g // 2
     info = jnp.stack([tensor_pos, side, low, shard_pos, high])
-    high_at = 4
 
     wide = cols + -(-group_cols // 128) * 128
     picks = pl.pallas_call(
@@ -465,7 +483,6 @@
             pltpu.SemaphoreType.DMA((8,)),
         ],
         compiler_params=params(60),
-        cost_estimate=cost(2 * drawn * tokens * (cols + 640), 5 * 2**20),
         name="picks",
     )(info, sample_rows.reshape(1, -1), acts, out_grad)
     one = swap(picks, 4)
@@ -485,27 +502,46 @@
             pltpu.VMEM((outs, cols), f32),
             pltpu.SemaphoreType.DMA((6,)),
         ],
-        compiler_params=params(60),
-        cost_estimate=cost(2 * outs * tokens * cols, 10 * 2**20),
+        compiler_params=params(56),
         name="partial",
     )(info, out_grad, acts)
     one, send_a, send_b = lax.optimization_barrier((one, send_a, send_b))
     got_a = swap(send_a, 1)
+    two = swap(jnp.stack([picks, one]), 2)
     got_b = swap(send_b, 2)
-    two = swap(jnp.stack([picks, one]), 2)
-    four = swap(jnp.concatenate([picks[None], one[None], two]), 1)
+
     send_a, keep_a = add_step(info, 2, True, got_a, keep_a)
     got_a = swap(send_a, 2)
+    blocks, packed_rows = block_places(count_a, width_a, count_g, width_g)
+    packed = pl.pallas_call(
+        lambda *refs: stats_kernel(blocks, *refs),
+        in_specs=[smem] + [vmem] * 3,
+        out_specs=vmem,
+        out_shape=shaped((packed_rows, width_a), jnp.int16),
+        scratch_shapes=[pltpu.VMEM((4, drawn, wide), bf16)],
+        compiler_params=params(16),
+        name="stats",
+    )(info, picks, one, two)
+    got_packed = swap(packed, 1)
     send_b, keep_b = add_step(info, 1, True, got_b, keep_b)
     got_b = swap(send_b, 1)
-    send_a, keep_a = add_step(info, high_at, True, got_a, keep_a)
-    got_a = swap(send_a, 4)
-    send_b, keep_b = add_step(info, high_at, True, got_b, keep_b)
-    got_b = swap(send_b, 4)
+
+    send, keep = pl.pallas_call(
+        last_add_kernel,
+        in_specs=[smem] + [vmem] * 4,
+        out_specs=[vmem, vmem],
+        out_shape=[
+            shaped((2, rows + GROUP, half), jnp.int16),
+            shaped((2, rows, half), f32),
+        ],
+        compiler_params=params(24),
+        name="last_add",
+    )(info, got_a, keep_a, got_b, keep_b)
+    got = swap(send, 4)
 
     new_a, new_g, inv_a, needed = pl.pallas_call(
-        lambda *refs: factor_kernel(share, *refs),
-        in_specs=[smem] * 3 + [vmem] * 6,
+        lambda *refs: factor_kernel(share, blocks, *refs),
+        in_specs=[smem] * 3 + [vmem] * 4,
         out_specs=[vmem] * 4,
         out_shape=[
             shaped(a_state.shape[1:], f32),
@@ -513,13 +549,10 @@
             shaped(a_state.shape[1:], f32),
             shaped((3, width_g, width_g), f32),
         ],
-        scratch_shapes=[
-            pltpu.VMEM((8, drawn, wide), bf16),
-            pltpu.VMEM(g_state.shape[1:], f32),
-        ],
+        scratch_shapes=[pltpu.VMEM(g_state.shape[1:], f32)],
         compiler_params=params(24),
         name="factors",
-    )(info, own_a, own_g, picks, one, two, four, a_state[0], g_state[0])
+    )(info, own_a, own_g, packed, got_packed, a_state[0], g_state[0])
     route = [
         ((2 * a + b) * 4 + c, (2 * c + b) * 4 + a)
         for a in range(4)
@@ -530,7 +563,7 @@
 
     top, middle, total = pl.pallas_call(
         precon_kernel,
-        in_specs=[smem] + [vmem] * 6,
+        in_specs=[smem] + [vmem] * 4,
         out_specs=[vmem] * 3,
         out_shape=[
             shaped((head, cols), f32),
@@ -539,7 +572,7 @@
         ],
         compiler_params=params(24),
         name="precon",
-    )(info, got_a, keep_a, got_b, keep_b, inv_rows, inv_a)
+    )(info, got, keep, inv_rows, inv_a)
 
     total = total + swap_t(total, 1)
     total = total + swap_t(total, 2)

time: 123 us -> 121 us (0.984)
  starting transfers between devices: 36.4 us -> 31.1 us
  waiting for transfers between devices: 53 us -> 57.7 us
    ppermute x18 -> x17, waiting for transfers between devices: 50.6 us -> 55.3 us  [swap(): return lax.ppermute(value, 'shard', [(i, i ^ bit) for i in range(8)])]
    ppermute x2, starting transfers between devices: 10.9 us -> 6.58 us  [swap_t(): return lax.ppermute(value, 'tensor', [(i, i ^ bit) for i in range(4)])]
    pallas_call x2 -> x4, Pallas kernels: 7.65 us -> 9.35 us  [the longest x1 5.14 us: fast(): pl.pallas_call(lambda *refs: factor_kernel(share, blocks, *refs), in_spec...]
    pallas_call x4 -> x2, Pallas kernels: 3.34 us -> 1.85 us  [add_step(): pl.pallas_call(lambda *refs: add_kernel(bit_at, inner, *refs), in_specs=[...]
    ppermute x18 -> x17, starting transfers between devices: 24.8 us -> 23.6 us  [swap(): return lax.ppermute(value, 'shard', [(i, i ^ bit) for i in range(8)])]
  transfers between devices with their start and end apart: 21 -> 20, of which waited for: 15 -> 15; matrix products, arithmetic and copies ran while one was open for 0% -> 0% of each run, Pallas kernels for 16% -> 16%
where the time goes in v4:
time: 121 us
  waiting for transfers between devices  57.7 us (48%)
  starting transfers between devices  31.1 us (26%)
  Pallas kernels  26.8 us (22%)
  other arithmetic  2.11 us (2%)
  local copies, waits for them, and re-layouts  1.99 us (2%)
    ppermute x17, waiting for transfers between devices, swap(): return lax.ppermute(value, 'shard', [(i, i ^ bit) for i in range(8)])  55.3 us
    ppermute x17, starting transfers between devices, swap(): return lax.ppermute(value, 'shard', [(i, i ^ bit) for i in range(8)])  23.6 us
    pallas_call x1, Pallas kernels, fast(): pl.pallas_call(lambda *refs: partial_kernel(group_cols, width_g, *refs),...  9.74 us
    ppermute x2, starting transfers between devices, swap_t(): return lax.ppermute(value, 'tensor', [(i, i ^ bit) for i in range(4)])  6.58 us
    pallas_call x1, Pallas kernels, fast(): pl.pallas_call(lambda *refs: factor_kernel(share, blocks, *refs), in_spec...  5.14 us
    pallas_call x1, Pallas kernels, fast(): pl.pallas_call(lambda *refs: picks_kernel(group_cols, *refs), in_specs=[s...  4.15 us
    ppermute x2, waiting for transfers between devices, swap_t(): return lax.ppermute(value, 'tensor', [(i, i ^ bit) for i in range(4)])  2.45 us
  transfers between devices with their start and end apart: 20, of which 15 were waited for; matrix products, arithmetic and copies ran while one was open for 0% of the time, Pallas kernels for 16%

profile of v4, /device:TPU:0, one launch (start us, length us, event | category | flops | bytes accessed | tf_op | source)
XLA Modules:
  0.0 120.6 jit_solution(6496851160114820336)
XLA Ops:
  1.2 4.2 %picks.1.refs_1_ = bf16[64,1024]{1,0:T(8,128)(2,1)} custom-call(s32[5]{0:T(128)} %stack.86.refs_0_.info, s32[1,64]{1,0:T(1,128)} %bitcast.44, bf16[2048,512]{1,0:T(8,128)(2,1)} %refs_2_.4, bf16[2048,1920]{1,0:T(8,128)(2,1)} %refs_1_.2), custom_call_target="tpu_custom_call" | custom-call | tf_op jit(solution)/shard_map/picks/pallas_call | solution.py:475
  5.4 4.1 %collective-permute-start = (bf16[64,1024]{1,0:T(8,128)(2,1)}, bf16[64,1024]{1,0:T(8,128)(2,1)S(1)}, u32[]{:S(2)}, u32[]{:S(2)}) collective-permute-start(bf16[64,1024]{1,0:T(8,128)(2,1)} %picks.1.refs_1_), channel_id=1, source_target_pairs={{0,16},{4,20},{8,24},{12,28},{16,0},{20,4},{24,8},{28,12},{1,17},{... | collective-permute-start | bytes 393224 | tf_op jit(solution)/shard_map/ppermute | solution.py:130
  9.5 9.7 %partial.1 = (s16[4,256,256]{2,1,0:T(8,128)(2,1)}, f32[4,240,256]{2,1,0:T(8,128)}, s16[4,256,256]{2,1,0:T(8,128)(2,1)}, f32[4,240,256]{2,1,0:T(8,128)}) custom-call(s32[5]{0:T(128)} %stack.86.refs_0_.info, bf16[2048,1920]{1,0:T(8,128)(2,1)} %refs_1_.2, bf16[2048,512]{1,0:T(8,128)(2,1)} %refs_2_.4), custom_call_target="tpu_custom_call" | custom-call | tf_op jit(solution)/shard_map/partial/pallas_call | solution.py:490
  19.3 1.6 %collective-permute-start.3 = (s16[4,256,256]{2,1,0:T(8,128)(2,1)}, s16[4,256,256]{2,1,0:T(8,128)(2,1)S(1)}, u32[]{:S(2)}, u32[]{:S(2)}) collective-permute-start(s16[4,256,256]{2,1,0:T(8,128)(2,1)} %get-tuple-element.34), channel_id=1, source_target_pairs={{0,4},{4,0},{8,12},{12,8},{16,20},{20,16},{24,28},{28,24},{1,5},{5... | collective-permute-start | bytes 1572872 | tf_op jit(solution)/shard_map/ppermute | solution.py:130
  20.8 1.6 %collective-permute-start.5 = (s16[4,256,256]{2,1,0:T(8,128)(2,1)}, s16[4,256,256]{2,1,0:T(8,128)(2,1)S(1)}, u32[]{:S(2)}, u32[]{:S(2)}) collective-permute-start(s16[4,256,256]{2,1,0:T(8,128)(2,1)} %get-tuple-element.38), channel_id=1, source_target_pairs={{0,8},{4,12},{8,0},{12,4},{16,24},{20,28},{24,16},{28,20},{1,9},{5... | collective-permute-start | bytes 1572872 | tf_op jit(solution)/shard_map/ppermute | solution.py:130
  23.0 10.1 %collective-permute-done.3.refs_1_ = s16[4,256,256]{2,1,0:T(8,128)(2,1)S(1)} collective-permute-done((s16[4,256,256]{2,1,0:T(8,128)(2,1)}, s16[4,256,256]{2,1,0:T(8,128)(2,1)S(1)}, u32[]{:S(2)}, u32[]{:S(2)}) %collective-permute-start.3) | collective-permute-done | bytes 524320 | tf_op jit(solution)/shard_map/ppermute | solution.py:130
  33.0 1.2 copy-done.2
  35.2 1.6 %collective-permute-start.4 = (s16[2,256,256]{2,1,0:T(8,128)(2,1)S(1)}, s16[2,256,256]{2,1,0:T(8,128)(2,1)S(1)}, u32[]{:S(2)}, u32[]{:S(2)}) collective-permute-start(s16[2,256,256]{2,1,0:T(8,128)(2,1)S(1)} %get-tuple-element.36), channel_id=1, source_target_pairs={{0,8},{4,12},{8,0},{12,4},{16,24},{20,28},{24,16},{28,20},{1,9},{5... | collective-permute-start | bytes 786440 | tf_op jit(solution)/shard_map/ppermute | solution.py:130
  37.8 1.6 %collective-permute-start.6 = (s16[2,256,256]{2,1,0:T(8,128)(2,1)S(1)}, s16[2,256,256]{2,1,0:T(8,128)(2,1)S(1)}, u32[]{:S(2)}, u32[]{:S(2)}) collective-permute-start(s16[2,256,256]{2,1,0:T(8,128)(2,1)S(1)} %get-tuple-element.40), channel_id=1, source_target_pairs={{0,4},{4,0},{8,12},{12,8},{16,20},{20,16},{24,28},{28,24},{1,5},{5... | collective-permute-start | bytes 786440 | tf_op jit(solution)/shard_map/ppermute | solution.py:130
  39.3 2.2 %collective-permute-done.1.refs_3_ = bf16[2,64,1024]{2,1,0:T(8,128)(2,1)S(1)} collective-permute-done((bf16[2,64,1024]{2,1,0:T(8,128)(2,1)S(1)}, bf16[2,64,1024]{2,1,0:T(8,128)(2,1)S(1)}, u32[]{:S(2)}, u32[]{:S(2)}) %collective-permute-start.1) | collective-permute-done | bytes 262176 | tf_op jit(solution)/shard_map/ppermute | solution.py:130
  43.3 2.2 %collective-permute-done.4.got_a = s16[2,256,256]{2,1,0:T(8,128)(2,1)S(1)} collective-permute-done((s16[2,256,256]{2,1,0:T(8,128)(2,1)S(1)}, s16[2,256,256]{2,1,0:T(8,128)(2,1)S(1)}, u32[]{:S(2)}, u32[]{:S(2)}) %collective-permute-start.4) | collective-permute-done | bytes 262176 | tf_op jit(solution)/shard_map/ppermute | solution.py:130
  45.5 1.5 %collective-permute-done.6.got_b = s16[2,256,256]{2,1,0:T(8,128)(2,1)S(1)} collective-permute-done((s16[2,256,256]{2,1,0:T(8,128)(2,1)S(1)}, s16[2,256,256]{2,1,0:T(8,128)(2,1)S(1)}, u32[]{:S(2)}, u32[]{:S(2)}) %collective-permute-start.6) | collective-permute-done | bytes 262176 | tf_op jit(solution)/shard_map/ppermute | solution.py:130
  48.3 2.4 %collective-permute-done.2.refs_4_ = s16[1136,128]{1,0:T(8,128)(2,1)S(1)} collective-permute-done((s16[1136,128]{1,0:T(8,128)(2,1)S(1)}, s16[1136,128]{1,0:T(8,128)(2,1)S(1)}, u32[]{:S(2)}, u32[]{:S(2)}) %collective-permute-start.2) | collective-permute-done | bytes 290848 | tf_op jit(solution)/shard_map/ppermute | solution.py:130
  50.8 5.1 %factors.1 = (f32[4,128,128]{2,1,0:T(8,128)}, f32[5,96,96]{2,1,0:T(8,128)}, f32[4,128,128]{2,1,0:T(8,128)S(1)}, f32[3,96,96]{2,1,0:T(8,128)S(1)}) custom-call(s32[5]{0:T(128)S(1)} %copy-done.7, s32[4,4]{1,0:T(4,128)S(1)} %copy-done.8, s32[4,5]{1,0:T(4,128)S(1)} %copy-done.9, s16[1136,128]{1,0:T(8,128)(2,1)S(1)} %stats.1.refs_3_, ...), custom_call_target="tpu_custom_call" | custom-call | tf_op jit(solution)/shard_map/factors/pallas_call | solution.py:542
  56.8 4.5 %collective-permute-done.7.got = s16[2,256,256]{2,1,0:T(8,128)(2,1)S(1)} collective-permute-done((s16[2,256,256]{2,1,0:T(8,128)(2,1)S(1)}, s16[2,256,256]{2,1,0:T(8,128)(2,1)S(1)}, u32[]{:S(2)}, u32[]{:S(2)}) %collective-permute-start.7) | collective-permute-done | bytes 262176 | tf_op jit(solution)/shard_map/ppermute | solution.py:130
  61.3 2.2 %precon.1 = (f32[192,512]{1,0:T(8,128)S(1)}, f32[96,256]{1,0:T(8,128)S(1)}, f32[8,256]{1,0:T(8,128)S(1)}) custom-call(s32[5]{0:T(128)S(1)} %copy-done.7, s16[2,256,256]{2,1,0:T(8,128)(2,1)S(1)} %collective-permute-done.7.got, f32[2,240,256]{2,1,0:T(8,128)S(1)} %get-tuple-element.43.held, f32[3,96,96]{2,1,0:T(8,128)S(1)} %collective-permute-done.8.inv_g, ...), custom_call_target="tpu_custom_call" | custom-call | tf_op jit(solution)/shard_map/precon/pallas_call | solution.py:564
  63.5 2.1 %collective-permute-start.9 = (f32[8,256]{1,0:T(8,128)S(1)}, f32[8,256]{1,0:T(8,128)S(1)}, u32[]{:S(2)}, u32[]{:S(2)}) collective-permute-start(f32[8,256]{1,0:T(8,128)S(1)} %get-tuple-element.46), channel_id=1, source_target_pairs={{0,1},{1,0},{2,3},{3,2},{4,5},{5,4},{6,7},{7,6},{8,9},{9,8},{10,11... | collective-permute-start | bytes 24584 | tf_op jit(solution)/shard_map/ppermute | solution.py:134
  66.5 4.4 %collective-permute-start.10 = (f32[8,256]{1,0:T(8,128)S(1)}, f32[8,256]{1,0:T(8,128)S(1)}, u32[]{:S(2)}, u32[]{:S(2)}) collective-permute-start(f32[8,256]{1,0:T(8,128)S(1)} %add.14), channel_id=1, source_target_pairs={{0,2},{1,3},{2,0},{3,1},{4,6},{5,7},{6,4},{7,5},{8,10},{9,11},{10,... | collective-permute-start | bytes 24584 | tf_op jit(solution)/shard_map/ppermute | solution.py:134
  70.9 1.6 %collective-permute-done.10 = f32[8,256]{1,0:T(8,128)S(1)} collective-permute-done((f32[8,256]{1,0:T(8,128)S(1)}, f32[8,256]{1,0:T(8,128)S(1)}, u32[]{:S(2)}, u32[]{:S(2)}) %collective-permute-start.10) | collective-permute-done | bytes 8224 | tf_op jit(solution)/shard_map/ppermute | solution.py:134
  72.6 1.7 %collective-permute-start.11 = (f32[56,256]{1,0:T(8,128)S(1)}, f32[56,256]{1,0:T(8,128)S(1)}, u32[]{:S(2)}, u32[]{:S(2)}) collective-permute-start(f32[56,256]{1,0:T(8,128)S(1)} %pad_maximum_fusion.8), channel_id=1, source_target_pairs={{0,4},{4,0},{8,12},{12,8},{16,20},{20,16},{24,28},{28,24},{1,5},{5... | collective-permute-start | bytes 172040 | tf_op jit(solution)/shard_map/ppermute | solution.py:130
  74.3 2.5 %collective-permute-done.11.refs_5_ = f32[56,256]{1,0:T(8,128)S(1)} collective-permute-done((f32[56,256]{1,0:T(8,128)S(1)}, f32[56,256]{1,0:T(8,128)S(1)}, u32[]{:S(2)}, u32[]{:S(2)}) %collective-permute-start.11) | collective-permute-done | bytes 57376 | tf_op jit(solution)/shard_map/ppermute | solution.py:130
  77.1 3.4 %collective-permute-done.12 = f32[8,256]{1,0:T(8,128)S(1)} collective-permute-done((f32[8,256]{1,0:T(8,128)S(1)}, f32[8,256]{1,0:T(8,128)S(1)}, u32[]{:S(2)}, u32[]{:S(2)}) %collective-permute-start.12) | collective-permute-done | bytes 8224 | tf_op jit(solution)/shard_map/ppermute | solution.py:130
  81.6 3.4 %collective-permute-done.13.refs_2_ = f32[8,256]{1,0:T(8,128)S(1)} collective-permute-done((f32[8,256]{1,0:T(8,128)S(1)}, f32[8,256]{1,0:T(8,128)S(1)}, u32[]{:S(2)}, u32[]{:S(2)}) %collective-permute-start.13) | collective-permute-done | bytes 8224 | tf_op jit(solution)/shard_map/ppermute | solution.py:130
  85.0 1.7 %update.1 = (f32[240,512]{1,0:T(8,128)}, f32[240,512]{1,0:T(8,128)}, bf16[240,256]{1,0:T(8,128)(2,1)S(1)}, bf16[240,256]{1,0:T(8,128)(2,1)S(1)}) custom-call(s32[5]{0:T(128)S(1)} %copy-done.7, f32[8,256]{1,0:T(8,128)S(1)} %add.17.refs_1_, f32[8,256]{1,0:T(8,128)S(1)} %collective-permute-done.13.refs_2_, f32[192,512]{1,0:T(8,128)S(1)} %get-tuple-element.48.refs_3_, ...), custom_call_target="tpu_custom_call" | custom-call | tf_op jit(solution)/shard_map/update/pallas_call | solution.py:583
  87.9 1.3 %collective-permute-start.17 = (bf16[240,256]{1,0:T(8,128)(2,1)S(1)}, bf16[240,256]{1,0:T(8,128)(2,1)S(1)}, u32[]{:S(2)}, u32[]{:S(2)}) collective-permute-start(bf16[240,256]{1,0:T(8,128)(2,1)S(1)} %get-tuple-element.52), channel_id=1, source_target_pairs={{0,4},{4,0},{8,12},{12,8},{16,20},{20,16},{24,28},{28,24},{1,5},{5... | collective-permute-start | bytes 368648 | tf_op jit(solution)/shard_map/ppermute | solution.py:130
  89.2 5.4 %collective-permute-done.14 = bf16[240,256]{1,0:T(8,128)(2,1)S(1)} collective-permute-done((bf16[240,256]{1,0:T(8,128)(2,1)S(1)}, bf16[240,256]{1,0:T(8,128)(2,1)S(1)}, u32[]{:S(2)}, u32[]{:S(2)}) %collective-permute-start.14) | collective-permute-done | bytes 122912 | tf_op jit(solution)/shard_map/ppermute | solution.py:130
  94.8 1.7 %collective-permute-start.18 = (bf16[2,240,256]{2,1,0:T(8,128)(2,1)S(1)}, bf16[2,240,256]{2,1,0:T(8,128)(2,1)S(1)}, u32[]{:S(2)}, u32[]{:S(2)}) collective-permute-start(bf16[2,240,256]{2,1,0:T(8,128)(2,1)S(1)} %pad_maximum_fusion.7), channel_id=1, source_target_pairs={{0,16},{4,20},{8,24},{12,28},{16,0},{20,4},{24,8},{28,12},{1,17},{... | collective-permute-start | bytes 737288 | tf_op jit(solution)/shard_map/ppermute | solution.py:130
  96.5 9.2 %collective-permute-done.15 = bf16[2,240,256]{2,1,0:T(8,128)(2,1)S(1)} collective-permute-done((bf16[2,240,256]{2,1,0:T(8,128)(2,1)S(1)}, bf16[2,240,256]{2,1,0:T(8,128)(2,1)S(1)}, u32[]{:S(2)}, u32[]{:S(2)}) %collective-permute-start.15) | collective-permute-done | bytes 245792 | tf_op jit(solution)/shard_map/ppermute | solution.py:130
  105.8 4.1 %collective-permute-start.16 = (bf16[2,2,240,256]{3,2,0,1:T(8,128)(2,1)S(1)}, bf16[2,2,240,256]{3,2,0,1:T(8,128)(2,1)S(1)}, u32[]{:S(2)}, u32[]{:S(2)}) collective-permute-start(bf16[2,2,240,256]{3,2,0,1:T(8,128)(2,1)S(1)} %pad_maximum_fusion.3), channel_id=1, source_target_pairs={{0,4},{4,0},{8,12},{12,8},{16,20},{20,16},{24,28},{28,24},{1,5},{5... | collective-permute-start | bytes 1474568 | tf_op jit(solution)/shard_map/ppermute | solution.py:130
  110.1 6.6 %collective-permute-done.16 = bf16[2,2,240,256]{3,2,0,1:T(8,128)(2,1)S(1)} collective-permute-done((bf16[2,2,240,256]{3,2,0,1:T(8,128)(2,1)S(1)}, bf16[2,2,240,256]{3,2,0,1:T(8,128)(2,1)S(1)}, u32[]{:S(2)}, u32[]{:S(2)}) %collective-permute-start.16) | collective-permute-done | bytes 491552 | tf_op jit(solution)/shard_map/ppermute | solution.py:130
  117.0 2.0 %collective-permute-done.19 = bf16[2,2,240,256]{3,2,1,0:T(8,128)(2,1)S(1)} collective-permute-done((bf16[2,2,240,256]{3,2,1,0:T(8,128)(2,1)S(1)}, bf16[2,2,240,256]{3,2,1,0:T(8,128)(2,1)S(1)}, u32[]{:S(2)}, u32[]{:S(2)}) %collective-permute-start.19) | collective-permute-done | bytes 491552 | tf_op jit(solution)/shard_map/ppermute | solution.py:130
  119.2 1.4 %pad_maximum_fusion = bf16[1920,512]{1,0:T(8,128)(2,1)} fusion(bf16[1920,256]{1,0:T(8,128)(2,1)S(1)} %bitcast.43, bf16[1920,256]{1,0:T(8,128)(2,1)S(1)} %bitcast.42), kind=kLoop, calls=%fused_computation | loop fusion | flops 3932160 | bytes 3932160 | tf_op jit(solution)/shard_map/concatenate | solution.py:609
  (60 shorter events, 11.4 us)
Async XLA Ops:
  5.4 17.0 %copy-start = (bf16[64,1024]{1,0:T(8,128)(2,1)S(1)}, bf16[64,1024]{1,0:T(8,128)(2,1)}, u32[]{:S(2)}) copy-start(bf16[64,1024]{1,0:T(8,128)(2,1)} %picks.1.refs_1_) | copy-start | bytes 393220
  5.4 27.6 %copy-start.7 = (s32[5]{0:T(128)S(1)}, s32[5]{0:T(128)}, u32[]{:S(2)}) copy-start(s32[5]{0:T(128)} %stack.86.refs_0_.info) | copy-start | bytes 64
  5.4 13.9 %collective-permute-start = (bf16[64,1024]{1,0:T(8,128)(2,1)}, bf16[64,1024]{1,0:T(8,128)(2,1)S(1)}, u32[]{:S(2)}, u32[]{:S(2)}) collective-permute-start(bf16[64,1024]{1,0:T(8,128)(2,1)} %picks.1.refs_1_), channel_id=1, source_target_pairs={{0,16},{4,20},{8,24},{12,28},{16,0},{20,4},{24,8},{28,12},{1,17},{... | collective-permute-start | bytes 393224 | tf_op jit(solution)/shard_map/ppermute | solution.py:130
  19.3 17.6 %copy-start.1 = (f32[4,240,256]{2,1,0:T(8,128)S(1)}, f32[4,240,256]{2,1,0:T(8,128)}, u32[]{:S(2)}) copy-start(f32[4,240,256]{2,1,0:T(8,128)} %get-tuple-element.39.refs_2_) | copy-start | bytes 2949124
  19.3 13.7 %collective-permute-start.3 = (s16[4,256,256]{2,1,0:T(8,128)(2,1)}, s16[4,256,256]{2,1,0:T(8,128)(2,1)S(1)}, u32[]{:S(2)}, u32[]{:S(2)}) collective-permute-start(s16[4,256,256]{2,1,0:T(8,128)(2,1)} %get-tuple-element.34), channel_id=1, source_target_pairs={{0,4},{4,0},{8,12},{12,8},{16,20},{20,16},{24,28},{28,24},{1,5},{5... | collective-permute-start | bytes 1572872 | tf_op jit(solution)/shard_map/ppermute | solution.py:130
  20.8 16.0 %collective-permute-start.5 = (s16[4,256,256]{2,1,0:T(8,128)(2,1)}, s16[4,256,256]{2,1,0:T(8,128)(2,1)S(1)}, u32[]{:S(2)}, u32[]{:S(2)}) collective-permute-start(s16[4,256,256]{2,1,0:T(8,128)(2,1)} %get-tuple-element.38), channel_id=1, source_target_pairs={{0,8},{4,12},{8,0},{12,4},{16,24},{20,28},{24,16},{28,20},{1,9},{5... | collective-permute-start | bytes 1572872 | tf_op jit(solution)/shard_map/ppermute | solution.py:130
  22.5 19.1 %collective-permute-start.1 = (bf16[2,64,1024]{2,1,0:T(8,128)(2,1)S(1)}, bf16[2,64,1024]{2,1,0:T(8,128)(2,1)S(1)}, u32[]{:S(2)}, u32[]{:S(2)}) collective-permute-start(bf16[2,64,1024]{2,1,0:T(8,128)(2,1)S(1)} %pad_maximum_fusion.5), channel_id=1, source_target_pairs={{0,8},{4,12},{8,0},{12,4},{16,24},{20,28},{24,16},{28,20},{1,9},{5... | collective-permute-start | bytes 786440 | tf_op jit(solution)/shard_map/ppermute | solution.py:130
  33.0 1.2 copy-start.2
  35.2 15.6 %copy-start.5 = (f32[1,4,128,128]{3,2,1,0:T(8,128)S(1)}, f32[1,4,128,128]{3,2,1,0:T(8,128)}, u32[]{:S(2)}) copy-start(f32[1,4,128,128]{3,2,1,0:T(8,128)} %param.14) | copy-start | bytes 786436
  35.2 15.6 %copy-start.6 = (f32[1,5,96,96]{3,2,1,0:T(8,128)S(1)}, f32[1,5,96,96]{3,2,1,0:T(8,128)}, u32[]{:S(2)}) copy-start(f32[1,5,96,96]{3,2,1,0:T(8,128)} %param.15) | copy-start | bytes 552964
  35.2 15.6 %copy-start.8 = (s32[4,4]{1,0:T(4,128)S(1)}, s32[4,4]{1,0:T(4,128)}, u32[]{:S(2)}) copy-start(s32[4,4]{1,0:T(4,128)} %refs_1_.3) | copy-start | bytes 196
  35.2 15.6 %copy-start.9 = (s32[4,5]{1,0:T(4,128)S(1)}, s32[4,5]{1,0:T(4,128)}, u32[]{:S(2)}) copy-start(s32[4,5]{1,0:T(4,128)} %refs_2_.5) | copy-start | bytes 244
  35.2 10.3 %collective-permute-start.4 = (s16[2,256,256]{2,1,0:T(8,128)(2,1)S(1)}, s16[2,256,256]{2,1,0:T(8,128)(2,1)S(1)}, u32[]{:S(2)}, u32[]{:S(2)}) collective-permute-start(s16[2,256,256]{2,1,0:T(8,128)(2,1)S(1)} %get-tuple-element.36), channel_id=1, source_target_pairs={{0,8},{4,12},{8,0},{12,4},{16,24},{20,28},{24,16},{28,20},{1,9},{5... | collective-permute-start | bytes 786440 | tf_op jit(solution)/shard_map/ppermute | solution.py:130
  37.8 9.2 %collective-permute-start.6 = (s16[2,256,256]{2,1,0:T(8,128)(2,1)S(1)}, s16[2,256,256]{2,1,0:T(8,128)(2,1)S(1)}, u32[]{:S(2)}, u32[]{:S(2)}) collective-permute-start(s16[2,256,256]{2,1,0:T(8,128)(2,1)S(1)} %get-tuple-element.40), channel_id=1, source_target_pairs={{0,4},{4,0},{8,12},{12,8},{16,20},{20,16},{24,28},{28,24},{1,5},{5... | collective-permute-start | bytes 786440 | tf_op jit(solution)/shard_map/ppermute | solution.py:130
  42.7 42.4 %copy-start.3 = (f32[240,512]{1,0:T(8,128)S(1)}, f32[240,512]{1,0:T(8,128)}, u32[]{:S(2)}) copy-start(f32[240,512]{1,0:T(8,128)} %refs_6_.1) | copy-start | bytes 1474564
  42.7 42.4 %copy-start.4 = (f32[240,512]{1,0:T(8,128)S(1)}, f32[240,512]{1,0:T(8,128)}, u32[]{:S(2)}) copy-start(f32[240,512]{1,0:T(8,128)} %refs_7_.1) | copy-start | bytes 1474564
  42.7 8.1 %collective-permute-start.2 = (s16[1136,128]{1,0:T(8,128)(2,1)S(1)}, s16[1136,128]{1,0:T(8,128)(2,1)S(1)}, u32[]{:S(2)}, u32[]{:S(2)}) collective-permute-start(s16[1136,128]{1,0:T(8,128)(2,1)S(1)} %stats.1.refs_3_), channel_id=1, source_target_pairs={{0,4},{4,0},{8,12},{12,8},{16,20},{20,16},{24,28},{28,24},{1,5},{5... | collective-permute-start | bytes 872456 | tf_op jit(solution)/shard_map/ppermute | solution.py:130
  47.9 13.4 %collective-permute-start.7 = (s16[2,256,256]{2,1,0:T(8,128)(2,1)S(1)}, s16[2,256,256]{2,1,0:T(8,128)(2,1)S(1)}, u32[]{:S(2)}, u32[]{:S(2)}) collective-permute-start(s16[2,256,256]{2,1,0:T(8,128)(2,1)S(1)} %get-tuple-element.42), channel_id=1, source_target_pairs={{0,16},{4,20},{8,24},{12,28},{16,0},{20,4},{24,8},{28,12},{1,17},{... | collective-permute-start | bytes 786440 | tf_op jit(solution)/shard_map/ppermute | solution.py:130
  55.9 0.9 collective-permute-start.8
  63.5 3.0 %collective-permute-start.9 = (f32[8,256]{1,0:T(8,128)S(1)}, f32[8,256]{1,0:T(8,128)S(1)}, u32[]{:S(2)}, u32[]{:S(2)}) collective-permute-start(f32[8,256]{1,0:T(8,128)S(1)} %get-tuple-element.46), channel_id=1, source_target_pairs={{0,1},{1,0},{2,3},{3,2},{4,5},{5,4},{6,7},{7,6},{8,9},{9,8},{10,11... | collective-permute-start | bytes 24584 | tf_op jit(solution)/shard_map/ppermute | solution.py:134
  66.5 6.1 %collective-permute-start.10 = (f32[8,256]{1,0:T(8,128)S(1)}, f32[8,256]{1,0:T(8,128)S(1)}, u32[]{:S(2)}, u32[]{:S(2)}) collective-permute-start(f32[8,256]{1,0:T(8,128)S(1)} %add.14), channel_id=1, source_target_pairs={{0,2},{1,3},{2,0},{3,1},{4,6},{5,7},{6,4},{7,5},{8,10},{9,11},{10,... | collective-permute-start | bytes 24584 | tf_op jit(solution)/shard_map/ppermute | solution.py:134
  72.6 4.2 %collective-permute-start.11 = (f32[56,256]{1,0:T(8,128)S(1)}, f32[56,256]{1,0:T(8,128)S(1)}, u32[]{:S(2)}, u32[]{:S(2)}) collective-permute-start(f32[56,256]{1,0:T(8,128)S(1)} %pad_maximum_fusion.8), channel_id=1, source_target_pairs={{0,4},{4,0},{8,12},{12,8},{16,20},{20,16},{24,28},{28,24},{1,5},{5... | collective-permute-start | bytes 172040 | tf_op jit(solution)/shard_map/ppermute | solution.py:130
  76.8 3.7 %collective-permute-start.12 = (f32[8,256]{1,0:T(8,128)S(1)}, f32[8,256]{1,0:T(8,128)S(1)}, u32[]{:S(2)}, u32[]{:S(2)}) collective-permute-start(f32[8,256]{1,0:T(8,128)S(1)} %slice_add_fusion), channel_id=1, source_target_pairs={{0,8},{4,12},{8,0},{12,4},{16,24},{20,28},{24,16},{28,20},{1,9},{5... | collective-permute-start | bytes 24584 | tf_op jit(solution)/shard_map/ppermute | solution.py:130
  80.5 4.5 %collective-permute-start.13 = (f32[8,256]{1,0:T(8,128)S(1)}, f32[8,256]{1,0:T(8,128)S(1)}, u32[]{:S(2)}, u32[]{:S(2)}) collective-permute-start(f32[8,256]{1,0:T(8,128)S(1)} %add.17.refs_1_), channel_id=1, source_target_pairs={{0,16},{4,20},{8,24},{12,28},{16,0},{20,4},{24,8},{28,12},{1,17},{... | collective-permute-start | bytes 24584 | tf_op jit(solution)/shard_map/ppermute | solution.py:130
  86.7 7.9 %collective-permute-start.14 = (bf16[240,256]{1,0:T(8,128)(2,1)S(1)}, bf16[240,256]{1,0:T(8,128)(2,1)S(1)}, u32[]{:S(2)}, u32[]{:S(2)}) collective-permute-start(bf16[240,256]{1,0:T(8,128)(2,1)S(1)} %get-tuple-element.51), channel_id=1, source_target_pairs={{0,16},{4,20},{8,24},{12,28},{16,0},{20,4},{24,8},{28,12},{1,17},{... | collective-permute-start | bytes 368648 | tf_op jit(solution)/shard_map/ppermute | solution.py:130
  87.9 6.9 %collective-permute-start.17 = (bf16[240,256]{1,0:T(8,128)(2,1)S(1)}, bf16[240,256]{1,0:T(8,128)(2,1)S(1)}, u32[]{:S(2)}, u32[]{:S(2)}) collective-permute-start(bf16[240,256]{1,0:T(8,128)(2,1)S(1)} %get-tuple-element.52), channel_id=1, source_target_pairs={{0,4},{4,0},{8,12},{12,8},{16,20},{20,16},{24,28},{28,24},{1,5},{5... | collective-permute-start | bytes 368648 | tf_op jit(solution)/shard_map/ppermute | solution.py:130
  94.7 11.0 %collective-permute-start.15 = (bf16[2,240,256]{2,1,0:T(8,128)(2,1)S(1)}, bf16[2,240,256]{2,1,0:T(8,128)(2,1)S(1)}, u32[]{:S(2)}, u32[]{:S(2)}) collective-permute-start(bf16[2,240,256]{2,1,0:T(8,128)(2,1)S(1)} %pad_maximum_fusion.6), channel_id=1, source_target_pairs={{0,8},{4,12},{8,0},{12,4},{16,24},{20,28},{24,16},{28,20},{1,9},{5... | collective-permute-start | bytes 737288 | tf_op jit(solution)/shard_map/ppermute | solution.py:130
  94.8 15.1 %collective-permute-start.18 = (bf16[2,240,256]{2,1,0:T(8,128)(2,1)S(1)}, bf16[2,240,256]{2,1,0:T(8,128)(2,1)S(1)}, u32[]{:S(2)}, u32[]{:S(2)}) collective-permute-start(bf16[2,240,256]{2,1,0:T(8,128)(2,1)S(1)} %pad_maximum_fusion.7), channel_id=1, source_target_pairs={{0,16},{4,20},{8,24},{12,28},{16,0},{20,4},{24,8},{28,12},{1,17},{... | collective-permute-start | bytes 737288 | tf_op jit(solution)/shard_map/ppermute | solution.py:130
  105.8 10.9 %collective-permute-start.16 = (bf16[2,2,240,256]{3,2,0,1:T(8,128)(2,1)S(1)}, bf16[2,2,240,256]{3,2,0,1:T(8,128)(2,1)S(1)}, u32[]{:S(2)}, u32[]{:S(2)}) collective-permute-start(bf16[2,2,240,256]{3,2,0,1:T(8,128)(2,1)S(1)} %pad_maximum_fusion.3), channel_id=1, source_target_pairs={{0,4},{4,0},{8,12},{12,8},{16,20},{20,16},{24,28},{28,24},{1,5},{5... | collective-permute-start | bytes 1474568 | tf_op jit(solution)/shard_map/ppermute | solution.py:130
  110.0 8.9 %collective-permute-start.19 = (bf16[2,2,240,256]{3,2,1,0:T(8,128)(2,1)S(1)}, bf16[2,2,240,256]{3,2,1,0:T(8,128)(2,1)S(1)}, u32[]{:S(2)}, u32[]{:S(2)}) collective-permute-start(bf16[2,2,240,256]{3,2,1,0:T(8,128)(2,1)S(1)} %pad_maximum_fusion.4), channel_id=1, source_target_pairs={{0,8},{4,12},{8,0},{12,4},{16,24},{20,28},{24,16},{28,20},{1,9},{5... | collective-permute-start | bytes 1474568 | tf_op jit(solution)/shard_map/ppermute | solution.py:130

commit v5 on v4

--- a/solution.py
+++ b/solution.py
@@ -134,6 +134,11 @@
     return lax.ppermute(value, "tensor", [(i, i ^ bit) for i in range(4)])
 
 
+def swap_both(value, bit, bit_t):
+    route = [(4 * s + t, 4 * (s ^ bit) + (t ^ bit_t)) for s in range(8) for t in range(4)]
+    return lax.ppermute(value, ("shard", "tensor"), route)
+
+
 def pick(flag, if_zero, if_one):
     return jnp.where(flag == 0, if_zero, if_one)
 
@@ -167,6 +172,66 @@
         ref[index, first : first + GROUP, :] = data
 
     encode(value, store)
+
+
+FINE = 8
+FULL = 32767.0
+STEPS = 128.0
+
+
+def encode_fine(value, ref):
+    rows, width = value.shape
+    powers = []
+    for first in range(0, rows, 2 * FINE):
+        scaled = []
+        for start in (first, first + FINE):
+            part = value[start : start + FINE]
+            top = jnp.max(jnp.abs(part), axis=0, keepdims=True)
+            power = jnp.ceil(jnp.log2(jnp.maximum(top, 1e-30)) * STEPS)
+            scale = jnp.exp2(power * (-1.0 / STEPS)) * FULL
+            scaled.append(jnp.clip(jnp.round(part * scale), -FULL, FULL))
+            powers.append(power)
+        ref[first : first + 2 * FINE, :] = (
+            jnp.concatenate(scaled, axis=0).astype(jnp.int32).astype(jnp.int16)
+        )
+    powers += [jnp.zeros((1, width), f32)] * (-len(powers) % (2 * FINE))
+    for first in range(0, len(powers), 2 * FINE):
+        ref[rows + first : rows + first + 2 * FINE, :] = (
+            jnp.concatenate(powers[first : first + 2 * FINE], axis=0)
+            .astype(jnp.int32)
+            .astype(jnp.int16)
+        )
+
+
+def decode_fine(ref, rows):
+    values = ref[:rows, :].astype(jnp.int32).astype(f32)
+    powers = ref[rows:, :].astype(jnp.int32).astype(f32)
+    scales = jnp.exp2(powers * (1.0 / STEPS)) * (1.0 / FULL)
+    parts = [
+        values[first : first + FINE] * scales[first // FINE : first // FINE + 1]
+        for first in range(0, rows, FINE)
+    ]
+    return jnp.concatenate(parts, axis=0)
+
+
+def fine_rows(rows):
+    return rows + -(-(rows // FINE) // (2 * FINE)) * 2 * FINE
+
+
+def base_kernel(momentum, weight, packed):
+    kept = momentum_rate * momentum[...] + decay_rate * weight[...]
+    encode_fine(weight[...] - learn_rate * kept, packed)
+
+
+def parts_of(value):
+    upper = value.astype(bf16)
+    return upper, (value - upper.astype(f32)).astype(bf16)
+
+
+def dot_of(left, right):
+    dot = lambda p, q: jnp.dot(p, q, preferred_element_type=f32)
+    small = dot(left[0], right[1]) + dot(left[1], right[0])
+    return dot(left[0], right[0]) + small
 
 
 def picks_kernel(group_cols, info, sampled, acts, out_grad, picks, acts_buf, grad_buf, sems):
@@ -322,7 +387,7 @@
 
 
 def stats_kernel(blocks, info, own, one, two, packed, picks):
-    place = info[3] >> 1
+    place = 2 * info[4] + info[1]
     picks[place] = own[...]
     picks[place ^ 2] = one[...]
     picks[place ^ 1] = two[0]
@@ -369,37 +434,38 @@
         inverses.append(identity + error)
         scales.append(bound)
     every = range(count_a + count_g)
-    dot = lambda p, q: jnp.dot(p, q, preferred_element_type=f32, precision=highest)
-    errors = [dot(errors[i], errors[i]) for i in every]
+    errors = [parts_of(errors[i]) for i in every]
+    errors = [parts_of(dot_of(errors[i], errors[i])) for i in every]
     for step in range(1, NS_IT - 1):
-        grown = [dot(inverses[i], errors[i]) for i in every]
-        squares = [dot(errors[i], errors[i]) for i in every]
+        grown = [dot_of(parts_of(inverses[i]), errors[i]) for i in every]
+        squares = [dot_of(errors[i], errors[i]) for i in every]
         inverses = [inverses[i] + grown[i] for i in every]
-        errors = squares
-    inverses = [(inverses[i] + dot(inverses[i], errors[i])) / scales[i] for i in every]
+        errors = [parts_of(squares[i]) for i in every]
+    grown = [dot_of(parts_of(inverses[i]), errors[i]) for i in every]
+    inverses = [(inverses[i] + grown[i]) / scales[i] for i in every]
     for index in every:
         if index < count_a:
             inv_a[index] = inverses[index]
         else:
             inv_g[index - count_a] = inverses[index]
     side = info[1]
-    needed[0] = inv_g[3 * side]
-    needed[1] = inv_g[1 + 3 * side]
-    needed[2] = inv_g[2]
-
-
-def precon_kernel(info, got, held, inv_g, inv_a, top, mid, total):
+    for index, place in enumerate((3 * side, 1 + 3 * side, 2)):
+        encode_to(needed, index, inv_g[place])
+
+
+def precon_kernel(info, got, held, inv_g, inv_a, top, mid, total, coded):
     side = info[1]
     width_g, width_a = inv_g.shape[-1], inv_a.shape[-1]
     half = width_g // 2
-    dot = lambda p, q: jnp.dot(p, q, preferred_element_type=f32, precision=highest)
+    dot = lambda p, q: dot_of(parts_of(p), parts_of(q))
+    left = [decode(inv_g[place], width_g) for place in range(3)]
     squares = jnp.zeros((width_g, width_a), f32)
     for piece in range(2):
         part = held[piece] + decode(got[piece], held.shape[1])
         for place in range(2):
             for block in range(2):
                 values = dot(
-                    inv_g[place],
+                    left[place],
                     part[
                         place * width_g : (place + 1) * width_g,
                         block * width_a : (block + 1) * width_a,
@@ -411,34 +477,17 @@
                 top[place * width_g : (place + 1) * width_g, column : column + width_a] = values
         packed = part[2 * width_g : 2 * width_g + half, :]
         values = jnp.concatenate([packed[:, :width_a], packed[:, width_a:]], axis=0)
-        values = dot(dot(inv_g[2], values), inv_a[2 * piece + side])
+        values = dot(dot(left[2], values), inv_a[2 * piece + side])
         squares += values * values
         mid[:, piece * width_a : (piece + 1) * width_a] = values
     total[...] = jnp.full(total.shape, jnp.sum(squares), f32)
-
-
-def update_kernel(
-    entries, info, total, got_total, top, middle, got, momentum, weight, momentum_new, weight_new,
-    rounded_a, rounded_b
-):
-    rows, cols = momentum.shape
-    half = cols // 2
-    quarter = half // 2
-    head = top.shape[0]
-    mid = rows - head
-    mean_sq = (total[0:1, :] + got_total[0:1, :]) / entries
-    factor = 1.0 / jnp.sqrt(mean_sq + epsilon_sq)
-    factor = jnp.concatenate([factor, factor], axis=1)
-
-    def step(place, precon):
-        span = slice(place, place + precon.shape[0])
-        moved = momentum_rate * momentum[span, :] + precon * factor + decay_rate * weight[span, :]
-        fresh = weight[span, :] - learn_rate * moved
-        momentum_new[span, :] = moved
-        weight_new[span, :] = fresh
-        rounded_a[span, :] = fresh[:, :half].astype(bf16)
-        rounded_b[span, :] = fresh[:, half:].astype(bf16)
-
+    encode_fine(top[...], coded)
+
+
+def middle_kernel(info, middle, got, total, along_y, along_both, rest, packed, sums):
+    mid, cols = rest.shape
+    quarter = cols // 4
+    sums[...] = (total[...] + got[mid:, :]) + (along_y[...] + along_both[...])
     for x in range(2):
 
         @pl.when(info[1] == x)
@@ -449,8 +498,56 @@
                 columns = slice(piece * quarter, (piece + 1) * quarter)
                 both = [own[:, columns], got[:mid, columns]]
                 pairs += both if x == 0 else both[::-1]
-            step(head * (1 - x), jnp.concatenate(pairs, axis=1))
-            step(mid * x, top[...])
+            rest[...] = jnp.concatenate(pairs, axis=1)
+
+    encode_fine(rest[...], packed)
+
+
+def update_kernel(
+    entries, info, total, along_l, along_h, along_both, top, rest, momentum, weight, base, base_far,
+    scaled, scaled_far, small, small_far, momentum_new, weight_new, rounded_a, rounded_b
+):
+    rows, cols = momentum.shape
+    half = cols // 2
+    head, mid = top.shape[0], rest.shape[0]
+    sums = [each[0:1, :] for each in (total, along_l, along_h, along_both)]
+    mean_sq = ((sums[0] + sums[1]) + (sums[2] + sums[3])) / entries
+    factor = 1.0 / jnp.sqrt(mean_sq + epsilon_sq)
+    factor = jnp.concatenate([factor, factor], axis=1)
+    fixed = [decode_fine(base, rows), decode_fine(base_far, rows)]
+    moving = [
+        (decode_fine(scaled, head), decode_fine(small, mid)),
+        (decode_fine(scaled_far, head), decode_fine(small_far, mid)),
+    ]
+
+    def step(order):
+        precon = jnp.concatenate([(top, rest)[which][...] for which in order], axis=0)
+        moved = momentum_rate * momentum[...] + precon * factor + decay_rate * weight[...]
+        momentum_new[...] = moved
+        weight_new[...] = weight[...] - learn_rate * moved
+        for place in range(2):
+            change = jnp.concatenate([moving[place][which] for which in order], axis=0)
+            fresh = fixed[place] - (learn_rate * factor) * change
+            rounded_a[place] = fresh[:, :half].astype(bf16)
+            rounded_b[place] = fresh[:, half:].astype(bf16)
+
+    for x, order in enumerate(((0, 1), (1, 0))):
+
+        @pl.when(info[1] == x)
+        def _():
+            step(order)
+
+
+def place_kernel(rows, info, *refs):
+    parts, out = refs[:6], refs[6]
+    shard = info[3]
+    half = out.shape[1] // 2
+    codes = ((0, 4), (2, 6), (1, 5, 3, 7), (0, 4), (1, 5), (2, 6, 3, 7))
+    for index, (part, units) in enumerate(zip(parts, codes)):
+        first = half * (index // 3)
+        for place, code in enumerate(units):
+            start = pl.multiple_of((shard ^ code) * rows, 16)
+            out[pl.ds(start, rows), first : first + half] = part[place]
 
 
 def fast(acts, out_grad, sample_rows, own_a, own_g, a_state, g_state, momentum, weight):
@@ -505,9 +602,18 @@
         compiler_params=params(56),
         name="partial",
     )(info, out_grad, acts)
-    one, send_a, send_b = lax.optimization_barrier((one, send_a, send_b))
+    base = pl.pallas_call(
+        base_kernel,
+        in_specs=[vmem, vmem],
+        out_specs=vmem,
+        out_shape=shaped((fine_rows(rows), cols), jnp.int16),
+        compiler_params=params(16),
+        name="base",
+    )(momentum, weight)
+    one, send_a, send_b, base = lax.optimization_barrier((one, send_a, send_b, base))
+    base_far = swap(base, 4)
     got_a = swap(send_a, 1)
-    two = swap(jnp.stack([picks, one]), 2)
+    two = swap(jnp.stack([picks, one]), 1)
     got_b = swap(send_b, 2)
 
     send_a, keep_a = add_step(info, 2, True, got_a, keep_a)
@@ -522,10 +628,11 @@
         compiler_params=params(16),
         name="stats",
     )(info, picks, one, two)
-    got_packed = swap(packed, 1)
+    got_packed = swap(packed, 2)
     send_b, keep_b = add_step(info, 1, True, got_b, keep_b)
     got_b = swap(send_b, 1)
 
+    got_a, base_far = lax.optimization_barrier((got_a, base_far))
     send, keep = pl.pallas_call(
         last_add_kernel,
         in_specs=[smem] + [vmem] * 4,
@@ -547,7 +654,7 @@
             shaped(a_state.shape[1:], f32),
             shaped(g_state.shape[1:], f32),
             shaped(a_state.shape[1:], f32),
-            shaped((3, width_g, width_g), f32),
+            shaped((3, width_g + GROUP, width_g), jnp.int16),
         ],
         scratch_shapes=[pltpu.VMEM(g_state.shape[1:], f32)],
         compiler_params=params(24),
@@ -561,52 +668,69 @@
     ]
     inv_rows = lax.ppermute(needed, ("shard", "tensor"), route)
 
-    top, middle, total = pl.pallas_call(
+    top, middle, total, scaled = pl.pallas_call(
         precon_kernel,
         in_specs=[smem] + [vmem] * 4,
-        out_specs=[vmem] * 3,
+        out_specs=[vmem] * 4,
         out_shape=[
             shaped((head, cols), f32),
             shaped((width_g, half), f32),
             shaped((8, half), f32),
+            shaped((fine_rows(head), cols), jnp.int16),
         ],
         compiler_params=params(24),
         name="precon",
     )(info, got, keep, inv_rows, inv_a)
 
-    total = total + swap_t(total, 1)
-    total = total + swap_t(total, 2)
+    scaled_far = swap(scaled, 4)
     give = pick(side, middle[mid:], middle[:mid])
     got = swap(jnp.concatenate([give, total], axis=0), 1)
-    total = total + got[mid:]
-    total = total + swap(total, 2)
+    along_y = swap_t(total, 2)
+    along_both = swap_both(total, 1, 2)
+    rest, small, total = pl.pallas_call(
+        middle_kernel,
+        in_specs=[smem] + [vmem] * 5,
+        out_specs=[vmem] * 3,
+        out_shape=[
+            shaped((mid, cols), f32),
+            shaped((fine_rows(mid), cols), jnp.int16),
+            shaped((8, half), f32),
+        ],
+        compiler_params=params(16),
+        name="middle",
+    )(info, middle, got, total, along_y, along_both)
+    small_far = swap(small, 4)
+    total = total + swap_t(total, 1)
+    others = [swap(total, bits) for bits in (2, 4, 6)]
     momentum_new, weight_new, rounded_a, rounded_b = pl.pallas_call(
         lambda *refs: update_kernel(rows * 8 * cols * 4, *refs),
-        in_specs=[smem] + [vmem] * 7,
+        in_specs=[smem] + [vmem] * 14,
         out_specs=[vmem] * 4,
         out_shape=[
             shaped((rows, cols), f32),
             shaped((rows, cols), f32),
-            shaped((rows, half), bf16),
-            shaped((rows, half), bf16),
+            shaped((2, rows, half), bf16),
+            shaped((2, rows, half), bf16),
         ],
         compiler_params=params(24),
         name="update",
-    )(info, total, swap(total, 4), top, middle, got, momentum, weight)
-
-    def spread(values, bit, flag, axis):
-        other = swap(values, bit)
-        return jnp.stack([pick(flag, values, other), pick(flag, other, values)], axis=axis)
-
-    piece = rounded_a
-    piece = spread(piece, 4, high, 0)
-    piece = spread(piece, 2, low, 1)
-    whole_a = spread(piece, 1, side, 2).reshape(-1, half)
-    piece = rounded_b
-    piece = spread(piece, 1, side, 0)
-    piece = spread(piece, 4, high, 0)
-    whole_b = spread(piece, 2, low, 1).reshape(-1, half)
-    gathered = jnp.concatenate([whole_a, whole_b], axis=1)
+    )(
+        info, total, *others, top, rest, momentum, weight, base, base_far, scaled, scaled_far,
+        small, small_far,
+    )
+
+    along_l = swap(rounded_a, 2)
+    along_x = swap(rounded_b, 1)
+    rest_a = swap(jnp.concatenate([rounded_a, along_l]), 1)
+    rest_b = swap(jnp.concatenate([rounded_b, along_x]), 2)
+    gathered = pl.pallas_call(
+        lambda *refs: place_kernel(rows, *refs),
+        in_specs=[smem] + [vmem] * 6,
+        out_specs=vmem,
+        out_shape=shaped((rows * 8, cols), bf16),
+        compiler_params=params(16),
+        name="place",
+    )(info, rounded_a, along_l, rest_a, rounded_b, along_x, rest_b)
     return (new_a[None], new_g[None], momentum_new, weight_new, gathered)
 
 

time: 121 us -> 113 us (0.934)
  waiting for transfers between devices: 57.7 us -> 46.5 us
  starting transfers between devices: 31.1 us -> 34.2 us
  Pallas kernels: 26.8 us -> 28.9 us
  other arithmetic: 2.11 us -> 0.13 us
    ppermute x17 -> x19, waiting for transfers between devices: 55.3 us -> 41.8 us  [swap(): return lax.ppermute(value, 'shard', [(i, i ^ bit) for i in range(8)])]
    ppermute x17 -> x19, starting transfers between devices: 23.6 us -> 30.6 us  [swap(): return lax.ppermute(value, 'shard', [(i, i ^ bit) for i in range(8)])]
    ppermute x2, starting transfers between devices: 6.58 us -> 0.11 us  [swap_t(): return lax.ppermute(value, 'tensor', [(i, i ^ bit) for i in range(4)])]
    pallas_call x0 -> x3, Pallas kernels: none -> 2.99 us  [the longest x1 1.97 us: fast(): pl.pallas_call(lambda *refs: place_kernel(rows, *refs), in_specs=[smem] +...]
    ppermute x0 -> x1, starting transfers between devices: none -> 2.86 us  [swap_both(): return lax.ppermute(value, ('shard', 'tensor'), route)]
    ppermute x0 -> x1, waiting for transfers between devices: none -> 2.13 us  [swap_both(): return lax.ppermute(value, ('shard', 'tensor'), route)]
    concatenate x1 -> x2, other arithmetic: 1.43 us -> 0.09 us  [the longest x1 0.04 us: fast(): rest_a = swap(jnp.concatenate([rounded_a, along_l]), 1)]
  transfers between devices with their start and end apart: 20 -> 23, of which waited for: 15 -> 14; matrix products, arithmetic and copies ran while one was open for 0% -> 0% of each run, Pallas kernels for 16% -> 17%
where the time goes in v5:
time: 113 us
  waiting for transfers between devices  46.5 us (41%)
  starting transfers between devices  34.2 us (30%)
  Pallas kernels  28.9 us (26%)
  local copies, waits for them, and re-layouts  1.94 us (2%)
    ppermute x19, waiting for transfers between devices, swap(): return lax.ppermute(value, 'shard', [(i, i ^ bit) for i in range(8)])  41.8 us
    ppermute x19, starting transfers between devices, swap(): return lax.ppermute(value, 'shard', [(i, i ^ bit) for i in range(8)])  30.6 us
    pallas_call x1, Pallas kernels, fast(): pl.pallas_call(lambda *refs: partial_kernel(group_cols, width_g, *refs),...  9.71 us
    pallas_call x1, Pallas kernels, fast(): pl.pallas_call(lambda *refs: factor_kernel(share, blocks, *refs), in_spec...  4.24 us
    pallas_call x1, Pallas kernels, fast(): pl.pallas_call(lambda *refs: picks_kernel(group_cols, *refs), in_specs=[s...  4.15 us
    ppermute x1, starting transfers between devices, swap_both(): return lax.ppermute(value, ('shard', 'tensor'), route)  2.86 us
    ppermute x2, waiting for transfers between devices, swap_t(): return lax.ppermute(value, 'tensor', [(i, i ^ bit) for i in range(4)])  2.58 us
  transfers between devices with their start and end apart: 23, of which 14 were waited for; matrix products, arithmetic and copies ran while one was open for 0% of the time, Pallas kernels for 17%

profile of v5, /device:TPU:0, one launch (start us, length us, event | category | flops | bytes accessed | tf_op | source)
XLA Modules:
  0.0 112.5 jit_solution(10848746563183825455)
XLA Ops:
  1.3 4.2 %picks.1.refs_1_ = bf16[64,1024]{1,0:T(8,128)(2,1)} custom-call(s32[5]{0:T(128)} %stack.32.refs_0_.info, s32[1,64]{1,0:T(1,128)} %bitcast.16, bf16[2048,512]{1,0:T(8,128)(2,1)} %refs_2_.4, bf16[2048,1920]{1,0:T(8,128)(2,1)} %refs_1_.2), custom_call_target="tpu_custom_call" | custom-call | tf_op jit(solution)/shard_map/picks/pallas_call | solution.py:572
  5.5 4.1 %collective-permute-start = (bf16[64,1024]{1,0:T(8,128)(2,1)}, bf16[64,1024]{1,0:T(8,128)(2,1)S(1)}, u32[]{:S(2)}, u32[]{:S(2)}) collective-permute-start(bf16[64,1024]{1,0:T(8,128)(2,1)} %picks.1.refs_1_), channel_id=1, source_target_pairs={{0,16},{4,20},{8,24},{12,28},{16,0},{20,4},{24,8},{28,12},{1,17},{... | collective-permute-start | bytes 393224 | tf_op jit(solution)/shard_map/ppermute | solution.py:130
  9.6 9.7 %partial.1 = (s16[4,256,256]{2,1,0:T(8,128)(2,1)}, f32[4,240,256]{2,1,0:T(8,128)}, s16[4,256,256]{2,1,0:T(8,128)(2,1)}, f32[4,240,256]{2,1,0:T(8,128)}) custom-call(s32[5]{0:T(128)} %stack.32.refs_0_.info, bf16[2048,1920]{1,0:T(8,128)(2,1)} %refs_1_.2, bf16[2048,512]{1,0:T(8,128)(2,1)} %refs_2_.4), custom_call_target="tpu_custom_call" | custom-call | tf_op jit(solution)/shard_map/partial/pallas_call | solution.py:587
  19.8 1.6 %collective-permute-start.3 = (s16[4,256,256]{2,1,0:T(8,128)(2,1)}, s16[4,256,256]{2,1,0:T(8,128)(2,1)S(1)}, u32[]{:S(2)}, u32[]{:S(2)}) collective-permute-start(s16[4,256,256]{2,1,0:T(8,128)(2,1)} %get-tuple-element.41), channel_id=1, source_target_pairs={{0,4},{4,0},{8,12},{12,8},{16,20},{20,16},{24,28},{28,24},{1,5},{5... | collective-permute-start | bytes 1572872 | tf_op jit(solution)/shard_map/ppermute | solution.py:130
  21.4 1.6 %collective-permute-start.6 = (s16[4,256,256]{2,1,0:T(8,128)(2,1)}, s16[4,256,256]{2,1,0:T(8,128)(2,1)S(1)}, u32[]{:S(2)}, u32[]{:S(2)}) collective-permute-start(s16[4,256,256]{2,1,0:T(8,128)(2,1)} %get-tuple-element.47), channel_id=1, source_target_pairs={{0,8},{4,12},{8,0},{12,4},{16,24},{20,28},{24,16},{28,20},{1,9},{5... | collective-permute-start | bytes 1572872 | tf_op jit(solution)/shard_map/ppermute | solution.py:130
  23.9 11.0 %collective-permute-done.3.refs_1_ = s16[4,256,256]{2,1,0:T(8,128)(2,1)S(1)} collective-permute-done((s16[4,256,256]{2,1,0:T(8,128)(2,1)}, s16[4,256,256]{2,1,0:T(8,128)(2,1)S(1)}, u32[]{:S(2)}, u32[]{:S(2)}) %collective-permute-start.3) | collective-permute-done | bytes 524320 | tf_op jit(solution)/shard_map/ppermute | solution.py:130
  34.9 1.2 %copy-done.4 = f32[4,240,256]{2,1,0:T(8,128)S(1)} copy-done((f32[4,240,256]{2,1,0:T(8,128)S(1)}, f32[4,240,256]{2,1,0:T(8,128)}, u32[]{:S(2)}) %copy-start.4) | copy-done | bytes 983064
  37.1 1.6 %collective-permute-start.4 = (s16[2,256,256]{2,1,0:T(8,128)(2,1)S(1)}, s16[2,256,256]{2,1,0:T(8,128)(2,1)S(1)}, u32[]{:S(2)}, u32[]{:S(2)}) collective-permute-start(s16[2,256,256]{2,1,0:T(8,128)(2,1)S(1)} %get-tuple-element.43), channel_id=1, source_target_pairs={{0,8},{4,12},{8,0},{12,4},{16,24},{20,28},{24,16},{28,20},{1,9},{5... | collective-permute-start | bytes 786440 | tf_op jit(solution)/shard_map/ppermute | solution.py:130
  38.7 3.7 %collective-permute-done.6.refs_1_ = s16[4,256,256]{2,1,0:T(8,128)(2,1)S(1)} collective-permute-done((s16[4,256,256]{2,1,0:T(8,128)(2,1)}, s16[4,256,256]{2,1,0:T(8,128)(2,1)S(1)}, u32[]{:S(2)}, u32[]{:S(2)}) %collective-permute-start.6) | collective-permute-done | bytes 524320 | tf_op jit(solution)/shard_map/ppermute | solution.py:130
  42.4 0.9 add.7
  43.9 1.1 stats.1.refs_3_
  45.1 2.9 %collective-permute-done.4.got_a = s16[2,256,256]{2,1,0:T(8,128)(2,1)S(1)} collective-permute-done((s16[2,256,256]{2,1,0:T(8,128)(2,1)S(1)}, s16[2,256,256]{2,1,0:T(8,128)(2,1)S(1)}, u32[]{:S(2)}, u32[]{:S(2)}) %collective-permute-start.4) | collective-permute-done | bytes 262176 | tf_op jit(solution)/shard_map/ppermute | solution.py:130
  48.0 1.7 %collective-permute-done.7.got_b = s16[2,256,256]{2,1,0:T(8,128)(2,1)S(1)} collective-permute-done((s16[2,256,256]{2,1,0:T(8,128)(2,1)S(1)}, s16[2,256,256]{2,1,0:T(8,128)(2,1)S(1)}, u32[]{:S(2)}, u32[]{:S(2)}) %collective-permute-start.7) | collective-permute-done | bytes 262176 | tf_op jit(solution)/shard_map/ppermute | solution.py:130
  49.8 0.9 last_add.1
  50.8 4.2 %collective-permute-done.2.refs_4_ = s16[1136,128]{1,0:T(8,128)(2,1)S(1)} collective-permute-done((s16[1136,128]{1,0:T(8,128)(2,1)S(1)}, s16[1136,128]{1,0:T(8,128)(2,1)S(1)}, u32[]{:S(2)}, u32[]{:S(2)}) %collective-permute-start.2) | collective-permute-done | bytes 290848 | tf_op jit(solution)/shard_map/ppermute | solution.py:130
  55.0 4.2 %factors.1 = (f32[4,128,128]{2,1,0:T(8,128)}, f32[5,96,96]{2,1,0:T(8,128)}, f32[4,128,128]{2,1,0:T(8,128)S(1)}, s16[3,112,96]{2,1,0:T(8,128)(2,1)S(1)}) custom-call(s32[5]{0:T(128)S(1)} %copy-done.7, s32[4,4]{1,0:T(4,128)S(1)} %copy-done.8, s32[4,5]{1,0:T(4,128)S(1)} %copy-done.9, s16[1136,128]{1,0:T(8,128)(2,1)S(1)} %stats.1.refs_3_, ...), custom_call_target="tpu_custom_call" | custom-call | tf_op jit(solution)/shard_map/factors/pallas_call | solution.py:649
  59.9 1.4 %collective-permute-done.8.got = s16[2,256,256]{2,1,0:T(8,128)(2,1)S(1)} collective-permute-done((s16[2,256,256]{2,1,0:T(8,128)(2,1)S(1)}, s16[2,256,256]{2,1,0:T(8,128)(2,1)S(1)}, u32[]{:S(2)}, u32[]{:S(2)}) %collective-permute-start.8) | collective-permute-done | bytes 262176 | tf_op jit(solution)/shard_map/ppermute | solution.py:130
  61.4 1.8 %precon.1 = (f32[192,512]{1,0:T(8,128)S(1)}, f32[96,256]{1,0:T(8,128)S(1)}, f32[8,256]{1,0:T(8,128)S(1)}, s16[224,512]{1,0:T(8,128)(2,1)S(1)}) custom-call(s32[5]{0:T(128)S(1)} %copy-done.7, s16[2,256,256]{2,1,0:T(8,128)(2,1)S(1)} %collective-permute-done.8.got, f32[2,240,256]{2,1,0:T(8,128)S(1)} %get-tuple-element.52.held, ...), custom_call_target="tpu_custom_call" | custom-call | tf_op jit(solution)/shard_map/precon/pallas_call | solution.py:671
  63.1 8.6 %collective-permute-start.17 = (s16[224,512]{1,0:T(8,128)(2,1)S(1)}, s16[224,512]{1,0:T(8,128)(2,1)S(1)}, u32[]{:S(2)}, u32[]{:S(2)}) collective-permute-start(s16[224,512]{1,0:T(8,128)(2,1)S(1)} %get-tuple-element.61.refs_11_), channel_id=1, source_target_pairs={{0,16},{4,20},{8,24},{12,28},{16,0},{20,4},{24,8},{28,12},{1,17},{... | collective-permute-start | bytes 688136 | tf_op jit(solution)/shard_map/ppermute | solution.py:130
  72.3 2.9 %collective-permute-start.12 = (f32[8,256]{1,0:T(8,128)S(1)}, f32[8,256]{1,0:T(8,128)S(1)}, u32[]{:S(2)}, u32[]{:S(2)}) collective-permute-start(f32[8,256]{1,0:T(8,128)S(1)} %get-tuple-element.56.total), channel_id=1, source_target_pairs={{0,6},{1,7},{2,4},{3,5},{4,2},{5,3},{6,0},{7,1},{8,14},{9,15},{10,... | collective-permute-start | bytes 24584 | tf_op jit(solution)/shard_map/ppermute | solution.py:139
  75.3 2.1 %collective-permute-done.12.along_both = f32[8,256]{1,0:T(8,128)S(1)} collective-permute-done((f32[8,256]{1,0:T(8,128)S(1)}, f32[8,256]{1,0:T(8,128)S(1)}, u32[]{:S(2)}, u32[]{:S(2)}) %collective-permute-start.12) | collective-permute-done | bytes 8224 | tf_op jit(solution)/shard_map/ppermute | solution.py:139
  77.4 1.4 %collective-permute-done.11.along_y = f32[8,256]{1,0:T(8,128)S(1)} collective-permute-done((f32[8,256]{1,0:T(8,128)S(1)}, f32[8,256]{1,0:T(8,128)S(1)}, u32[]{:S(2)}, u32[]{:S(2)}) %collective-permute-start.11) | collective-permute-done | bytes 8224 | tf_op jit(solution)/shard_map/ppermute | solution.py:134
  79.5 3.0 %collective-permute-start.18 = (s16[64,512]{1,0:T(8,128)(2,1)S(1)}, s16[64,512]{1,0:T(8,128)(2,1)S(1)}, u32[]{:S(2)}, u32[]{:S(2)}) collective-permute-start(s16[64,512]{1,0:T(8,128)(2,1)S(1)} %get-tuple-element.62.refs_13_), channel_id=1, source_target_pairs={{0,16},{4,20},{8,24},{12,28},{16,0},{20,4},{24,8},{28,12},{1,17},{... | collective-permute-start | bytes 196616 | tf_op jit(solution)/shard_map/ppermute | solution.py:130
  82.4 1.2 %collective-permute-done.13 = f32[8,256]{1,0:T(8,128)S(1)} collective-permute-done((f32[8,256]{1,0:T(8,128)S(1)}, f32[8,256]{1,0:T(8,128)S(1)}, u32[]{:S(2)}, u32[]{:S(2)}) %collective-permute-start.13) | collective-permute-done | bytes 8224 | tf_op jit(solution)/shard_map/ppermute | solution.py:134
  83.7 4.3 %collective-permute-start.14 = (f32[8,256]{1,0:T(8,128)S(1)}, f32[8,256]{1,0:T(8,128)S(1)}, u32[]{:S(2)}, u32[]{:S(2)}) collective-permute-start(f32[8,256]{1,0:T(8,128)S(1)} %add.5.refs_1_), channel_id=1, source_target_pairs={{0,8},{4,12},{8,0},{12,4},{16,24},{20,28},{24,16},{28,20},{1,9},{5... | collective-permute-start | bytes 24584 | tf_op jit(solution)/shard_map/ppermute | solution.py:130
  88.0 1.1 collective-permute-done.16.refs_4_
  89.6 2.1 %update.1 = (f32[240,512]{1,0:T(8,128)}, f32[240,512]{1,0:T(8,128)}, bf16[2,240,256]{2,1,0:T(8,128)(2,1)S(1)}, bf16[2,240,256]{2,1,0:T(8,128)(2,1)S(1)}) custom-call(s32[5]{0:T(128)S(1)} %copy-done.7, f32[8,256]{1,0:T(8,128)S(1)} %add.5.refs_1_, f32[8,256]{1,0:T(8,128)S(1)} %collective-permute-done.14.refs_2_, f32[8,256]{1,0:T(8,128)S(1)} %collective-permute-done.15.refs_3_, ...), custom_call_target="tpu_custom_call" | custom-call | tf_op jit(solution)/shard_map/update/pallas_call | solution.py:705
  91.8 2.0 %collective-permute-start.19 = (bf16[2,240,256]{2,1,0:T(8,128)(2,1)S(1)}, bf16[2,240,256]{2,1,0:T(8,128)(2,1)S(1)}, u32[]{:S(2)}, u32[]{:S(2)}) collective-permute-start(bf16[2,240,256]{2,1,0:T(8,128)(2,1)S(1)} %get-tuple-element.65.refs_1_), channel_id=1, source_target_pairs={{0,8},{4,12},{8,0},{12,4},{16,24},{20,28},{24,16},{28,20},{1,9},{5... | collective-permute-start | bytes 737288 | tf_op jit(solution)/shard_map/ppermute | solution.py:130
  94.3 4.3 %collective-permute-done.19.refs_2_ = bf16[2,240,256]{2,1,0:T(8,128)(2,1)S(1)} collective-permute-done((bf16[2,240,256]{2,1,0:T(8,128)(2,1)S(1)}, bf16[2,240,256]{2,1,0:T(8,128)(2,1)S(1)}, u32[]{:S(2)}, u32[]{:S(2)}) %collective-permute-start.19) | collective-permute-done | bytes 245792 | tf_op jit(solution)/shard_map/ppermute | solution.py:130
  99.3 1.1 %collective-permute-done.21.refs_5_ = bf16[2,240,256]{2,1,0:T(8,128)(2,1)S(1)} collective-permute-done((bf16[2,240,256]{2,1,0:T(8,128)(2,1)S(1)}, bf16[2,240,256]{2,1,0:T(8,128)(2,1)S(1)}, u32[]{:S(2)}, u32[]{:S(2)}) %collective-permute-start.21) | collective-permute-done | bytes 245792 | tf_op jit(solution)/shard_map/ppermute | solution.py:130
  100.8 9.7 %collective-permute-done.20.refs_3_ = bf16[4,240,256]{2,1,0:T(8,128)(2,1)S(1)} collective-permute-done((bf16[4,240,256]{2,1,0:T(8,128)(2,1)S(1)}, bf16[4,240,256]{2,1,0:T(8,128)(2,1)S(1)}, u32[]{:S(2)}, u32[]{:S(2)}) %collective-permute-start.20) | collective-permute-done | bytes 491552 | tf_op jit(solution)/shard_map/ppermute | solution.py:130
  110.5 2.0 %place.1 = bf16[1920,512]{1,0:T(8,128)(2,1)} custom-call(s32[5]{0:T(128)S(1)} %copy-done.7, bf16[2,240,256]{2,1,0:T(8,128)(2,1)S(1)} %get-tuple-element.65.refs_1_, bf16[2,240,256]{2,1,0:T(8,128)(2,1)S(1)} %collective-permute-done.19.refs_2_, bf16[4,240,256]{2,1,0:T(8,128)(2,1)S(1)} %collective-permute-done.20.refs_3_, ...), custom_call_target="tpu_custom_call" | custom-call | tf_op jit(solution)/shard_map/place/pallas_call | solution.py:726
  (53 shorter events, 8.0 us)
Async XLA Ops:
  5.5 13.9 %copy-start = (f32[240,512]{1,0:T(8,128)S(1)}, f32[240,512]{1,0:T(8,128)}, u32[]{:S(2)}) copy-start(f32[240,512]{1,0:T(8,128)} %refs_7_.1) | copy-start | bytes 1474564
  5.5 13.9 %copy-start.1 = (f32[240,512]{1,0:T(8,128)S(1)}, f32[240,512]{1,0:T(8,128)}, u32[]{:S(2)}) copy-start(f32[240,512]{1,0:T(8,128)} %refs_8_.1) | copy-start | bytes 1474564
  5.5 17.4 %copy-start.2 = (bf16[64,1024]{1,0:T(8,128)(2,1)S(1)}, bf16[64,1024]{1,0:T(8,128)(2,1)}, u32[]{:S(2)}) copy-start(bf16[64,1024]{1,0:T(8,128)(2,1)} %picks.1.refs_1_) | copy-start | bytes 393220
  5.5 29.4 %copy-start.7 = (s32[5]{0:T(128)S(1)}, s32[5]{0:T(128)}, u32[]{:S(2)}) copy-start(s32[5]{0:T(128)} %stack.32.refs_0_.info) | copy-start | bytes 64
  5.5 14.3 %collective-permute-start = (bf16[64,1024]{1,0:T(8,128)(2,1)}, bf16[64,1024]{1,0:T(8,128)(2,1)S(1)}, u32[]{:S(2)}, u32[]{:S(2)}) collective-permute-start(bf16[64,1024]{1,0:T(8,128)(2,1)} %picks.1.refs_1_), channel_id=1, source_target_pairs={{0,16},{4,20},{8,24},{12,28},{16,0},{20,4},{24,8},{28,12},{1,17},{... | collective-permute-start | bytes 393224 | tf_op jit(solution)/shard_map/ppermute | solution.py:130
  19.4 23.0 %copy-start.3 = (f32[4,240,256]{2,1,0:T(8,128)S(1)}, f32[4,240,256]{2,1,0:T(8,128)}, u32[]{:S(2)}) copy-start(f32[4,240,256]{2,1,0:T(8,128)} %get-tuple-element.48.refs_2_) | copy-start | bytes 2949124
  19.8 15.1 %collective-permute-start.3 = (s16[4,256,256]{2,1,0:T(8,128)(2,1)}, s16[4,256,256]{2,1,0:T(8,128)(2,1)S(1)}, u32[]{:S(2)}, u32[]{:S(2)}) collective-permute-start(s16[4,256,256]{2,1,0:T(8,128)(2,1)} %get-tuple-element.41), channel_id=1, source_target_pairs={{0,4},{4,0},{8,12},{12,8},{16,20},{20,16},{24,28},{28,24},{1,5},{5... | collective-permute-start | bytes 1572872 | tf_op jit(solution)/shard_map/ppermute | solution.py:130
  21.4 21.0 %collective-permute-start.6 = (s16[4,256,256]{2,1,0:T(8,128)(2,1)}, s16[4,256,256]{2,1,0:T(8,128)(2,1)S(1)}, u32[]{:S(2)}, u32[]{:S(2)}) collective-permute-start(s16[4,256,256]{2,1,0:T(8,128)(2,1)} %get-tuple-element.47), channel_id=1, source_target_pairs={{0,8},{4,12},{8,0},{12,4},{16,24},{20,28},{24,16},{28,20},{1,9},{5... | collective-permute-start | bytes 1572872 | tf_op jit(solution)/shard_map/ppermute | solution.py:130
  23.0 21.0 %collective-permute-start.1 = (bf16[2,64,1024]{2,1,0:T(8,128)(2,1)S(1)}, bf16[2,64,1024]{2,1,0:T(8,128)(2,1)S(1)}, u32[]{:S(2)}, u32[]{:S(2)}) collective-permute-start(bf16[2,64,1024]{2,1,0:T(8,128)(2,1)S(1)} %pad_maximum_fusion.2), channel_id=1, source_target_pairs={{0,4},{4,0},{8,12},{12,8},{16,20},{20,16},{24,28},{28,24},{1,5},{5... | collective-permute-start | bytes 786440 | tf_op jit(solution)/shard_map/ppermute | solution.py:130
  23.6 21.6 %collective-permute-start.5 = (s16[272,512]{1,0:T(8,128)(2,1)S(1)}, s16[272,512]{1,0:T(8,128)(2,1)S(1)}, u32[]{:S(2)}, u32[]{:S(2)}) collective-permute-start(s16[272,512]{1,0:T(8,128)(2,1)S(1)} %base.1.refs_9_), channel_id=1, source_target_pairs={{0,16},{4,20},{8,24},{12,28},{16,0},{20,4},{24,8},{28,12},{1,17},{... | collective-permute-start | bytes 835592 | tf_op jit(solution)/shard_map/ppermute | solution.py:130
  37.0 18.0 %copy-start.5 = (f32[1,4,128,128]{3,2,1,0:T(8,128)S(1)}, f32[1,4,128,128]{3,2,1,0:T(8,128)}, u32[]{:S(2)}) copy-start(f32[1,4,128,128]{3,2,1,0:T(8,128)} %param.14) | copy-start | bytes 786436
  37.0 18.0 %copy-start.6 = (f32[1,5,96,96]{3,2,1,0:T(8,128)S(1)}, f32[1,5,96,96]{3,2,1,0:T(8,128)}, u32[]{:S(2)}) copy-start(f32[1,5,96,96]{3,2,1,0:T(8,128)} %param.15) | copy-start | bytes 552964
  37.1 18.0 %copy-start.8 = (s32[4,4]{1,0:T(4,128)S(1)}, s32[4,4]{1,0:T(4,128)}, u32[]{:S(2)}) copy-start(s32[4,4]{1,0:T(4,128)} %refs_1_.3) | copy-start | bytes 196
  37.1 17.9 %copy-start.9 = (s32[4,5]{1,0:T(4,128)S(1)}, s32[4,5]{1,0:T(4,128)}, u32[]{:S(2)}) copy-start(s32[4,5]{1,0:T(4,128)} %refs_2_.5) | copy-start | bytes 244
  37.1 10.9 %collective-permute-start.4 = (s16[2,256,256]{2,1,0:T(8,128)(2,1)S(1)}, s16[2,256,256]{2,1,0:T(8,128)(2,1)S(1)}, u32[]{:S(2)}, u32[]{:S(2)}) collective-permute-start(s16[2,256,256]{2,1,0:T(8,128)(2,1)S(1)} %get-tuple-element.43), channel_id=1, source_target_pairs={{0,8},{4,12},{8,0},{12,4},{16,24},{20,28},{24,16},{28,20},{1,9},{5... | collective-permute-start | bytes 786440 | tf_op jit(solution)/shard_map/ppermute | solution.py:130
  43.3 6.4 %collective-permute-start.7 = (s16[2,256,256]{2,1,0:T(8,128)(2,1)S(1)}, s16[2,256,256]{2,1,0:T(8,128)(2,1)S(1)}, u32[]{:S(2)}, u32[]{:S(2)}) collective-permute-start(s16[2,256,256]{2,1,0:T(8,128)(2,1)S(1)} %get-tuple-element.49), channel_id=1, source_target_pairs={{0,4},{4,0},{8,12},{12,8},{16,20},{20,16},{24,28},{28,24},{1,5},{5... | collective-permute-start | bytes 786440 | tf_op jit(solution)/shard_map/ppermute | solution.py:130
  45.0 10.0 %collective-permute-start.2 = (s16[1136,128]{1,0:T(8,128)(2,1)S(1)}, s16[1136,128]{1,0:T(8,128)(2,1)S(1)}, u32[]{:S(2)}, u32[]{:S(2)}) collective-permute-start(s16[1136,128]{1,0:T(8,128)(2,1)S(1)} %stats.1.refs_3_), channel_id=1, source_target_pairs={{0,8},{4,12},{8,0},{12,4},{16,24},{20,28},{24,16},{28,20},{1,9},{5... | collective-permute-start | bytes 872456 | tf_op jit(solution)/shard_map/ppermute | solution.py:130
  50.7 10.7 %collective-permute-start.8 = (s16[2,256,256]{2,1,0:T(8,128)(2,1)S(1)}, s16[2,256,256]{2,1,0:T(8,128)(2,1)S(1)}, u32[]{:S(2)}, u32[]{:S(2)}) collective-permute-start(s16[2,256,256]{2,1,0:T(8,128)(2,1)S(1)} %get-tuple-element.51), channel_id=1, source_target_pairs={{0,16},{4,20},{8,24},{12,28},{16,0},{20,4},{24,8},{28,12},{1,17},{... | collective-permute-start | bytes 786440 | tf_op jit(solution)/shard_map/ppermute | solution.py:130
  59.3 0.7 collective-permute-start.9
  63.1 26.5 %collective-permute-start.17 = (s16[224,512]{1,0:T(8,128)(2,1)S(1)}, s16[224,512]{1,0:T(8,128)(2,1)S(1)}, u32[]{:S(2)}, u32[]{:S(2)}) collective-permute-start(s16[224,512]{1,0:T(8,128)(2,1)S(1)} %get-tuple-element.61.refs_11_), channel_id=1, source_target_pairs={{0,16},{4,20},{8,24},{12,28},{16,0},{20,4},{24,8},{28,12},{1,17},{... | collective-permute-start | bytes 688136 | tf_op jit(solution)/shard_map/ppermute | solution.py:130
  71.7 7.1 %collective-permute-start.10 = (f32[56,256]{1,0:T(8,128)S(1)}, f32[56,256]{1,0:T(8,128)S(1)}, u32[]{:S(2)}, u32[]{:S(2)}) collective-permute-start(f32[56,256]{1,0:T(8,128)S(1)} %pad_maximum_fusion.3), channel_id=1, source_target_pairs={{0,4},{4,0},{8,12},{12,8},{16,20},{20,16},{24,28},{28,24},{1,5},{5... | collective-permute-start | bytes 172040 | tf_op jit(solution)/shard_map/ppermute | solution.py:130
  72.3 5.1 %collective-permute-start.12 = (f32[8,256]{1,0:T(8,128)S(1)}, f32[8,256]{1,0:T(8,128)S(1)}, u32[]{:S(2)}, u32[]{:S(2)}) collective-permute-start(f32[8,256]{1,0:T(8,128)S(1)} %get-tuple-element.56.total), channel_id=1, source_target_pairs={{0,6},{1,7},{2,4},{3,5},{4,2},{5,3},{6,0},{7,1},{8,14},{9,15},{10,... | collective-permute-start | bytes 24584 | tf_op jit(solution)/shard_map/ppermute | solution.py:139
  75.2 3.7 %collective-permute-start.11 = (f32[8,256]{1,0:T(8,128)S(1)}, f32[8,256]{1,0:T(8,128)S(1)}, u32[]{:S(2)}, u32[]{:S(2)}) collective-permute-start(f32[8,256]{1,0:T(8,128)S(1)} %get-tuple-element.56.total), channel_id=1, source_target_pairs={{0,2},{1,3},{2,0},{3,1},{4,6},{5,7},{6,4},{7,5},{8,10},{9,11},{10,... | collective-permute-start | bytes 24584 | tf_op jit(solution)/shard_map/ppermute | solution.py:134
  79.5 10.2 %collective-permute-start.18 = (s16[64,512]{1,0:T(8,128)(2,1)S(1)}, s16[64,512]{1,0:T(8,128)(2,1)S(1)}, u32[]{:S(2)}, u32[]{:S(2)}) collective-permute-start(s16[64,512]{1,0:T(8,128)(2,1)S(1)} %get-tuple-element.62.refs_13_), channel_id=1, source_target_pairs={{0,16},{4,20},{8,24},{12,28},{16,0},{20,4},{24,8},{28,12},{1,17},{... | collective-permute-start | bytes 196616 | tf_op jit(solution)/shard_map/ppermute | solution.py:130
  82.4 1.2 %collective-permute-start.13 = (f32[8,256]{1,0:T(8,128)S(1)}, f32[8,256]{1,0:T(8,128)S(1)}, u32[]{:S(2)}, u32[]{:S(2)}) collective-permute-start(f32[8,256]{1,0:T(8,128)S(1)} %get-tuple-element.57), channel_id=1, source_target_pairs={{0,1},{1,0},{2,3},{3,2},{4,5},{5,4},{6,7},{7,6},{8,9},{9,8},{10,11... | collective-permute-start | bytes 24584 | tf_op jit(solution)/shard_map/ppermute | solution.py:134
  83.6 5.4 %collective-permute-start.16 = (f32[8,256]{1,0:T(8,128)S(1)}, f32[8,256]{1,0:T(8,128)S(1)}, u32[]{:S(2)}, u32[]{:S(2)}) collective-permute-start(f32[8,256]{1,0:T(8,128)S(1)} %add.5.refs_1_), channel_id=1, source_target_pairs={{0,24},{4,28},{8,16},{12,20},{16,8},{20,12},{24,0},{28,4},{1,25},{... | collective-permute-start | bytes 24584 | tf_op jit(solution)/shard_map/ppermute | solution.py:130
  83.6 5.4 %collective-permute-start.15 = (f32[8,256]{1,0:T(8,128)S(1)}, f32[8,256]{1,0:T(8,128)S(1)}, u32[]{:S(2)}, u32[]{:S(2)}) collective-permute-start(f32[8,256]{1,0:T(8,128)S(1)} %add.5.refs_1_), channel_id=1, source_target_pairs={{0,16},{4,20},{8,24},{12,28},{16,0},{20,4},{24,8},{28,12},{1,17},{... | collective-permute-start | bytes 24584 | tf_op jit(solution)/shard_map/ppermute | solution.py:130
  83.7 5.9 %collective-permute-start.14 = (f32[8,256]{1,0:T(8,128)S(1)}, f32[8,256]{1,0:T(8,128)S(1)}, u32[]{:S(2)}, u32[]{:S(2)}) collective-permute-start(f32[8,256]{1,0:T(8,128)S(1)} %add.5.refs_1_), channel_id=1, source_target_pairs={{0,8},{4,12},{8,0},{12,4},{16,24},{20,28},{24,16},{28,20},{1,9},{5... | collective-permute-start | bytes 24584 | tf_op jit(solution)/shard_map/ppermute | solution.py:130
  91.8 6.9 %collective-permute-start.19 = (bf16[2,240,256]{2,1,0:T(8,128)(2,1)S(1)}, bf16[2,240,256]{2,1,0:T(8,128)(2,1)S(1)}, u32[]{:S(2)}, u32[]{:S(2)}) collective-permute-start(bf16[2,240,256]{2,1,0:T(8,128)(2,1)S(1)} %get-tuple-element.65.refs_1_), channel_id=1, source_target_pairs={{0,8},{4,12},{8,0},{12,4},{16,24},{20,28},{24,16},{28,20},{1,9},{5... | collective-permute-start | bytes 737288 | tf_op jit(solution)/shard_map/ppermute | solution.py:130
  93.8 6.6 %collective-permute-start.21 = (bf16[2,240,256]{2,1,0:T(8,128)(2,1)S(1)}, bf16[2,240,256]{2,1,0:T(8,128)(2,1)S(1)}, u32[]{:S(2)}, u32[]{:S(2)}) collective-permute-start(bf16[2,240,256]{2,1,0:T(8,128)(2,1)S(1)} %get-tuple-element.66.refs_4_), channel_id=1, source_target_pairs={{0,4},{4,0},{8,12},{12,8},{16,20},{20,16},{24,28},{28,24},{1,5},{5... | collective-permute-start | bytes 737288 | tf_op jit(solution)/shard_map/ppermute | solution.py:130
  98.7 11.8 %collective-permute-start.20 = (bf16[4,240,256]{2,1,0:T(8,128)(2,1)S(1)}, bf16[4,240,256]{2,1,0:T(8,128)(2,1)S(1)}, u32[]{:S(2)}, u32[]{:S(2)}) collective-permute-start(bf16[4,240,256]{2,1,0:T(8,128)(2,1)S(1)} %pad_maximum_fusion), channel_id=1, source_target_pairs={{0,4},{4,0},{8,12},{12,8},{16,20},{20,16},{24,28},{28,24},{1,5},{5... | collective-permute-start | bytes 1474568 | tf_op jit(solution)/shard_map/ppermute | solution.py:130
  100.5 10.1 %collective-permute-start.22 = (bf16[4,240,256]{2,1,0:T(8,128)(2,1)S(1)}, bf16[4,240,256]{2,1,0:T(8,128)(2,1)S(1)}, u32[]{:S(2)}, u32[]{:S(2)}) collective-permute-start(bf16[4,240,256]{2,1,0:T(8,128)(2,1)S(1)} %pad_maximum_fusion.1), channel_id=1, source_target_pairs={{0,8},{4,12},{8,0},{12,4},{16,24},{20,28},{24,16},{28,20},{1,9},{5... | collective-permute-start | bytes 1474568 | tf_op jit(solution)/shard_map/ppermute | solution.py:130
  (1 other events, 1.2 us)

commit v6 on v5

--- a/solution.py
+++ b/solution.py
@@ -568,22 +568,6 @@
     mid = width_g // 2
     info = jnp.stack([tensor_pos, side, low, shard_pos, high])
 
-    wide = cols + -(-group_cols // 128) * 128
-    picks = pl.pallas_call(
-        lambda *refs: picks_kernel(group_cols, *refs),
-        in_specs=[smem, vmem, main, main],
-        out_specs=vmem,
-        out_shape=shaped((drawn, wide), bf16),
-        scratch_shapes=[
-            pltpu.VMEM((tokens, cols), bf16),
-            pltpu.VMEM((tokens, 640), bf16),
-            pltpu.SemaphoreType.DMA((8,)),
-        ],
-        compiler_params=params(60),
-        name="picks",
-    )(info, sample_rows.reshape(1, -1), acts, out_grad)
-    one = swap(picks, 4)
-
     send_a, keep_a, send_b, keep_b = pl.pallas_call(
         lambda *refs: partial_kernel(group_cols, width_g, *refs),
         in_specs=[smem, main, main],
@@ -602,6 +586,26 @@
         compiler_params=params(56),
         name="partial",
     )(info, out_grad, acts)
+    sample_rows, send_a, send_b = lax.optimization_barrier((sample_rows, send_a, send_b))
+    got_a = swap(send_a, 1)
+    got_b = swap(send_b, 2)
+
+    wide = cols + -(-group_cols // 128) * 128
+    picks = pl.pallas_call(
+        lambda *refs: picks_kernel(group_cols, *refs),
+        in_specs=[smem, vmem, main, main],
+        out_specs=vmem,
+        out_shape=shaped((drawn, wide), bf16),
+        scratch_shapes=[
+            pltpu.VMEM((tokens, cols), bf16),
+            pltpu.VMEM((tokens, 640), bf16),
+            pltpu.SemaphoreType.DMA((8,)),
+        ],
+        compiler_params=params(60),
+        name="picks",
+    )(info, sample_rows.reshape(1, -1), acts, out_grad)
+    one = swap(picks, 4)
+
     base = pl.pallas_call(
         base_kernel,
         in_specs=[vmem, vmem],
@@ -610,11 +614,8 @@
         compiler_params=params(16),
         name="base",
     )(momentum, weight)
-    one, send_a, send_b, base = lax.optimization_barrier((one, send_a, send_b, base))
     base_far = swap(base, 4)
-    got_a = swap(send_a, 1)
     two = swap(jnp.stack([picks, one]), 1)
-    got_b = swap(send_b, 2)
 
     send_a, keep_a = add_step(info, 2, True, got_a, keep_a)
     got_a = swap(send_a, 2)
@@ -629,10 +630,10 @@
         name="stats",
     )(info, picks, one, two)
     got_packed = swap(packed, 2)
+    got_b, base_far = lax.optimization_barrier((got_b, base_far))
     send_b, keep_b = add_step(info, 1, True, got_b, keep_b)
     got_b = swap(send_b, 1)
 
-    got_a, base_far = lax.optimization_barrier((got_a, base_far))
     send, keep = pl.pallas_call(
         last_add_kernel,
         in_specs=[smem] + [vmem] * 4,

time: 113 us -> 108 us (0.956)
  starting transfers between devices: 34.2 us -> 31.1 us
  waiting for transfers between devices: 46.5 us -> 45.2 us
  local copies, waits for them, and re-layouts: 1.94 us -> 0.73 us
    ppermute x1, starting transfers between devices: 2.86 us -> 0.01 us  [swap_both(): return lax.ppermute(value, ('shard', 'tensor'), route)]
    ppermute x19, starting transfers between devices: 30.6 us -> 28.9 us  [swap(): return lax.ppermute(value, 'shard', [(i, i ^ bit) for i in range(8)])]
    ppermute x2, starting transfers between devices: 0.11 us -> 1.54 us  [swap_t(): return lax.ppermute(value, 'tensor', [(i, i ^ bit) for i in range(4)])]
    ppermute x2, waiting for transfers between devices: 2.58 us -> 1.17 us  [swap_t(): return lax.ppermute(value, 'tensor', [(i, i ^ bit) for i in range(4)])]
    unnamed x20, local copies, waits for them, and re-layouts: 1.25 us -> 0.05 us
  transfers between devices with their start and end apart: 23 -> 23, of which waited for: 14 -> 12; matrix products, arithmetic and copies ran while one was open for 0% -> 1% of each run, Pallas kernels for 17% -> 12%
where the time goes in v6:
time: 108 us
  waiting for transfers between devices  45.2 us (42%)
  starting transfers between devices  31.1 us (29%)
  Pallas kernels  29 us (27%)
    ppermute x19, waiting for transfers between devices, swap(): return lax.ppermute(value, 'shard', [(i, i ^ bit) for i in range(8)])  41 us
    ppermute x19, starting transfers between devices, swap(): return lax.ppermute(value, 'shard', [(i, i ^ bit) for i in range(8)])  28.9 us
    pallas_call x1, Pallas kernels, fast(): pl.pallas_call(lambda *refs: partial_kernel(group_cols, width_g, *refs),...  9.71 us
    pallas_call x1, Pallas kernels, fast(): pl.pallas_call(lambda *refs: picks_kernel(group_cols, *refs), in_specs=[s...  4.3 us
    pallas_call x1, Pallas kernels, fast(): pl.pallas_call(lambda *refs: factor_kernel(share, blocks, *refs), in_spec...  4.24 us
    ppermute x1, waiting for transfers between devices, swap_both(): return lax.ppermute(value, ('shard', 'tensor'), route)  3.01 us
  transfers between devices with their start and end apart: 23, of which 12 were waited for; matrix products, arithmetic and copies ran while one was open for 1% of the time, Pallas kernels for 12%

profile of v6, /device:TPU:0, one launch (start us, length us, event | category | flops | bytes accessed | tf_op | source)
XLA Modules:
  0.0 108.0 jit_solution(2180131706172984456)
XLA Ops:
  1.3 9.7 %partial.1 = (s16[4,256,256]{2,1,0:T(8,128)(2,1)}, f32[4,240,256]{2,1,0:T(8,128)}, s16[4,256,256]{2,1,0:T(8,128)(2,1)}, f32[4,240,256]{2,1,0:T(8,128)}) custom-call(s32[5]{0:T(128)} %stack.32.refs_0_.info, bf16[2048,1920]{1,0:T(8,128)(2,1)} %refs_3_.1, bf16[2048,512]{1,0:T(8,128)(2,1)} %refs_2_.4), custom_call_target="tpu_custom_call" | custom-call | tf_op jit(solution)/shard_map/partial/pallas_call | solution.py:571
  11.0 3.0 %collective-permute-start.3 = (s16[4,256,256]{2,1,0:T(8,128)(2,1)}, s16[4,256,256]{2,1,0:T(8,128)(2,1)S(1)}, u32[]{:S(2)}, u32[]{:S(2)}) collective-permute-start(s16[4,256,256]{2,1,0:T(8,128)(2,1)} %get-tuple-element.40), channel_id=1, source_target_pairs={{0,4},{4,0},{8,12},{12,8},{16,20},{20,16},{24,28},{28,24},{1,5},{5... | collective-permute-start | bytes 1572872 | tf_op jit(solution)/shard_map/ppermute | solution.py:130
  14.0 1.6 %collective-permute-start.5 = (s16[4,256,256]{2,1,0:T(8,128)(2,1)}, s16[4,256,256]{2,1,0:T(8,128)(2,1)S(1)}, u32[]{:S(2)}, u32[]{:S(2)}) collective-permute-start(s16[4,256,256]{2,1,0:T(8,128)(2,1)} %get-tuple-element.44), channel_id=1, source_target_pairs={{0,8},{4,12},{8,0},{12,4},{16,24},{20,28},{24,16},{28,20},{1,9},{5... | collective-permute-start | bytes 1572872 | tf_op jit(solution)/shard_map/ppermute | solution.py:130
  15.6 4.3 %picks.1.refs_1_ = bf16[64,1024]{1,0:T(8,128)(2,1)} custom-call(s32[5]{0:T(128)} %stack.32.refs_0_.info, s32[1,64]{1,0:T(1,128)} %bitcast.16, bf16[2048,512]{1,0:T(8,128)(2,1)} %refs_2_.4, bf16[2048,1920]{1,0:T(8,128)(2,1)} %refs_3_.1), custom_call_target="tpu_custom_call" | custom-call | tf_op jit(solution)/shard_map/picks/pallas_call | solution.py:594
  20.0 2.7 %collective-permute-start = (bf16[64,1024]{1,0:T(8,128)(2,1)}, bf16[64,1024]{1,0:T(8,128)(2,1)S(1)}, u32[]{:S(2)}, u32[]{:S(2)}) collective-permute-start(bf16[64,1024]{1,0:T(8,128)(2,1)} %picks.1.refs_1_), channel_id=1, source_target_pairs={{0,16},{4,20},{8,24},{12,28},{16,0},{20,4},{24,8},{28,12},{1,17},{... | collective-permute-start | bytes 393224 | tf_op jit(solution)/shard_map/ppermute | solution.py:130
  23.4 7.7 %collective-permute-done.refs_2_ = bf16[64,1024]{1,0:T(8,128)(2,1)S(1)} collective-permute-done((bf16[64,1024]{1,0:T(8,128)(2,1)}, bf16[64,1024]{1,0:T(8,128)(2,1)S(1)}, u32[]{:S(2)}, u32[]{:S(2)}) %collective-permute-start) | collective-permute-done | bytes 131104 | tf_op jit(solution)/shard_map/ppermute | solution.py:130
  33.7 3.5 %collective-permute-start.4 = (s16[2,256,256]{2,1,0:T(8,128)(2,1)S(1)}, s16[2,256,256]{2,1,0:T(8,128)(2,1)S(1)}, u32[]{:S(2)}, u32[]{:S(2)}) collective-permute-start(s16[2,256,256]{2,1,0:T(8,128)(2,1)S(1)} %get-tuple-element.42), channel_id=1, source_target_pairs={{0,8},{4,12},{8,0},{12,4},{16,24},{20,28},{24,16},{28,20},{1,9},{5... | collective-permute-start | bytes 786440 | tf_op jit(solution)/shard_map/ppermute | solution.py:130
  37.2 3.8 %collective-permute-done.6.refs_10_ = s16[272,512]{1,0:T(8,128)(2,1)S(1)} collective-permute-done((s16[272,512]{1,0:T(8,128)(2,1)S(1)}, s16[272,512]{1,0:T(8,128)(2,1)S(1)}, u32[]{:S(2)}, u32[]{:S(2)}) %collective-permute-start.6) | collective-permute-done | bytes 278560 | tf_op jit(solution)/shard_map/ppermute | solution.py:130
  42.5 1.1 %stats.1.refs_3_ = s16[1136,128]{1,0:T(8,128)(2,1)S(1)} custom-call(s32[5]{0:T(128)S(1)} %copy-done.7, bf16[64,1024]{1,0:T(8,128)(2,1)S(1)} %copy-done.2, bf16[64,1024]{1,0:T(8,128)(2,1)S(1)} %collective-permute-done.refs_2_, bf16[2,64,1024]{2,1,0:T(8,128)(2,1)S(1)} %collective-permute-done.1.refs_3_), custom_call_target="tpu_custom_call" | custom-call | tf_op jit(solution)/shard_map/stats/pallas_call | solution.py:623
  43.7 4.6 %collective-permute-done.7.got_b = s16[2,256,256]{2,1,0:T(8,128)(2,1)S(1)} collective-permute-done((s16[2,256,256]{2,1,0:T(8,128)(2,1)S(1)}, s16[2,256,256]{2,1,0:T(8,128)(2,1)S(1)}, u32[]{:S(2)}, u32[]{:S(2)}) %collective-permute-start.7) | collective-permute-done | bytes 262176 | tf_op jit(solution)/shard_map/ppermute | solution.py:130
  49.3 2.5 %collective-permute-done.2.refs_4_ = s16[1136,128]{1,0:T(8,128)(2,1)S(1)} collective-permute-done((s16[1136,128]{1,0:T(8,128)(2,1)S(1)}, s16[1136,128]{1,0:T(8,128)(2,1)S(1)}, u32[]{:S(2)}, u32[]{:S(2)}) %collective-permute-start.2) | collective-permute-done | bytes 290848 | tf_op jit(solution)/shard_map/ppermute | solution.py:130
  51.9 4.2 %factors.1 = (f32[4,128,128]{2,1,0:T(8,128)}, f32[5,96,96]{2,1,0:T(8,128)}, f32[4,128,128]{2,1,0:T(8,128)S(1)}, s16[3,112,96]{2,1,0:T(8,128)(2,1)S(1)}) custom-call(s32[5]{0:T(128)S(1)} %copy-done.7, s32[4,4]{1,0:T(4,128)S(1)} %copy-done.8, s32[4,5]{1,0:T(4,128)S(1)} %copy-done.9, s16[1136,128]{1,0:T(8,128)(2,1)S(1)} %stats.1.refs_3_, ...), custom_call_target="tpu_custom_call" | custom-call | tf_op jit(solution)/shard_map/factors/pallas_call | solution.py:650
  56.8 6.6 %collective-permute-done.8.got = s16[2,256,256]{2,1,0:T(8,128)(2,1)S(1)} collective-permute-done((s16[2,256,256]{2,1,0:T(8,128)(2,1)S(1)}, s16[2,256,256]{2,1,0:T(8,128)(2,1)S(1)}, u32[]{:S(2)}, u32[]{:S(2)}) %collective-permute-start.8) | collective-permute-done | bytes 262176 | tf_op jit(solution)/shard_map/ppermute | solution.py:130
  63.4 1.8 %precon.1 = (f32[192,512]{1,0:T(8,128)S(1)}, f32[96,256]{1,0:T(8,128)S(1)}, f32[8,256]{1,0:T(8,128)S(1)}, s16[224,512]{1,0:T(8,128)(2,1)S(1)}) custom-call(s32[5]{0:T(128)S(1)} %copy-done.7, s16[2,256,256]{2,1,0:T(8,128)(2,1)S(1)} %collective-permute-done.8.got, f32[2,240,256]{2,1,0:T(8,128)S(1)} %get-tuple-element.50.held, ...), custom_call_target="tpu_custom_call" | custom-call | tf_op jit(solution)/shard_map/precon/pallas_call | solution.py:672
  65.2 2.6 %collective-permute-start.17 = (s16[224,512]{1,0:T(8,128)(2,1)S(1)}, s16[224,512]{1,0:T(8,128)(2,1)S(1)}, u32[]{:S(2)}, u32[]{:S(2)}) collective-permute-start(s16[224,512]{1,0:T(8,128)(2,1)S(1)} %get-tuple-element.59.refs_11_), channel_id=1, source_target_pairs={{0,16},{4,20},{8,24},{12,28},{16,0},{20,4},{24,8},{28,12},{1,17},{... | collective-permute-start | bytes 688136 | tf_op jit(solution)/shard_map/ppermute | solution.py:130
  67.8 2.5 %collective-permute-start.10 = (f32[56,256]{1,0:T(8,128)S(1)}, f32[56,256]{1,0:T(8,128)S(1)}, u32[]{:S(2)}, u32[]{:S(2)}) collective-permute-start(f32[56,256]{1,0:T(8,128)S(1)} %pad_maximum_fusion.3), channel_id=1, source_target_pairs={{0,4},{4,0},{8,12},{12,8},{16,20},{20,16},{24,28},{28,24},{1,5},{5... | collective-permute-start | bytes 172040 | tf_op jit(solution)/shard_map/ppermute | solution.py:130
  70.3 1.5 %collective-permute-start.11 = (f32[8,256]{1,0:T(8,128)S(1)}, f32[8,256]{1,0:T(8,128)S(1)}, u32[]{:S(2)}, u32[]{:S(2)}) collective-permute-start(f32[8,256]{1,0:T(8,128)S(1)} %get-tuple-element.54.total), channel_id=1, source_target_pairs={{0,2},{1,3},{2,0},{3,1},{4,6},{5,7},{6,4},{7,5},{8,10},{9,11},{10,... | collective-permute-start | bytes 24584 | tf_op jit(solution)/shard_map/ppermute | solution.py:134
  71.8 3.0 %collective-permute-done.12.along_both = f32[8,256]{1,0:T(8,128)S(1)} collective-permute-done((f32[8,256]{1,0:T(8,128)S(1)}, f32[8,256]{1,0:T(8,128)S(1)}, u32[]{:S(2)}, u32[]{:S(2)}) %collective-permute-start.12) | collective-permute-done | bytes 8224 | tf_op jit(solution)/shard_map/ppermute | solution.py:139
  75.5 1.2 %collective-permute-start.18 = (s16[64,512]{1,0:T(8,128)(2,1)S(1)}, s16[64,512]{1,0:T(8,128)(2,1)S(1)}, u32[]{:S(2)}, u32[]{:S(2)}) collective-permute-start(s16[64,512]{1,0:T(8,128)(2,1)S(1)} %get-tuple-element.60.refs_13_), channel_id=1, source_target_pairs={{0,16},{4,20},{8,24},{12,28},{16,0},{20,4},{24,8},{28,12},{1,17},{... | collective-permute-start | bytes 196616 | tf_op jit(solution)/shard_map/ppermute | solution.py:130
  76.6 1.2 %collective-permute-done.13 = f32[8,256]{1,0:T(8,128)S(1)} collective-permute-done((f32[8,256]{1,0:T(8,128)S(1)}, f32[8,256]{1,0:T(8,128)S(1)}, u32[]{:S(2)}, u32[]{:S(2)}) %collective-permute-start.13) | collective-permute-done | bytes 8224 | tf_op jit(solution)/shard_map/ppermute | solution.py:134
  77.8 2.5 %collective-permute-start.16 = (f32[8,256]{1,0:T(8,128)S(1)}, f32[8,256]{1,0:T(8,128)S(1)}, u32[]{:S(2)}, u32[]{:S(2)}) collective-permute-start(f32[8,256]{1,0:T(8,128)S(1)} %add.5.refs_1_), channel_id=1, source_target_pairs={{0,24},{4,28},{8,16},{12,20},{16,8},{20,12},{24,0},{28,4},{1,25},{... | collective-permute-start | bytes 24584 | tf_op jit(solution)/shard_map/ppermute | solution.py:130
  80.3 1.9 %collective-permute-start.14 = (f32[8,256]{1,0:T(8,128)S(1)}, f32[8,256]{1,0:T(8,128)S(1)}, u32[]{:S(2)}, u32[]{:S(2)}) collective-permute-start(f32[8,256]{1,0:T(8,128)S(1)} %add.5.refs_1_), channel_id=1, source_target_pairs={{0,8},{4,12},{8,0},{12,4},{16,24},{20,28},{24,16},{28,20},{1,9},{5... | collective-permute-start | bytes 24584 | tf_op jit(solution)/shard_map/ppermute | solution.py:130
  82.2 1.1 collective-permute-done.16.refs_4_
  83.3 1.6 %collective-permute-done.15.refs_3_ = f32[8,256]{1,0:T(8,128)S(1)} collective-permute-done((f32[8,256]{1,0:T(8,128)S(1)}, f32[8,256]{1,0:T(8,128)S(1)}, u32[]{:S(2)}, u32[]{:S(2)}) %collective-permute-start.15) | collective-permute-done | bytes 8224 | tf_op jit(solution)/shard_map/ppermute | solution.py:130
  84.8 2.2 %update.1 = (f32[240,512]{1,0:T(8,128)}, f32[240,512]{1,0:T(8,128)}, bf16[2,240,256]{2,1,0:T(8,128)(2,1)S(1)}, bf16[2,240,256]{2,1,0:T(8,128)(2,1)S(1)}) custom-call(s32[5]{0:T(128)S(1)} %copy-done.7, f32[8,256]{1,0:T(8,128)S(1)} %add.5.refs_1_, f32[8,256]{1,0:T(8,128)S(1)} %collective-permute-done.14.refs_2_, f32[8,256]{1,0:T(8,128)S(1)} %collective-permute-done.15.refs_3_, ...), custom_call_target="tpu_custom_call" | custom-call | tf_op jit(solution)/shard_map/update/pallas_call | solution.py:706
  88.0 1.9 %collective-permute-start.21 = (bf16[2,240,256]{2,1,0:T(8,128)(2,1)S(1)}, bf16[2,240,256]{2,1,0:T(8,128)(2,1)S(1)}, u32[]{:S(2)}, u32[]{:S(2)}) collective-permute-start(bf16[2,240,256]{2,1,0:T(8,128)(2,1)S(1)} %get-tuple-element.64.refs_4_), channel_id=1, source_target_pairs={{0,4},{4,0},{8,12},{12,8},{16,20},{20,16},{24,28},{28,24},{1,5},{5... | collective-permute-start | bytes 737288 | tf_op jit(solution)/shard_map/ppermute | solution.py:130
  90.0 3.6 %collective-permute-done.19.refs_2_ = bf16[2,240,256]{2,1,0:T(8,128)(2,1)S(1)} collective-permute-done((bf16[2,240,256]{2,1,0:T(8,128)(2,1)S(1)}, bf16[2,240,256]{2,1,0:T(8,128)(2,1)S(1)}, u32[]{:S(2)}, u32[]{:S(2)}) %collective-permute-start.19) | collective-permute-done | bytes 245792 | tf_op jit(solution)/shard_map/ppermute | solution.py:130
  93.6 1.3 %collective-permute-start.20 = (bf16[4,240,256]{2,1,0:T(8,128)(2,1)S(1)}, bf16[4,240,256]{2,1,0:T(8,128)(2,1)S(1)}, u32[]{:S(2)}, u32[]{:S(2)}) collective-permute-start(bf16[4,240,256]{2,1,0:T(8,128)(2,1)S(1)} %pad_maximum_fusion), channel_id=1, source_target_pairs={{0,4},{4,0},{8,12},{12,8},{16,20},{20,16},{24,28},{28,24},{1,5},{5... | collective-permute-start | bytes 1474568 | tf_op jit(solution)/shard_map/ppermute | solution.py:130
  95.0 1.5 %collective-permute-start.22 = (bf16[4,240,256]{2,1,0:T(8,128)(2,1)S(1)}, bf16[4,240,256]{2,1,0:T(8,128)(2,1)S(1)}, u32[]{:S(2)}, u32[]{:S(2)}) collective-permute-start(bf16[4,240,256]{2,1,0:T(8,128)(2,1)S(1)} %pad_maximum_fusion.1), channel_id=1, source_target_pairs={{0,8},{4,12},{8,0},{12,4},{16,24},{20,28},{24,16},{28,20},{1,9},{5... | collective-permute-start | bytes 1474568 | tf_op jit(solution)/shard_map/ppermute | solution.py:130
  96.5 8.4 %collective-permute-done.20.refs_3_ = bf16[4,240,256]{2,1,0:T(8,128)(2,1)S(1)} collective-permute-done((bf16[4,240,256]{2,1,0:T(8,128)(2,1)S(1)}, bf16[4,240,256]{2,1,0:T(8,128)(2,1)S(1)}, u32[]{:S(2)}, u32[]{:S(2)}) %collective-permute-start.20) | collective-permute-done | bytes 491552 | tf_op jit(solution)/shard_map/ppermute | solution.py:130
  104.9 1.1 %collective-permute-done.22.refs_6_ = bf16[4,240,256]{2,1,0:T(8,128)(2,1)S(1)} collective-permute-done((bf16[4,240,256]{2,1,0:T(8,128)(2,1)S(1)}, bf16[4,240,256]{2,1,0:T(8,128)(2,1)S(1)}, u32[]{:S(2)}, u32[]{:S(2)}) %collective-permute-start.22) | collective-permute-done | bytes 491552 | tf_op jit(solution)/shard_map/ppermute | solution.py:130
  106.0 2.0 %place.1 = bf16[1920,512]{1,0:T(8,128)(2,1)} custom-call(s32[5]{0:T(128)S(1)} %copy-done.7, bf16[2,240,256]{2,1,0:T(8,128)(2,1)S(1)} %get-tuple-element.63.refs_1_, bf16[2,240,256]{2,1,0:T(8,128)(2,1)S(1)} %collective-permute-done.19.refs_2_, bf16[4,240,256]{2,1,0:T(8,128)(2,1)S(1)} %collective-permute-done.20.refs_3_, ...), custom_call_target="tpu_custom_call" | custom-call | tf_op jit(solution)/shard_map/place/pallas_call | solution.py:727
  (53 shorter events, 9.0 us)
Async XLA Ops:
  11.0 21.7 %collective-permute-start.3 = (s16[4,256,256]{2,1,0:T(8,128)(2,1)}, s16[4,256,256]{2,1,0:T(8,128)(2,1)S(1)}, u32[]{:S(2)}, u32[]{:S(2)}) collective-permute-start(s16[4,256,256]{2,1,0:T(8,128)(2,1)} %get-tuple-element.40), channel_id=1, source_target_pairs={{0,4},{4,0},{8,12},{12,8},{16,20},{20,16},{24,28},{28,24},{1,5},{5... | collective-permute-start | bytes 1572872 | tf_op jit(solution)/shard_map/ppermute | solution.py:130
  14.0 26.9 %collective-permute-start.5 = (s16[4,256,256]{2,1,0:T(8,128)(2,1)}, s16[4,256,256]{2,1,0:T(8,128)(2,1)S(1)}, u32[]{:S(2)}, u32[]{:S(2)}) collective-permute-start(s16[4,256,256]{2,1,0:T(8,128)(2,1)} %get-tuple-element.44), channel_id=1, source_target_pairs={{0,8},{4,12},{8,0},{12,4},{16,24},{20,28},{24,16},{28,20},{1,9},{5... | collective-permute-start | bytes 1572872 | tf_op jit(solution)/shard_map/ppermute | solution.py:130
  15.6 7.0 %copy-start.1 = (f32[240,512]{1,0:T(8,128)S(1)}, f32[240,512]{1,0:T(8,128)}, u32[]{:S(2)}) copy-start(f32[240,512]{1,0:T(8,128)} %refs_8_.1) | copy-start | bytes 1474564
  15.6 17.1 %copy-start.4 = (f32[4,240,256]{2,1,0:T(8,128)S(1)}, f32[4,240,256]{2,1,0:T(8,128)}, u32[]{:S(2)}) copy-start(f32[4,240,256]{2,1,0:T(8,128)} %get-tuple-element.41.refs_2_) | copy-start | bytes 2949124
  15.6 17.1 %copy-start.7 = (s32[5]{0:T(128)S(1)}, s32[5]{0:T(128)}, u32[]{:S(2)}) copy-start(s32[5]{0:T(128)} %stack.32.refs_0_.info) | copy-start | bytes 64
  19.9 21.0 %copy-start.3 = (f32[4,240,256]{2,1,0:T(8,128)S(1)}, f32[4,240,256]{2,1,0:T(8,128)}, u32[]{:S(2)}) copy-start(f32[4,240,256]{2,1,0:T(8,128)} %get-tuple-element.46.refs_2_) | copy-start | bytes 2949124
  19.9 22.5 %copy-start.2 = (bf16[64,1024]{1,0:T(8,128)(2,1)S(1)}, bf16[64,1024]{1,0:T(8,128)(2,1)}, u32[]{:S(2)}) copy-start(bf16[64,1024]{1,0:T(8,128)(2,1)} %picks.1.refs_1_) | copy-start | bytes 393220
  20.0 11.2 %collective-permute-start = (bf16[64,1024]{1,0:T(8,128)(2,1)}, bf16[64,1024]{1,0:T(8,128)(2,1)S(1)}, u32[]{:S(2)}, u32[]{:S(2)}) collective-permute-start(bf16[64,1024]{1,0:T(8,128)(2,1)} %picks.1.refs_1_), channel_id=1, source_target_pairs={{0,16},{4,20},{8,24},{12,28},{16,0},{20,4},{24,8},{28,12},{1,17},{... | collective-permute-start | bytes 393224 | tf_op jit(solution)/shard_map/ppermute | solution.py:130
  23.0 17.9 %collective-permute-start.6 = (s16[272,512]{1,0:T(8,128)(2,1)S(1)}, s16[272,512]{1,0:T(8,128)(2,1)S(1)}, u32[]{:S(2)}, u32[]{:S(2)}) collective-permute-start(s16[272,512]{1,0:T(8,128)(2,1)S(1)} %base.1.refs_9_), channel_id=1, source_target_pairs={{0,16},{4,20},{8,24},{12,28},{16,0},{20,4},{24,8},{28,12},{1,17},{... | collective-permute-start | bytes 835592 | tf_op jit(solution)/shard_map/ppermute | solution.py:130
  32.1 10.4 %collective-permute-start.1 = (bf16[2,64,1024]{2,1,0:T(8,128)(2,1)S(1)}, bf16[2,64,1024]{2,1,0:T(8,128)(2,1)S(1)}, u32[]{:S(2)}, u32[]{:S(2)}) collective-permute-start(bf16[2,64,1024]{2,1,0:T(8,128)(2,1)S(1)} %pad_maximum_fusion.2), channel_id=1, source_target_pairs={{0,4},{4,0},{8,12},{12,8},{16,20},{20,16},{24,28},{28,24},{1,5},{5... | collective-permute-start | bytes 786440 | tf_op jit(solution)/shard_map/ppermute | solution.py:130
  33.6 18.2 %copy-start.5 = (f32[1,4,128,128]{3,2,1,0:T(8,128)S(1)}, f32[1,4,128,128]{3,2,1,0:T(8,128)}, u32[]{:S(2)}) copy-start(f32[1,4,128,128]{3,2,1,0:T(8,128)} %param.14) | copy-start | bytes 786436
  33.6 18.2 %copy-start.6 = (f32[1,5,96,96]{3,2,1,0:T(8,128)S(1)}, f32[1,5,96,96]{3,2,1,0:T(8,128)}, u32[]{:S(2)}) copy-start(f32[1,5,96,96]{3,2,1,0:T(8,128)} %param.15) | copy-start | bytes 552964
  33.7 18.2 %copy-start.8 = (s32[4,4]{1,0:T(4,128)S(1)}, s32[4,4]{1,0:T(4,128)}, u32[]{:S(2)}) copy-start(s32[4,4]{1,0:T(4,128)} %refs_1_.3) | copy-start | bytes 196
  33.7 18.2 %copy-start.9 = (s32[4,5]{1,0:T(4,128)S(1)}, s32[4,5]{1,0:T(4,128)}, u32[]{:S(2)}) copy-start(s32[4,5]{1,0:T(4,128)} %refs_2_.5) | copy-start | bytes 244
  33.7 10.0 %collective-permute-start.4 = (s16[2,256,256]{2,1,0:T(8,128)(2,1)S(1)}, s16[2,256,256]{2,1,0:T(8,128)(2,1)S(1)}, u32[]{:S(2)}, u32[]{:S(2)}) collective-permute-start(s16[2,256,256]{2,1,0:T(8,128)(2,1)S(1)} %get-tuple-element.42), channel_id=1, source_target_pairs={{0,8},{4,12},{8,0},{12,4},{16,24},{20,28},{24,16},{28,20},{1,9},{5... | collective-permute-start | bytes 786440 | tf_op jit(solution)/shard_map/ppermute | solution.py:130
  41.9 6.4 %collective-permute-start.7 = (s16[2,256,256]{2,1,0:T(8,128)(2,1)S(1)}, s16[2,256,256]{2,1,0:T(8,128)(2,1)S(1)}, u32[]{:S(2)}, u32[]{:S(2)}) collective-permute-start(s16[2,256,256]{2,1,0:T(8,128)(2,1)S(1)} %get-tuple-element.47), channel_id=1, source_target_pairs={{0,4},{4,0},{8,12},{12,8},{16,20},{20,16},{24,28},{28,24},{1,5},{5... | collective-permute-start | bytes 786440 | tf_op jit(solution)/shard_map/ppermute | solution.py:130
  43.6 8.3 %collective-permute-start.2 = (s16[1136,128]{1,0:T(8,128)(2,1)S(1)}, s16[1136,128]{1,0:T(8,128)(2,1)S(1)}, u32[]{:S(2)}, u32[]{:S(2)}) collective-permute-start(s16[1136,128]{1,0:T(8,128)(2,1)S(1)} %stats.1.refs_3_), channel_id=1, source_target_pairs={{0,8},{4,12},{8,0},{12,4},{16,24},{20,28},{24,16},{28,20},{1,9},{5... | collective-permute-start | bytes 872456 | tf_op jit(solution)/shard_map/ppermute | solution.py:130
  49.2 14.1 %collective-permute-start.8 = (s16[2,256,256]{2,1,0:T(8,128)(2,1)S(1)}, s16[2,256,256]{2,1,0:T(8,128)(2,1)S(1)}, u32[]{:S(2)}, u32[]{:S(2)}) collective-permute-start(s16[2,256,256]{2,1,0:T(8,128)(2,1)S(1)} %get-tuple-element.49), channel_id=1, source_target_pairs={{0,16},{4,20},{8,24},{12,28},{16,0},{20,4},{24,8},{28,12},{1,17},{... | collective-permute-start | bytes 786440 | tf_op jit(solution)/shard_map/ppermute | solution.py:130
  56.1 0.7 collective-permute-start.9
  65.2 19.7 %collective-permute-start.17 = (s16[224,512]{1,0:T(8,128)(2,1)S(1)}, s16[224,512]{1,0:T(8,128)(2,1)S(1)}, u32[]{:S(2)}, u32[]{:S(2)}) collective-permute-start(s16[224,512]{1,0:T(8,128)(2,1)S(1)} %get-tuple-element.59.refs_11_), channel_id=1, source_target_pairs={{0,16},{4,20},{8,24},{12,28},{16,0},{20,4},{24,8},{28,12},{1,17},{... | collective-permute-start | bytes 688136 | tf_op jit(solution)/shard_map/ppermute | solution.py:130
  67.8 7.1 %collective-permute-start.10 = (f32[56,256]{1,0:T(8,128)S(1)}, f32[56,256]{1,0:T(8,128)S(1)}, u32[]{:S(2)}, u32[]{:S(2)}) collective-permute-start(f32[56,256]{1,0:T(8,128)S(1)} %pad_maximum_fusion.3), channel_id=1, source_target_pairs={{0,4},{4,0},{8,12},{12,8},{16,20},{20,16},{24,28},{28,24},{1,5},{5... | collective-permute-start | bytes 172040 | tf_op jit(solution)/shard_map/ppermute | solution.py:130
  70.3 4.5 %collective-permute-start.12 = (f32[8,256]{1,0:T(8,128)S(1)}, f32[8,256]{1,0:T(8,128)S(1)}, u32[]{:S(2)}, u32[]{:S(2)}) collective-permute-start(f32[8,256]{1,0:T(8,128)S(1)} %get-tuple-element.54.total), channel_id=1, source_target_pairs={{0,6},{1,7},{2,4},{3,5},{4,2},{5,3},{6,0},{7,1},{8,14},{9,15},{10,... | collective-permute-start | bytes 24584 | tf_op jit(solution)/shard_map/ppermute | solution.py:139
  70.3 4.5 %collective-permute-start.11 = (f32[8,256]{1,0:T(8,128)S(1)}, f32[8,256]{1,0:T(8,128)S(1)}, u32[]{:S(2)}, u32[]{:S(2)}) collective-permute-start(f32[8,256]{1,0:T(8,128)S(1)} %get-tuple-element.54.total), channel_id=1, source_target_pairs={{0,2},{1,3},{2,0},{3,1},{4,6},{5,7},{6,4},{7,5},{8,10},{9,11},{10,... | collective-permute-start | bytes 24584 | tf_op jit(solution)/shard_map/ppermute | solution.py:134
  75.5 9.4 %collective-permute-start.18 = (s16[64,512]{1,0:T(8,128)(2,1)S(1)}, s16[64,512]{1,0:T(8,128)(2,1)S(1)}, u32[]{:S(2)}, u32[]{:S(2)}) collective-permute-start(s16[64,512]{1,0:T(8,128)(2,1)S(1)} %get-tuple-element.60.refs_13_), channel_id=1, source_target_pairs={{0,16},{4,20},{8,24},{12,28},{16,0},{20,4},{24,8},{28,12},{1,17},{... | collective-permute-start | bytes 196616 | tf_op jit(solution)/shard_map/ppermute | solution.py:130
  76.6 1.2 %collective-permute-start.13 = (f32[8,256]{1,0:T(8,128)S(1)}, f32[8,256]{1,0:T(8,128)S(1)}, u32[]{:S(2)}, u32[]{:S(2)}) collective-permute-start(f32[8,256]{1,0:T(8,128)S(1)} %get-tuple-element.55), channel_id=1, source_target_pairs={{0,1},{1,0},{2,3},{3,2},{4,5},{5,4},{6,7},{7,6},{8,9},{9,8},{10,11... | collective-permute-start | bytes 24584 | tf_op jit(solution)/shard_map/ppermute | solution.py:134
  77.8 5.4 %collective-permute-start.16 = (f32[8,256]{1,0:T(8,128)S(1)}, f32[8,256]{1,0:T(8,128)S(1)}, u32[]{:S(2)}, u32[]{:S(2)}) collective-permute-start(f32[8,256]{1,0:T(8,128)S(1)} %add.5.refs_1_), channel_id=1, source_target_pairs={{0,24},{4,28},{8,16},{12,20},{16,8},{20,12},{24,0},{28,4},{1,25},{... | collective-permute-start | bytes 24584 | tf_op jit(solution)/shard_map/ppermute | solution.py:130
  80.3 4.5 %collective-permute-start.15 = (f32[8,256]{1,0:T(8,128)S(1)}, f32[8,256]{1,0:T(8,128)S(1)}, u32[]{:S(2)}, u32[]{:S(2)}) collective-permute-start(f32[8,256]{1,0:T(8,128)S(1)} %add.5.refs_1_), channel_id=1, source_target_pairs={{0,16},{4,20},{8,24},{12,28},{16,0},{20,4},{24,8},{28,12},{1,17},{... | collective-permute-start | bytes 24584 | tf_op jit(solution)/shard_map/ppermute | solution.py:130
  80.3 4.5 %collective-permute-start.14 = (f32[8,256]{1,0:T(8,128)S(1)}, f32[8,256]{1,0:T(8,128)S(1)}, u32[]{:S(2)}, u32[]{:S(2)}) collective-permute-start(f32[8,256]{1,0:T(8,128)S(1)} %add.5.refs_1_), channel_id=1, source_target_pairs={{0,8},{4,12},{8,0},{12,4},{16,24},{20,28},{24,16},{28,20},{1,9},{5... | collective-permute-start | bytes 24584 | tf_op jit(solution)/shard_map/ppermute | solution.py:130
  87.0 6.6 %collective-permute-start.19 = (bf16[2,240,256]{2,1,0:T(8,128)(2,1)S(1)}, bf16[2,240,256]{2,1,0:T(8,128)(2,1)S(1)}, u32[]{:S(2)}, u32[]{:S(2)}) collective-permute-start(bf16[2,240,256]{2,1,0:T(8,128)(2,1)S(1)} %get-tuple-element.63.refs_1_), channel_id=1, source_target_pairs={{0,8},{4,12},{8,0},{12,4},{16,24},{20,28},{24,16},{28,20},{1,9},{5... | collective-permute-start | bytes 737288 | tf_op jit(solution)/shard_map/ppermute | solution.py:130
  88.0 6.9 %collective-permute-start.21 = (bf16[2,240,256]{2,1,0:T(8,128)(2,1)S(1)}, bf16[2,240,256]{2,1,0:T(8,128)(2,1)S(1)}, u32[]{:S(2)}, u32[]{:S(2)}) collective-permute-start(bf16[2,240,256]{2,1,0:T(8,128)(2,1)S(1)} %get-tuple-element.64.refs_4_), channel_id=1, source_target_pairs={{0,4},{4,0},{8,12},{12,8},{16,20},{20,16},{24,28},{28,24},{1,5},{5... | collective-permute-start | bytes 737288 | tf_op jit(solution)/shard_map/ppermute | solution.py:130
  93.6 11.2 %collective-permute-start.20 = (bf16[4,240,256]{2,1,0:T(8,128)(2,1)S(1)}, bf16[4,240,256]{2,1,0:T(8,128)(2,1)S(1)}, u32[]{:S(2)}, u32[]{:S(2)}) collective-permute-start(bf16[4,240,256]{2,1,0:T(8,128)(2,1)S(1)} %pad_maximum_fusion), channel_id=1, source_target_pairs={{0,4},{4,0},{8,12},{12,8},{16,20},{20,16},{24,28},{28,24},{1,5},{5... | collective-permute-start | bytes 1474568 | tf_op jit(solution)/shard_map/ppermute | solution.py:130
  95.0 11.0 %collective-permute-start.22 = (bf16[4,240,256]{2,1,0:T(8,128)(2,1)S(1)}, bf16[4,240,256]{2,1,0:T(8,128)(2,1)S(1)}, u32[]{:S(2)}, u32[]{:S(2)}) collective-permute-start(bf16[4,240,256]{2,1,0:T(8,128)(2,1)S(1)} %pad_maximum_fusion.1), channel_id=1, source_target_pairs={{0,8},{4,12},{8,0},{12,4},{16,24},{20,28},{24,16},{28,20},{1,9},{5... | collective-permute-start | bytes 1474568 | tf_op jit(solution)/shard_map/ppermute | solution.py:130
  (1 other events, 7.0 us)

commit v7 on v6

--- a/solution.py
+++ b/solution.py
@@ -218,9 +218,63 @@
     return rows + -(-(rows // FINE) // (2 * FINE)) * 2 * FINE
 
 
+def fold(rows):
+    half = rows.shape[0] // 2
+    return jnp.concatenate([rows[:half], rows[half:]], axis=1)
+
+
+def fold(rows):
+    half = rows.shape[0] // 2
+    return jnp.concatenate([rows[:half], rows[half:]], axis=1)
+
+
 def base_kernel(momentum, weight, packed):
     kept = momentum_rate * momentum[...] + decay_rate * weight[...]
     encode_fine(weight[...] - learn_rate * kept, packed)
+
+
+def shared_rows(side, head, mid):
+    return slice(head * (1 - side), head * (1 - side) + mid)
+
+
+def kept_columns(value, side):
+    quarter = value.shape[1] // 4
+    blocks = [value[:, (2 * p + side) * quarter : (2 * p + side + 1) * quarter] for p in (0, 1)]
+    return jnp.concatenate(blocks, axis=1)
+
+
+def side_kernel(head, mid, info, own, far, give):
+    rows = head + mid
+    for x in range(2):
+
+        @pl.when(info[1] == x)
+        def _():
+            span = shared_rows(x, head, mid)
+            first = span.start // FINE
+            for place, packed in enumerate((own, far)):
+                values = packed[:rows, :].astype(jnp.int32)[span]
+                powers = packed[rows:, :].astype(jnp.int32)[first : first + mid // FINE]
+                missing = jnp.zeros((2 * FINE - powers.shape[0], powers.shape[1]), jnp.int32)
+                all_rows = jnp.concatenate([values, powers, missing], axis=0)
+                give[place] = kept_columns(all_rows, 1 - x).astype(jnp.int16)
+
+
+def pack_kernel(head, mid, info, own, far, got, units):
+    for x in range(2):
+
+        @pl.when(info[1] == x)
+        def _():
+            for place, packed in enumerate((own, far)):
+                values = decode_fine(packed, head + mid)
+                shared = kept_columns(values[shared_rows(x, head, mid)], x)
+                other = decode_fine(got.at[place], mid)
+                both = (shared, other) if x == 0 else (other, shared)
+                quarter = shared.shape[1] // 2
+                pairs = []
+                for piece in range(2):
+                    pairs += [each[:, piece * quarter : (piece + 1) * quarter] for each in both]
+                units[place, :head, :] = values[mid * x : mid * x + head]
+                units[place, head:, :] = jnp.concatenate(pairs, axis=1)
 
 
 def parts_of(value):
@@ -481,13 +535,41 @@
         squares += values * values
         mid[:, piece * width_a : (piece + 1) * width_a] = values
     total[...] = jnp.full(total.shape, jnp.sum(squares), f32)
-    encode_fine(top[...], coded)
-
-
-def middle_kernel(info, middle, got, total, along_y, along_both, rest, packed, sums):
-    mid, cols = rest.shape
+    width = mid.shape[1] // 2
+    folded = [fold(mid[:, :width]), fold(mid[:, width:])]
+    unit = jnp.concatenate([top[...], jnp.concatenate(folded, axis=1)], axis=0)
+    encode_fine(unit, coded)
+
+
+def round_kernel(
+    entries, total, along_l, along_h, along_both, base, scaled, scaled_far, factor,
+    rounded_a, rounded_b
+):
+    rows, half = rounded_a.shape[1:]
+    sums = [each[0:1, :] for each in (total, along_l, along_h, along_both)]
+    mean_sq = ((sums[0] + sums[1]) + (sums[2] + sums[3])) / entries
+    norm = 1.0 / jnp.sqrt(mean_sq + epsilon_sq)
+    norm = jnp.concatenate([norm, norm], axis=1)
+    factor[...] = jnp.broadcast_to(norm, factor.shape)
+    for place, moving in enumerate((scaled, scaled_far)):
+        fresh = base[place] - (learn_rate * norm) * decode_fine(moving, rows)
+        rounded_a[place] = fresh[:, :half].astype(bf16)
+        rounded_b[place] = fresh[:, half:].astype(bf16)
+
+
+def update_kernel(info, factor, top, middle, got, momentum, weight, momentum_new, weight_new):
+    rows, cols = momentum.shape
     quarter = cols // 4
-    sums[...] = (total[...] + got[mid:, :]) + (along_y[...] + along_both[...])
+    head = top.shape[0]
+    mid = rows - head
+    norm = factor[0:1, :]
+
+    def step(place, precon):
+        span = slice(place, place + precon.shape[0])
+        moved = momentum_rate * momentum[span, :] + precon * norm + decay_rate * weight[span, :]
+        momentum_new[span, :] = moved
+        weight_new[span, :] = weight[span, :] - learn_rate * moved
+
     for x in range(2):
 
         @pl.when(info[1] == x)
@@ -498,56 +580,31 @@
                 columns = slice(piece * quarter, (piece + 1) * quarter)
                 both = [own[:, columns], got[:mid, columns]]
                 pairs += both if x == 0 else both[::-1]
-            rest[...] = jnp.concatenate(pairs, axis=1)
-
-    encode_fine(rest[...], packed)
-
-
-def update_kernel(
-    entries, info, total, along_l, along_h, along_both, top, rest, momentum, weight, base, base_far,
-    scaled, scaled_far, small, small_far, momentum_new, weight_new, rounded_a, rounded_b
-):
-    rows, cols = momentum.shape
-    half = cols // 2
-    head, mid = top.shape[0], rest.shape[0]
-    sums = [each[0:1, :] for each in (total, along_l, along_h, along_both)]
-    mean_sq = ((sums[0] + sums[1]) + (sums[2] + sums[3])) / entries
-    factor = 1.0 / jnp.sqrt(mean_sq + epsilon_sq)
-    factor = jnp.concatenate([factor, factor], axis=1)
-    fixed = [decode_fine(base, rows), decode_fine(base_far, rows)]
-    moving = [
-        (decode_fine(scaled, head), decode_fine(small, mid)),
-        (decode_fine(scaled_far, head), decode_fine(small_far, mid)),
-    ]
-
-    def step(order):
-        precon = jnp.concatenate([(top, rest)[which][...] for which in order], axis=0)
-        moved = momentum_rate * momentum[...] + precon * factor + decay_rate * weight[...]
-        momentum_new[...] = moved
-        weight_new[...] = weight[...] - learn_rate * moved
-        for place in range(2):
-            change = jnp.concatenate([moving[place][which] for which in order], axis=0)
-            fresh = fixed[place] - (learn_rate * factor) * change
-            rounded_a[place] = fresh[:, :half].astype(bf16)
-            rounded_b[place] = fresh[:, half:].astype(bf16)
-
-    for x, order in enumerate(((0, 1), (1, 0))):
-
-        @pl.when(info[1] == x)
-        def _():
-            step(order)
-
-
-def place_kernel(rows, info, *refs):
+            step(head * (1 - x), jnp.concatenate(pairs, axis=1))
+            step(mid * x, top[...])
+
+
+def place_kernel(head, info, *refs):
     parts, out = refs[:6], refs[6]
     shard = info[3]
-    half = out.shape[1] // 2
+    rows, half = parts[0].shape[1:]
+    mid = rows - head
+    quarter = half // 2
     codes = ((0, 4), (2, 6), (1, 5, 3, 7), (0, 4), (1, 5), (2, 6, 3, 7))
     for index, (part, units) in enumerate(zip(parts, codes)):
         first = half * (index // 3)
         for place, code in enumerate(units):
-            start = pl.multiple_of((shard ^ code) * rows, 16)
-            out[pl.ds(start, rows), first : first + half] = part[place]
+            unit = shard ^ code
+            side = unit & 1
+            start = (unit >> 1) * (2 * rows)
+            own = pl.multiple_of(start + side * (head + 2 * mid), 16)
+            out[pl.ds(own, head), first : first + half] = part[place, :head, :]
+            columns = pl.ds(pl.multiple_of(first + side * quarter, 128), quarter)
+            for which in range(2):
+                shared = pl.multiple_of(start + head + which * mid, 16)
+                out[pl.ds(shared, mid), columns] = part[
+                    place, head:, which * quarter : (which + 1) * quarter
+                ]
 
 
 def fast(acts, out_grad, sample_rows, own_a, own_g, a_state, g_state, momentum, weight):
@@ -601,7 +658,7 @@
             pltpu.VMEM((tokens, 640), bf16),
             pltpu.SemaphoreType.DMA((8,)),
         ],
-        compiler_params=params(60),
+        compiler_params=params(50),
         name="picks",
     )(info, sample_rows.reshape(1, -1), acts, out_grad)
     one = swap(picks, 4)
@@ -618,7 +675,11 @@
     two = swap(jnp.stack([picks, one]), 1)
 
     send_a, keep_a = add_step(info, 2, True, got_a, keep_a)
+    send_b, keep_b = add_step(info, 1, True, got_b, keep_b)
+    send_a, send_b = lax.optimization_barrier((send_a, send_b))
     got_a = swap(send_a, 2)
+    got_b = swap(send_b, 1)
+    two, base_far = lax.optimization_barrier((two, base_far))
     blocks, packed_rows = block_places(count_a, width_a, count_g, width_g)
     packed = pl.pallas_call(
         lambda *refs: stats_kernel(blocks, *refs),
@@ -630,9 +691,6 @@
         name="stats",
     )(info, picks, one, two)
     got_packed = swap(packed, 2)
-    got_b, base_far = lax.optimization_barrier((got_b, base_far))
-    send_b, keep_b = add_step(info, 1, True, got_b, keep_b)
-    got_b = swap(send_b, 1)
 
     send, keep = pl.pallas_call(
         last_add_kernel,
@@ -646,6 +704,24 @@
         name="last_add",
     )(info, got_a, keep_a, got_b, keep_b)
     got = swap(send, 4)
+
+    give = pl.pallas_call(
+        lambda *refs: side_kernel(head, mid, *refs),
+        in_specs=[smem] + [vmem] * 2,
+        out_specs=vmem,
+        out_shape=shaped((2, fine_rows(mid), half), jnp.int16),
+        compiler_params=params(16),
+        name="sides",
+    )(info, base, base_far)
+    base_units = pl.pallas_call(
+        lambda *refs: pack_kernel(head, mid, *refs),
+        in_specs=[smem] + [vmem] * 3,
+        out_specs=vmem,
+        out_shape=shaped((2, rows, cols), f32),
+        compiler_params=params(16),
+        name="pack",
+    )(info, base, base_far, swap(give, 1))
+    got_packed, base_units = lax.optimization_barrier((got_packed, base_units))
 
     new_a, new_g, inv_a, needed = pl.pallas_call(
         lambda *refs: factor_kernel(share, blocks, *refs),
@@ -677,7 +753,7 @@
             shaped((head, cols), f32),
             shaped((width_g, half), f32),
             shaped((8, half), f32),
-            shaped((fine_rows(head), cols), jnp.int16),
+            shaped((fine_rows(rows), cols), jnp.int16),
         ],
         compiler_params=params(24),
         name="precon",
@@ -688,44 +764,39 @@
     got = swap(jnp.concatenate([give, total], axis=0), 1)
     along_y = swap_t(total, 2)
     along_both = swap_both(total, 1, 2)
-    rest, small, total = pl.pallas_call(
-        middle_kernel,
-        in_specs=[smem] + [vmem] * 5,
+    total = (total + got[mid:]) + (along_y + along_both)
+    total = total + swap_t(total, 1)
+    others = [swap(total, bits) for bits in (2, 4, 6)]
+    factor, rounded_a, rounded_b = pl.pallas_call(
+        lambda *refs: round_kernel(rows * 8 * cols * 4, *refs),
+        in_specs=[vmem] * 7,
         out_specs=[vmem] * 3,
         out_shape=[
-            shaped((mid, cols), f32),
-            shaped((fine_rows(mid), cols), jnp.int16),
-            shaped((8, half), f32),
-        ],
-        compiler_params=params(16),
-        name="middle",
-    )(info, middle, got, total, along_y, along_both)
-    small_far = swap(small, 4)
-    total = total + swap_t(total, 1)
-    others = [swap(total, bits) for bits in (2, 4, 6)]
-    momentum_new, weight_new, rounded_a, rounded_b = pl.pallas_call(
-        lambda *refs: update_kernel(rows * 8 * cols * 4, *refs),
-        in_specs=[smem] + [vmem] * 14,
-        out_specs=[vmem] * 4,
-        out_shape=[
-            shaped((rows, cols), f32),
-            shaped((rows, cols), f32),
+            shaped((8, cols), f32),
             shaped((2, rows, half), bf16),
             shaped((2, rows, half), bf16),
         ],
         compiler_params=params(24),
-        name="update",
-    )(
-        info, total, *others, top, rest, momentum, weight, base, base_far, scaled, scaled_far,
-        small, small_far,
-    )
+        name="round",
+    )(total, *others, base_units, scaled, scaled_far)
 
     along_l = swap(rounded_a, 2)
     along_x = swap(rounded_b, 1)
+    momentum_new, weight_new = pl.pallas_call(
+        update_kernel,
+        in_specs=[smem] + [vmem] * 6,
+        out_specs=[vmem] * 2,
+        out_shape=[shaped((rows, cols), f32)] * 2,
+        compiler_params=params(16),
+        name="update",
+    )(info, factor, top, middle, got, momentum, weight)
+    along_l, along_x, momentum_new, weight_new = lax.optimization_barrier(
+        (along_l, along_x, momentum_new, weight_new)
+    )
     rest_a = swap(jnp.concatenate([rounded_a, along_l]), 1)
     rest_b = swap(jnp.concatenate([rounded_b, along_x]), 2)
     gathered = pl.pallas_call(
-        lambda *refs: place_kernel(rows, *refs),
+        lambda *refs: place_kernel(head, *refs),
         in_specs=[smem] + [vmem] * 6,
         out_specs=vmem,
         out_shape=shaped((rows * 8, cols), bf16),

time: 108 us -> 107 us (level)
  starting transfers between devices: 31.1 us -> 38.8 us
  waiting for transfers between devices: 45.2 us -> 37.8 us
    ppermute x19, waiting for transfers between devices: 41 us -> 35 us  [swap(): return lax.ppermute(value, 'shard', [(i, i ^ bit) for i in range(8)])]
    ppermute x19, starting transfers between devices: 28.9 us -> 34.5 us  [swap(): return lax.ppermute(value, 'shard', [(i, i ^ bit) for i in range(8)])]
    ppermute x1, starting transfers between devices: 0.01 us -> 2.87 us  [swap_both(): return lax.ppermute(value, ('shard', 'tensor'), route)]
    ppermute x1, waiting for transfers between devices: 3.01 us -> 1.44 us  [swap_both(): return lax.ppermute(value, ('shard', 'tensor'), route)]
    pallas_call x1, Pallas kernels: 4.3 us -> 3.16 us  [fast(): pl.pallas_call(lambda *refs: picks_kernel(group_cols, *refs), in_specs=[s...]
    pallas_call x3 -> x5, Pallas kernels: 4.76 us -> 5.16 us  [the longest x1 2.03 us: fast(): pl.pallas_call(lambda *refs: place_kernel(head, *refs), in_specs=[smem] +...]
  transfers between devices with their start and end apart: 23 -> 23, of which waited for: 12 -> 16; matrix products, arithmetic and copies ran while one was open for 1% -> 0% of each run, Pallas kernels for 12% -> 14%
where the time goes in v7:
time: 107 us
  starting transfers between devices  38.8 us (36%)
  waiting for transfers between devices  37.8 us (35%)
  Pallas kernels  28.5 us (27%)
    ppermute x19, waiting for transfers between devices, swap(): return lax.ppermute(value, 'shard', [(i, i ^ bit) for i in range(8)])  35 us
    ppermute x19, starting transfers between devices, swap(): return lax.ppermute(value, 'shard', [(i, i ^ bit) for i in range(8)])  34.5 us
    pallas_call x1, Pallas kernels, fast(): pl.pallas_call(lambda *refs: partial_kernel(group_cols, width_g, *refs),...  9.85 us
    pallas_call x1, Pallas kernels, fast(): pl.pallas_call(lambda *refs: factor_kernel(share, blocks, *refs), in_spec...  4.24 us
    pallas_call x1, Pallas kernels, fast(): pl.pallas_call(lambda *refs: picks_kernel(group_cols, *refs), in_specs=[s...  3.16 us
    ppermute x1, starting transfers between devices, swap_both(): return lax.ppermute(value, ('shard', 'tensor'), route)  2.87 us
  transfers between devices with their start and end apart: 23, of which 16 were waited for; matrix products, arithmetic and copies ran while one was open for 0% of the time, Pallas kernels for 14%

profile of v7, /device:TPU:0, one launch (start us, length us, event | category | flops | bytes accessed | tf_op | source)
XLA Modules:
  0.0 106.8 jit_solution(8253096652640057361)
XLA Ops:
  1.3 9.8 %partial.1 = (s16[4,256,256]{2,1,0:T(8,128)(2,1)}, f32[4,240,256]{2,1,0:T(8,128)}, s16[4,256,256]{2,1,0:T(8,128)(2,1)}, f32[4,240,256]{2,1,0:T(8,128)}) custom-call(s32[5]{0:T(128)} %stack.32.refs_0_.info, bf16[2048,1920]{1,0:T(8,128)(2,1)} %refs_3_.1, bf16[2048,512]{1,0:T(8,128)(2,1)} %refs_2_.4), custom_call_target="tpu_custom_call" | custom-call | tf_op jit(solution)/shard_map/partial/pallas_call | solution.py:628
  11.2 3.0 %collective-permute-start.5 = (s16[4,256,256]{2,1,0:T(8,128)(2,1)}, s16[4,256,256]{2,1,0:T(8,128)(2,1)S(1)}, u32[]{:S(2)}, u32[]{:S(2)}) collective-permute-start(s16[4,256,256]{2,1,0:T(8,128)(2,1)} %get-tuple-element.49), channel_id=1, source_target_pairs={{0,4},{4,0},{8,12},{12,8},{16,20},{20,16},{24,28},{28,24},{1,5},{5... | collective-permute-start | bytes 1572872 | tf_op jit(solution)/shard_map/ppermute | solution.py:130
  14.2 1.6 %collective-permute-start.6 = (s16[4,256,256]{2,1,0:T(8,128)(2,1)}, s16[4,256,256]{2,1,0:T(8,128)(2,1)S(1)}, u32[]{:S(2)}, u32[]{:S(2)}) collective-permute-start(s16[4,256,256]{2,1,0:T(8,128)(2,1)} %get-tuple-element.52), channel_id=1, source_target_pairs={{0,8},{4,12},{8,0},{12,4},{16,24},{20,28},{24,16},{28,20},{1,9},{5... | collective-permute-start | bytes 1572872 | tf_op jit(solution)/shard_map/ppermute | solution.py:130
  15.8 3.2 %picks.1.refs_1_ = bf16[64,1024]{1,0:T(8,128)(2,1)S(1)} custom-call(s32[5]{0:T(128)S(1)} %copy-done.7, s32[1,64]{1,0:T(1,128)S(1)} %bitcast.16, bf16[2048,512]{1,0:T(8,128)(2,1)S(1)} %copy-done, bf16[2048,1920]{1,0:T(8,128)(2,1)} %refs_3_.1), custom_call_target="tpu_custom_call" | custom-call | tf_op jit(solution)/shard_map/picks/pallas_call | solution.py:651
  19.0 2.7 %collective-permute-start = (bf16[64,1024]{1,0:T(8,128)(2,1)S(1)}, bf16[64,1024]{1,0:T(8,128)(2,1)S(1)}, u32[]{:S(2)}, u32[]{:S(2)}) collective-permute-start(bf16[64,1024]{1,0:T(8,128)(2,1)S(1)} %picks.1.refs_1_), channel_id=1, source_target_pairs={{0,16},{4,20},{8,24},{12,28},{16,0},{20,4},{24,8},{28,12},{1,17},{... | collective-permute-start | bytes 393224 | tf_op jit(solution)/shard_map/ppermute | solution.py:130
  22.4 8.8 %collective-permute-done.refs_2_ = bf16[64,1024]{1,0:T(8,128)(2,1)S(1)} collective-permute-done((bf16[64,1024]{1,0:T(8,128)(2,1)S(1)}, bf16[64,1024]{1,0:T(8,128)(2,1)S(1)}, u32[]{:S(2)}, u32[]{:S(2)}) %collective-permute-start) | collective-permute-done | bytes 131104 | tf_op jit(solution)/shard_map/ppermute | solution.py:130
  32.7 2.8 %collective-permute-done.6.refs_1_ = s16[4,256,256]{2,1,0:T(8,128)(2,1)S(1)} collective-permute-done((s16[4,256,256]{2,1,0:T(8,128)(2,1)}, s16[4,256,256]{2,1,0:T(8,128)(2,1)S(1)}, u32[]{:S(2)}, u32[]{:S(2)}) %collective-permute-start.6) | collective-permute-done | bytes 524320 | tf_op jit(solution)/shard_map/ppermute | solution.py:130
  37.4 1.5 %collective-permute-start.8 = (s16[2,256,256]{2,1,0:T(8,128)(2,1)S(1)}, s16[2,256,256]{2,1,0:T(8,128)(2,1)S(1)}, u32[]{:S(2)}, u32[]{:S(2)}) collective-permute-start(s16[2,256,256]{2,1,0:T(8,128)(2,1)S(1)} %get-tuple-element.57), channel_id=1, source_target_pairs={{0,4},{4,0},{8,12},{12,8},{16,20},{20,16},{24,28},{28,24},{1,5},{5... | collective-permute-start | bytes 786440 | tf_op jit(solution)/shard_map/ppermute | solution.py:130
  39.8 1.1 %stats.1.refs_3_ = s16[1136,128]{1,0:T(8,128)(2,1)S(1)} custom-call(s32[5]{0:T(128)S(1)} %copy-done.7, bf16[64,1024]{1,0:T(8,128)(2,1)S(1)} %picks.1.refs_1_, bf16[64,1024]{1,0:T(8,128)(2,1)S(1)} %collective-permute-done.refs_2_, bf16[2,64,1024]{2,1,0:T(8,128)(2,1)S(1)} %collective-permute-done.1.refs_3_), custom_call_target="tpu_custom_call" | custom-call | tf_op jit(solution)/shard_map/stats/pallas_call | solution.py:684
  40.9 3.1 %collective-permute-start.3 = (s16[1136,128]{1,0:T(8,128)(2,1)S(1)}, s16[1136,128]{1,0:T(8,128)(2,1)S(1)}, u32[]{:S(2)}, u32[]{:S(2)}) collective-permute-start(s16[1136,128]{1,0:T(8,128)(2,1)S(1)} %stats.1.refs_3_), channel_id=1, source_target_pairs={{0,8},{4,12},{8,0},{12,4},{16,24},{20,28},{24,16},{28,20},{1,9},{5... | collective-permute-start | bytes 872456 | tf_op jit(solution)/shard_map/ppermute | solution.py:130
  44.0 1.9 %collective-permute-done.7.got_a = s16[2,256,256]{2,1,0:T(8,128)(2,1)S(1)} collective-permute-done((s16[2,256,256]{2,1,0:T(8,128)(2,1)S(1)}, s16[2,256,256]{2,1,0:T(8,128)(2,1)S(1)}, u32[]{:S(2)}, u32[]{:S(2)}) %collective-permute-start.7) | collective-permute-done | bytes 262176 | tf_op jit(solution)/shard_map/ppermute | solution.py:130
  46.8 1.0 collective-permute-start.9
  48.9 3.8 %collective-permute-done.4.refs_3_ = s16[2,64,256]{2,1,0:T(8,128)(2,1)S(1)} collective-permute-done((s16[2,64,256]{2,1,0:T(8,128)(2,1)S(1)}, s16[2,64,256]{2,1,0:T(8,128)(2,1)S(1)}, u32[]{:S(2)}, u32[]{:S(2)}) %collective-permute-start.4) | collective-permute-done | bytes 65568 | tf_op jit(solution)/shard_map/ppermute | solution.py:130
  53.7 4.2 %factors.1 = (f32[4,128,128]{2,1,0:T(8,128)}, f32[5,96,96]{2,1,0:T(8,128)}, f32[4,128,128]{2,1,0:T(8,128)S(1)}, s16[3,112,96]{2,1,0:T(8,128)(2,1)S(1)}) custom-call(s32[5]{0:T(128)S(1)} %copy-done.7, s32[4,4]{1,0:T(4,128)S(1)} %copy-done.8, s32[4,5]{1,0:T(4,128)S(1)} %copy-done.9, s16[1136,128]{1,0:T(8,128)(2,1)S(1)} %stats.1.refs_3_, ...), custom_call_target="tpu_custom_call" | custom-call | tf_op jit(solution)/shard_map/factors/pallas_call | solution.py:726
  58.9 1.8 %precon.1 = (f32[192,512]{1,0:T(8,128)S(1)}, f32[96,256]{1,0:T(8,128)S(1)}, f32[8,256]{1,0:T(8,128)S(1)}, s16[272,512]{1,0:T(8,128)(2,1)S(1)}) custom-call(s32[5]{0:T(128)S(1)} %copy-done.7, s16[2,256,256]{2,1,0:T(8,128)(2,1)S(1)} %collective-permute-done.9.got, f32[2,240,256]{2,1,0:T(8,128)S(1)} %get-tuple-element.60.held, ...), custom_call_target="tpu_custom_call" | custom-call | tf_op jit(solution)/shard_map/precon/pallas_call | solution.py:748
  60.7 1.1 %collective-permute-start.11 = (f32[56,256]{1,0:T(8,128)S(1)}, f32[56,256]{1,0:T(8,128)S(1)}, u32[]{:S(2)}, u32[]{:S(2)}) collective-permute-start(f32[56,256]{1,0:T(8,128)S(1)} %pad_maximum_fusion.3), channel_id=1, source_target_pairs={{0,4},{4,0},{8,12},{12,8},{16,20},{20,16},{24,28},{28,24},{1,5},{5... | collective-permute-start | bytes 172040 | tf_op jit(solution)/shard_map/ppermute | solution.py:130
  61.8 8.7 %collective-permute-start.18 = (s16[272,512]{1,0:T(8,128)(2,1)S(1)}, s16[272,512]{1,0:T(8,128)(2,1)S(1)}, u32[]{:S(2)}, u32[]{:S(2)}) collective-permute-start(s16[272,512]{1,0:T(8,128)(2,1)S(1)} %get-tuple-element.66.refs_5_), channel_id=1, source_target_pairs={{0,16},{4,20},{8,24},{12,28},{16,0},{20,4},{24,8},{28,12},{1,17},{... | collective-permute-start | bytes 835592 | tf_op jit(solution)/shard_map/ppermute | solution.py:130
  71.1 2.9 %collective-permute-start.13 = (f32[8,256]{1,0:T(8,128)S(1)}, f32[8,256]{1,0:T(8,128)S(1)}, u32[]{:S(2)}, u32[]{:S(2)}) collective-permute-start(f32[8,256]{1,0:T(8,128)S(1)} %get-tuple-element.63), channel_id=1, source_target_pairs={{0,6},{1,7},{2,4},{3,5},{4,2},{5,3},{6,0},{7,1},{8,14},{9,15},{10,... | collective-permute-start | bytes 24584 | tf_op jit(solution)/shard_map/ppermute | solution.py:139
  74.2 1.4 %collective-permute-done.13 = f32[8,256]{1,0:T(8,128)S(1)} collective-permute-done((f32[8,256]{1,0:T(8,128)S(1)}, f32[8,256]{1,0:T(8,128)S(1)}, u32[]{:S(2)}, u32[]{:S(2)}) %collective-permute-start.13) | collective-permute-done | bytes 8224 | tf_op jit(solution)/shard_map/ppermute | solution.py:139
  75.8 1.2 %collective-permute-done.14 = f32[8,256]{1,0:T(8,128)S(1)} collective-permute-done((f32[8,256]{1,0:T(8,128)S(1)}, f32[8,256]{1,0:T(8,128)S(1)}, u32[]{:S(2)}, u32[]{:S(2)}) %collective-permute-start.14) | collective-permute-done | bytes 8224 | tf_op jit(solution)/shard_map/ppermute | solution.py:134
  76.9 1.4 %collective-permute-start.15 = (f32[8,256]{1,0:T(8,128)S(1)}, f32[8,256]{1,0:T(8,128)S(1)}, u32[]{:S(2)}, u32[]{:S(2)}) collective-permute-start(f32[8,256]{1,0:T(8,128)S(1)} %add.17.refs_0_), channel_id=1, source_target_pairs={{0,8},{4,12},{8,0},{12,4},{16,24},{20,28},{24,16},{28,20},{1,9},{5... | collective-permute-start | bytes 24584 | tf_op jit(solution)/shard_map/ppermute | solution.py:130
  78.3 2.1 %collective-permute-start.16 = (f32[8,256]{1,0:T(8,128)S(1)}, f32[8,256]{1,0:T(8,128)S(1)}, u32[]{:S(2)}, u32[]{:S(2)}) collective-permute-start(f32[8,256]{1,0:T(8,128)S(1)} %add.17.refs_0_), channel_id=1, source_target_pairs={{0,16},{4,20},{8,24},{12,28},{16,0},{20,4},{24,8},{28,12},{1,17},{... | collective-permute-start | bytes 24584 | tf_op jit(solution)/shard_map/ppermute | solution.py:130
  81.3 1.6 %collective-permute-done.16.refs_2_ = f32[8,256]{1,0:T(8,128)S(1)} collective-permute-done((f32[8,256]{1,0:T(8,128)S(1)}, f32[8,256]{1,0:T(8,128)S(1)}, u32[]{:S(2)}, u32[]{:S(2)}) %collective-permute-start.16) | collective-permute-done | bytes 8224 | tf_op jit(solution)/shard_map/ppermute | solution.py:130
  82.9 3.0 %collective-permute-done.17.refs_3_ = f32[8,256]{1,0:T(8,128)S(1)} collective-permute-done((f32[8,256]{1,0:T(8,128)S(1)}, f32[8,256]{1,0:T(8,128)S(1)}, u32[]{:S(2)}, u32[]{:S(2)}) %collective-permute-start.17) | collective-permute-done | bytes 8224 | tf_op jit(solution)/shard_map/ppermute | solution.py:130
  86.2 1.6 %collective-permute-start.20 = (bf16[2,240,256]{2,1,0:T(8,128)(2,1)S(1)}, bf16[2,240,256]{2,1,0:T(8,128)(2,1)S(1)}, u32[]{:S(2)}, u32[]{:S(2)}) collective-permute-start(bf16[2,240,256]{2,1,0:T(8,128)(2,1)S(1)} %get-tuple-element.68.refs_4_), channel_id=1, source_target_pairs={{0,4},{4,0},{8,12},{12,8},{16,20},{20,16},{24,28},{28,24},{1,5},{5... | collective-permute-start | bytes 737288 | tf_op jit(solution)/shard_map/ppermute | solution.py:130
  87.8 1.6 %update.1 = (f32[240,512]{1,0:T(8,128)}, f32[240,512]{1,0:T(8,128)}) custom-call(s32[5]{0:T(128)S(1)} %copy-done.7, f32[8,512]{1,0:T(8,128)S(1)} %get-tuple-element.69.factor, f32[192,512]{1,0:T(8,128)S(1)} %get-tuple-element.70.top, f32[96,256]{1,0:T(8,128)S(1)} %get-tuple-element.64.middle, f32[56,256]{1,0:T(8,128)S(1)} %collective-permute-done.11.got, ...), custom_call_target="tpu_custom_call" | custom-call | tf_op jit(solution)/shard_map/update/pallas_call | solution.py:785
  89.4 3.1 %collective-permute-done.19.refs_2_ = bf16[2,240,256]{2,1,0:T(8,128)(2,1)S(1)} collective-permute-done((bf16[2,240,256]{2,1,0:T(8,128)(2,1)S(1)}, bf16[2,240,256]{2,1,0:T(8,128)(2,1)S(1)}, u32[]{:S(2)}, u32[]{:S(2)}) %collective-permute-start.19) | collective-permute-done | bytes 245792 | tf_op jit(solution)/shard_map/ppermute | solution.py:130
  92.6 1.9 %collective-permute-start.22 = (bf16[4,240,256]{2,1,0:T(8,128)(2,1)S(1)}, bf16[4,240,256]{2,1,0:T(8,128)(2,1)S(1)}, u32[]{:S(2)}, u32[]{:S(2)}) collective-permute-start(bf16[4,240,256]{2,1,0:T(8,128)(2,1)S(1)} %pad_maximum_fusion.1), channel_id=1, source_target_pairs={{0,8},{4,12},{8,0},{12,4},{16,24},{20,28},{24,16},{28,20},{1,9},{5... | collective-permute-start | bytes 1474568 | tf_op jit(solution)/shard_map/ppermute | solution.py:130
  94.6 1.6 %collective-permute-start.21 = (bf16[4,240,256]{2,1,0:T(8,128)(2,1)S(1)}, bf16[4,240,256]{2,1,0:T(8,128)(2,1)S(1)}, u32[]{:S(2)}, u32[]{:S(2)}) collective-permute-start(bf16[4,240,256]{2,1,0:T(8,128)(2,1)S(1)} %pad_maximum_fusion), channel_id=1, source_target_pairs={{0,4},{4,0},{8,12},{12,8},{16,20},{20,16},{24,28},{28,24},{1,5},{5... | collective-permute-start | bytes 1474568 | tf_op jit(solution)/shard_map/ppermute | solution.py:130
  96.1 7.2 %collective-permute-done.22.refs_6_ = bf16[4,240,256]{2,1,0:T(8,128)(2,1)S(1)} collective-permute-done((bf16[4,240,256]{2,1,0:T(8,128)(2,1)S(1)}, bf16[4,240,256]{2,1,0:T(8,128)(2,1)S(1)}, u32[]{:S(2)}, u32[]{:S(2)}) %collective-permute-start.22) | collective-permute-done | bytes 491552 | tf_op jit(solution)/shard_map/ppermute | solution.py:130
  103.3 1.5 %collective-permute-done.21.refs_3_ = bf16[4,240,256]{2,1,0:T(8,128)(2,1)S(1)} collective-permute-done((bf16[4,240,256]{2,1,0:T(8,128)(2,1)S(1)}, bf16[4,240,256]{2,1,0:T(8,128)(2,1)S(1)}, u32[]{:S(2)}, u32[]{:S(2)}) %collective-permute-start.21) | collective-permute-done | bytes 491552 | tf_op jit(solution)/shard_map/ppermute | solution.py:130
  104.8 2.0 %place.1 = bf16[1920,512]{1,0:T(8,128)(2,1)} custom-call(s32[5]{0:T(128)S(1)} %copy-done.7, bf16[2,240,256]{2,1,0:T(8,128)(2,1)S(1)} %get-tuple-element.67.refs_1_, bf16[2,240,256]{2,1,0:T(8,128)(2,1)S(1)} %collective-permute-done.19.refs_2_, bf16[4,240,256]{2,1,0:T(8,128)(2,1)S(1)} %collective-permute-done.21.refs_3_, ...), custom_call_target="tpu_custom_call" | custom-call | tf_op jit(solution)/shard_map/place/pallas_call | solution.py:798
  (58 shorter events, 11.9 us)
Async XLA Ops:
  1.3 14.4 %copy-start = (bf16[2048,512]{1,0:T(8,128)(2,1)S(1)}, bf16[2048,512]{1,0:T(8,128)(2,1)}, u32[]{:S(2)}) copy-start(bf16[2048,512]{1,0:T(8,128)(2,1)} %refs_2_.4) | copy-start | bytes 6291460
  1.3 14.4 %copy-start.7 = (s32[5]{0:T(128)S(1)}, s32[5]{0:T(128)}, u32[]{:S(2)}) copy-start(s32[5]{0:T(128)} %stack.32.refs_0_.info) | copy-start | bytes 64
  1.3 14.4 %copy-start.10 = (s32[64]{0:T(128)S(1)}, s32[64]{0:T(128)}, u32[]{:S(2)}) copy-start(s32[64]{0:T(128)} %param.11) | copy-start | bytes 772
  11.2 20.6 %collective-permute-start.5 = (s16[4,256,256]{2,1,0:T(8,128)(2,1)}, s16[4,256,256]{2,1,0:T(8,128)(2,1)S(1)}, u32[]{:S(2)}, u32[]{:S(2)}) collective-permute-start(s16[4,256,256]{2,1,0:T(8,128)(2,1)} %get-tuple-element.49), channel_id=1, source_target_pairs={{0,4},{4,0},{8,12},{12,8},{16,20},{20,16},{24,28},{28,24},{1,5},{5... | collective-permute-start | bytes 1572872 | tf_op jit(solution)/shard_map/ppermute | solution.py:130
  14.2 21.4 %collective-permute-start.6 = (s16[4,256,256]{2,1,0:T(8,128)(2,1)}, s16[4,256,256]{2,1,0:T(8,128)(2,1)S(1)}, u32[]{:S(2)}, u32[]{:S(2)}) collective-permute-start(s16[4,256,256]{2,1,0:T(8,128)(2,1)} %get-tuple-element.52), channel_id=1, source_target_pairs={{0,8},{4,12},{8,0},{12,4},{16,24},{20,28},{24,16},{28,20},{1,9},{5... | collective-permute-start | bytes 1572872 | tf_op jit(solution)/shard_map/ppermute | solution.py:130
  15.8 16.0 %copy-start.4 = (f32[4,240,256]{2,1,0:T(8,128)S(1)}, f32[4,240,256]{2,1,0:T(8,128)}, u32[]{:S(2)}) copy-start(f32[4,240,256]{2,1,0:T(8,128)} %get-tuple-element.50.refs_2_) | copy-start | bytes 2949124
  19.0 16.6 %copy-start.3 = (f32[4,240,256]{2,1,0:T(8,128)S(1)}, f32[4,240,256]{2,1,0:T(8,128)}, u32[]{:S(2)}) copy-start(f32[4,240,256]{2,1,0:T(8,128)} %get-tuple-element.53.refs_2_) | copy-start | bytes 2949124
  19.0 12.2 %collective-permute-start = (bf16[64,1024]{1,0:T(8,128)(2,1)S(1)}, bf16[64,1024]{1,0:T(8,128)(2,1)S(1)}, u32[]{:S(2)}, u32[]{:S(2)}) collective-permute-start(bf16[64,1024]{1,0:T(8,128)(2,1)S(1)} %picks.1.refs_1_), channel_id=1, source_target_pairs={{0,16},{4,20},{8,24},{12,28},{16,0},{20,4},{24,8},{28,12},{1,17},{... | collective-permute-start | bytes 393224 | tf_op jit(solution)/shard_map/ppermute | solution.py:130
  22.0 17.7 %collective-permute-start.2 = (s16[272,512]{1,0:T(8,128)(2,1)S(1)}, s16[272,512]{1,0:T(8,128)(2,1)S(1)}, u32[]{:S(2)}, u32[]{:S(2)}) collective-permute-start(s16[272,512]{1,0:T(8,128)(2,1)S(1)} %base.1.refs_1_), channel_id=1, source_target_pairs={{0,16},{4,20},{8,24},{12,28},{16,0},{20,4},{24,8},{28,12},{1,17},{... | collective-permute-start | bytes 835592 | tf_op jit(solution)/shard_map/ppermute | solution.py:130
  31.2 8.5 %collective-permute-start.1 = (bf16[2,64,1024]{2,1,0:T(8,128)(2,1)S(1)}, bf16[2,64,1024]{2,1,0:T(8,128)(2,1)S(1)}, u32[]{:S(2)}, u32[]{:S(2)}) collective-permute-start(bf16[2,64,1024]{2,1,0:T(8,128)(2,1)S(1)} %pad_maximum_fusion.2), channel_id=1, source_target_pairs={{0,4},{4,0},{8,12},{12,8},{16,20},{20,16},{24,28},{28,24},{1,5},{5... | collective-permute-start | bytes 786440 | tf_op jit(solution)/shard_map/ppermute | solution.py:130
  36.5 17.2 %copy-start.5 = (f32[1,4,128,128]{3,2,1,0:T(8,128)S(1)}, f32[1,4,128,128]{3,2,1,0:T(8,128)}, u32[]{:S(2)}) copy-start(f32[1,4,128,128]{3,2,1,0:T(8,128)} %param.14) | copy-start | bytes 786436
  36.5 17.2 %copy-start.6 = (f32[1,5,96,96]{3,2,1,0:T(8,128)S(1)}, f32[1,5,96,96]{3,2,1,0:T(8,128)}, u32[]{:S(2)}) copy-start(f32[1,5,96,96]{3,2,1,0:T(8,128)} %param.15) | copy-start | bytes 552964
  36.5 17.2 %copy-start.8 = (s32[4,4]{1,0:T(4,128)S(1)}, s32[4,4]{1,0:T(4,128)}, u32[]{:S(2)}) copy-start(s32[4,4]{1,0:T(4,128)} %refs_1_.3) | copy-start | bytes 196
  36.5 17.2 %copy-start.9 = (s32[4,5]{1,0:T(4,128)S(1)}, s32[4,5]{1,0:T(4,128)}, u32[]{:S(2)}) copy-start(s32[4,5]{1,0:T(4,128)} %refs_2_.5) | copy-start | bytes 244
  36.6 9.3 %collective-permute-start.7 = (s16[2,256,256]{2,1,0:T(8,128)(2,1)S(1)}, s16[2,256,256]{2,1,0:T(8,128)(2,1)S(1)}, u32[]{:S(2)}, u32[]{:S(2)}) collective-permute-start(s16[2,256,256]{2,1,0:T(8,128)(2,1)S(1)} %get-tuple-element.55), channel_id=1, source_target_pairs={{0,8},{4,12},{8,0},{12,4},{16,24},{20,28},{24,16},{28,20},{1,9},{5... | collective-permute-start | bytes 786440 | tf_op jit(solution)/shard_map/ppermute | solution.py:130
  37.4 8.5 %collective-permute-start.8 = (s16[2,256,256]{2,1,0:T(8,128)(2,1)S(1)}, s16[2,256,256]{2,1,0:T(8,128)(2,1)S(1)}, u32[]{:S(2)}, u32[]{:S(2)}) collective-permute-start(s16[2,256,256]{2,1,0:T(8,128)(2,1)S(1)} %get-tuple-element.57), channel_id=1, source_target_pairs={{0,4},{4,0},{8,12},{12,8},{16,20},{20,16},{24,28},{28,24},{1,5},{5... | collective-permute-start | bytes 786440 | tf_op jit(solution)/shard_map/ppermute | solution.py:130
  40.9 12.9 %collective-permute-start.3 = (s16[1136,128]{1,0:T(8,128)(2,1)S(1)}, s16[1136,128]{1,0:T(8,128)(2,1)S(1)}, u32[]{:S(2)}, u32[]{:S(2)}) collective-permute-start(s16[1136,128]{1,0:T(8,128)(2,1)S(1)} %stats.1.refs_3_), channel_id=1, source_target_pairs={{0,8},{4,12},{8,0},{12,4},{16,24},{20,28},{24,16},{28,20},{1,9},{5... | collective-permute-start | bytes 872456 | tf_op jit(solution)/shard_map/ppermute | solution.py:130
  46.8 12.1 %collective-permute-start.9 = (s16[2,256,256]{2,1,0:T(8,128)(2,1)S(1)}, s16[2,256,256]{2,1,0:T(8,128)(2,1)S(1)}, u32[]{:S(2)}, u32[]{:S(2)}) collective-permute-start(s16[2,256,256]{2,1,0:T(8,128)(2,1)S(1)} %get-tuple-element.59), channel_id=1, source_target_pairs={{0,16},{4,20},{8,24},{12,28},{16,0},{20,4},{24,8},{28,12},{1,17},{... | collective-permute-start | bytes 786440 | tf_op jit(solution)/shard_map/ppermute | solution.py:130
  48.3 4.3 %collective-permute-start.4 = (s16[2,64,256]{2,1,0:T(8,128)(2,1)S(1)}, s16[2,64,256]{2,1,0:T(8,128)(2,1)S(1)}, u32[]{:S(2)}, u32[]{:S(2)}) collective-permute-start(s16[2,64,256]{2,1,0:T(8,128)(2,1)S(1)} %sides.1), channel_id=1, source_target_pairs={{0,4},{4,0},{8,12},{12,8},{16,20},{20,16},{24,28},{28,24},{1,5},{5... | collective-permute-start | bytes 196616 | tf_op jit(solution)/shard_map/ppermute | solution.py:130
  58.0 0.9 collective-permute-start.10
  60.7 14.9 %collective-permute-start.11 = (f32[56,256]{1,0:T(8,128)S(1)}, f32[56,256]{1,0:T(8,128)S(1)}, u32[]{:S(2)}, u32[]{:S(2)}) collective-permute-start(f32[56,256]{1,0:T(8,128)S(1)} %pad_maximum_fusion.3), channel_id=1, source_target_pairs={{0,4},{4,0},{8,12},{12,8},{16,20},{20,16},{24,28},{28,24},{1,5},{5... | collective-permute-start | bytes 172040 | tf_op jit(solution)/shard_map/ppermute | solution.py:130
  61.8 24.0 %collective-permute-start.18 = (s16[272,512]{1,0:T(8,128)(2,1)S(1)}, s16[272,512]{1,0:T(8,128)(2,1)S(1)}, u32[]{:S(2)}, u32[]{:S(2)}) collective-permute-start(s16[272,512]{1,0:T(8,128)(2,1)S(1)} %get-tuple-element.66.refs_5_), channel_id=1, source_target_pairs={{0,16},{4,20},{8,24},{12,28},{16,0},{20,4},{24,8},{28,12},{1,17},{... | collective-permute-start | bytes 835592 | tf_op jit(solution)/shard_map/ppermute | solution.py:130
  70.6 3.7 %collective-permute-start.12 = (f32[8,256]{1,0:T(8,128)S(1)}, f32[8,256]{1,0:T(8,128)S(1)}, u32[]{:S(2)}, u32[]{:S(2)}) collective-permute-start(f32[8,256]{1,0:T(8,128)S(1)} %get-tuple-element.63), channel_id=1, source_target_pairs={{0,2},{1,3},{2,0},{3,1},{4,6},{5,7},{6,4},{7,5},{8,10},{9,11},{10,... | collective-permute-start | bytes 24584 | tf_op jit(solution)/shard_map/ppermute | solution.py:134
  71.1 4.5 %collective-permute-start.13 = (f32[8,256]{1,0:T(8,128)S(1)}, f32[8,256]{1,0:T(8,128)S(1)}, u32[]{:S(2)}, u32[]{:S(2)}) collective-permute-start(f32[8,256]{1,0:T(8,128)S(1)} %get-tuple-element.63), channel_id=1, source_target_pairs={{0,6},{1,7},{2,4},{3,5},{4,2},{5,3},{6,0},{7,1},{8,14},{9,15},{10,... | collective-permute-start | bytes 24584 | tf_op jit(solution)/shard_map/ppermute | solution.py:139
  75.7 1.2 %collective-permute-start.14 = (f32[8,256]{1,0:T(8,128)S(1)}, f32[8,256]{1,0:T(8,128)S(1)}, u32[]{:S(2)}, u32[]{:S(2)}) collective-permute-start(f32[8,256]{1,0:T(8,128)S(1)} %fusion), channel_id=1, source_target_pairs={{0,1},{1,0},{2,3},{3,2},{4,5},{5,4},{6,7},{7,6},{8,9},{9,8},{10,11... | collective-permute-start | bytes 24584 | tf_op jit(solution)/shard_map/ppermute | solution.py:134
  76.9 4.4 %collective-permute-start.15 = (f32[8,256]{1,0:T(8,128)S(1)}, f32[8,256]{1,0:T(8,128)S(1)}, u32[]{:S(2)}, u32[]{:S(2)}) collective-permute-start(f32[8,256]{1,0:T(8,128)S(1)} %add.17.refs_0_), channel_id=1, source_target_pairs={{0,8},{4,12},{8,0},{12,4},{16,24},{20,28},{24,16},{28,20},{1,9},{5... | collective-permute-start | bytes 24584 | tf_op jit(solution)/shard_map/ppermute | solution.py:130
  78.3 4.5 %collective-permute-start.16 = (f32[8,256]{1,0:T(8,128)S(1)}, f32[8,256]{1,0:T(8,128)S(1)}, u32[]{:S(2)}, u32[]{:S(2)}) collective-permute-start(f32[8,256]{1,0:T(8,128)S(1)} %add.17.refs_0_), channel_id=1, source_target_pairs={{0,16},{4,20},{8,24},{12,28},{16,0},{20,4},{24,8},{28,12},{1,17},{... | collective-permute-start | bytes 24584 | tf_op jit(solution)/shard_map/ppermute | solution.py:130
  80.4 5.4 %collective-permute-start.17 = (f32[8,256]{1,0:T(8,128)S(1)}, f32[8,256]{1,0:T(8,128)S(1)}, u32[]{:S(2)}, u32[]{:S(2)}) collective-permute-start(f32[8,256]{1,0:T(8,128)S(1)} %add.17.refs_0_), channel_id=1, source_target_pairs={{0,24},{4,28},{8,16},{12,20},{16,8},{20,12},{24,0},{28,4},{1,25},{... | collective-permute-start | bytes 24584 | tf_op jit(solution)/shard_map/ppermute | solution.py:130
  86.1 6.4 %collective-permute-start.19 = (bf16[2,240,256]{2,1,0:T(8,128)(2,1)S(1)}, bf16[2,240,256]{2,1,0:T(8,128)(2,1)S(1)}, u32[]{:S(2)}, u32[]{:S(2)}) collective-permute-start(bf16[2,240,256]{2,1,0:T(8,128)(2,1)S(1)} %get-tuple-element.67.refs_1_), channel_id=1, source_target_pairs={{0,8},{4,12},{8,0},{12,4},{16,24},{20,28},{24,16},{28,20},{1,9},{5... | collective-permute-start | bytes 737288 | tf_op jit(solution)/shard_map/ppermute | solution.py:130
  86.2 6.4 %collective-permute-start.20 = (bf16[2,240,256]{2,1,0:T(8,128)(2,1)S(1)}, bf16[2,240,256]{2,1,0:T(8,128)(2,1)S(1)}, u32[]{:S(2)}, u32[]{:S(2)}) collective-permute-start(bf16[2,240,256]{2,1,0:T(8,128)(2,1)S(1)} %get-tuple-element.68.refs_4_), channel_id=1, source_target_pairs={{0,4},{4,0},{8,12},{12,8},{16,20},{20,16},{24,28},{28,24},{1,5},{5... | collective-permute-start | bytes 737288 | tf_op jit(solution)/shard_map/ppermute | solution.py:130
  92.6 10.7 %collective-permute-start.22 = (bf16[4,240,256]{2,1,0:T(8,128)(2,1)S(1)}, bf16[4,240,256]{2,1,0:T(8,128)(2,1)S(1)}, u32[]{:S(2)}, u32[]{:S(2)}) collective-permute-start(bf16[4,240,256]{2,1,0:T(8,128)(2,1)S(1)} %pad_maximum_fusion.1), channel_id=1, source_target_pairs={{0,8},{4,12},{8,0},{12,4},{16,24},{20,28},{24,16},{28,20},{1,9},{5... | collective-permute-start | bytes 1474568 | tf_op jit(solution)/shard_map/ppermute | solution.py:130
  94.6 10.2 %collective-permute-start.21 = (bf16[4,240,256]{2,1,0:T(8,128)(2,1)S(1)}, bf16[4,240,256]{2,1,0:T(8,128)(2,1)S(1)}, u32[]{:S(2)}, u32[]{:S(2)}) collective-permute-start(bf16[4,240,256]{2,1,0:T(8,128)(2,1)S(1)} %pad_maximum_fusion), channel_id=1, source_target_pairs={{0,4},{4,0},{8,12},{12,8},{16,20},{20,16},{24,28},{28,24},{1,5},{5... | collective-permute-start | bytes 1474568 | tf_op jit(solution)/shard_map/ppermute | solution.py:130
  (2 other events, 11.7 us)

commit v8 on v7

--- a/solution.py
+++ b/solution.py
@@ -542,12 +542,11 @@
 
 
 def round_kernel(
-    entries, total, along_l, along_h, along_both, base, scaled, scaled_far, factor,
+    entries, total, got_total, base, scaled, scaled_far, factor,
     rounded_a, rounded_b
 ):
     rows, half = rounded_a.shape[1:]
-    sums = [each[0:1, :] for each in (total, along_l, along_h, along_both)]
-    mean_sq = ((sums[0] + sums[1]) + (sums[2] + sums[3])) / entries
+    mean_sq = (total[0:1, :] + got_total[0:1, :]) / entries
     norm = 1.0 / jnp.sqrt(mean_sq + epsilon_sq)
     norm = jnp.concatenate([norm, norm], axis=1)
     factor[...] = jnp.broadcast_to(norm, factor.shape)
@@ -766,10 +765,10 @@
     along_both = swap_both(total, 1, 2)
     total = (total + got[mid:]) + (along_y + along_both)
     total = total + swap_t(total, 1)
-    others = [swap(total, bits) for bits in (2, 4, 6)]
+    total = total + swap(total, 4)
     factor, rounded_a, rounded_b = pl.pallas_call(
         lambda *refs: round_kernel(rows * 8 * cols * 4, *refs),
-        in_specs=[vmem] * 7,
+        in_specs=[vmem] * 5,
         out_specs=[vmem] * 3,
         out_shape=[
             shaped((8, cols), f32),
@@ -778,7 +777,7 @@
         ],
         compiler_params=params(24),
         name="round",
-    )(total, *others, base_units, scaled, scaled_far)
+    )(total, swap(total, 2), base_units, scaled, scaled_far)
 
     along_l = swap(rounded_a, 2)
     along_x = swap(rounded_b, 1)

time: 107 us -> 106 us (level)
    ppermute x19 -> x18, waiting for transfers between devices: 35 us -> 34.3 us  [swap(): return lax.ppermute(value, 'shard', [(i, i ^ bit) for i in range(8)])]
    ppermute x19 -> x18, starting transfers between devices: 34.5 us -> 34.2 us  [swap(): return lax.ppermute(value, 'shard', [(i, i ^ bit) for i in range(8)])]
  transfers between devices with their start and end apart: 23 -> 22, of which waited for: 16 -> 16; matrix products, arithmetic and copies ran while one was open for 0% -> 0% of each run, Pallas kernels for 14% -> 14%
where the time goes in v8:
time: 106 us
  starting transfers between devices  38.6 us (36%)
  waiting for transfers between devices  37.2 us (35%)
  Pallas kernels  28.5 us (27%)
    ppermute x18, waiting for transfers between devices, swap(): return lax.ppermute(value, 'shard', [(i, i ^ bit) for i in range(8)])  34.3 us
    ppermute x18, starting transfers between devices, swap(): return lax.ppermute(value, 'shard', [(i, i ^ bit) for i in range(8)])  34.2 us
    pallas_call x1, Pallas kernels, fast(): pl.pallas_call(lambda *refs: partial_kernel(group_cols, width_g, *refs),...  9.85 us
    pallas_call x1, Pallas kernels, fast(): pl.pallas_call(lambda *refs: factor_kernel(share, blocks, *refs), in_spec...  4.24 us
    pallas_call x1, Pallas kernels, fast(): pl.pallas_call(lambda *refs: picks_kernel(group_cols, *refs), in_specs=[s...  3.15 us
    ppermute x1, starting transfers between devices, swap_both(): return lax.ppermute(value, ('shard', 'tensor'), route)  2.85 us
  transfers between devices with their start and end apart: 22, of which 16 were waited for; matrix products, arithmetic and copies ran while one was open for 0% of the time, Pallas kernels for 14%

profile of v8, /device:TPU:0, one launch (start us, length us, event | category | flops | bytes accessed | tf_op | source)
XLA Modules:
  0.0 106.0 jit_solution(16274114382937409777)
XLA Ops:
  1.3 9.9 %partial.1 = (s16[4,256,256]{2,1,0:T(8,128)(2,1)}, f32[4,240,256]{2,1,0:T(8,128)}, s16[4,256,256]{2,1,0:T(8,128)(2,1)}, f32[4,240,256]{2,1,0:T(8,128)}) custom-call(s32[5]{0:T(128)} %stack.32.refs_0_.info, bf16[2048,1920]{1,0:T(8,128)(2,1)} %refs_3_.1, bf16[2048,512]{1,0:T(8,128)(2,1)} %refs_2_.4), custom_call_target="tpu_custom_call" | custom-call | tf_op jit(solution)/shard_map/partial/pallas_call | solution.py:627
  11.2 3.0 %collective-permute-start.5 = (s16[4,256,256]{2,1,0:T(8,128)(2,1)}, s16[4,256,256]{2,1,0:T(8,128)(2,1)S(1)}, u32[]{:S(2)}, u32[]{:S(2)}) collective-permute-start(s16[4,256,256]{2,1,0:T(8,128)(2,1)} %get-tuple-element.49), channel_id=1, source_target_pairs={{0,4},{4,0},{8,12},{12,8},{16,20},{20,16},{24,28},{28,24},{1,5},{5... | collective-permute-start | bytes 1572872 | tf_op jit(solution)/shard_map/ppermute | solution.py:130
  14.2 1.6 %collective-permute-start.6 = (s16[4,256,256]{2,1,0:T(8,128)(2,1)}, s16[4,256,256]{2,1,0:T(8,128)(2,1)S(1)}, u32[]{:S(2)}, u32[]{:S(2)}) collective-permute-start(s16[4,256,256]{2,1,0:T(8,128)(2,1)} %get-tuple-element.52), channel_id=1, source_target_pairs={{0,8},{4,12},{8,0},{12,4},{16,24},{20,28},{24,16},{28,20},{1,9},{5... | collective-permute-start | bytes 1572872 | tf_op jit(solution)/shard_map/ppermute | solution.py:130
  15.8 3.2 %picks.1.refs_1_ = bf16[64,1024]{1,0:T(8,128)(2,1)S(1)} custom-call(s32[5]{0:T(128)S(1)} %copy-done.7, s32[1,64]{1,0:T(1,128)S(1)} %bitcast.16, bf16[2048,512]{1,0:T(8,128)(2,1)S(1)} %copy-done, bf16[2048,1920]{1,0:T(8,128)(2,1)} %refs_3_.1), custom_call_target="tpu_custom_call" | custom-call | tf_op jit(solution)/shard_map/picks/pallas_call | solution.py:650
  19.0 2.7 %collective-permute-start = (bf16[64,1024]{1,0:T(8,128)(2,1)S(1)}, bf16[64,1024]{1,0:T(8,128)(2,1)S(1)}, u32[]{:S(2)}, u32[]{:S(2)}) collective-permute-start(bf16[64,1024]{1,0:T(8,128)(2,1)S(1)} %picks.1.refs_1_), channel_id=1, source_target_pairs={{0,16},{4,20},{8,24},{12,28},{16,0},{20,4},{24,8},{28,12},{1,17},{... | collective-permute-start | bytes 393224 | tf_op jit(solution)/shard_map/ppermute | solution.py:130
  22.4 8.8 %collective-permute-done.refs_2_ = bf16[64,1024]{1,0:T(8,128)(2,1)S(1)} collective-permute-done((bf16[64,1024]{1,0:T(8,128)(2,1)S(1)}, bf16[64,1024]{1,0:T(8,128)(2,1)S(1)}, u32[]{:S(2)}, u32[]{:S(2)}) %collective-permute-start) | collective-permute-done | bytes 131104 | tf_op jit(solution)/shard_map/ppermute | solution.py:130
  32.8 2.8 %collective-permute-done.6.refs_1_ = s16[4,256,256]{2,1,0:T(8,128)(2,1)S(1)} collective-permute-done((s16[4,256,256]{2,1,0:T(8,128)(2,1)}, s16[4,256,256]{2,1,0:T(8,128)(2,1)S(1)}, u32[]{:S(2)}, u32[]{:S(2)}) %collective-permute-start.6) | collective-permute-done | bytes 524320 | tf_op jit(solution)/shard_map/ppermute | solution.py:130
  37.4 1.5 %collective-permute-start.8 = (s16[2,256,256]{2,1,0:T(8,128)(2,1)S(1)}, s16[2,256,256]{2,1,0:T(8,128)(2,1)S(1)}, u32[]{:S(2)}, u32[]{:S(2)}) collective-permute-start(s16[2,256,256]{2,1,0:T(8,128)(2,1)S(1)} %get-tuple-element.57), channel_id=1, source_target_pairs={{0,4},{4,0},{8,12},{12,8},{16,20},{20,16},{24,28},{28,24},{1,5},{5... | collective-permute-start | bytes 786440 | tf_op jit(solution)/shard_map/ppermute | solution.py:130
  39.8 1.1 %stats.1.refs_3_ = s16[1136,128]{1,0:T(8,128)(2,1)S(1)} custom-call(s32[5]{0:T(128)S(1)} %copy-done.7, bf16[64,1024]{1,0:T(8,128)(2,1)S(1)} %picks.1.refs_1_, bf16[64,1024]{1,0:T(8,128)(2,1)S(1)} %collective-permute-done.refs_2_, bf16[2,64,1024]{2,1,0:T(8,128)(2,1)S(1)} %collective-permute-done.1.refs_3_), custom_call_target="tpu_custom_call" | custom-call | tf_op jit(solution)/shard_map/stats/pallas_call | solution.py:683
  40.9 3.1 %collective-permute-start.3 = (s16[1136,128]{1,0:T(8,128)(2,1)S(1)}, s16[1136,128]{1,0:T(8,128)(2,1)S(1)}, u32[]{:S(2)}, u32[]{:S(2)}) collective-permute-start(s16[1136,128]{1,0:T(8,128)(2,1)S(1)} %stats.1.refs_3_), channel_id=1, source_target_pairs={{0,8},{4,12},{8,0},{12,4},{16,24},{20,28},{24,16},{28,20},{1,9},{5... | collective-permute-start | bytes 872456 | tf_op jit(solution)/shard_map/ppermute | solution.py:130
  44.0 1.9 %collective-permute-done.7.got_a = s16[2,256,256]{2,1,0:T(8,128)(2,1)S(1)} collective-permute-done((s16[2,256,256]{2,1,0:T(8,128)(2,1)S(1)}, s16[2,256,256]{2,1,0:T(8,128)(2,1)S(1)}, u32[]{:S(2)}, u32[]{:S(2)}) %collective-permute-start.7) | collective-permute-done | bytes 262176 | tf_op jit(solution)/shard_map/ppermute | solution.py:130
  46.8 1.0 collective-permute-start.9
  48.9 3.8 %collective-permute-done.4.refs_3_ = s16[2,64,256]{2,1,0:T(8,128)(2,1)S(1)} collective-permute-done((s16[2,64,256]{2,1,0:T(8,128)(2,1)S(1)}, s16[2,64,256]{2,1,0:T(8,128)(2,1)S(1)}, u32[]{:S(2)}, u32[]{:S(2)}) %collective-permute-start.4) | collective-permute-done | bytes 65568 | tf_op jit(solution)/shard_map/ppermute | solution.py:130
  53.8 4.2 %factors.1 = (f32[4,128,128]{2,1,0:T(8,128)}, f32[5,96,96]{2,1,0:T(8,128)}, f32[4,128,128]{2,1,0:T(8,128)S(1)}, s16[3,112,96]{2,1,0:T(8,128)(2,1)S(1)}) custom-call(s32[5]{0:T(128)S(1)} %copy-done.7, s32[4,4]{1,0:T(4,128)S(1)} %copy-done.8, s32[4,5]{1,0:T(4,128)S(1)} %copy-done.9, s16[1136,128]{1,0:T(8,128)(2,1)S(1)} %stats.1.refs_3_, ...), custom_call_target="tpu_custom_call" | custom-call | tf_op jit(solution)/shard_map/factors/pallas_call | solution.py:725
  58.9 1.8 %precon.1 = (f32[192,512]{1,0:T(8,128)S(1)}, f32[96,256]{1,0:T(8,128)S(1)}, f32[8,256]{1,0:T(8,128)S(1)}, s16[272,512]{1,0:T(8,128)(2,1)S(1)}) custom-call(s32[5]{0:T(128)S(1)} %copy-done.7, s16[2,256,256]{2,1,0:T(8,128)(2,1)S(1)} %collective-permute-done.9.got, f32[2,240,256]{2,1,0:T(8,128)S(1)} %get-tuple-element.60.held, ...), custom_call_target="tpu_custom_call" | custom-call | tf_op jit(solution)/shard_map/precon/pallas_call | solution.py:747
  60.8 1.1 %collective-permute-start.11 = (f32[56,256]{1,0:T(8,128)S(1)}, f32[56,256]{1,0:T(8,128)S(1)}, u32[]{:S(2)}, u32[]{:S(2)}) collective-permute-start(f32[56,256]{1,0:T(8,128)S(1)} %pad_maximum_fusion.3), channel_id=1, source_target_pairs={{0,4},{4,0},{8,12},{12,8},{16,20},{20,16},{24,28},{28,24},{1,5},{5... | collective-permute-start | bytes 172040 | tf_op jit(solution)/shard_map/ppermute | solution.py:130
  61.8 8.7 %collective-permute-start.17 = (s16[272,512]{1,0:T(8,128)(2,1)S(1)}, s16[272,512]{1,0:T(8,128)(2,1)S(1)}, u32[]{:S(2)}, u32[]{:S(2)}) collective-permute-start(s16[272,512]{1,0:T(8,128)(2,1)S(1)} %get-tuple-element.66.refs_3_), channel_id=1, source_target_pairs={{0,16},{4,20},{8,24},{12,28},{16,0},{20,4},{24,8},{28,12},{1,17},{... | collective-permute-start | bytes 835592 | tf_op jit(solution)/shard_map/ppermute | solution.py:130
  71.1 2.9 %collective-permute-start.13 = (f32[8,256]{1,0:T(8,128)S(1)}, f32[8,256]{1,0:T(8,128)S(1)}, u32[]{:S(2)}, u32[]{:S(2)}) collective-permute-start(f32[8,256]{1,0:T(8,128)S(1)} %get-tuple-element.63), channel_id=1, source_target_pairs={{0,6},{1,7},{2,4},{3,5},{4,2},{5,3},{6,0},{7,1},{8,14},{9,15},{10,... | collective-permute-start | bytes 24584 | tf_op jit(solution)/shard_map/ppermute | solution.py:139
  74.2 1.5 %collective-permute-done.13 = f32[8,256]{1,0:T(8,128)S(1)} collective-permute-done((f32[8,256]{1,0:T(8,128)S(1)}, f32[8,256]{1,0:T(8,128)S(1)}, u32[]{:S(2)}, u32[]{:S(2)}) %collective-permute-start.13) | collective-permute-done | bytes 8224 | tf_op jit(solution)/shard_map/ppermute | solution.py:139
  75.8 1.2 %collective-permute-done.14 = f32[8,256]{1,0:T(8,128)S(1)} collective-permute-done((f32[8,256]{1,0:T(8,128)S(1)}, f32[8,256]{1,0:T(8,128)S(1)}, u32[]{:S(2)}, u32[]{:S(2)}) %collective-permute-start.14) | collective-permute-done | bytes 8224 | tf_op jit(solution)/shard_map/ppermute | solution.py:134
  77.0 2.9 %collective-permute-start.15 = (f32[8,256]{1,0:T(8,128)S(1)}, f32[8,256]{1,0:T(8,128)S(1)}, u32[]{:S(2)}, u32[]{:S(2)}) collective-permute-start(f32[8,256]{1,0:T(8,128)S(1)} %add.20), channel_id=1, source_target_pairs={{0,16},{4,20},{8,24},{12,28},{16,0},{20,4},{24,8},{28,12},{1,17},{... | collective-permute-start | bytes 24584 | tf_op jit(solution)/shard_map/ppermute | solution.py:130
  79.9 1.6 %collective-permute-done.15 = f32[8,256]{1,0:T(8,128)S(1)} collective-permute-done((f32[8,256]{1,0:T(8,128)S(1)}, f32[8,256]{1,0:T(8,128)S(1)}, u32[]{:S(2)}, u32[]{:S(2)}) %collective-permute-start.15) | collective-permute-done | bytes 8224 | tf_op jit(solution)/shard_map/ppermute | solution.py:130
  81.5 1.4 %collective-permute-start.16 = (f32[8,256]{1,0:T(8,128)S(1)}, f32[8,256]{1,0:T(8,128)S(1)}, u32[]{:S(2)}, u32[]{:S(2)}) collective-permute-start(f32[8,256]{1,0:T(8,128)S(1)} %add.21.refs_0_), channel_id=1, source_target_pairs={{0,8},{4,12},{8,0},{12,4},{16,24},{20,28},{24,16},{28,20},{1,9},{5... | collective-permute-start | bytes 24584 | tf_op jit(solution)/shard_map/ppermute | solution.py:130
  82.9 2.3 %collective-permute-done.16.refs_1_ = f32[8,256]{1,0:T(8,128)S(1)} collective-permute-done((f32[8,256]{1,0:T(8,128)S(1)}, f32[8,256]{1,0:T(8,128)S(1)}, u32[]{:S(2)}, u32[]{:S(2)}) %collective-permute-start.16) | collective-permute-done | bytes 8224 | tf_op jit(solution)/shard_map/ppermute | solution.py:130
  85.4 1.4 %collective-permute-start.18 = (bf16[2,240,256]{2,1,0:T(8,128)(2,1)S(1)}, bf16[2,240,256]{2,1,0:T(8,128)(2,1)S(1)}, u32[]{:S(2)}, u32[]{:S(2)}) collective-permute-start(bf16[2,240,256]{2,1,0:T(8,128)(2,1)S(1)} %get-tuple-element.67.refs_1_), channel_id=1, source_target_pairs={{0,8},{4,12},{8,0},{12,4},{16,24},{20,28},{24,16},{28,20},{1,9},{5... | collective-permute-start | bytes 737288 | tf_op jit(solution)/shard_map/ppermute | solution.py:130
  86.9 1.3 %collective-permute-start.19 = (bf16[2,240,256]{2,1,0:T(8,128)(2,1)S(1)}, bf16[2,240,256]{2,1,0:T(8,128)(2,1)S(1)}, u32[]{:S(2)}, u32[]{:S(2)}) collective-permute-start(bf16[2,240,256]{2,1,0:T(8,128)(2,1)S(1)} %get-tuple-element.68.refs_4_), channel_id=1, source_target_pairs={{0,4},{4,0},{8,12},{12,8},{16,20},{20,16},{24,28},{28,24},{1,5},{5... | collective-permute-start | bytes 737288 | tf_op jit(solution)/shard_map/ppermute | solution.py:130
  88.1 1.6 %update.1 = (f32[240,512]{1,0:T(8,128)}, f32[240,512]{1,0:T(8,128)}) custom-call(s32[5]{0:T(128)S(1)} %copy-done.7, f32[8,512]{1,0:T(8,128)S(1)} %get-tuple-element.69.factor, f32[192,512]{1,0:T(8,128)S(1)} %get-tuple-element.70.top, f32[96,256]{1,0:T(8,128)S(1)} %get-tuple-element.64.middle, f32[56,256]{1,0:T(8,128)S(1)} %collective-permute-done.11.got, ...), custom_call_target="tpu_custom_call" | custom-call | tf_op jit(solution)/shard_map/update/pallas_call | solution.py:784
  89.8 1.9 %collective-permute-done.18.refs_2_ = bf16[2,240,256]{2,1,0:T(8,128)(2,1)S(1)} collective-permute-done((bf16[2,240,256]{2,1,0:T(8,128)(2,1)S(1)}, bf16[2,240,256]{2,1,0:T(8,128)(2,1)S(1)}, u32[]{:S(2)}, u32[]{:S(2)}) %collective-permute-start.18) | collective-permute-done | bytes 245792 | tf_op jit(solution)/shard_map/ppermute | solution.py:130
  91.7 1.4 %collective-permute-done.19.refs_5_ = bf16[2,240,256]{2,1,0:T(8,128)(2,1)S(1)} collective-permute-done((bf16[2,240,256]{2,1,0:T(8,128)(2,1)S(1)}, bf16[2,240,256]{2,1,0:T(8,128)(2,1)S(1)}, u32[]{:S(2)}, u32[]{:S(2)}) %collective-permute-start.19) | collective-permute-done | bytes 245792 | tf_op jit(solution)/shard_map/ppermute | solution.py:130
  93.9 1.6 %collective-permute-start.20 = (bf16[4,240,256]{2,1,0:T(8,128)(2,1)S(1)}, bf16[4,240,256]{2,1,0:T(8,128)(2,1)S(1)}, u32[]{:S(2)}, u32[]{:S(2)}) collective-permute-start(bf16[4,240,256]{2,1,0:T(8,128)(2,1)S(1)} %pad_maximum_fusion), channel_id=1, source_target_pairs={{0,4},{4,0},{8,12},{12,8},{16,20},{20,16},{24,28},{28,24},{1,5},{5... | collective-permute-start | bytes 1474568 | tf_op jit(solution)/shard_map/ppermute | solution.py:130
  95.4 7.7 %collective-permute-done.21.refs_6_ = bf16[4,240,256]{2,1,0:T(8,128)(2,1)S(1)} collective-permute-done((bf16[4,240,256]{2,1,0:T(8,128)(2,1)S(1)}, bf16[4,240,256]{2,1,0:T(8,128)(2,1)S(1)}, u32[]{:S(2)}, u32[]{:S(2)}) %collective-permute-start.21) | collective-permute-done | bytes 491552 | tf_op jit(solution)/shard_map/ppermute | solution.py:130
  103.9 2.0 %place.1 = bf16[1920,512]{1,0:T(8,128)(2,1)} custom-call(s32[5]{0:T(128)S(1)} %copy-done.7, bf16[2,240,256]{2,1,0:T(8,128)(2,1)S(1)} %get-tuple-element.67.refs_1_, bf16[2,240,256]{2,1,0:T(8,128)(2,1)S(1)} %collective-permute-done.18.refs_2_, bf16[4,240,256]{2,1,0:T(8,128)(2,1)S(1)} %collective-permute-done.20.refs_3_, ...), custom_call_target="tpu_custom_call" | custom-call | tf_op jit(solution)/shard_map/place/pallas_call | solution.py:797
  (57 shorter events, 12.5 us)
Async XLA Ops:
  1.3 14.4 %copy-start = (bf16[2048,512]{1,0:T(8,128)(2,1)S(1)}, bf16[2048,512]{1,0:T(8,128)(2,1)}, u32[]{:S(2)}) copy-start(bf16[2048,512]{1,0:T(8,128)(2,1)} %refs_2_.4) | copy-start | bytes 6291460
  1.3 14.4 %copy-start.7 = (s32[5]{0:T(128)S(1)}, s32[5]{0:T(128)}, u32[]{:S(2)}) copy-start(s32[5]{0:T(128)} %stack.32.refs_0_.info) | copy-start | bytes 64
  1.3 14.5 %copy-start.10 = (s32[64]{0:T(128)S(1)}, s32[64]{0:T(128)}, u32[]{:S(2)}) copy-start(s32[64]{0:T(128)} %param.11) | copy-start | bytes 772
  11.2 20.6 %collective-permute-start.5 = (s16[4,256,256]{2,1,0:T(8,128)(2,1)}, s16[4,256,256]{2,1,0:T(8,128)(2,1)S(1)}, u32[]{:S(2)}, u32[]{:S(2)}) collective-permute-start(s16[4,256,256]{2,1,0:T(8,128)(2,1)} %get-tuple-element.49), channel_id=1, source_target_pairs={{0,4},{4,0},{8,12},{12,8},{16,20},{20,16},{24,28},{28,24},{1,5},{5... | collective-permute-start | bytes 1572872 | tf_op jit(solution)/shard_map/ppermute | solution.py:130
  14.2 21.4 %collective-permute-start.6 = (s16[4,256,256]{2,1,0:T(8,128)(2,1)}, s16[4,256,256]{2,1,0:T(8,128)(2,1)S(1)}, u32[]{:S(2)}, u32[]{:S(2)}) collective-permute-start(s16[4,256,256]{2,1,0:T(8,128)(2,1)} %get-tuple-element.52), channel_id=1, source_target_pairs={{0,8},{4,12},{8,0},{12,4},{16,24},{20,28},{24,16},{28,20},{1,9},{5... | collective-permute-start | bytes 1572872 | tf_op jit(solution)/shard_map/ppermute | solution.py:130
  15.8 5.9 %copy-start.1 = (f32[240,512]{1,0:T(8,128)S(1)}, f32[240,512]{1,0:T(8,128)}, u32[]{:S(2)}) copy-start(f32[240,512]{1,0:T(8,128)} %momentum.3) | copy-start | bytes 1474564
  15.8 16.0 %copy-start.4 = (f32[4,240,256]{2,1,0:T(8,128)S(1)}, f32[4,240,256]{2,1,0:T(8,128)}, u32[]{:S(2)}) copy-start(f32[4,240,256]{2,1,0:T(8,128)} %get-tuple-element.50.refs_2_) | copy-start | bytes 2949124
  19.0 16.6 %copy-start.3 = (f32[4,240,256]{2,1,0:T(8,128)S(1)}, f32[4,240,256]{2,1,0:T(8,128)}, u32[]{:S(2)}) copy-start(f32[4,240,256]{2,1,0:T(8,128)} %get-tuple-element.53.refs_2_) | copy-start | bytes 2949124
  19.0 12.2 %collective-permute-start = (bf16[64,1024]{1,0:T(8,128)(2,1)S(1)}, bf16[64,1024]{1,0:T(8,128)(2,1)S(1)}, u32[]{:S(2)}, u32[]{:S(2)}) collective-permute-start(bf16[64,1024]{1,0:T(8,128)(2,1)S(1)} %picks.1.refs_1_), channel_id=1, source_target_pairs={{0,16},{4,20},{8,24},{12,28},{16,0},{20,4},{24,8},{28,12},{1,17},{... | collective-permute-start | bytes 393224 | tf_op jit(solution)/shard_map/ppermute | solution.py:130
  22.0 17.7 %collective-permute-start.2 = (s16[272,512]{1,0:T(8,128)(2,1)S(1)}, s16[272,512]{1,0:T(8,128)(2,1)S(1)}, u32[]{:S(2)}, u32[]{:S(2)}) collective-permute-start(s16[272,512]{1,0:T(8,128)(2,1)S(1)} %base.1.refs_1_), channel_id=1, source_target_pairs={{0,16},{4,20},{8,24},{12,28},{16,0},{20,4},{24,8},{28,12},{1,17},{... | collective-permute-start | bytes 835592 | tf_op jit(solution)/shard_map/ppermute | solution.py:130
  31.2 8.5 %collective-permute-start.1 = (bf16[2,64,1024]{2,1,0:T(8,128)(2,1)S(1)}, bf16[2,64,1024]{2,1,0:T(8,128)(2,1)S(1)}, u32[]{:S(2)}, u32[]{:S(2)}) collective-permute-start(bf16[2,64,1024]{2,1,0:T(8,128)(2,1)S(1)} %pad_maximum_fusion.2), channel_id=1, source_target_pairs={{0,4},{4,0},{8,12},{12,8},{16,20},{20,16},{24,28},{28,24},{1,5},{5... | collective-permute-start | bytes 786440 | tf_op jit(solution)/shard_map/ppermute | solution.py:130
  36.5 17.2 %copy-start.5 = (f32[1,4,128,128]{3,2,1,0:T(8,128)S(1)}, f32[1,4,128,128]{3,2,1,0:T(8,128)}, u32[]{:S(2)}) copy-start(f32[1,4,128,128]{3,2,1,0:T(8,128)} %param.14) | copy-start | bytes 786436
  36.5 17.2 %copy-start.6 = (f32[1,5,96,96]{3,2,1,0:T(8,128)S(1)}, f32[1,5,96,96]{3,2,1,0:T(8,128)}, u32[]{:S(2)}) copy-start(f32[1,5,96,96]{3,2,1,0:T(8,128)} %param.15) | copy-start | bytes 552964
  36.6 17.2 %copy-start.8 = (s32[4,4]{1,0:T(4,128)S(1)}, s32[4,4]{1,0:T(4,128)}, u32[]{:S(2)}) copy-start(s32[4,4]{1,0:T(4,128)} %refs_1_.3) | copy-start | bytes 196
  36.6 17.2 %copy-start.9 = (s32[4,5]{1,0:T(4,128)S(1)}, s32[4,5]{1,0:T(4,128)}, u32[]{:S(2)}) copy-start(s32[4,5]{1,0:T(4,128)} %refs_2_.5) | copy-start | bytes 244
  36.6 9.3 %collective-permute-start.7 = (s16[2,256,256]{2,1,0:T(8,128)(2,1)S(1)}, s16[2,256,256]{2,1,0:T(8,128)(2,1)S(1)}, u32[]{:S(2)}, u32[]{:S(2)}) collective-permute-start(s16[2,256,256]{2,1,0:T(8,128)(2,1)S(1)} %get-tuple-element.55), channel_id=1, source_target_pairs={{0,8},{4,12},{8,0},{12,4},{16,24},{20,28},{24,16},{28,20},{1,9},{5... | collective-permute-start | bytes 786440 | tf_op jit(solution)/shard_map/ppermute | solution.py:130
  37.4 8.5 %collective-permute-start.8 = (s16[2,256,256]{2,1,0:T(8,128)(2,1)S(1)}, s16[2,256,256]{2,1,0:T(8,128)(2,1)S(1)}, u32[]{:S(2)}, u32[]{:S(2)}) collective-permute-start(s16[2,256,256]{2,1,0:T(8,128)(2,1)S(1)} %get-tuple-element.57), channel_id=1, source_target_pairs={{0,4},{4,0},{8,12},{12,8},{16,20},{20,16},{24,28},{28,24},{1,5},{5... | collective-permute-start | bytes 786440 | tf_op jit(solution)/shard_map/ppermute | solution.py:130
  40.9 12.8 %collective-permute-start.3 = (s16[1136,128]{1,0:T(8,128)(2,1)S(1)}, s16[1136,128]{1,0:T(8,128)(2,1)S(1)}, u32[]{:S(2)}, u32[]{:S(2)}) collective-permute-start(s16[1136,128]{1,0:T(8,128)(2,1)S(1)} %stats.1.refs_3_), channel_id=1, source_target_pairs={{0,8},{4,12},{8,0},{12,4},{16,24},{20,28},{24,16},{28,20},{1,9},{5... | collective-permute-start | bytes 872456 | tf_op jit(solution)/shard_map/ppermute | solution.py:130
  46.8 12.1 %collective-permute-start.9 = (s16[2,256,256]{2,1,0:T(8,128)(2,1)S(1)}, s16[2,256,256]{2,1,0:T(8,128)(2,1)S(1)}, u32[]{:S(2)}, u32[]{:S(2)}) collective-permute-start(s16[2,256,256]{2,1,0:T(8,128)(2,1)S(1)} %get-tuple-element.59), channel_id=1, source_target_pairs={{0,16},{4,20},{8,24},{12,28},{16,0},{20,4},{24,8},{28,12},{1,17},{... | collective-permute-start | bytes 786440 | tf_op jit(solution)/shard_map/ppermute | solution.py:130
  48.3 4.3 %collective-permute-start.4 = (s16[2,64,256]{2,1,0:T(8,128)(2,1)S(1)}, s16[2,64,256]{2,1,0:T(8,128)(2,1)S(1)}, u32[]{:S(2)}, u32[]{:S(2)}) collective-permute-start(s16[2,64,256]{2,1,0:T(8,128)(2,1)S(1)} %sides.1), channel_id=1, source_target_pairs={{0,4},{4,0},{8,12},{12,8},{16,20},{20,16},{24,28},{28,24},{1,5},{5... | collective-permute-start | bytes 196616 | tf_op jit(solution)/shard_map/ppermute | solution.py:130
  58.0 0.9 collective-permute-start.10
  60.8 14.9 %collective-permute-start.11 = (f32[56,256]{1,0:T(8,128)S(1)}, f32[56,256]{1,0:T(8,128)S(1)}, u32[]{:S(2)}, u32[]{:S(2)}) collective-permute-start(f32[56,256]{1,0:T(8,128)S(1)} %pad_maximum_fusion.3), channel_id=1, source_target_pairs={{0,4},{4,0},{8,12},{12,8},{16,20},{20,16},{24,28},{28,24},{1,5},{5... | collective-permute-start | bytes 172040 | tf_op jit(solution)/shard_map/ppermute | solution.py:130
  61.8 23.3 %collective-permute-start.17 = (s16[272,512]{1,0:T(8,128)(2,1)S(1)}, s16[272,512]{1,0:T(8,128)(2,1)S(1)}, u32[]{:S(2)}, u32[]{:S(2)}) collective-permute-start(s16[272,512]{1,0:T(8,128)(2,1)S(1)} %get-tuple-element.66.refs_3_), channel_id=1, source_target_pairs={{0,16},{4,20},{8,24},{12,28},{16,0},{20,4},{24,8},{28,12},{1,17},{... | collective-permute-start | bytes 835592 | tf_op jit(solution)/shard_map/ppermute | solution.py:130
  70.6 3.7 %collective-permute-start.12 = (f32[8,256]{1,0:T(8,128)S(1)}, f32[8,256]{1,0:T(8,128)S(1)}, u32[]{:S(2)}, u32[]{:S(2)}) collective-permute-start(f32[8,256]{1,0:T(8,128)S(1)} %get-tuple-element.63), channel_id=1, source_target_pairs={{0,2},{1,3},{2,0},{3,1},{4,6},{5,7},{6,4},{7,5},{8,10},{9,11},{10,... | collective-permute-start | bytes 24584 | tf_op jit(solution)/shard_map/ppermute | solution.py:134
  71.1 4.5 %collective-permute-start.13 = (f32[8,256]{1,0:T(8,128)S(1)}, f32[8,256]{1,0:T(8,128)S(1)}, u32[]{:S(2)}, u32[]{:S(2)}) collective-permute-start(f32[8,256]{1,0:T(8,128)S(1)} %get-tuple-element.63), channel_id=1, source_target_pairs={{0,6},{1,7},{2,4},{3,5},{4,2},{5,3},{6,0},{7,1},{8,14},{9,15},{10,... | collective-permute-start | bytes 24584 | tf_op jit(solution)/shard_map/ppermute | solution.py:139
  75.7 1.2 %collective-permute-start.14 = (f32[8,256]{1,0:T(8,128)S(1)}, f32[8,256]{1,0:T(8,128)S(1)}, u32[]{:S(2)}, u32[]{:S(2)}) collective-permute-start(f32[8,256]{1,0:T(8,128)S(1)} %fusion), channel_id=1, source_target_pairs={{0,1},{1,0},{2,3},{3,2},{4,5},{5,4},{6,7},{7,6},{8,9},{9,8},{10,11... | collective-permute-start | bytes 24584 | tf_op jit(solution)/shard_map/ppermute | solution.py:134
  77.0 4.6 %collective-permute-start.15 = (f32[8,256]{1,0:T(8,128)S(1)}, f32[8,256]{1,0:T(8,128)S(1)}, u32[]{:S(2)}, u32[]{:S(2)}) collective-permute-start(f32[8,256]{1,0:T(8,128)S(1)} %add.20), channel_id=1, source_target_pairs={{0,16},{4,20},{8,24},{12,28},{16,0},{20,4},{24,8},{28,12},{1,17},{... | collective-permute-start | bytes 24584 | tf_op jit(solution)/shard_map/ppermute | solution.py:130
  81.5 3.7 %collective-permute-start.16 = (f32[8,256]{1,0:T(8,128)S(1)}, f32[8,256]{1,0:T(8,128)S(1)}, u32[]{:S(2)}, u32[]{:S(2)}) collective-permute-start(f32[8,256]{1,0:T(8,128)S(1)} %add.21.refs_0_), channel_id=1, source_target_pairs={{0,8},{4,12},{8,0},{12,4},{16,24},{20,28},{24,16},{28,20},{1,9},{5... | collective-permute-start | bytes 24584 | tf_op jit(solution)/shard_map/ppermute | solution.py:130
  85.4 6.3 %collective-permute-start.18 = (bf16[2,240,256]{2,1,0:T(8,128)(2,1)S(1)}, bf16[2,240,256]{2,1,0:T(8,128)(2,1)S(1)}, u32[]{:S(2)}, u32[]{:S(2)}) collective-permute-start(bf16[2,240,256]{2,1,0:T(8,128)(2,1)S(1)} %get-tuple-element.67.refs_1_), channel_id=1, source_target_pairs={{0,8},{4,12},{8,0},{12,4},{16,24},{20,28},{24,16},{28,20},{1,9},{5... | collective-permute-start | bytes 737288 | tf_op jit(solution)/shard_map/ppermute | solution.py:130
  86.9 6.2 %collective-permute-start.19 = (bf16[2,240,256]{2,1,0:T(8,128)(2,1)S(1)}, bf16[2,240,256]{2,1,0:T(8,128)(2,1)S(1)}, u32[]{:S(2)}, u32[]{:S(2)}) collective-permute-start(bf16[2,240,256]{2,1,0:T(8,128)(2,1)S(1)} %get-tuple-element.68.refs_4_), channel_id=1, source_target_pairs={{0,4},{4,0},{8,12},{12,8},{16,20},{20,16},{24,28},{28,24},{1,5},{5... | collective-permute-start | bytes 737288 | tf_op jit(solution)/shard_map/ppermute | solution.py:130
  93.1 10.0 %collective-permute-start.21 = (bf16[4,240,256]{2,1,0:T(8,128)(2,1)S(1)}, bf16[4,240,256]{2,1,0:T(8,128)(2,1)S(1)}, u32[]{:S(2)}, u32[]{:S(2)}) collective-permute-start(bf16[4,240,256]{2,1,0:T(8,128)(2,1)S(1)} %pad_maximum_fusion.1), channel_id=1, source_target_pairs={{0,8},{4,12},{8,0},{12,4},{16,24},{20,28},{24,16},{28,20},{1,9},{5... | collective-permute-start | bytes 1474568 | tf_op jit(solution)/shard_map/ppermute | solution.py:130
  93.9 10.1 %collective-permute-start.20 = (bf16[4,240,256]{2,1,0:T(8,128)(2,1)S(1)}, bf16[4,240,256]{2,1,0:T(8,128)(2,1)S(1)}, u32[]{:S(2)}, u32[]{:S(2)}) collective-permute-start(bf16[4,240,256]{2,1,0:T(8,128)(2,1)S(1)} %pad_maximum_fusion), channel_id=1, source_target_pairs={{0,4},{4,0},{8,12},{12,8},{16,20},{20,16},{24,28},{28,24},{1,5},{5... | collective-permute-start | bytes 1474568 | tf_op jit(solution)/shard_map/ppermute | solution.py:130
  (1 other events, 5.9 us)

commit v9 on v8

--- a/solution.py
+++ b/solution.py
@@ -737,7 +737,7 @@
         name="factors",
     )(info, own_a, own_g, packed, got_packed, a_state[0], g_state[0])
     route = [
-        ((2 * a + b) * 4 + c, (2 * c + b) * 4 + a)
+        ((2 * a + b) * 4 + c, (2 * c + b) * 4 + (a ^ 2))
         for a in range(4)
         for b in range(2)
         for c in range(4)

time: 106 us -> 105 us (level)
  starting transfers between devices: 38.6 us -> 28.7 us
  waiting for transfers between devices: 37.2 us -> 45.5 us
    ppermute x18, starting transfers between devices: 34.2 us -> 23.9 us  [swap(): return lax.ppermute(value, 'shard', [(i, i ^ bit) for i in range(8)])]
    ppermute x1, waiting for transfers between devices: 0.01 us -> 4.98 us  [fast(): inv_rows = lax.ppermute(needed, ('shard', 'tensor'), route)]
    ppermute x18, waiting for transfers between devices: 34.3 us -> 36.1 us  [swap(): return lax.ppermute(value, 'shard', [(i, i ^ bit) for i in range(8)])]
    ppermute x1, starting transfers between devices: 2.85 us -> 1.27 us  [swap_both(): return lax.ppermute(value, ('shard', 'tensor'), route)]
    ppermute x2, starting transfers between devices: 0.63 us -> 2.13 us  [swap_t(): return lax.ppermute(value, 'tensor', [(i, i ^ bit) for i in range(4)])]
    ppermute x1, waiting for transfers between devices: 1.46 us -> 2.92 us  [swap_both(): return lax.ppermute(value, ('shard', 'tensor'), route)]
where the time goes in v9:
time: 105 us; the launch traced here: 104 us
  waiting for transfers between devices  45.5 us (43%)
  starting transfers between devices  28.7 us (27%)
  Pallas kernels  28.5 us (27%)
    ppermute x18, waiting for transfers between devices, swap(): return lax.ppermute(value, 'shard', [(i, i ^ bit) for i in range(8)])  36.1 us
    ppermute x18, starting transfers between devices, swap(): return lax.ppermute(value, 'shard', [(i, i ^ bit) for i in range(8)])  23.9 us
    pallas_call x1, Pallas kernels, fast(): pl.pallas_call(lambda *refs: partial_kernel(group_cols, width_g, *refs),...  9.85 us
    ppermute x1, waiting for transfers between devices, fast(): inv_rows = lax.ppermute(needed, ('shard', 'tensor'), route)  4.98 us
    pallas_call x1, Pallas kernels, fast(): pl.pallas_call(lambda *refs: factor_kernel(share, blocks, *refs), in_spec...  4.24 us
    pallas_call x1, Pallas kernels, fast(): pl.pallas_call(lambda *refs: picks_kernel(group_cols, *refs), in_specs=[s...  3.15 us
    ppermute x1, waiting for transfers between devices, swap_both(): return lax.ppermute(value, ('shard', 'tensor'), route)  2.92 us
    ppermute x2, starting transfers between devices, swap_t(): return lax.ppermute(value, 'tensor', [(i, i ^ bit) for i in range(4)])  2.13 us
  transfers between devices with their start and end apart: 22, of which 16 were waited for; matrix products, arithmetic and copies ran while one was open for 0% of the time, Pallas kernels for 14%

profile of v9, /device:TPU:0, one launch (start us, length us, event | category | flops | bytes accessed | tf_op | source)
XLA Modules:
  0.0 104.4 jit_solution(16426733304827148146)
XLA Ops:
  1.3 9.9 %partial.1 = (s16[4,256,256]{2,1,0:T(8,128)(2,1)}, f32[4,240,256]{2,1,0:T(8,128)}, s16[4,256,256]{2,1,0:T(8,128)(2,1)}, f32[4,240,256]{2,1,0:T(8,128)}) custom-call(s32[5]{0:T(128)} %stack.32.refs_0_.info, bf16[2048,1920]{1,0:T(8,128)(2,1)} %refs_3_.1, bf16[2048,512]{1,0:T(8,128)(2,1)} %refs_2_.4), custom_call_target="tpu_custom_call" | custom-call | tf_op jit(solution)/shard_map/partial/pallas_call | solution.py:627
  11.2 3.0 %collective-permute-start.5 = (s16[4,256,256]{2,1,0:T(8,128)(2,1)}, s16[4,256,256]{2,1,0:T(8,128)(2,1)S(1)}, u32[]{:S(2)}, u32[]{:S(2)}) collective-permute-start(s16[4,256,256]{2,1,0:T(8,128)(2,1)} %get-tuple-element.49), channel_id=1, source_target_pairs={{0,4},{4,0},{8,12},{12,8},{16,20},{20,16},{24,28},{28,24},{1,5},{5... | collective-permute-start | bytes 1572872 | tf_op jit(solution)/shard_map/ppermute | solution.py:130
  14.2 1.6 %collective-permute-start.6 = (s16[4,256,256]{2,1,0:T(8,128)(2,1)}, s16[4,256,256]{2,1,0:T(8,128)(2,1)S(1)}, u32[]{:S(2)}, u32[]{:S(2)}) collective-permute-start(s16[4,256,256]{2,1,0:T(8,128)(2,1)} %get-tuple-element.52), channel_id=1, source_target_pairs={{0,8},{4,12},{8,0},{12,4},{16,24},{20,28},{24,16},{28,20},{1,9},{5... | collective-permute-start | bytes 1572872 | tf_op jit(solution)/shard_map/ppermute | solution.py:130
  15.8 3.2 %picks.1.refs_1_ = bf16[64,1024]{1,0:T(8,128)(2,1)S(1)} custom-call(s32[5]{0:T(128)S(1)} %copy-done.7, s32[1,64]{1,0:T(1,128)S(1)} %bitcast.16, bf16[2048,512]{1,0:T(8,128)(2,1)S(1)} %copy-done, bf16[2048,1920]{1,0:T(8,128)(2,1)} %refs_3_.1), custom_call_target="tpu_custom_call" | custom-call | tf_op jit(solution)/shard_map/picks/pallas_call | solution.py:650
  19.0 2.7 %collective-permute-start = (bf16[64,1024]{1,0:T(8,128)(2,1)S(1)}, bf16[64,1024]{1,0:T(8,128)(2,1)S(1)}, u32[]{:S(2)}, u32[]{:S(2)}) collective-permute-start(bf16[64,1024]{1,0:T(8,128)(2,1)S(1)} %picks.1.refs_1_), channel_id=1, source_target_pairs={{0,16},{4,20},{8,24},{12,28},{16,0},{20,4},{24,8},{28,12},{1,17},{... | collective-permute-start | bytes 393224 | tf_op jit(solution)/shard_map/ppermute | solution.py:130
  22.4 8.8 %collective-permute-done.refs_2_ = bf16[64,1024]{1,0:T(8,128)(2,1)S(1)} collective-permute-done((bf16[64,1024]{1,0:T(8,128)(2,1)S(1)}, bf16[64,1024]{1,0:T(8,128)(2,1)S(1)}, u32[]{:S(2)}, u32[]{:S(2)}) %collective-permute-start) | collective-permute-done | bytes 131104 | tf_op jit(solution)/shard_map/ppermute | solution.py:130
  32.8 2.8 %collective-permute-done.6.refs_1_ = s16[4,256,256]{2,1,0:T(8,128)(2,1)S(1)} collective-permute-done((s16[4,256,256]{2,1,0:T(8,128)(2,1)}, s16[4,256,256]{2,1,0:T(8,128)(2,1)S(1)}, u32[]{:S(2)}, u32[]{:S(2)}) %collective-permute-start.6) | collective-permute-done | bytes 524320 | tf_op jit(solution)/shard_map/ppermute | solution.py:130
  37.4 1.5 %collective-permute-start.8 = (s16[2,256,256]{2,1,0:T(8,128)(2,1)S(1)}, s16[2,256,256]{2,1,0:T(8,128)(2,1)S(1)}, u32[]{:S(2)}, u32[]{:S(2)}) collective-permute-start(s16[2,256,256]{2,1,0:T(8,128)(2,1)S(1)} %get-tuple-element.57), channel_id=1, source_target_pairs={{0,4},{4,0},{8,12},{12,8},{16,20},{20,16},{24,28},{28,24},{1,5},{5... | collective-permute-start | bytes 786440 | tf_op jit(solution)/shard_map/ppermute | solution.py:130
  39.8 1.1 %stats.1.refs_3_ = s16[1136,128]{1,0:T(8,128)(2,1)S(1)} custom-call(s32[5]{0:T(128)S(1)} %copy-done.7, bf16[64,1024]{1,0:T(8,128)(2,1)S(1)} %picks.1.refs_1_, bf16[64,1024]{1,0:T(8,128)(2,1)S(1)} %collective-permute-done.refs_2_, bf16[2,64,1024]{2,1,0:T(8,128)(2,1)S(1)} %collective-permute-done.1.refs_3_), custom_call_target="tpu_custom_call" | custom-call | tf_op jit(solution)/shard_map/stats/pallas_call | solution.py:683
  40.9 3.1 %collective-permute-start.3 = (s16[1136,128]{1,0:T(8,128)(2,1)S(1)}, s16[1136,128]{1,0:T(8,128)(2,1)S(1)}, u32[]{:S(2)}, u32[]{:S(2)}) collective-permute-start(s16[1136,128]{1,0:T(8,128)(2,1)S(1)} %stats.1.refs_3_), channel_id=1, source_target_pairs={{0,8},{4,12},{8,0},{12,4},{16,24},{20,28},{24,16},{28,20},{1,9},{5... | collective-permute-start | bytes 872456 | tf_op jit(solution)/shard_map/ppermute | solution.py:130
  44.0 1.9 %collective-permute-done.7.got_a = s16[2,256,256]{2,1,0:T(8,128)(2,1)S(1)} collective-permute-done((s16[2,256,256]{2,1,0:T(8,128)(2,1)S(1)}, s16[2,256,256]{2,1,0:T(8,128)(2,1)S(1)}, u32[]{:S(2)}, u32[]{:S(2)}) %collective-permute-start.7) | collective-permute-done | bytes 262176 | tf_op jit(solution)/shard_map/ppermute | solution.py:130
  48.9 3.8 %collective-permute-done.4.refs_3_ = s16[2,64,256]{2,1,0:T(8,128)(2,1)S(1)} collective-permute-done((s16[2,64,256]{2,1,0:T(8,128)(2,1)S(1)}, s16[2,64,256]{2,1,0:T(8,128)(2,1)S(1)}, u32[]{:S(2)}, u32[]{:S(2)}) %collective-permute-start.4) | collective-permute-done | bytes 65568 | tf_op jit(solution)/shard_map/ppermute | solution.py:130
  53.8 4.2 %factors.1 = (f32[4,128,128]{2,1,0:T(8,128)}, f32[5,96,96]{2,1,0:T(8,128)}, f32[4,128,128]{2,1,0:T(8,128)S(1)}, s16[3,112,96]{2,1,0:T(8,128)(2,1)S(1)}) custom-call(s32[5]{0:T(128)S(1)} %copy-done.7, s32[4,4]{1,0:T(4,128)S(1)} %copy-done.8, s32[4,5]{1,0:T(4,128)S(1)} %copy-done.9, s16[1136,128]{1,0:T(8,128)(2,1)S(1)} %stats.1.refs_3_, ...), custom_call_target="tpu_custom_call" | custom-call | tf_op jit(solution)/shard_map/factors/pallas_call | solution.py:725
  58.0 1.4 %collective-permute-start.10 = (s16[3,112,96]{2,1,0:T(8,128)(2,1)S(1)}, s16[3,112,96]{2,1,0:T(8,128)(2,1)S(1)}, u32[]{:S(2)}, u32[]{:S(2)}) collective-permute-start(s16[3,112,96]{2,1,0:T(8,128)(2,1)S(1)} %get-tuple-element.61), channel_id=1, source_target_pairs={{0,2},{1,10},{2,18},{3,26},{4,6},{5,14},{6,22},{7,30},{8,3},{9,11}... | collective-permute-start | bytes 193544 | tf_op jit(solution)/shard_map/ppermute | solution.py:745
  59.4 5.0 %collective-permute-done.10.inv_g = s16[3,112,96]{2,1,0:T(8,128)(2,1)S(1)} collective-permute-done((s16[3,112,96]{2,1,0:T(8,128)(2,1)S(1)}, s16[3,112,96]{2,1,0:T(8,128)(2,1)S(1)}, u32[]{:S(2)}, u32[]{:S(2)}) %collective-permute-start.10) | collective-permute-done | bytes 64544 | tf_op jit(solution)/shard_map/ppermute | solution.py:745
  64.4 1.8 %precon.1 = (f32[192,512]{1,0:T(8,128)S(1)}, f32[96,256]{1,0:T(8,128)S(1)}, f32[8,256]{1,0:T(8,128)S(1)}, s16[272,512]{1,0:T(8,128)(2,1)S(1)}) custom-call(s32[5]{0:T(128)S(1)} %copy-done.7, s16[2,256,256]{2,1,0:T(8,128)(2,1)S(1)} %collective-permute-done.9.got, f32[2,240,256]{2,1,0:T(8,128)S(1)} %get-tuple-element.60.held, ...), custom_call_target="tpu_custom_call" | custom-call | tf_op jit(solution)/shard_map/precon/pallas_call | solution.py:747
  66.3 1.0 collective-permute-start.11
  67.4 2.1 %collective-permute-start.12 = (f32[8,256]{1,0:T(8,128)S(1)}, f32[8,256]{1,0:T(8,128)S(1)}, u32[]{:S(2)}, u32[]{:S(2)}) collective-permute-start(f32[8,256]{1,0:T(8,128)S(1)} %get-tuple-element.63), channel_id=1, source_target_pairs={{0,2},{1,3},{2,0},{3,1},{4,6},{5,7},{6,4},{7,5},{8,10},{9,11},{10,... | collective-permute-start | bytes 24584 | tf_op jit(solution)/shard_map/ppermute | solution.py:134
  69.4 1.3 %collective-permute-start.13 = (f32[8,256]{1,0:T(8,128)S(1)}, f32[8,256]{1,0:T(8,128)S(1)}, u32[]{:S(2)}, u32[]{:S(2)}) collective-permute-start(f32[8,256]{1,0:T(8,128)S(1)} %get-tuple-element.63), channel_id=1, source_target_pairs={{0,6},{1,7},{2,4},{3,5},{4,2},{5,3},{6,0},{7,1},{8,14},{9,15},{10,... | collective-permute-start | bytes 24584 | tf_op jit(solution)/shard_map/ppermute | solution.py:139
  71.1 2.9 %collective-permute-done.13 = f32[8,256]{1,0:T(8,128)S(1)} collective-permute-done((f32[8,256]{1,0:T(8,128)S(1)}, f32[8,256]{1,0:T(8,128)S(1)}, u32[]{:S(2)}, u32[]{:S(2)}) %collective-permute-start.13) | collective-permute-done | bytes 8224 | tf_op jit(solution)/shard_map/ppermute | solution.py:139
  74.1 1.2 %collective-permute-done.14 = f32[8,256]{1,0:T(8,128)S(1)} collective-permute-done((f32[8,256]{1,0:T(8,128)S(1)}, f32[8,256]{1,0:T(8,128)S(1)}, u32[]{:S(2)}, u32[]{:S(2)}) %collective-permute-start.14) | collective-permute-done | bytes 8224 | tf_op jit(solution)/shard_map/ppermute | solution.py:134
  76.0 3.8 %collective-permute-done.15 = f32[8,256]{1,0:T(8,128)S(1)} collective-permute-done((f32[8,256]{1,0:T(8,128)S(1)}, f32[8,256]{1,0:T(8,128)S(1)}, u32[]{:S(2)}, u32[]{:S(2)}) %collective-permute-start.15) | collective-permute-done | bytes 8224 | tf_op jit(solution)/shard_map/ppermute | solution.py:130
  79.8 1.9 %collective-permute-start.16 = (f32[8,256]{1,0:T(8,128)S(1)}, f32[8,256]{1,0:T(8,128)S(1)}, u32[]{:S(2)}, u32[]{:S(2)}) collective-permute-start(f32[8,256]{1,0:T(8,128)S(1)} %add.21.refs_0_), channel_id=1, source_target_pairs={{0,8},{4,12},{8,0},{12,4},{16,24},{20,28},{24,16},{28,20},{1,9},{5... | collective-permute-start | bytes 24584 | tf_op jit(solution)/shard_map/ppermute | solution.py:130
  81.7 1.7 %collective-permute-done.16.refs_1_ = f32[8,256]{1,0:T(8,128)S(1)} collective-permute-done((f32[8,256]{1,0:T(8,128)S(1)}, f32[8,256]{1,0:T(8,128)S(1)}, u32[]{:S(2)}, u32[]{:S(2)}) %collective-permute-start.16) | collective-permute-done | bytes 8224 | tf_op jit(solution)/shard_map/ppermute | solution.py:130
  83.7 2.0 %collective-permute-start.18 = (bf16[2,240,256]{2,1,0:T(8,128)(2,1)S(1)}, bf16[2,240,256]{2,1,0:T(8,128)(2,1)S(1)}, u32[]{:S(2)}, u32[]{:S(2)}) collective-permute-start(bf16[2,240,256]{2,1,0:T(8,128)(2,1)S(1)} %get-tuple-element.67.refs_1_), channel_id=1, source_target_pairs={{0,8},{4,12},{8,0},{12,4},{16,24},{20,28},{24,16},{28,20},{1,9},{5... | collective-permute-start | bytes 737288 | tf_op jit(solution)/shard_map/ppermute | solution.py:130
  85.7 1.3 %collective-permute-start.19 = (bf16[2,240,256]{2,1,0:T(8,128)(2,1)S(1)}, bf16[2,240,256]{2,1,0:T(8,128)(2,1)S(1)}, u32[]{:S(2)}, u32[]{:S(2)}) collective-permute-start(bf16[2,240,256]{2,1,0:T(8,128)(2,1)S(1)} %get-tuple-element.68.refs_4_), channel_id=1, source_target_pairs={{0,4},{4,0},{8,12},{12,8},{16,20},{20,16},{24,28},{28,24},{1,5},{5... | collective-permute-start | bytes 737288 | tf_op jit(solution)/shard_map/ppermute | solution.py:130
  86.9 1.6 %update.1 = (f32[240,512]{1,0:T(8,128)}, f32[240,512]{1,0:T(8,128)}) custom-call(s32[5]{0:T(128)S(1)} %copy-done.7, f32[8,512]{1,0:T(8,128)S(1)} %get-tuple-element.69.factor, f32[192,512]{1,0:T(8,128)S(1)} %get-tuple-element.70.top, f32[96,256]{1,0:T(8,128)S(1)} %get-tuple-element.64.middle, f32[56,256]{1,0:T(8,128)S(1)} %collective-permute-done.11.got, ...), custom_call_target="tpu_custom_call" | custom-call | tf_op jit(solution)/shard_map/update/pallas_call | solution.py:784
  88.6 1.4 %collective-permute-done.18.refs_2_ = bf16[2,240,256]{2,1,0:T(8,128)(2,1)S(1)} collective-permute-done((bf16[2,240,256]{2,1,0:T(8,128)(2,1)S(1)}, bf16[2,240,256]{2,1,0:T(8,128)(2,1)S(1)}, u32[]{:S(2)}, u32[]{:S(2)}) %collective-permute-start.18) | collective-permute-done | bytes 245792 | tf_op jit(solution)/shard_map/ppermute | solution.py:130
  90.0 2.3 %collective-permute-done.19.refs_5_ = bf16[2,240,256]{2,1,0:T(8,128)(2,1)S(1)} collective-permute-done((bf16[2,240,256]{2,1,0:T(8,128)(2,1)S(1)}, bf16[2,240,256]{2,1,0:T(8,128)(2,1)S(1)}, u32[]{:S(2)}, u32[]{:S(2)}) %collective-permute-start.19) | collective-permute-done | bytes 245792 | tf_op jit(solution)/shard_map/ppermute | solution.py:130
  92.4 1.7 %collective-permute-start.20 = (bf16[4,240,256]{2,1,0:T(8,128)(2,1)S(1)}, bf16[4,240,256]{2,1,0:T(8,128)(2,1)S(1)}, u32[]{:S(2)}, u32[]{:S(2)}) collective-permute-start(bf16[4,240,256]{2,1,0:T(8,128)(2,1)S(1)} %pad_maximum_fusion), channel_id=1, source_target_pairs={{0,4},{4,0},{8,12},{12,8},{16,20},{20,16},{24,28},{28,24},{1,5},{5... | collective-permute-start | bytes 1474568 | tf_op jit(solution)/shard_map/ppermute | solution.py:130
  94.1 7.7 %collective-permute-done.21.refs_6_ = bf16[4,240,256]{2,1,0:T(8,128)(2,1)S(1)} collective-permute-done((bf16[4,240,256]{2,1,0:T(8,128)(2,1)S(1)}, bf16[4,240,256]{2,1,0:T(8,128)(2,1)S(1)}, u32[]{:S(2)}, u32[]{:S(2)}) %collective-permute-start.21) | collective-permute-done | bytes 491552 | tf_op jit(solution)/shard_map/ppermute | solution.py:130
  102.4 2.0 %place.1 = bf16[1920,512]{1,0:T(8,128)(2,1)} custom-call(s32[5]{0:T(128)S(1)} %copy-done.7, bf16[2,240,256]{2,1,0:T(8,128)(2,1)S(1)} %get-tuple-element.67.refs_1_, bf16[2,240,256]{2,1,0:T(8,128)(2,1)S(1)} %collective-permute-done.18.refs_2_, bf16[4,240,256]{2,1,0:T(8,128)(2,1)S(1)} %collective-permute-done.20.refs_3_, ...), custom_call_target="tpu_custom_call" | custom-call | tf_op jit(solution)/shard_map/place/pallas_call | solution.py:797
  (57 shorter events, 12.0 us)
Async XLA Ops:
  1.3 14.4 %copy-start = (bf16[2048,512]{1,0:T(8,128)(2,1)S(1)}, bf16[2048,512]{1,0:T(8,128)(2,1)}, u32[]{:S(2)}) copy-start(bf16[2048,512]{1,0:T(8,128)(2,1)} %refs_2_.4) | copy-start | bytes 6291460
  1.3 14.4 %copy-start.7 = (s32[5]{0:T(128)S(1)}, s32[5]{0:T(128)}, u32[]{:S(2)}) copy-start(s32[5]{0:T(128)} %stack.32.refs_0_.info) | copy-start | bytes 64
  1.3 14.5 %copy-start.10 = (s32[64]{0:T(128)S(1)}, s32[64]{0:T(128)}, u32[]{:S(2)}) copy-start(s32[64]{0:T(128)} %param.11) | copy-start | bytes 772
  11.2 20.6 %collective-permute-start.5 = (s16[4,256,256]{2,1,0:T(8,128)(2,1)}, s16[4,256,256]{2,1,0:T(8,128)(2,1)S(1)}, u32[]{:S(2)}, u32[]{:S(2)}) collective-permute-start(s16[4,256,256]{2,1,0:T(8,128)(2,1)} %get-tuple-element.49), channel_id=1, source_target_pairs={{0,4},{4,0},{8,12},{12,8},{16,20},{20,16},{24,28},{28,24},{1,5},{5... | collective-permute-start | bytes 1572872 | tf_op jit(solution)/shard_map/ppermute | solution.py:130
  14.2 21.4 %collective-permute-start.6 = (s16[4,256,256]{2,1,0:T(8,128)(2,1)}, s16[4,256,256]{2,1,0:T(8,128)(2,1)S(1)}, u32[]{:S(2)}, u32[]{:S(2)}) collective-permute-start(s16[4,256,256]{2,1,0:T(8,128)(2,1)} %get-tuple-element.52), channel_id=1, source_target_pairs={{0,8},{4,12},{8,0},{12,4},{16,24},{20,28},{24,16},{28,20},{1,9},{5... | collective-permute-start | bytes 1572872 | tf_op jit(solution)/shard_map/ppermute | solution.py:130
  15.8 5.9 %copy-start.1 = (f32[240,512]{1,0:T(8,128)S(1)}, f32[240,512]{1,0:T(8,128)}, u32[]{:S(2)}) copy-start(f32[240,512]{1,0:T(8,128)} %momentum.3) | copy-start | bytes 1474564
  15.8 16.0 %copy-start.4 = (f32[4,240,256]{2,1,0:T(8,128)S(1)}, f32[4,240,256]{2,1,0:T(8,128)}, u32[]{:S(2)}) copy-start(f32[4,240,256]{2,1,0:T(8,128)} %get-tuple-element.50.refs_2_) | copy-start | bytes 2949124
  19.0 16.6 %copy-start.3 = (f32[4,240,256]{2,1,0:T(8,128)S(1)}, f32[4,240,256]{2,1,0:T(8,128)}, u32[]{:S(2)}) copy-start(f32[4,240,256]{2,1,0:T(8,128)} %get-tuple-element.53.refs_2_) | copy-start | bytes 2949124
  19.0 12.2 %collective-permute-start = (bf16[64,1024]{1,0:T(8,128)(2,1)S(1)}, bf16[64,1024]{1,0:T(8,128)(2,1)S(1)}, u32[]{:S(2)}, u32[]{:S(2)}) collective-permute-start(bf16[64,1024]{1,0:T(8,128)(2,1)S(1)} %picks.1.refs_1_), channel_id=1, source_target_pairs={{0,16},{4,20},{8,24},{12,28},{16,0},{20,4},{24,8},{28,12},{1,17},{... | collective-permute-start | bytes 393224 | tf_op jit(solution)/shard_map/ppermute | solution.py:130
  22.0 17.7 %collective-permute-start.2 = (s16[272,512]{1,0:T(8,128)(2,1)S(1)}, s16[272,512]{1,0:T(8,128)(2,1)S(1)}, u32[]{:S(2)}, u32[]{:S(2)}) collective-permute-start(s16[272,512]{1,0:T(8,128)(2,1)S(1)} %base.1.refs_1_), channel_id=1, source_target_pairs={{0,16},{4,20},{8,24},{12,28},{16,0},{20,4},{24,8},{28,12},{1,17},{... | collective-permute-start | bytes 835592 | tf_op jit(solution)/shard_map/ppermute | solution.py:130
  31.2 8.5 %collective-permute-start.1 = (bf16[2,64,1024]{2,1,0:T(8,128)(2,1)S(1)}, bf16[2,64,1024]{2,1,0:T(8,128)(2,1)S(1)}, u32[]{:S(2)}, u32[]{:S(2)}) collective-permute-start(bf16[2,64,1024]{2,1,0:T(8,128)(2,1)S(1)} %pad_maximum_fusion.2), channel_id=1, source_target_pairs={{0,4},{4,0},{8,12},{12,8},{16,20},{20,16},{24,28},{28,24},{1,5},{5... | collective-permute-start | bytes 786440 | tf_op jit(solution)/shard_map/ppermute | solution.py:130
  36.5 17.2 %copy-start.5 = (f32[1,4,128,128]{3,2,1,0:T(8,128)S(1)}, f32[1,4,128,128]{3,2,1,0:T(8,128)}, u32[]{:S(2)}) copy-start(f32[1,4,128,128]{3,2,1,0:T(8,128)} %param.14) | copy-start | bytes 786436
  36.5 17.2 %copy-start.6 = (f32[1,5,96,96]{3,2,1,0:T(8,128)S(1)}, f32[1,5,96,96]{3,2,1,0:T(8,128)}, u32[]{:S(2)}) copy-start(f32[1,5,96,96]{3,2,1,0:T(8,128)} %param.15) | copy-start | bytes 552964
  36.6 17.2 %copy-start.8 = (s32[4,4]{1,0:T(4,128)S(1)}, s32[4,4]{1,0:T(4,128)}, u32[]{:S(2)}) copy-start(s32[4,4]{1,0:T(4,128)} %refs_1_.3) | copy-start | bytes 196
  36.6 17.2 %copy-start.9 = (s32[4,5]{1,0:T(4,128)S(1)}, s32[4,5]{1,0:T(4,128)}, u32[]{:S(2)}) copy-start(s32[4,5]{1,0:T(4,128)} %refs_2_.5) | copy-start | bytes 244
  36.6 9.3 %collective-permute-start.7 = (s16[2,256,256]{2,1,0:T(8,128)(2,1)S(1)}, s16[2,256,256]{2,1,0:T(8,128)(2,1)S(1)}, u32[]{:S(2)}, u32[]{:S(2)}) collective-permute-start(s16[2,256,256]{2,1,0:T(8,128)(2,1)S(1)} %get-tuple-element.55), channel_id=1, source_target_pairs={{0,8},{4,12},{8,0},{12,4},{16,24},{20,28},{24,16},{28,20},{1,9},{5... | collective-permute-start | bytes 786440 | tf_op jit(solution)/shard_map/ppermute | solution.py:130
  37.4 8.5 %collective-permute-start.8 = (s16[2,256,256]{2,1,0:T(8,128)(2,1)S(1)}, s16[2,256,256]{2,1,0:T(8,128)(2,1)S(1)}, u32[]{:S(2)}, u32[]{:S(2)}) collective-permute-start(s16[2,256,256]{2,1,0:T(8,128)(2,1)S(1)} %get-tuple-element.57), channel_id=1, source_target_pairs={{0,4},{4,0},{8,12},{12,8},{16,20},{20,16},{24,28},{28,24},{1,5},{5... | collective-permute-start | bytes 786440 | tf_op jit(solution)/shard_map/ppermute | solution.py:130
  40.9 12.8 %collective-permute-start.3 = (s16[1136,128]{1,0:T(8,128)(2,1)S(1)}, s16[1136,128]{1,0:T(8,128)(2,1)S(1)}, u32[]{:S(2)}, u32[]{:S(2)}) collective-permute-start(s16[1136,128]{1,0:T(8,128)(2,1)S(1)} %stats.1.refs_3_), channel_id=1, source_target_pairs={{0,8},{4,12},{8,0},{12,4},{16,24},{20,28},{24,16},{28,20},{1,9},{5... | collective-permute-start | bytes 872456 | tf_op jit(solution)/shard_map/ppermute | solution.py:130
  46.8 17.6 %collective-permute-start.9 = (s16[2,256,256]{2,1,0:T(8,128)(2,1)S(1)}, s16[2,256,256]{2,1,0:T(8,128)(2,1)S(1)}, u32[]{:S(2)}, u32[]{:S(2)}) collective-permute-start(s16[2,256,256]{2,1,0:T(8,128)(2,1)S(1)} %get-tuple-element.59), channel_id=1, source_target_pairs={{0,16},{4,20},{8,24},{12,28},{16,0},{20,4},{24,8},{28,12},{1,17},{... | collective-permute-start | bytes 786440 | tf_op jit(solution)/shard_map/ppermute | solution.py:130
  48.3 4.3 %collective-permute-start.4 = (s16[2,64,256]{2,1,0:T(8,128)(2,1)S(1)}, s16[2,64,256]{2,1,0:T(8,128)(2,1)S(1)}, u32[]{:S(2)}, u32[]{:S(2)}) collective-permute-start(s16[2,64,256]{2,1,0:T(8,128)(2,1)S(1)} %sides.1), channel_id=1, source_target_pairs={{0,4},{4,0},{8,12},{12,8},{16,20},{20,16},{24,28},{28,24},{1,5},{5... | collective-permute-start | bytes 196616 | tf_op jit(solution)/shard_map/ppermute | solution.py:130
  58.0 6.4 %collective-permute-start.10 = (s16[3,112,96]{2,1,0:T(8,128)(2,1)S(1)}, s16[3,112,96]{2,1,0:T(8,128)(2,1)S(1)}, u32[]{:S(2)}, u32[]{:S(2)}) collective-permute-start(s16[3,112,96]{2,1,0:T(8,128)(2,1)S(1)} %get-tuple-element.61), channel_id=1, source_target_pairs={{0,2},{1,10},{2,18},{3,26},{4,6},{5,14},{6,22},{7,30},{8,3},{9,11}... | collective-permute-start | bytes 193544 | tf_op jit(solution)/shard_map/ppermute | solution.py:745
  66.3 7.7 %collective-permute-start.11 = (f32[56,256]{1,0:T(8,128)S(1)}, f32[56,256]{1,0:T(8,128)S(1)}, u32[]{:S(2)}, u32[]{:S(2)}) collective-permute-start(f32[56,256]{1,0:T(8,128)S(1)} %pad_maximum_fusion.3), channel_id=1, source_target_pairs={{0,4},{4,0},{8,12},{12,8},{16,20},{20,16},{24,28},{28,24},{1,5},{5... | collective-permute-start | bytes 172040 | tf_op jit(solution)/shard_map/ppermute | solution.py:130
  67.2 16.2 %collective-permute-start.17 = (s16[272,512]{1,0:T(8,128)(2,1)S(1)}, s16[272,512]{1,0:T(8,128)(2,1)S(1)}, u32[]{:S(2)}, u32[]{:S(2)}) collective-permute-start(s16[272,512]{1,0:T(8,128)(2,1)S(1)} %get-tuple-element.66.refs_3_), channel_id=1, source_target_pairs={{0,16},{4,20},{8,24},{12,28},{16,0},{20,4},{24,8},{28,12},{1,17},{... | collective-permute-start | bytes 835592 | tf_op jit(solution)/shard_map/ppermute | solution.py:130
  67.4 3.7 %collective-permute-start.12 = (f32[8,256]{1,0:T(8,128)S(1)}, f32[8,256]{1,0:T(8,128)S(1)}, u32[]{:S(2)}, u32[]{:S(2)}) collective-permute-start(f32[8,256]{1,0:T(8,128)S(1)} %get-tuple-element.63), channel_id=1, source_target_pairs={{0,2},{1,3},{2,0},{3,1},{4,6},{5,7},{6,4},{7,5},{8,10},{9,11},{10,... | collective-permute-start | bytes 24584 | tf_op jit(solution)/shard_map/ppermute | solution.py:134
  69.4 4.5 %collective-permute-start.13 = (f32[8,256]{1,0:T(8,128)S(1)}, f32[8,256]{1,0:T(8,128)S(1)}, u32[]{:S(2)}, u32[]{:S(2)}) collective-permute-start(f32[8,256]{1,0:T(8,128)S(1)} %get-tuple-element.63), channel_id=1, source_target_pairs={{0,6},{1,7},{2,4},{3,5},{4,2},{5,3},{6,0},{7,1},{8,14},{9,15},{10,... | collective-permute-start | bytes 24584 | tf_op jit(solution)/shard_map/ppermute | solution.py:139
  74.0 1.2 %collective-permute-start.14 = (f32[8,256]{1,0:T(8,128)S(1)}, f32[8,256]{1,0:T(8,128)S(1)}, u32[]{:S(2)}, u32[]{:S(2)}) collective-permute-start(f32[8,256]{1,0:T(8,128)S(1)} %fusion), channel_id=1, source_target_pairs={{0,1},{1,0},{2,3},{3,2},{4,5},{5,4},{6,7},{7,6},{8,9},{9,8},{10,11... | collective-permute-start | bytes 24584 | tf_op jit(solution)/shard_map/ppermute | solution.py:134
  75.2 4.5 %collective-permute-start.15 = (f32[8,256]{1,0:T(8,128)S(1)}, f32[8,256]{1,0:T(8,128)S(1)}, u32[]{:S(2)}, u32[]{:S(2)}) collective-permute-start(f32[8,256]{1,0:T(8,128)S(1)} %add.20), channel_id=1, source_target_pairs={{0,16},{4,20},{8,24},{12,28},{16,0},{20,4},{24,8},{28,12},{1,17},{... | collective-permute-start | bytes 24584 | tf_op jit(solution)/shard_map/ppermute | solution.py:130
  79.8 3.7 %collective-permute-start.16 = (f32[8,256]{1,0:T(8,128)S(1)}, f32[8,256]{1,0:T(8,128)S(1)}, u32[]{:S(2)}, u32[]{:S(2)}) collective-permute-start(f32[8,256]{1,0:T(8,128)S(1)} %add.21.refs_0_), channel_id=1, source_target_pairs={{0,8},{4,12},{8,0},{12,4},{16,24},{20,28},{24,16},{28,20},{1,9},{5... | collective-permute-start | bytes 24584 | tf_op jit(solution)/shard_map/ppermute | solution.py:130
  83.7 6.3 %collective-permute-start.18 = (bf16[2,240,256]{2,1,0:T(8,128)(2,1)S(1)}, bf16[2,240,256]{2,1,0:T(8,128)(2,1)S(1)}, u32[]{:S(2)}, u32[]{:S(2)}) collective-permute-start(bf16[2,240,256]{2,1,0:T(8,128)(2,1)S(1)} %get-tuple-element.67.refs_1_), channel_id=1, source_target_pairs={{0,8},{4,12},{8,0},{12,4},{16,24},{20,28},{24,16},{28,20},{1,9},{5... | collective-permute-start | bytes 737288 | tf_op jit(solution)/shard_map/ppermute | solution.py:130
  85.7 6.6 %collective-permute-start.19 = (bf16[2,240,256]{2,1,0:T(8,128)(2,1)S(1)}, bf16[2,240,256]{2,1,0:T(8,128)(2,1)S(1)}, u32[]{:S(2)}, u32[]{:S(2)}) collective-permute-start(bf16[2,240,256]{2,1,0:T(8,128)(2,1)S(1)} %get-tuple-element.68.refs_4_), channel_id=1, source_target_pairs={{0,4},{4,0},{8,12},{12,8},{16,20},{20,16},{24,28},{28,24},{1,5},{5... | collective-permute-start | bytes 737288 | tf_op jit(solution)/shard_map/ppermute | solution.py:130
  92.3 9.6 %collective-permute-start.21 = (bf16[4,240,256]{2,1,0:T(8,128)(2,1)S(1)}, bf16[4,240,256]{2,1,0:T(8,128)(2,1)S(1)}, u32[]{:S(2)}, u32[]{:S(2)}) collective-permute-start(bf16[4,240,256]{2,1,0:T(8,128)(2,1)S(1)} %pad_maximum_fusion.1), channel_id=1, source_target_pairs={{0,8},{4,12},{8,0},{12,4},{16,24},{20,28},{24,16},{28,20},{1,9},{5... | collective-permute-start | bytes 1474568 | tf_op jit(solution)/shard_map/ppermute | solution.py:130
  92.4 10.0 %collective-permute-start.20 = (bf16[4,240,256]{2,1,0:T(8,128)(2,1)S(1)}, bf16[4,240,256]{2,1,0:T(8,128)(2,1)S(1)}, u32[]{:S(2)}, u32[]{:S(2)}) collective-permute-start(bf16[4,240,256]{2,1,0:T(8,128)(2,1)S(1)} %pad_maximum_fusion), channel_id=1, source_target_pairs={{0,4},{4,0},{8,12},{12,8},{16,20},{20,16},{24,28},{28,24},{1,5},{5... | collective-permute-start | bytes 1474568 | tf_op jit(solution)/shard_map/ppermute | solution.py:130
  (1 other events, 5.9 us)

commit v10 on v7

--- a/solution.py
+++ b/solution.py
@@ -738,7 +738,7 @@
         name="factors",
     )(info, own_a, own_g, packed, got_packed, a_state[0], g_state[0])
     route = [
-        ((2 * a + b) * 4 + c, (2 * c + b) * 4 + a)
+        ((2 * a + b) * 4 + c, (2 * c + b) * 4 + (a ^ 2))
         for a in range(4)
         for b in range(2)
         for c in range(4)

time: 107 us -> 104 us (0.972)
  starting transfers between devices: 38.8 us -> 30.6 us
  waiting for transfers between devices: 37.8 us -> 43.1 us
    ppermute x19, starting transfers between devices: 34.5 us -> 25.7 us  [swap(): return lax.ppermute(value, 'shard', [(i, i ^ bit) for i in range(8)])]
    ppermute x1, waiting for transfers between devices: 0.01 us -> 4.98 us  [fast(): inv_rows = lax.ppermute(needed, ('shard', 'tensor'), route)]
    ppermute x1, starting transfers between devices: 2.87 us -> 1.27 us  [swap_both(): return lax.ppermute(value, ('shard', 'tensor'), route)]
    ppermute x2, starting transfers between devices: 0.61 us -> 2.13 us  [swap_t(): return lax.ppermute(value, 'tensor', [(i, i ^ bit) for i in range(4)])]
    ppermute x1, waiting for transfers between devices: 1.44 us -> 2.92 us  [swap_both(): return lax.ppermute(value, ('shard', 'tensor'), route)]
    ppermute x19, waiting for transfers between devices: 35 us -> 33.7 us  [swap(): return lax.ppermute(value, 'shard', [(i, i ^ bit) for i in range(8)])]
where the time goes in v10:
time: 104 us
  waiting for transfers between devices  43.1 us (41%)
  starting transfers between devices  30.6 us (29%)
  Pallas kernels  28.5 us (27%)
    ppermute x19, waiting for transfers between devices, swap(): return lax.ppermute(value, 'shard', [(i, i ^ bit) for i in range(8)])  33.7 us
    ppermute x19, starting transfers between devices, swap(): return lax.ppermute(value, 'shard', [(i, i ^ bit) for i in range(8)])  25.7 us
    pallas_call x1, Pallas kernels, fast(): pl.pallas_call(lambda *refs: partial_kernel(group_cols, width_g, *refs),...  9.85 us
    ppermute x1, waiting for transfers between devices, fast(): inv_rows = lax.ppermute(needed, ('shard', 'tensor'), route)  4.98 us
    pallas_call x1, Pallas kernels, fast(): pl.pallas_call(lambda *refs: factor_kernel(share, blocks, *refs), in_spec...  4.24 us
    pallas_call x1, Pallas kernels, fast(): pl.pallas_call(lambda *refs: picks_kernel(group_cols, *refs), in_specs=[s...  3.16 us
    ppermute x1, waiting for transfers between devices, swap_both(): return lax.ppermute(value, ('shard', 'tensor'), route)  2.92 us
    ppermute x2, starting transfers between devices, swap_t(): return lax.ppermute(value, 'tensor', [(i, i ^ bit) for i in range(4)])  2.13 us
  transfers between devices with their start and end apart: 23, of which 16 were waited for; matrix products, arithmetic and copies ran while one was open for 0% of the time, Pallas kernels for 14%

profile of v10, /device:TPU:0, one launch (start us, length us, event | category | flops | bytes accessed | tf_op | source)
XLA Modules:
  0.0 103.9 jit_solution(8873633350955749065)
XLA Ops:
  1.3 9.8 %partial.1 = (s16[4,256,256]{2,1,0:T(8,128)(2,1)}, f32[4,240,256]{2,1,0:T(8,128)}, s16[4,256,256]{2,1,0:T(8,128)(2,1)}, f32[4,240,256]{2,1,0:T(8,128)}) custom-call(s32[5]{0:T(128)} %stack.32.refs_0_.info, bf16[2048,1920]{1,0:T(8,128)(2,1)} %refs_3_.1, bf16[2048,512]{1,0:T(8,128)(2,1)} %refs_2_.4), custom_call_target="tpu_custom_call" | custom-call | tf_op jit(solution)/shard_map/partial/pallas_call | solution.py:628
  11.2 3.0 %collective-permute-start.5 = (s16[4,256,256]{2,1,0:T(8,128)(2,1)}, s16[4,256,256]{2,1,0:T(8,128)(2,1)S(1)}, u32[]{:S(2)}, u32[]{:S(2)}) collective-permute-start(s16[4,256,256]{2,1,0:T(8,128)(2,1)} %get-tuple-element.49), channel_id=1, source_target_pairs={{0,4},{4,0},{8,12},{12,8},{16,20},{20,16},{24,28},{28,24},{1,5},{5... | collective-permute-start | bytes 1572872 | tf_op jit(solution)/shard_map/ppermute | solution.py:130
  14.2 1.6 %collective-permute-start.6 = (s16[4,256,256]{2,1,0:T(8,128)(2,1)}, s16[4,256,256]{2,1,0:T(8,128)(2,1)S(1)}, u32[]{:S(2)}, u32[]{:S(2)}) collective-permute-start(s16[4,256,256]{2,1,0:T(8,128)(2,1)} %get-tuple-element.52), channel_id=1, source_target_pairs={{0,8},{4,12},{8,0},{12,4},{16,24},{20,28},{24,16},{28,20},{1,9},{5... | collective-permute-start | bytes 1572872 | tf_op jit(solution)/shard_map/ppermute | solution.py:130
  15.8 3.2 %picks.1.refs_1_ = bf16[64,1024]{1,0:T(8,128)(2,1)S(1)} custom-call(s32[5]{0:T(128)S(1)} %copy-done.7, s32[1,64]{1,0:T(1,128)S(1)} %bitcast.16, bf16[2048,512]{1,0:T(8,128)(2,1)S(1)} %copy-done, bf16[2048,1920]{1,0:T(8,128)(2,1)} %refs_3_.1), custom_call_target="tpu_custom_call" | custom-call | tf_op jit(solution)/shard_map/picks/pallas_call | solution.py:651
  19.0 2.7 %collective-permute-start = (bf16[64,1024]{1,0:T(8,128)(2,1)S(1)}, bf16[64,1024]{1,0:T(8,128)(2,1)S(1)}, u32[]{:S(2)}, u32[]{:S(2)}) collective-permute-start(bf16[64,1024]{1,0:T(8,128)(2,1)S(1)} %picks.1.refs_1_), channel_id=1, source_target_pairs={{0,16},{4,20},{8,24},{12,28},{16,0},{20,4},{24,8},{28,12},{1,17},{... | collective-permute-start | bytes 393224 | tf_op jit(solution)/shard_map/ppermute | solution.py:130
  22.4 8.8 %collective-permute-done.refs_2_ = bf16[64,1024]{1,0:T(8,128)(2,1)S(1)} collective-permute-done((bf16[64,1024]{1,0:T(8,128)(2,1)S(1)}, bf16[64,1024]{1,0:T(8,128)(2,1)S(1)}, u32[]{:S(2)}, u32[]{:S(2)}) %collective-permute-start) | collective-permute-done | bytes 131104 | tf_op jit(solution)/shard_map/ppermute | solution.py:130
  32.7 2.8 %collective-permute-done.6.refs_1_ = s16[4,256,256]{2,1,0:T(8,128)(2,1)S(1)} collective-permute-done((s16[4,256,256]{2,1,0:T(8,128)(2,1)}, s16[4,256,256]{2,1,0:T(8,128)(2,1)S(1)}, u32[]{:S(2)}, u32[]{:S(2)}) %collective-permute-start.6) | collective-permute-done | bytes 524320 | tf_op jit(solution)/shard_map/ppermute | solution.py:130
  37.4 1.5 %collective-permute-start.8 = (s16[2,256,256]{2,1,0:T(8,128)(2,1)S(1)}, s16[2,256,256]{2,1,0:T(8,128)(2,1)S(1)}, u32[]{:S(2)}, u32[]{:S(2)}) collective-permute-start(s16[2,256,256]{2,1,0:T(8,128)(2,1)S(1)} %get-tuple-element.57), channel_id=1, source_target_pairs={{0,4},{4,0},{8,12},{12,8},{16,20},{20,16},{24,28},{28,24},{1,5},{5... | collective-permute-start | bytes 786440 | tf_op jit(solution)/shard_map/ppermute | solution.py:130
  39.8 1.1 %stats.1.refs_3_ = s16[1136,128]{1,0:T(8,128)(2,1)S(1)} custom-call(s32[5]{0:T(128)S(1)} %copy-done.7, bf16[64,1024]{1,0:T(8,128)(2,1)S(1)} %picks.1.refs_1_, bf16[64,1024]{1,0:T(8,128)(2,1)S(1)} %collective-permute-done.refs_2_, bf16[2,64,1024]{2,1,0:T(8,128)(2,1)S(1)} %collective-permute-done.1.refs_3_), custom_call_target="tpu_custom_call" | custom-call | tf_op jit(solution)/shard_map/stats/pallas_call | solution.py:684
  40.9 3.1 %collective-permute-start.3 = (s16[1136,128]{1,0:T(8,128)(2,1)S(1)}, s16[1136,128]{1,0:T(8,128)(2,1)S(1)}, u32[]{:S(2)}, u32[]{:S(2)}) collective-permute-start(s16[1136,128]{1,0:T(8,128)(2,1)S(1)} %stats.1.refs_3_), channel_id=1, source_target_pairs={{0,8},{4,12},{8,0},{12,4},{16,24},{20,28},{24,16},{28,20},{1,9},{5... | collective-permute-start | bytes 872456 | tf_op jit(solution)/shard_map/ppermute | solution.py:130
  44.0 1.9 %collective-permute-done.7.got_a = s16[2,256,256]{2,1,0:T(8,128)(2,1)S(1)} collective-permute-done((s16[2,256,256]{2,1,0:T(8,128)(2,1)S(1)}, s16[2,256,256]{2,1,0:T(8,128)(2,1)S(1)}, u32[]{:S(2)}, u32[]{:S(2)}) %collective-permute-start.7) | collective-permute-done | bytes 262176 | tf_op jit(solution)/shard_map/ppermute | solution.py:130
  48.9 3.8 %collective-permute-done.4.refs_3_ = s16[2,64,256]{2,1,0:T(8,128)(2,1)S(1)} collective-permute-done((s16[2,64,256]{2,1,0:T(8,128)(2,1)S(1)}, s16[2,64,256]{2,1,0:T(8,128)(2,1)S(1)}, u32[]{:S(2)}, u32[]{:S(2)}) %collective-permute-start.4) | collective-permute-done | bytes 65568 | tf_op jit(solution)/shard_map/ppermute | solution.py:130
  53.7 4.2 %factors.1 = (f32[4,128,128]{2,1,0:T(8,128)}, f32[5,96,96]{2,1,0:T(8,128)}, f32[4,128,128]{2,1,0:T(8,128)S(1)}, s16[3,112,96]{2,1,0:T(8,128)(2,1)S(1)}) custom-call(s32[5]{0:T(128)S(1)} %copy-done.7, s32[4,4]{1,0:T(4,128)S(1)} %copy-done.8, s32[4,5]{1,0:T(4,128)S(1)} %copy-done.9, s16[1136,128]{1,0:T(8,128)(2,1)S(1)} %stats.1.refs_3_, ...), custom_call_target="tpu_custom_call" | custom-call | tf_op jit(solution)/shard_map/factors/pallas_call | solution.py:726
  58.0 1.4 %collective-permute-start.10 = (s16[3,112,96]{2,1,0:T(8,128)(2,1)S(1)}, s16[3,112,96]{2,1,0:T(8,128)(2,1)S(1)}, u32[]{:S(2)}, u32[]{:S(2)}) collective-permute-start(s16[3,112,96]{2,1,0:T(8,128)(2,1)S(1)} %get-tuple-element.61), channel_id=1, source_target_pairs={{0,2},{1,10},{2,18},{3,26},{4,6},{5,14},{6,22},{7,30},{8,3},{9,11}... | collective-permute-start | bytes 193544 | tf_op jit(solution)/shard_map/ppermute | solution.py:746
  59.4 5.0 %collective-permute-done.10.inv_g = s16[3,112,96]{2,1,0:T(8,128)(2,1)S(1)} collective-permute-done((s16[3,112,96]{2,1,0:T(8,128)(2,1)S(1)}, s16[3,112,96]{2,1,0:T(8,128)(2,1)S(1)}, u32[]{:S(2)}, u32[]{:S(2)}) %collective-permute-start.10) | collective-permute-done | bytes 64544 | tf_op jit(solution)/shard_map/ppermute | solution.py:746
  64.4 1.8 %precon.1 = (f32[192,512]{1,0:T(8,128)S(1)}, f32[96,256]{1,0:T(8,128)S(1)}, f32[8,256]{1,0:T(8,128)S(1)}, s16[272,512]{1,0:T(8,128)(2,1)S(1)}) custom-call(s32[5]{0:T(128)S(1)} %copy-done.7, s16[2,256,256]{2,1,0:T(8,128)(2,1)S(1)} %collective-permute-done.9.got, f32[2,240,256]{2,1,0:T(8,128)S(1)} %get-tuple-element.60.held, ...), custom_call_target="tpu_custom_call" | custom-call | tf_op jit(solution)/shard_map/precon/pallas_call | solution.py:748
  67.4 2.1 %collective-permute-start.12 = (f32[8,256]{1,0:T(8,128)S(1)}, f32[8,256]{1,0:T(8,128)S(1)}, u32[]{:S(2)}, u32[]{:S(2)}) collective-permute-start(f32[8,256]{1,0:T(8,128)S(1)} %get-tuple-element.63), channel_id=1, source_target_pairs={{0,2},{1,3},{2,0},{3,1},{4,6},{5,7},{6,4},{7,5},{8,10},{9,11},{10,... | collective-permute-start | bytes 24584 | tf_op jit(solution)/shard_map/ppermute | solution.py:134
  69.4 1.3 %collective-permute-start.13 = (f32[8,256]{1,0:T(8,128)S(1)}, f32[8,256]{1,0:T(8,128)S(1)}, u32[]{:S(2)}, u32[]{:S(2)}) collective-permute-start(f32[8,256]{1,0:T(8,128)S(1)} %get-tuple-element.63), channel_id=1, source_target_pairs={{0,6},{1,7},{2,4},{3,5},{4,2},{5,3},{6,0},{7,1},{8,14},{9,15},{10,... | collective-permute-start | bytes 24584 | tf_op jit(solution)/shard_map/ppermute | solution.py:139
  71.1 2.9 %collective-permute-done.13 = f32[8,256]{1,0:T(8,128)S(1)} collective-permute-done((f32[8,256]{1,0:T(8,128)S(1)}, f32[8,256]{1,0:T(8,128)S(1)}, u32[]{:S(2)}, u32[]{:S(2)}) %collective-permute-start.13) | collective-permute-done | bytes 8224 | tf_op jit(solution)/shard_map/ppermute | solution.py:139
  74.1 1.2 %collective-permute-done.14 = f32[8,256]{1,0:T(8,128)S(1)} collective-permute-done((f32[8,256]{1,0:T(8,128)S(1)}, f32[8,256]{1,0:T(8,128)S(1)}, u32[]{:S(2)}, u32[]{:S(2)}) %collective-permute-start.14) | collective-permute-done | bytes 8224 | tf_op jit(solution)/shard_map/ppermute | solution.py:134
  75.2 1.9 %collective-permute-start.15 = (f32[8,256]{1,0:T(8,128)S(1)}, f32[8,256]{1,0:T(8,128)S(1)}, u32[]{:S(2)}, u32[]{:S(2)}) collective-permute-start(f32[8,256]{1,0:T(8,128)S(1)} %add.17.refs_0_), channel_id=1, source_target_pairs={{0,8},{4,12},{8,0},{12,4},{16,24},{20,28},{24,16},{28,20},{1,9},{5... | collective-permute-start | bytes 24584 | tf_op jit(solution)/shard_map/ppermute | solution.py:130
  77.5 2.2 %collective-permute-start.17 = (f32[8,256]{1,0:T(8,128)S(1)}, f32[8,256]{1,0:T(8,128)S(1)}, u32[]{:S(2)}, u32[]{:S(2)}) collective-permute-start(f32[8,256]{1,0:T(8,128)S(1)} %add.17.refs_0_), channel_id=1, source_target_pairs={{0,24},{4,28},{8,16},{12,20},{16,8},{20,12},{24,0},{28,4},{1,25},{... | collective-permute-start | bytes 24584 | tf_op jit(solution)/shard_map/ppermute | solution.py:130
  79.6 2.1 %collective-permute-done.16.refs_2_ = f32[8,256]{1,0:T(8,128)S(1)} collective-permute-done((f32[8,256]{1,0:T(8,128)S(1)}, f32[8,256]{1,0:T(8,128)S(1)}, u32[]{:S(2)}, u32[]{:S(2)}) %collective-permute-start.16) | collective-permute-done | bytes 8224 | tf_op jit(solution)/shard_map/ppermute | solution.py:130
  81.7 1.2 %collective-permute-done.17.refs_3_ = f32[8,256]{1,0:T(8,128)S(1)} collective-permute-done((f32[8,256]{1,0:T(8,128)S(1)}, f32[8,256]{1,0:T(8,128)S(1)}, u32[]{:S(2)}, u32[]{:S(2)}) %collective-permute-start.17) | collective-permute-done | bytes 8224 | tf_op jit(solution)/shard_map/ppermute | solution.py:130
  83.2 1.6 %collective-permute-start.20 = (bf16[2,240,256]{2,1,0:T(8,128)(2,1)S(1)}, bf16[2,240,256]{2,1,0:T(8,128)(2,1)S(1)}, u32[]{:S(2)}, u32[]{:S(2)}) collective-permute-start(bf16[2,240,256]{2,1,0:T(8,128)(2,1)S(1)} %get-tuple-element.68.refs_4_), channel_id=1, source_target_pairs={{0,4},{4,0},{8,12},{12,8},{16,20},{20,16},{24,28},{28,24},{1,5},{5... | collective-permute-start | bytes 737288 | tf_op jit(solution)/shard_map/ppermute | solution.py:130
  84.8 1.6 %update.1 = (f32[240,512]{1,0:T(8,128)}, f32[240,512]{1,0:T(8,128)}) custom-call(s32[5]{0:T(128)S(1)} %copy-done.7, f32[8,512]{1,0:T(8,128)S(1)} %get-tuple-element.69.factor, f32[192,512]{1,0:T(8,128)S(1)} %get-tuple-element.70.top, f32[96,256]{1,0:T(8,128)S(1)} %get-tuple-element.64.middle, f32[56,256]{1,0:T(8,128)S(1)} %collective-permute-done.11.got, ...), custom_call_target="tpu_custom_call" | custom-call | tf_op jit(solution)/shard_map/update/pallas_call | solution.py:785
  86.4 3.1 %collective-permute-done.19.refs_2_ = bf16[2,240,256]{2,1,0:T(8,128)(2,1)S(1)} collective-permute-done((bf16[2,240,256]{2,1,0:T(8,128)(2,1)S(1)}, bf16[2,240,256]{2,1,0:T(8,128)(2,1)S(1)}, u32[]{:S(2)}, u32[]{:S(2)}) %collective-permute-start.19) | collective-permute-done | bytes 245792 | tf_op jit(solution)/shard_map/ppermute | solution.py:130
  89.7 1.9 %collective-permute-start.22 = (bf16[4,240,256]{2,1,0:T(8,128)(2,1)S(1)}, bf16[4,240,256]{2,1,0:T(8,128)(2,1)S(1)}, u32[]{:S(2)}, u32[]{:S(2)}) collective-permute-start(bf16[4,240,256]{2,1,0:T(8,128)(2,1)S(1)} %pad_maximum_fusion.1), channel_id=1, source_target_pairs={{0,8},{4,12},{8,0},{12,4},{16,24},{20,28},{24,16},{28,20},{1,9},{5... | collective-permute-start | bytes 1474568 | tf_op jit(solution)/shard_map/ppermute | solution.py:130
  91.6 1.6 %collective-permute-start.21 = (bf16[4,240,256]{2,1,0:T(8,128)(2,1)S(1)}, bf16[4,240,256]{2,1,0:T(8,128)(2,1)S(1)}, u32[]{:S(2)}, u32[]{:S(2)}) collective-permute-start(bf16[4,240,256]{2,1,0:T(8,128)(2,1)S(1)} %pad_maximum_fusion), channel_id=1, source_target_pairs={{0,4},{4,0},{8,12},{12,8},{16,20},{20,16},{24,28},{28,24},{1,5},{5... | collective-permute-start | bytes 1474568 | tf_op jit(solution)/shard_map/ppermute | solution.py:130
  93.2 7.2 %collective-permute-done.22.refs_6_ = bf16[4,240,256]{2,1,0:T(8,128)(2,1)S(1)} collective-permute-done((bf16[4,240,256]{2,1,0:T(8,128)(2,1)S(1)}, bf16[4,240,256]{2,1,0:T(8,128)(2,1)S(1)}, u32[]{:S(2)}, u32[]{:S(2)}) %collective-permute-start.22) | collective-permute-done | bytes 491552 | tf_op jit(solution)/shard_map/ppermute | solution.py:130
  100.4 1.5 %collective-permute-done.21.refs_3_ = bf16[4,240,256]{2,1,0:T(8,128)(2,1)S(1)} collective-permute-done((bf16[4,240,256]{2,1,0:T(8,128)(2,1)S(1)}, bf16[4,240,256]{2,1,0:T(8,128)(2,1)S(1)}, u32[]{:S(2)}, u32[]{:S(2)}) %collective-permute-start.21) | collective-permute-done | bytes 491552 | tf_op jit(solution)/shard_map/ppermute | solution.py:130
  101.8 2.0 %place.1 = bf16[1920,512]{1,0:T(8,128)(2,1)} custom-call(s32[5]{0:T(128)S(1)} %copy-done.7, bf16[2,240,256]{2,1,0:T(8,128)(2,1)S(1)} %get-tuple-element.67.refs_1_, bf16[2,240,256]{2,1,0:T(8,128)(2,1)S(1)} %collective-permute-done.19.refs_2_, bf16[4,240,256]{2,1,0:T(8,128)(2,1)S(1)} %collective-permute-done.21.refs_3_, ...), custom_call_target="tpu_custom_call" | custom-call | tf_op jit(solution)/shard_map/place/pallas_call | solution.py:798
  (58 shorter events, 12.1 us)
Async XLA Ops:
  1.3 14.4 %copy-start = (bf16[2048,512]{1,0:T(8,128)(2,1)S(1)}, bf16[2048,512]{1,0:T(8,128)(2,1)}, u32[]{:S(2)}) copy-start(bf16[2048,512]{1,0:T(8,128)(2,1)} %refs_2_.4) | copy-start | bytes 6291460
  1.3 14.4 %copy-start.7 = (s32[5]{0:T(128)S(1)}, s32[5]{0:T(128)}, u32[]{:S(2)}) copy-start(s32[5]{0:T(128)} %stack.32.refs_0_.info) | copy-start | bytes 64
  1.3 14.4 %copy-start.10 = (s32[64]{0:T(128)S(1)}, s32[64]{0:T(128)}, u32[]{:S(2)}) copy-start(s32[64]{0:T(128)} %param.11) | copy-start | bytes 772
  11.2 20.6 %collective-permute-start.5 = (s16[4,256,256]{2,1,0:T(8,128)(2,1)}, s16[4,256,256]{2,1,0:T(8,128)(2,1)S(1)}, u32[]{:S(2)}, u32[]{:S(2)}) collective-permute-start(s16[4,256,256]{2,1,0:T(8,128)(2,1)} %get-tuple-element.49), channel_id=1, source_target_pairs={{0,4},{4,0},{8,12},{12,8},{16,20},{20,16},{24,28},{28,24},{1,5},{5... | collective-permute-start | bytes 1572872 | tf_op jit(solution)/shard_map/ppermute | solution.py:130
  14.2 21.4 %collective-permute-start.6 = (s16[4,256,256]{2,1,0:T(8,128)(2,1)}, s16[4,256,256]{2,1,0:T(8,128)(2,1)S(1)}, u32[]{:S(2)}, u32[]{:S(2)}) collective-permute-start(s16[4,256,256]{2,1,0:T(8,128)(2,1)} %get-tuple-element.52), channel_id=1, source_target_pairs={{0,8},{4,12},{8,0},{12,4},{16,24},{20,28},{24,16},{28,20},{1,9},{5... | collective-permute-start | bytes 1572872 | tf_op jit(solution)/shard_map/ppermute | solution.py:130
  15.8 16.0 %copy-start.4 = (f32[4,240,256]{2,1,0:T(8,128)S(1)}, f32[4,240,256]{2,1,0:T(8,128)}, u32[]{:S(2)}) copy-start(f32[4,240,256]{2,1,0:T(8,128)} %get-tuple-element.50.refs_2_) | copy-start | bytes 2949124
  19.0 16.6 %copy-start.3 = (f32[4,240,256]{2,1,0:T(8,128)S(1)}, f32[4,240,256]{2,1,0:T(8,128)}, u32[]{:S(2)}) copy-start(f32[4,240,256]{2,1,0:T(8,128)} %get-tuple-element.53.refs_2_) | copy-start | bytes 2949124
  19.0 12.2 %collective-permute-start = (bf16[64,1024]{1,0:T(8,128)(2,1)S(1)}, bf16[64,1024]{1,0:T(8,128)(2,1)S(1)}, u32[]{:S(2)}, u32[]{:S(2)}) collective-permute-start(bf16[64,1024]{1,0:T(8,128)(2,1)S(1)} %picks.1.refs_1_), channel_id=1, source_target_pairs={{0,16},{4,20},{8,24},{12,28},{16,0},{20,4},{24,8},{28,12},{1,17},{... | collective-permute-start | bytes 393224 | tf_op jit(solution)/shard_map/ppermute | solution.py:130
  22.0 17.7 %collective-permute-start.2 = (s16[272,512]{1,0:T(8,128)(2,1)S(1)}, s16[272,512]{1,0:T(8,128)(2,1)S(1)}, u32[]{:S(2)}, u32[]{:S(2)}) collective-permute-start(s16[272,512]{1,0:T(8,128)(2,1)S(1)} %base.1.refs_1_), channel_id=1, source_target_pairs={{0,16},{4,20},{8,24},{12,28},{16,0},{20,4},{24,8},{28,12},{1,17},{... | collective-permute-start | bytes 835592 | tf_op jit(solution)/shard_map/ppermute | solution.py:130
  31.2 8.5 %collective-permute-start.1 = (bf16[2,64,1024]{2,1,0:T(8,128)(2,1)S(1)}, bf16[2,64,1024]{2,1,0:T(8,128)(2,1)S(1)}, u32[]{:S(2)}, u32[]{:S(2)}) collective-permute-start(bf16[2,64,1024]{2,1,0:T(8,128)(2,1)S(1)} %pad_maximum_fusion.2), channel_id=1, source_target_pairs={{0,4},{4,0},{8,12},{12,8},{16,20},{20,16},{24,28},{28,24},{1,5},{5... | collective-permute-start | bytes 786440 | tf_op jit(solution)/shard_map/ppermute | solution.py:130
  36.5 17.2 %copy-start.5 = (f32[1,4,128,128]{3,2,1,0:T(8,128)S(1)}, f32[1,4,128,128]{3,2,1,0:T(8,128)}, u32[]{:S(2)}) copy-start(f32[1,4,128,128]{3,2,1,0:T(8,128)} %param.14) | copy-start | bytes 786436
  36.5 17.2 %copy-start.6 = (f32[1,5,96,96]{3,2,1,0:T(8,128)S(1)}, f32[1,5,96,96]{3,2,1,0:T(8,128)}, u32[]{:S(2)}) copy-start(f32[1,5,96,96]{3,2,1,0:T(8,128)} %param.15) | copy-start | bytes 552964
  36.5 17.2 %copy-start.8 = (s32[4,4]{1,0:T(4,128)S(1)}, s32[4,4]{1,0:T(4,128)}, u32[]{:S(2)}) copy-start(s32[4,4]{1,0:T(4,128)} %refs_1_.3) | copy-start | bytes 196
  36.5 17.2 %copy-start.9 = (s32[4,5]{1,0:T(4,128)S(1)}, s32[4,5]{1,0:T(4,128)}, u32[]{:S(2)}) copy-start(s32[4,5]{1,0:T(4,128)} %refs_2_.5) | copy-start | bytes 244
  36.6 9.3 %collective-permute-start.7 = (s16[2,256,256]{2,1,0:T(8,128)(2,1)S(1)}, s16[2,256,256]{2,1,0:T(8,128)(2,1)S(1)}, u32[]{:S(2)}, u32[]{:S(2)}) collective-permute-start(s16[2,256,256]{2,1,0:T(8,128)(2,1)S(1)} %get-tuple-element.55), channel_id=1, source_target_pairs={{0,8},{4,12},{8,0},{12,4},{16,24},{20,28},{24,16},{28,20},{1,9},{5... | collective-permute-start | bytes 786440 | tf_op jit(solution)/shard_map/ppermute | solution.py:130
  37.4 8.5 %collective-permute-start.8 = (s16[2,256,256]{2,1,0:T(8,128)(2,1)S(1)}, s16[2,256,256]{2,1,0:T(8,128)(2,1)S(1)}, u32[]{:S(2)}, u32[]{:S(2)}) collective-permute-start(s16[2,256,256]{2,1,0:T(8,128)(2,1)S(1)} %get-tuple-element.57), channel_id=1, source_target_pairs={{0,4},{4,0},{8,12},{12,8},{16,20},{20,16},{24,28},{28,24},{1,5},{5... | collective-permute-start | bytes 786440 | tf_op jit(solution)/shard_map/ppermute | solution.py:130
  40.9 12.9 %collective-permute-start.3 = (s16[1136,128]{1,0:T(8,128)(2,1)S(1)}, s16[1136,128]{1,0:T(8,128)(2,1)S(1)}, u32[]{:S(2)}, u32[]{:S(2)}) collective-permute-start(s16[1136,128]{1,0:T(8,128)(2,1)S(1)} %stats.1.refs_3_), channel_id=1, source_target_pairs={{0,8},{4,12},{8,0},{12,4},{16,24},{20,28},{24,16},{28,20},{1,9},{5... | collective-permute-start | bytes 872456 | tf_op jit(solution)/shard_map/ppermute | solution.py:130
  46.8 17.6 %collective-permute-start.9 = (s16[2,256,256]{2,1,0:T(8,128)(2,1)S(1)}, s16[2,256,256]{2,1,0:T(8,128)(2,1)S(1)}, u32[]{:S(2)}, u32[]{:S(2)}) collective-permute-start(s16[2,256,256]{2,1,0:T(8,128)(2,1)S(1)} %get-tuple-element.59), channel_id=1, source_target_pairs={{0,16},{4,20},{8,24},{12,28},{16,0},{20,4},{24,8},{28,12},{1,17},{... | collective-permute-start | bytes 786440 | tf_op jit(solution)/shard_map/ppermute | solution.py:130
  48.3 4.3 %collective-permute-start.4 = (s16[2,64,256]{2,1,0:T(8,128)(2,1)S(1)}, s16[2,64,256]{2,1,0:T(8,128)(2,1)S(1)}, u32[]{:S(2)}, u32[]{:S(2)}) collective-permute-start(s16[2,64,256]{2,1,0:T(8,128)(2,1)S(1)} %sides.1), channel_id=1, source_target_pairs={{0,4},{4,0},{8,12},{12,8},{16,20},{20,16},{24,28},{28,24},{1,5},{5... | collective-permute-start | bytes 196616 | tf_op jit(solution)/shard_map/ppermute | solution.py:130
  58.0 6.4 %collective-permute-start.10 = (s16[3,112,96]{2,1,0:T(8,128)(2,1)S(1)}, s16[3,112,96]{2,1,0:T(8,128)(2,1)S(1)}, u32[]{:S(2)}, u32[]{:S(2)}) collective-permute-start(s16[3,112,96]{2,1,0:T(8,128)(2,1)S(1)} %get-tuple-element.61), channel_id=1, source_target_pairs={{0,2},{1,10},{2,18},{3,26},{4,6},{5,14},{6,22},{7,30},{8,3},{9,11}... | collective-permute-start | bytes 193544 | tf_op jit(solution)/shard_map/ppermute | solution.py:746
  66.2 7.7 %collective-permute-start.11 = (f32[56,256]{1,0:T(8,128)S(1)}, f32[56,256]{1,0:T(8,128)S(1)}, u32[]{:S(2)}, u32[]{:S(2)}) collective-permute-start(f32[56,256]{1,0:T(8,128)S(1)} %pad_maximum_fusion.3), channel_id=1, source_target_pairs={{0,4},{4,0},{8,12},{12,8},{16,20},{20,16},{24,28},{28,24},{1,5},{5... | collective-permute-start | bytes 172040 | tf_op jit(solution)/shard_map/ppermute | solution.py:130
  67.2 15.8 %collective-permute-start.18 = (s16[272,512]{1,0:T(8,128)(2,1)S(1)}, s16[272,512]{1,0:T(8,128)(2,1)S(1)}, u32[]{:S(2)}, u32[]{:S(2)}) collective-permute-start(s16[272,512]{1,0:T(8,128)(2,1)S(1)} %get-tuple-element.66.refs_5_), channel_id=1, source_target_pairs={{0,16},{4,20},{8,24},{12,28},{16,0},{20,4},{24,8},{28,12},{1,17},{... | collective-permute-start | bytes 835592 | tf_op jit(solution)/shard_map/ppermute | solution.py:130
  67.4 3.7 %collective-permute-start.12 = (f32[8,256]{1,0:T(8,128)S(1)}, f32[8,256]{1,0:T(8,128)S(1)}, u32[]{:S(2)}, u32[]{:S(2)}) collective-permute-start(f32[8,256]{1,0:T(8,128)S(1)} %get-tuple-element.63), channel_id=1, source_target_pairs={{0,2},{1,3},{2,0},{3,1},{4,6},{5,7},{6,4},{7,5},{8,10},{9,11},{10,... | collective-permute-start | bytes 24584 | tf_op jit(solution)/shard_map/ppermute | solution.py:134
  69.4 4.5 %collective-permute-start.13 = (f32[8,256]{1,0:T(8,128)S(1)}, f32[8,256]{1,0:T(8,128)S(1)}, u32[]{:S(2)}, u32[]{:S(2)}) collective-permute-start(f32[8,256]{1,0:T(8,128)S(1)} %get-tuple-element.63), channel_id=1, source_target_pairs={{0,6},{1,7},{2,4},{3,5},{4,2},{5,3},{6,0},{7,1},{8,14},{9,15},{10,... | collective-permute-start | bytes 24584 | tf_op jit(solution)/shard_map/ppermute | solution.py:139
  74.0 1.2 %collective-permute-start.14 = (f32[8,256]{1,0:T(8,128)S(1)}, f32[8,256]{1,0:T(8,128)S(1)}, u32[]{:S(2)}, u32[]{:S(2)}) collective-permute-start(f32[8,256]{1,0:T(8,128)S(1)} %fusion), channel_id=1, source_target_pairs={{0,1},{1,0},{2,3},{3,2},{4,5},{5,4},{6,7},{7,6},{8,9},{9,8},{10,11... | collective-permute-start | bytes 24584 | tf_op jit(solution)/shard_map/ppermute | solution.py:134
  75.2 4.4 %collective-permute-start.15 = (f32[8,256]{1,0:T(8,128)S(1)}, f32[8,256]{1,0:T(8,128)S(1)}, u32[]{:S(2)}, u32[]{:S(2)}) collective-permute-start(f32[8,256]{1,0:T(8,128)S(1)} %add.17.refs_0_), channel_id=1, source_target_pairs={{0,8},{4,12},{8,0},{12,4},{16,24},{20,28},{24,16},{28,20},{1,9},{5... | collective-permute-start | bytes 24584 | tf_op jit(solution)/shard_map/ppermute | solution.py:130
  77.1 4.5 %collective-permute-start.16 = (f32[8,256]{1,0:T(8,128)S(1)}, f32[8,256]{1,0:T(8,128)S(1)}, u32[]{:S(2)}, u32[]{:S(2)}) collective-permute-start(f32[8,256]{1,0:T(8,128)S(1)} %add.17.refs_0_), channel_id=1, source_target_pairs={{0,16},{4,20},{8,24},{12,28},{16,0},{20,4},{24,8},{28,12},{1,17},{... | collective-permute-start | bytes 24584 | tf_op jit(solution)/shard_map/ppermute | solution.py:130
  77.5 5.4 %collective-permute-start.17 = (f32[8,256]{1,0:T(8,128)S(1)}, f32[8,256]{1,0:T(8,128)S(1)}, u32[]{:S(2)}, u32[]{:S(2)}) collective-permute-start(f32[8,256]{1,0:T(8,128)S(1)} %add.17.refs_0_), channel_id=1, source_target_pairs={{0,24},{4,28},{8,16},{12,20},{16,8},{20,12},{24,0},{28,4},{1,25},{... | collective-permute-start | bytes 24584 | tf_op jit(solution)/shard_map/ppermute | solution.py:130
  83.2 6.4 %collective-permute-start.19 = (bf16[2,240,256]{2,1,0:T(8,128)(2,1)S(1)}, bf16[2,240,256]{2,1,0:T(8,128)(2,1)S(1)}, u32[]{:S(2)}, u32[]{:S(2)}) collective-permute-start(bf16[2,240,256]{2,1,0:T(8,128)(2,1)S(1)} %get-tuple-element.67.refs_1_), channel_id=1, source_target_pairs={{0,8},{4,12},{8,0},{12,4},{16,24},{20,28},{24,16},{28,20},{1,9},{5... | collective-permute-start | bytes 737288 | tf_op jit(solution)/shard_map/ppermute | solution.py:130
  83.2 6.4 %collective-permute-start.20 = (bf16[2,240,256]{2,1,0:T(8,128)(2,1)S(1)}, bf16[2,240,256]{2,1,0:T(8,128)(2,1)S(1)}, u32[]{:S(2)}, u32[]{:S(2)}) collective-permute-start(bf16[2,240,256]{2,1,0:T(8,128)(2,1)S(1)} %get-tuple-element.68.refs_4_), channel_id=1, source_target_pairs={{0,4},{4,0},{8,12},{12,8},{16,20},{20,16},{24,28},{28,24},{1,5},{5... | collective-permute-start | bytes 737288 | tf_op jit(solution)/shard_map/ppermute | solution.py:130
  89.7 10.7 %collective-permute-start.22 = (bf16[4,240,256]{2,1,0:T(8,128)(2,1)S(1)}, bf16[4,240,256]{2,1,0:T(8,128)(2,1)S(1)}, u32[]{:S(2)}, u32[]{:S(2)}) collective-permute-start(bf16[4,240,256]{2,1,0:T(8,128)(2,1)S(1)} %pad_maximum_fusion.1), channel_id=1, source_target_pairs={{0,8},{4,12},{8,0},{12,4},{16,24},{20,28},{24,16},{28,20},{1,9},{5... | collective-permute-start | bytes 1474568 | tf_op jit(solution)/shard_map/ppermute | solution.py:130
  91.6 10.2 %collective-permute-start.21 = (bf16[4,240,256]{2,1,0:T(8,128)(2,1)S(1)}, bf16[4,240,256]{2,1,0:T(8,128)(2,1)S(1)}, u32[]{:S(2)}, u32[]{:S(2)}) collective-permute-start(bf16[4,240,256]{2,1,0:T(8,128)(2,1)S(1)} %pad_maximum_fusion), channel_id=1, source_target_pairs={{0,4},{4,0},{8,12},{12,8},{16,20},{20,16},{24,28},{28,24},{1,5},{5... | collective-permute-start | bytes 1474568 | tf_op jit(solution)/shard_map/ppermute | solution.py:130
  (2 other events, 11.7 us)
